TPU v7x, 32 devices: a whole 2x2x4 slice. The times are simulated.
32 devices in a mesh: prompt: 4 (over x, core), resp: 8 (over z, y).
Axes of the slice: x: 2, y: 2, z: 4, core: 2. Of those that a mesh axis runs over, the one named last changes fastest.
Arguments:
- queries: bfloat16 [4, 1024, 8192], P('prompt', 'resp'), may hold values from -6 to 6
- resp_kv: bfloat16 [4, 1024, 2048], P('prompt', 'resp'), may hold values from -6 to 6
- resp_segments: int32 [4, 1024], P('prompt', 'resp'), may hold values from 0 to 1, never falling along the last dimension, each value on 1 to 896 neighbouring positions
- prefix_kv: bfloat16 [128, 8, 2048], P(('prompt', 'resp')), may hold values from -6 to 6
- tile_plan: int32 [128, 2], P(('prompt', 'resp')), may hold values from 0 to 31, as said below
- prompt_lengths: int32 [4], P('prompt'), may hold values from 8 to 256
Outputs:
- attended: bfloat16 [4, 1024, 8192], P('prompt', 'resp')
Inputs may be any that keep to these rules, and one draw needn't show every extreme that they name: `tile_plan`: column 0 is a group in 0 .. 3 and column 1 a place in 0 .. 31; each pair of group and place stands once; the 4 tiles of each device hold one tile of every group, in any order. `resp_segments`: response numbers never fall along a group's tokens; each response has 1 to 896 tokens.
All inputs are finite; a program needn't handle non-finite values.
Results may differ from a plain program's by a relative error of at most 0.0055.
Values may be sent and summed in bfloat16 or wider, within the bound.
No kernel may reach another device: no remote copies, remote signals or barrier semaphores. Data moves between devices by JAX's collectives and lax.ppermute only.
A program may use at most 128 MiB of HBM per device.

v0:
```python
import functools
import math

import jax
import jax.numpy as jnp
from jax import lax
from jax.experimental import pallas as pl
from jax.experimental.pallas import tpu as pltpu
from jax.sharding import PartitionSpec as P

H = 64
KVH = 8
HD = 128
GQ = H // KVH
REACH = 7
STEP = 256
FILL = -1e30
CHUNKS = (2, 2, 2, 2)


def attend_kernel(
    meta_ref, seg_q_ref, seg_k_ref, prefix_bias_ref, q_ref, k_ref, v_ref, pk_ref, pv_ref, *rest
):
    o_ref, s_ref, top_ref, acc_ref, bias_ref = rest[-5:]
    rows = q_ref.shape[0]
    prefix_steps = pk_ref.shape[0] // STEP
    first, last, row0 = meta_ref[0], meta_ref[1], meta_ref[2]
    scale = math.log2(math.e) / math.sqrt(HD)
    nt = (((1,), (1,)), ((), ()))

    @pl.when(pl.program_id(0) == 0)
    def _():
        def fill(step, _):
            start = pl.multiple_of(step * STEP, STEP)
            seg_k = seg_k_ref[:, pl.ds(start, STEP)]
            key_pos = start + lax.broadcasted_iota(jnp.int32, (rows, STEP), 1)
            row_pos = row0 + lax.broadcasted_iota(jnp.int32, (rows, STEP), 0)
            seen = (seg_k == seg_q_ref[...]) & (key_pos <= row_pos)
            bias_ref[step - first] = jnp.where(seen, 0.0, FILL)
            return 0

        lax.fori_loop(first, last + 1, fill, 0)

    q = jnp.concatenate([q_ref[:, g * HD : (g + 1) * HD] for g in range(GQ)], axis=0)

    def scores(keys, bias, slot, fresh):
        s = lax.dot_general(q, keys, nt, preferred_element_type=jnp.float32)
        s = (s.reshape(GQ, -1, STEP) + bias[None]).reshape(-1, STEP)
        s_ref[slot] = s
        top = jnp.maximum(s[:, :HD], s[:, HD:])
        top_ref[...] = top if fresh else jnp.maximum(top_ref[...], top)

    for step in range(prefix_steps):
        at = pl.ds(step * STEP, STEP)
        scores(pk_ref[at, :], prefix_bias_ref[:, at], step, step == 0)

    def score_step(step, _):
        at = pl.ds(pl.multiple_of(step * STEP, STEP), STEP)
        scores(k_ref[at, :], bias_ref[step - first], prefix_steps + step - first, False)
        return 0

    lax.fori_loop(first, last + 1, score_step, 0)
    top = jnp.max(top_ref[...], axis=1, keepdims=True)
    top_ref[...] = jnp.broadcast_to(top, top_ref.shape)
    ones = jnp.ones((STEP, HD), jnp.bfloat16)

    def weigh(values, slot, fresh):
        both = jnp.concatenate([values, ones], axis=1)
        for g in range(GQ):
            at = pl.ds(g * rows, rows)
            s = s_ref[slot, at, :]
            t = top_ref[at, :]
            w = jnp.concatenate(
                [jnp.exp2((s[:, :HD] - t) * scale), jnp.exp2((s[:, HD:] - t) * scale)], axis=1
            )
            add = jnp.dot(w.astype(jnp.bfloat16), both, preferred_element_type=jnp.float32)
            acc_ref[at, :] = add if fresh else acc_ref[at, :] + add

    for step in range(prefix_steps):
        weigh(pv_ref[pl.ds(step * STEP, STEP), :], step, step == 0)

    def weigh_step(step, _):
        at = pl.ds(pl.multiple_of(step * STEP, STEP), STEP)
        weigh(v_ref[at, :], prefix_steps + step - first, False)
        return 0

    lax.fori_loop(first, last + 1, weigh_step, 0)
    for g in range(GQ):
        at = pl.ds(g * rows, rows)
        o_ref[:, g * HD : (g + 1) * HD] = (acc_ref[at, :HD] / acc_ref[at, HD:]).astype(o_ref.dtype)


def attend(meta, seg_q, seg_k, prefix_bias, queries, kv, prefix, out, head0, heads):
    rows = queries.shape[0]
    keys, prefix_keys = kv.shape[0], prefix.shape[0]
    slots = min(-(-keys // STEP), REACH * rows // STEP + 2)
    wide = (rows, GQ * HD)
    in_specs = [
        pl.BlockSpec((rows, 1), lambda i, m: (0, 0)),
        pl.BlockSpec((1, keys), lambda i, m: (0, 0)),
        pl.BlockSpec((1, prefix_keys), lambda i, m: (0, 0)),
        pl.BlockSpec(wide, lambda i, m: (0, head0 + i)),
        pl.BlockSpec((keys, HD), lambda i, m: (0, i)),
        pl.BlockSpec((keys, HD), lambda i, m: (0, heads + i)),
        pl.BlockSpec((prefix_keys, HD), lambda i, m: (0, head0 + i)),
        pl.BlockSpec((prefix_keys, HD), lambda i, m: (0, KVH + head0 + i)),
    ]
    args = [meta, seg_q, seg_k, prefix_bias, queries, kv, kv, prefix, prefix]
    aliases = {}
    if out is not None:
        in_specs.append(pl.BlockSpec(memory_space=pl.ANY))
        args.append(out)
        aliases = {len(args) - 1: 0}
    return pl.pallas_call(
        attend_kernel,
        grid_spec=pltpu.PrefetchScalarGridSpec(
            num_scalar_prefetch=1,
            grid=(heads,),
            in_specs=in_specs,
            out_specs=pl.BlockSpec(wide, lambda i, m: (0, head0 + i)),
            scratch_shapes=[
                pltpu.VMEM((slots + prefix_keys // STEP, GQ * rows, STEP), jnp.float32),
                pltpu.VMEM((GQ * rows, HD), jnp.float32),
                pltpu.VMEM((GQ * rows, 2 * HD), jnp.float32),
                pltpu.VMEM((slots, rows, STEP), jnp.float32),
            ],
        ),
        out_shape=jax.ShapeDtypeStruct(queries.shape, queries.dtype),
        input_output_aliases=aliases,
        compiler_params=pltpu.CompilerParams(vmem_limit_bytes=40 * 1024 * 1024),
    )(*args)


def on_device(queries, resp_kv, resp_segments, prefix_kv, tile_plan, prompt_lengths):
    rows = queries.shape[1]
    split = KVH * HD
    tiles, tile = prefix_kv.shape[:2]
    groups = lax.axis_size("prompt")
    per = tiles // groups
    group = lax.axis_index("prompt")
    block = lax.axis_index("resp")

    owner, place = tile_plan[:, 0], tile_plan[:, 1]
    index = jnp.arange(tiles, dtype=jnp.int32)
    ahead = (owner[None, :] < owner[:, None]) | (
        (owner[None, :] == owner[:, None]) & (index[None, :] < index[:, None])
    )
    rank = jnp.sum(ahead, axis=1, dtype=jnp.int32)
    pick = rank[None, :] == index[:, None]
    sorted_place = jnp.sum(jnp.where(pick, place[None, :], 0), axis=1, dtype=jnp.int32)
    sorted_tiles = jnp.sum(
        jnp.where(pick[:, :, None, None], prefix_kv[None], 0).astype(jnp.float32), axis=1
    ).astype(prefix_kv.dtype)

    ints = jnp.concatenate([resp_segments[0], sorted_place])
    ints = lax.all_gather(ints, ("prompt", "resp"), axis=0, tiled=False)
    ints = ints.reshape(groups, -1, rows + tiles)

    pieces = []
    head = 0
    for heads in CHUNKS:
        k = resp_kv[0, :, head * HD : (head + heads) * HD]
        v = resp_kv[0, :, split + head * HD : split + (head + heads) * HD]
        piece = jnp.concatenate([k, v], axis=1)
        pieces.append((head, heads, lax.all_gather(piece, "resp", axis=0, tiled=True)))
        head += heads
    moved = lax.all_to_all(sorted_tiles, "prompt", split_axis=0, concat_axis=0, tiled=True)
    prefix = lax.all_gather(moved, "resp", axis=0, tiled=True).reshape(-1, 2 * split)

    seg_k = lax.dynamic_index_in_dim(ints, group, 0, keepdims=False)[:, :rows].reshape(1, -1)
    places = lax.dynamic_slice_in_dim(ints, rows + group * per, per, 2)
    places = jnp.transpose(places, (1, 0, 2)).reshape(-1, 1)
    places = places * tile + jnp.arange(tile, dtype=jnp.int32)[None, :]
    prefix_bias = jnp.where(places < prompt_lengths[0], 0.0, FILL).reshape(1, -1)
    seg_q = resp_segments[0][:, None]
    before = jnp.sum(seg_k < resp_segments[0, 0], dtype=jnp.int32)
    row0 = block * rows
    meta = jnp.stack([before // STEP, row0 // STEP, row0])

    out = None
    for head, heads, kv in pieces:
        out = attend(meta, seg_q, seg_k, prefix_bias, queries[0], kv, prefix, out, head, heads)
    return out[None]


def solution(mesh):
    return jax.shard_map(
        on_device,
        mesh=mesh,
        in_specs=(
            P("prompt", "resp", None),
            P("prompt", "resp", None),
            P("prompt", "resp"),
            P(("prompt", "resp"), None, None),
            P(("prompt", "resp"), None),
            P("prompt"),
        ),
        out_specs=P("prompt", "resp", None),
        check_vma=False,
    )
```

profile of v0, /device:TPU:26, one launch (start us, length us, event | category | flops | bytes accessed | tf_op | source)
XLA Modules:
  0.0 227.1 jit_solution(17552656157515450793)
XLA Ops:
  6.5 1.3 slice_bitcast_fusion.1
  7.8 0.7 pad_maximum_fusion.3
  8.5 0.8 slice_bitcast_fusion.9
  9.3 0.2 convert_reduce_fusion.1
  9.5 1.0 select_reduce_fusion
  10.5 6.5 %all_to_all.5 = bf16[4,8,2048]{2,1,0:T(8,128)(2,1)} all-to-all(bf16[4,8,2048]{2,1,0:T(8,128)(2,1)S(1)} %select_reduce_fusion), channel_id=1, replica_groups=mesh['prompt'=4,'resp'=8] {'prompt'}, dimensions={0} | all-to-all | bytes 262144 | tf_op jit(solution)/shard_map/all_to_all | solution.py:167
  17.1 0.7 pad_maximum_fusion.2
  17.9 0.7 pad_maximum_fusion.1
  18.6 0.7 pad_maximum_fusion
  19.3 0.1 select_reduce_fusion.1
  19.4 0.1 add_dynamic-update-slice_fusion
  19.6 40.6 %all-reduce = s32[4224]{0:T(1024)S(1)} all-reduce(s32[4224]{0:T(1024)S(1)} %add_dynamic-update-slice_fusion), channel_id=2, replica_groups=mesh['prompt'=4,'resp'=8] {'prompt','resp'}, use_global_device_ids=true, to_apply=%add | all-reduce | flops 4224 | bytes 33792
  60.2 0.1 reshape.77
  60.4 0.7 fusion.3
  63.4 0.1 multiply_bitcast_fusion
  63.5 0.1 copy.24
  63.6 0.1 mul.24
  64.4 0.1 select_n.43.prefix_bias_ref
  64.5 0.1 copy.28.seg_q_ref
  64.7 25.9 %all-gather.9.cloned.1.call-done = bf16[32,8,2048]{2,1,0:T(8,128)(2,1)} async-done(((bf16[4,8,2048]{2,1,0:T(8,128)(2,1)}), bf16[32,8,2048]{2,1,0:T(8,128)(2,1)}) %all-gather.9.cloned.1.call-update) | async-done | bytes 1048592 | tf_op jit(solution)/shard_map/all_gather | solution.py:168
  90.6 1.2 copy-done
  91.8 1.2 copy-done.3
  93.0 5.8 %shard_map.64.rest_0_ = bf16[128,8192]{1,0:T(8,128)(2,1)} custom-call(s32[3]{0:T(128)S(1)} %pad_add_fusion.meta_ref, s32[128,1]{1,0:T(8,128)S(1)} %copy.28.seg_q_ref, s32[1,1024]{1,0:T(1,128)S(1)} %bitcast.51, f32[1,256]{1,0:T(1,128)S(1)} %select_n.43.prefix_bias_ref, bf16[128,8192]{1,0:T(8,128)(2,1)S(1)} %bitcast.47, bf16[1024,512]{1,0:T(8,128)(2,1)S(1)} %copy-done.3, ...), custom_call_target="tpu_custom_call" | custom-call | tf_op jit(solution)/shard_map/pallas_call | solution.py:114
  98.8 32.8 %all-gather.13.cloned.1.call-done.k_ref.v_ref = bf16[1024,512]{1,0:T(8,128)(2,1)} async-done(((bf16[128,512]{1,0:T(8,128)(2,1)}), bf16[1024,512]{1,0:T(8,128)(2,1)}) %all-gather.13.cloned.1.call-update) | async-done | bytes 1048592 | tf_op jit(solution)/shard_map/all_gather | solution.py:165
  131.6 1.2 copy-done.4
  132.9 5.8 %shard_map.65.rest_0_ = bf16[128,8192]{1,0:T(8,128)(2,1)} custom-call(s32[3]{0:T(128)S(1)} %pad_add_fusion.meta_ref, s32[128,1]{1,0:T(8,128)S(1)} %copy.28.seg_q_ref, s32[1,1024]{1,0:T(1,128)S(1)} %bitcast.52, f32[1,256]{1,0:T(1,128)S(1)} %select_n.43.prefix_bias_ref, bf16[128,8192]{1,0:T(8,128)(2,1)S(1)} %bitcast.48, ...), custom_call_target="tpu_custom_call", output_to_operand_aliasing={{}: (9, {})} | custom-call | tf_op jit(solution)/shard_map/pallas_call | solution.py:114
  138.7 33.9 %all-gather.11.cloned.1.call-done.k_ref.v_ref = bf16[1024,512]{1,0:T(8,128)(2,1)} async-done(((bf16[128,512]{1,0:T(8,128)(2,1)}), bf16[1024,512]{1,0:T(8,128)(2,1)}) %all-gather.11.cloned.1.call-update) | async-done | bytes 1048592 | tf_op jit(solution)/shard_map/all_gather | solution.py:165
  172.6 1.2 copy-done.5
  173.8 5.8 %shard_map.66.rest_0_ = bf16[128,8192]{1,0:T(8,128)(2,1)} custom-call(s32[3]{0:T(128)S(1)} %pad_add_fusion.meta_ref, s32[128,1]{1,0:T(8,128)S(1)} %copy.28.seg_q_ref, s32[1,1024]{1,0:T(1,128)S(1)} %bitcast.53, f32[1,256]{1,0:T(1,128)S(1)} %select_n.43.prefix_bias_ref, bf16[128,8192]{1,0:T(8,128)(2,1)S(1)} %bitcast.49, ...), custom_call_target="tpu_custom_call", output_to_operand_aliasing={{}: (9, {})} | custom-call | tf_op jit(solution)/shard_map/pallas_call | solution.py:114
  179.6 33.9 %all-gather.7.cloned.1.call-done.k_ref.v_ref = bf16[1024,512]{1,0:T(8,128)(2,1)} async-done(((bf16[128,512]{1,0:T(8,128)(2,1)}), bf16[1024,512]{1,0:T(8,128)(2,1)}) %all-gather.7.cloned.1.call-update) | async-done | bytes 1048592 | tf_op jit(solution)/shard_map/all_gather | solution.py:165
  213.5 1.2 copy-done.6
  214.7 5.8 %shard_map.67 = bf16[128,8192]{1,0:T(8,128)(2,1)} custom-call(s32[3]{0:T(128)S(1)} %pad_add_fusion.meta_ref, s32[128,1]{1,0:T(8,128)S(1)} %copy.28.seg_q_ref, s32[1,1024]{1,0:T(1,128)S(1)} %bitcast.54, f32[1,256]{1,0:T(1,128)S(1)} %select_n.43.prefix_bias_ref, bf16[128,8192]{1,0:T(8,128)(2,1)S(1)} %bitcast.50, ...), custom_call_target="tpu_custom_call", output_to_operand_aliasing={{}: (9, {})} | custom-call | tf_op jit(solution)/shard_map/pallas_call | solution.py:114
  (27 shorter events, 0.4 us)
Async XLA Ops:
  6.5 12.9 %copy-start.7 = (s32[1,128]{1,0:T(1,128)S(1)}, s32[1,128]{1,0:T(1,128)}, u32[]{:S(2)}) copy-start(s32[1,128]{1,0:T(1,128)} %param.8) | copy-start | bytes 1540
  6.5 84.0 %copy-start.2 = (bf16[1,128,8192]{2,1,0:T(8,128)(2,1)S(1)}, bf16[1,128,8192]{2,1,0:T(8,128)(2,1)}, u32[]{:S(2)}) copy-start(bf16[1,128,8192]{2,1,0:T(8,128)(2,1)} %param.6) | copy-start | bytes 6291460
  6.5 58.2 %all-gather.15.cloned.1.call-start = ((), (), s32[]{:S(2)}) async-start(), calls=%async_computation.5 | async-start | bytes 1179648 | tf_op jit(solution)/shard_map/all_gather | solution.py:165
  8.5 82.1 %all-gather.9.cloned.1.call-start = ((), (), s32[]{:S(2)}) async-start(), calls=%async_computation.2 | async-start | bytes 1179648 | tf_op jit(solution)/shard_map/all_gather | solution.py:168
  17.1 114.5 %all-gather.13.cloned.1.call-start = ((), (), s32[]{:S(2)}) async-start(), calls=%async_computation.4 | async-start | bytes 1179648 | tf_op jit(solution)/shard_map/all_gather | solution.py:165
  17.8 154.7 %all-gather.11.cloned.1.call-start = ((), (), s32[]{:S(2)}) async-start(), calls=%async_computation.3 | async-start | bytes 1179648 | tf_op jit(solution)/shard_map/all_gather | solution.py:165
  18.6 194.9 %all-gather.7.cloned.1.call-start = ((), (), s32[]{:S(2)}) async-start(), calls=%async_computation.1 | async-start | bytes 1179648 | tf_op jit(solution)/shard_map/all_gather | solution.py:165
  90.6 1.2 copy-start
  91.8 1.2 copy-start.3
  93.0 38.6 %copy-start.1 = (bf16[32,8,2048]{2,1,0:T(8,128)(2,1)S(1)}, bf16[32,8,2048]{2,1,0:T(8,128)(2,1)}, u32[]{:S(2)}) copy-start(bf16[32,8,2048]{2,1,0:T(8,128)(2,1)} %all-gather.9.cloned.1.call-done) | copy-start | bytes 3145732
  131.6 1.2 copy-start.4
  172.6 1.2 copy-start.5
  213.5 1.2 copy-start.6
Sparse Core Ops, SparseCore 0:
  9.5 39.9 all-gather.14
  51.6 38.9 all-gather.8
  92.7 38.8 all-gather.12
  133.6 38.8 all-gather.10
  174.5 38.8 all-gather.6
where the time goes:
time: 230 us; the launch traced here: 227 us
  waiting for transfers between devices  126 us (55%)
  blocking collectives  47.2 us (21%)
  Pallas kernels  23.3 us (10%)
  between operations  16.2 us (7%)
  local copies, waits for them, and re-layouts  8.71 us (4%)
  other arithmetic  5.02 us (2%)
    all_gather x4, waiting for transfers between devices, on_device(): lax.all_gather(piece, 'resp', axis=0, tiled=True)  101 us
    unnamed x1, blocking collectives  40.6 us
    all_gather x1, waiting for transfers between devices, on_device(): lax.all_gather(moved, 'resp', axis=0, tiled=True).reshape(-1, 2 * split)  25.9 us
    pallas_call x4, Pallas kernels, attend(): pl.pallas_call(attend_kernel, grid_spec=pltpu.PrefetchScalarGridSpec(num_...  23.3 us
    all_to_all x1, blocking collectives, on_device(): lax.all_to_all(sorted_tiles, 'prompt', split_axis=0, concat_axis=0, tiled...  6.54 us
    unnamed x17, local copies, waits for them, and re-layouts  6.14 us
  transfers between devices with their start and end apart: 5, of which 4 were waited for; matrix products, arithmetic and copies ran while one was open for 2% of the time, Pallas kernels for 8%

commit v1 on v0

v1 whole, which is shorter than its diff:
```python
import functools
import math

import jax
import jax.numpy as jnp
from jax import lax
from jax.experimental import pallas as pl
from jax.experimental.pallas import tpu as pltpu
from jax.sharding import PartitionSpec as P

H = 64
KVH = 8
HD = 128
GQ = H // KVH
REACH = 7
STEP = 256
FILL = -1e30
CHUNKS = 1


def attend_kernel(pairs, meta_ref, seg_q_ref, seg_k_ref, prefix_bias_ref, q_ref, pk_ref, pv_ref, *rest):
    k_refs, v_refs = rest[:pairs], rest[pairs : 2 * pairs]
    o_ref, s_ref, top_ref, acc_ref, bias_ref = rest[-5:]
    rows = q_ref.shape[0]
    span = k_refs[0].shape[0]
    prefix_steps = pk_ref.shape[0] // STEP
    own_pair, reach, row0 = meta_ref[0], meta_ref[1], meta_ref[2]
    scale = math.log2(math.e) / math.sqrt(HD)
    nt = (((1,), (1,)), ((), ()))

    def each_pair(body):
        for k in range(pairs):
            pl.when(k <= reach)(functools.partial(body, k))

    @pl.when(pl.program_id(0) == 0)
    def _():
        def fill(k):
            start = pl.multiple_of((own_pair - k) * span, span)
            seg_k = seg_k_ref[:, pl.ds(start, span)]
            key_pos = start + lax.broadcasted_iota(jnp.int32, (rows, span), 1)
            row_pos = row0 + lax.broadcasted_iota(jnp.int32, (rows, span), 0)
            seen = (seg_k == seg_q_ref[...]) & (key_pos <= row_pos)
            bias_ref[k] = jnp.where(seen, 0.0, FILL)

        each_pair(fill)

    q = jnp.concatenate([q_ref[:, g * HD : (g + 1) * HD] for g in range(GQ)], axis=0)

    def scores(keys, bias, slot, fresh):
        s = lax.dot_general(q, keys, nt, preferred_element_type=jnp.float32)
        s = (s.reshape(GQ, rows, -1) + bias[None]).reshape(GQ * rows, -1)
        s_ref[slot] = s
        top = jnp.maximum(s[:, :HD], s[:, HD:])
        top_ref[...] = top if fresh else jnp.maximum(top_ref[...], top)

    for step in range(prefix_steps):
        at = pl.ds(step * STEP, STEP)
        scores(pk_ref[at, :], prefix_bias_ref[:, at], step, step == 0)
    each_pair(lambda k: scores(k_refs[k][...], bias_ref[k], prefix_steps + k, False))

    top = jnp.max(top_ref[...], axis=1, keepdims=True)
    top_ref[...] = jnp.broadcast_to(top, top_ref.shape)

    def weigh(values, slot, fresh):
        both = jnp.concatenate([values, jnp.ones((values.shape[0], HD), values.dtype)], axis=1)
        for g in range(GQ):
            at = pl.ds(g * rows, rows)
            s = s_ref[slot, at, :]
            t = top_ref[at, :]
            w = jnp.concatenate(
                [jnp.exp2((s[:, :HD] - t) * scale), jnp.exp2((s[:, HD:] - t) * scale)], axis=1
            )
            add = jnp.dot(w.astype(jnp.bfloat16), both, preferred_element_type=jnp.float32)
            acc_ref[at, :] = add if fresh else acc_ref[at, :] + add

    for step in range(prefix_steps):
        weigh(pv_ref[pl.ds(step * STEP, STEP), :], step, step == 0)
    each_pair(lambda k: weigh(v_refs[k][...], prefix_steps + k, False))
    for g in range(GQ):
        at = pl.ds(g * rows, rows)
        o_ref[:, g * HD : (g + 1) * HD] = (acc_ref[at, :HD] / acc_ref[at, HD:]).astype(o_ref.dtype)


def attend(meta, seg_q, seg_k, prefix_bias, queries, pieces, prefix, out):
    rows = queries.shape[0]
    prefix_keys = prefix.shape[0]
    pairs, span = len(pieces), pieces[0].shape[0]
    heads = pieces[0].shape[1] // (2 * HD)
    wide = (rows, GQ * HD)
    in_specs = [
        pl.BlockSpec((rows, 1), lambda i, m: (0, 0)),
        pl.BlockSpec(seg_k.shape, lambda i, m: (0, 0)),
        pl.BlockSpec((1, prefix_keys), lambda i, m: (0, 0)),
        pl.BlockSpec(wide, lambda i, m: (0, m[3] + i)),
        pl.BlockSpec((prefix_keys, HD), lambda i, m: (0, m[3] + i)),
        pl.BlockSpec((prefix_keys, HD), lambda i, m: (0, KVH + m[3] + i)),
        *[pl.BlockSpec((span, HD), lambda i, m: (0, i))] * pairs,
        *[pl.BlockSpec((span, HD), lambda i, m: (0, heads + i))] * pairs,
    ]
    args = [meta, seg_q, seg_k, prefix_bias, queries, prefix, prefix, *pieces, *pieces]
    aliases = {}
    if out is not None:
        in_specs.append(pl.BlockSpec(memory_space=pl.ANY))
        args.append(out)
        aliases = {len(args) - 1: 0}
    return pl.pallas_call(
        functools.partial(attend_kernel, pairs),
        grid_spec=pltpu.PrefetchScalarGridSpec(
            num_scalar_prefetch=1,
            grid=(heads,),
            in_specs=in_specs,
            out_specs=pl.BlockSpec(wide, lambda i, m: (0, m[3] + i)),
            scratch_shapes=[
                pltpu.VMEM((pairs + prefix_keys // STEP, GQ * rows, span), jnp.float32),
                pltpu.VMEM((GQ * rows, HD), jnp.float32),
                pltpu.VMEM((GQ * rows, 2 * HD), jnp.float32),
                pltpu.VMEM((pairs, rows, span), jnp.float32),
            ],
        ),
        out_shape=jax.ShapeDtypeStruct(queries.shape, queries.dtype),
        input_output_aliases=aliases,
        compiler_params=pltpu.CompilerParams(vmem_limit_bytes=40 * 1024 * 1024),
    )(*args)


def on_device(queries, resp_kv, resp_segments, prefix_kv, tile_plan, prompt_lengths):
    rows = queries.shape[1]
    split = KVH * HD
    tiles, tile = prefix_kv.shape[:2]
    groups, count = lax.axis_size("prompt"), lax.axis_size("resp")
    per = tiles // groups
    group = lax.axis_index("prompt")
    block = lax.axis_index("resp")
    side = block % 2
    steps = min(count // 2 - 1, (REACH + 1) // 2)
    heads = KVH // 2 // CHUNKS

    def part(owner, chunk):
        head = (owner * (KVH // 2) + chunk * heads) * HD
        k = lax.dynamic_slice_in_dim(resp_kv[0], head, heads * HD, 1)
        v = lax.dynamic_slice_in_dim(resp_kv[0], split + head, heads * HD, 1)
        return jnp.concatenate([k, v], axis=1)

    def swap(value, first):
        return lax.ppermute(value, "resp", [(r, r ^ 1) for r in range(2 * first, count)])

    def pair_of(own, other):
        return jnp.where(
            side == 0, jnp.concatenate([own, other]), jnp.concatenate([other, own])
        )

    straight, crossed = [], []
    for chunk in range(CHUNKS):
        mine, theirs = part(side, chunk), part(1 - side, chunk)
        straight.append([pair_of(mine, swap(theirs, 0))])
        upper = lax.ppermute(mine, "resp", [(r, r + 1) for r in range(0, count, 2)])
        crossed.append([pair_of(theirs, upper)])
    for step in range(1, steps + 1):
        for chunk in range(CHUNKS):
            moved = lax.ppermute(
                straight[chunk][-1], "resp", [(r, r + 2) for r in range(2 * step - 2, count - 2)]
            )
            straight[chunk].append(moved)
            crossed[chunk].append(swap(moved, step))

    owner, place = tile_plan[:, 0], tile_plan[:, 1]
    index = jnp.arange(tiles, dtype=jnp.int32)
    ahead = (owner[None, :] < owner[:, None]) | (
        (owner[None, :] == owner[:, None]) & (index[None, :] < index[:, None])
    )
    rank = jnp.sum(ahead, axis=1, dtype=jnp.int32)
    pick = rank[None, :] == index[:, None]
    sorted_place = jnp.sum(jnp.where(pick, place[None, :], 0), axis=1, dtype=jnp.int32)
    sorted_tiles = jnp.sum(
        jnp.where(pick[:, :, None, None], prefix_kv[None], 0).astype(jnp.float32), axis=1
    ).astype(prefix_kv.dtype)

    ints = jnp.concatenate([resp_segments[0], sorted_place])
    ints = jnp.broadcast_to(ints[None], (groups * count, rows + tiles))
    ints = lax.all_to_all(ints, ("prompt", "resp"), split_axis=0, concat_axis=0, tiled=True)
    ints = ints.reshape(groups, count, rows + tiles)
    moved = lax.all_to_all(sorted_tiles, "prompt", split_axis=0, concat_axis=0, tiled=True)
    prefix = lax.all_gather(moved, "resp", axis=0, tiled=True).reshape(-1, 2 * split)

    seg_k = lax.dynamic_index_in_dim(ints, group, 0, keepdims=False)[:, :rows].reshape(1, -1)
    places = lax.dynamic_slice_in_dim(ints, rows + group * per, per, 2)
    places = jnp.transpose(places, (1, 0, 2)).reshape(-1, 1)
    places = places * tile + jnp.arange(tile, dtype=jnp.int32)[None, :]
    prefix_bias = jnp.where(places < prompt_lengths[0], 0.0, FILL).reshape(1, -1)
    seg_q = resp_segments[0][:, None]
    before = jnp.sum(seg_k < resp_segments[0, 0], dtype=jnp.int32)
    own_pair = block // 2

    out = None
    for pieces_of, owner_side in ((straight, side), (crossed, 1 - side)):
        for chunk in range(CHUNKS):
            head0 = owner_side * (KVH // 2) + chunk * heads
            meta = jnp.stack([own_pair, own_pair - before // (2 * rows), block * rows, head0])
            out = attend(
                meta, seg_q, seg_k, prefix_bias, queries[0], pieces_of[chunk], prefix, out
            )
    return out[None]


def solution(mesh):
    return jax.shard_map(
        on_device,
        mesh=mesh,
        in_specs=(
            P("prompt", "resp", None),
            P("prompt", "resp", None),
            P("prompt", "resp"),
            P(("prompt", "resp"), None, None),
            P(("prompt", "resp"), None),
            P("prompt"),
        ),
        out_specs=P("prompt", "resp", None),
        check_vma=False,
    )
```

time: 230 us -> 119 us (0.52)
  waiting for transfers between devices: 126 us -> 32.4 us
  blocking collectives: 47.2 us -> 6.54 us
  starting transfers between devices: 0.17 us -> 26.2 us
  local copies, waits for them, and re-layouts: 8.71 us -> 4.19 us
  Pallas kernels: 23.3 us -> 26.7 us
    all_gather x4 -> x0, waiting for transfers between devices: 101 us -> none  [on_device(): lax.all_gather(piece, 'resp', axis=0, tiled=True)]
    unnamed x1 -> x0, blocking collectives: 40.6 us -> none
    ppermute x0 -> x8, waiting for transfers between devices: none -> 32.3 us  [the longest x3 23.8 us: on_device(): lax.ppermute(straight[chunk][-1], 'resp', [(r, r + 2) for r in range(2 *...]
    all_gather x1, waiting for transfers between devices: 25.9 us -> 0.02 us  [on_device(): lax.all_gather(moved, 'resp', axis=0, tiled=True).reshape(-1, 2 * split)]
    ppermute x0 -> x8, starting transfers between devices: none -> 19.1 us  [the longest x4 11.1 us: swap(): lax.ppermute(value, 'resp', [(r, r ^ 1) for r in range(2 * first, count)])]
    all_to_all x0 -> x1, starting transfers between devices: none -> 7.04 us  [on_device(): lax.all_to_all(ints, ('prompt', 'resp'), split_axis=0, concat_axis=0, til...]
    unnamed x17 -> x9, local copies, waits for them, and re-layouts: 6.14 us -> 1.24 us
    pallas_call x4 -> x2, Pallas kernels: 23.3 us -> 26.7 us  [attend(): pl.pallas_call(functools.partial(attend_kernel, pairs), grid_spec=pltpu.P...]
  transfers between devices with their start and end apart: 5 -> 10, of which waited for: 4 -> 5; matrix products, arithmetic and copies ran while one was open for 2% -> 5% of each run, Pallas kernels for 8% -> 11%
where the time goes in v1:
time: 119 us; the launch traced here: 118 us
  waiting for transfers between devices  32.4 us (27%)
  Pallas kernels  26.7 us (22%)
  starting transfers between devices  26.2 us (22%)
  between operations  16.8 us (14%)
  blocking collectives  6.54 us (5%)
  other arithmetic  4.75 us (4%)
  local copies, waits for them, and re-layouts  4.19 us (4%)
    pallas_call x2, Pallas kernels, attend(): pl.pallas_call(functools.partial(attend_kernel, pairs), grid_spec=pltpu.P...  26.7 us
    ppermute x3, waiting for transfers between devices, on_device(): lax.ppermute(straight[chunk][-1], 'resp', [(r, r + 2) for r in range(2 *...  23.8 us
    ppermute x4, starting transfers between devices, swap(): lax.ppermute(value, 'resp', [(r, r ^ 1) for r in range(2 * first, count)])  11.1 us
    ppermute x4, waiting for transfers between devices, swap(): lax.ppermute(value, 'resp', [(r, r ^ 1) for r in range(2 * first, count)])  8.56 us
    all_to_all x1, starting transfers between devices, on_device(): lax.all_to_all(ints, ('prompt', 'resp'), split_axis=0, concat_axis=0, til...  7.04 us
    all_to_all x1, blocking collectives, on_device(): lax.all_to_all(sorted_tiles, 'prompt', split_axis=0, concat_axis=0, tiled...  6.54 us
    ppermute x1, starting transfers between devices, on_device(): upper = lax.ppermute(mine, 'resp', [(r, r + 1) for r in range(0, count, 2)])  4.13 us
    ppermute x3, starting transfers between devices, on_device(): lax.ppermute(straight[chunk][-1], 'resp', [(r, r + 2) for r in range(2 *...  3.85 us
  transfers between devices with their start and end apart: 10, of which 5 were waited for; matrix products, arithmetic and copies ran while one was open for 5% of the time, Pallas kernels for 11%

profile of v1, /device:TPU:26, one launch (start us, length us, event | category | flops | bytes accessed | tf_op | source)
XLA Modules:
  0.0 117.5 jit_solution(5371334293904000277)
XLA Ops:
  6.5 1.1 dynamic-slice_bitcast_fusion.3
  7.7 1.6 %collective-permute-start.1 = (bf16[128,1024]{1,0:T(8,128)(2,1)S(1)}, bf16[128,1024]{1,0:T(8,128)(2,1)}, u32[]{:S(2)}, u32[]{:S(2)}) collective-permute-start(bf16[128,1024]{1,0:T(8,128)(2,1)S(1)} %pad_maximum_fusion), channel_id=1, source_target_pairs={{0,1},{1,0},{2,3},{3,2},{4,5},{5,4},{6,7},{7,6},{8,9},{9,8},{10,11... | collective-permute-start | bytes 786440 | tf_op jit(solution)/shard_map/ppermute | solution.py:145
  9.3 0.8 slice_bitcast_fusion.1
  10.1 5.9 %collective-permute-done.1 = bf16[128,1024]{1,0:T(8,128)(2,1)} collective-permute-done((bf16[128,1024]{1,0:T(8,128)(2,1)S(1)}, bf16[128,1024]{1,0:T(8,128)(2,1)}, u32[]{:S(2)}, u32[]{:S(2)}) %collective-permute-start.1) | collective-permute-done | bytes 262176 | tf_op jit(solution)/shard_map/ppermute | solution.py:145
  15.9 1.2 %maximum_select_fusion.1.rest_0_.rest_4_ = bf16[256,1024]{1,0:T(8,128)(2,1)S(1)} fusion(bf16[128,1024]{1,0:T(8,128)(2,1)} %collective-permute-done.1, bf16[128,512]{1,0:T(8,128)(2,1)S(1)} %get-tuple-element.9, bf16[128,512]{1,0:T(8,128)(2,1)S(1)} %get-tuple-element.10, pred[]{:T(512)S(6)} %eq.17), kind=kLoop, calls=%fused_computation.1 | loop fusion | flops 3407872 | bytes 1048577 | tf_op jit(solution)/shard_map/jit(_where)/select_n | solution.py:148
  17.1 1.3 %collective-permute-start.2 = (bf16[256,1024]{1,0:T(8,128)(2,1)S(1)}, bf16[256,1024]{1,0:T(8,128)(2,1)}, u32[]{:S(2)}, u32[]{:S(2)}) collective-permute-start(bf16[256,1024]{1,0:T(8,128)(2,1)S(1)} %maximum_select_fusion.1.rest_0_.rest_4_), channel_id=1, source_target_pairs={{0,2},{1,3},{2,4},{3,5},{4,6},{5,7},{8,10},{9,11},{10,12},{11,13},... | collective-permute-start | bytes 1572872 | tf_op jit(solution)/shard_map/ppermute | solution.py:160
  18.4 0.2 convert_reduce_fusion.1
  18.6 1.0 select_reduce_fusion
  19.7 6.5 %all_to_all.11 = bf16[4,8,2048]{2,1,0:T(8,128)(2,1)} all-to-all(bf16[4,8,2048]{2,1,0:T(8,128)(2,1)S(1)} %select_reduce_fusion), channel_id=1, replica_groups=mesh['prompt'=4,'resp'=8] {'prompt'}, dimensions={0} | all-to-all | bytes 262144 | tf_op jit(solution)/shard_map/all_to_all | solution.py:182
  26.2 5.7 %collective-permute-done.2.rest_1_.rest_5_ = bf16[256,1024]{1,0:T(8,128)(2,1)} collective-permute-done((bf16[256,1024]{1,0:T(8,128)(2,1)S(1)}, bf16[256,1024]{1,0:T(8,128)(2,1)}, u32[]{:S(2)}, u32[]{:S(2)}) %collective-permute-start.2) | collective-permute-done | bytes 524320 | tf_op jit(solution)/shard_map/ppermute | solution.py:160
  31.9 1.3 %collective-permute-start.4 = (bf16[256,1024]{1,0:T(8,128)(2,1)}, bf16[256,1024]{1,0:T(8,128)(2,1)}, u32[]{:S(2)}, u32[]{:S(2)}) collective-permute-start(bf16[256,1024]{1,0:T(8,128)(2,1)} %collective-permute-done.2.rest_1_.rest_5_), channel_id=1, source_target_pairs={{2,4},{3,5},{4,6},{5,7},{10,12},{11,13},{12,14},{13,15},{18,20},{1... | collective-permute-start | bytes 1572872 | tf_op jit(solution)/shard_map/ppermute | solution.py:160
  33.2 0.1 select_reduce_fusion.1
  33.4 0.6 broadcast_in_dim.61
  34.0 7.0 %all-to-all-start = ((s32[32,1,132]{2,1,0:T(1,128)}), s32[32,1,132]{2,1,0:T(1,128)S(1)}, u32[]{:S(2)}, u32[]{:S(2)}) async-start(s32[32,1,132]{2,1,0:T(1,128)} %broadcast_in_dim.61), calls=%async_computation | async-start | bytes 65536 | tf_op jit(solution)/shard_map/all_to_all | solution.py:180
  41.0 9.5 %collective-permute-done.4.rest_2_.rest_6_ = bf16[256,1024]{1,0:T(8,128)(2,1)} collective-permute-done((bf16[256,1024]{1,0:T(8,128)(2,1)}, bf16[256,1024]{1,0:T(8,128)(2,1)}, u32[]{:S(2)}, u32[]{:S(2)}) %collective-permute-start.4) | collective-permute-done | bytes 524320 | tf_op jit(solution)/shard_map/ppermute | solution.py:160
  50.6 1.3 %collective-permute-start.6 = (bf16[256,1024]{1,0:T(8,128)(2,1)}, bf16[256,1024]{1,0:T(8,128)(2,1)}, u32[]{:S(2)}, u32[]{:S(2)}) collective-permute-start(bf16[256,1024]{1,0:T(8,128)(2,1)} %collective-permute-done.4.rest_2_.rest_6_), channel_id=1, source_target_pairs={{4,6},{5,7},{12,14},{13,15},{20,22},{21,23},{28,30},{29,31}} | collective-permute-start | bytes 1572872 | tf_op jit(solution)/shard_map/ppermute | solution.py:160
  51.9 4.1 %collective-permute-start = (bf16[128,1024]{1,0:T(8,128)(2,1)S(1)}, bf16[128,1024]{1,0:T(8,128)(2,1)}, u32[]{:S(2)}, u32[]{:S(2)}) collective-permute-start(bf16[128,1024]{1,0:T(8,128)(2,1)S(1)} %pad_maximum_fusion.1), channel_id=1, source_target_pairs={{0,1},{2,3},{4,5},{6,7},{8,9},{10,11},{12,13},{14,15},{16,17},{18,... | collective-permute-start | bytes 786440 | tf_op jit(solution)/shard_map/ppermute | solution.py:156
  56.7 0.1 copy.18.seg_q_ref
  56.8 0.1 multiply_bitcast_fusion
  56.9 0.1 copy.16
  57.0 0.1 mul.40
  57.2 1.9 %collective-permute-start.3 = (bf16[256,1024]{1,0:T(8,128)(2,1)}, bf16[256,1024]{1,0:T(8,128)(2,1)}, u32[]{:S(2)}, u32[]{:S(2)}) collective-permute-start(bf16[256,1024]{1,0:T(8,128)(2,1)} %collective-permute-done.2.rest_1_.rest_5_), channel_id=1, source_target_pairs={{2,3},{3,2},{4,5},{5,4},{6,7},{7,6},{10,11},{11,10},{12,13},{13,12... | collective-permute-start | bytes 1572872 | tf_op jit(solution)/shard_map/ppermute | solution.py:145
  59.1 3.9 %collective-permute-start.5 = (bf16[256,1024]{1,0:T(8,128)(2,1)}, bf16[256,1024]{1,0:T(8,128)(2,1)}, u32[]{:S(2)}, u32[]{:S(2)}) collective-permute-start(bf16[256,1024]{1,0:T(8,128)(2,1)} %collective-permute-done.4.rest_2_.rest_6_), channel_id=1, source_target_pairs={{4,5},{5,4},{6,7},{7,6},{12,13},{13,12},{14,15},{15,14},{20,21},{2... | collective-permute-start | bytes 1572872 | tf_op jit(solution)/shard_map/ppermute | solution.py:145
  63.0 8.6 %collective-permute-done.6.rest_3_.rest_7_ = bf16[256,1024]{1,0:T(8,128)(2,1)} collective-permute-done((bf16[256,1024]{1,0:T(8,128)(2,1)}, bf16[256,1024]{1,0:T(8,128)(2,1)}, u32[]{:S(2)}, u32[]{:S(2)}) %collective-permute-start.6) | collective-permute-done | bytes 524320 | tf_op jit(solution)/shard_map/ppermute | solution.py:160
  71.6 3.7 %collective-permute-start.7 = (bf16[256,1024]{1,0:T(8,128)(2,1)}, bf16[256,1024]{1,0:T(8,128)(2,1)}, u32[]{:S(2)}, u32[]{:S(2)}) collective-permute-start(bf16[256,1024]{1,0:T(8,128)(2,1)} %collective-permute-done.6.rest_3_.rest_7_), channel_id=1, source_target_pairs={{6,7},{7,6},{14,15},{15,14},{22,23},{23,22},{30,31},{31,30}} | collective-permute-start | bytes 1572872 | tf_op jit(solution)/shard_map/ppermute | solution.py:145
  75.3 0.7 fusion.3
  78.7 0.1 select_n.75.prefix_bias_ref
  78.9 1.2 %maximum_select_fusion.rest_0_.rest_4_ = bf16[256,1024]{1,0:T(8,128)(2,1)S(1)} fusion(bf16[128,1024]{1,0:T(8,128)(2,1)} %collective-permute-done, bf16[128,512]{1,0:T(8,128)(2,1)S(1)} %get-tuple-element.8, bf16[128,512]{1,0:T(8,128)(2,1)S(1)} %get-tuple-element.7, pred[]{:T(512)S(6)} %eq.17), kind=kLoop, calls=%fused_computation | loop fusion | flops 3407872 | bytes 1048577 | tf_op jit(solution)/shard_map/jit(_where)/select_n | solution.py:148
  80.1 1.2 %copy-done = bf16[32,8,2048]{2,1,0:T(8,128)(2,1)S(1)} copy-done((bf16[32,8,2048]{2,1,0:T(8,128)(2,1)S(1)}, bf16[32,8,2048]{2,1,0:T(8,128)(2,1)}, u32[]{:S(2)}) %copy-start) | copy-done | bytes 1048600
  81.3 13.3 %shard_map.64.rest_8_ = bf16[128,8192]{1,0:T(8,128)(2,1)} custom-call(s32[4]{0:T(128)S(1)} %get-tuple-element.5.meta_ref, s32[128,1]{1,0:T(8,128)S(1)} %copy.18.seg_q_ref, s32[1,1024]{1,0:T(1,128)S(1)} %bitcast.42, f32[1,256]{1,0:T(1,128)S(1)} %select_n.75.prefix_bias_ref, bf16[128,8192]{1,0:T(8,128)(2,1)S(1)} %bitcast.40, bf16[256,2048]{1,0:T(8,128)(2,1)S(1)} %bitcast.36, ...), custom_call_target="tpu_custom_call" | custom-call | tf_op jit(solution)/shard_map/pallas_call | solution.py:106
  94.7 2.7 %collective-permute-done.7.rest_3_.rest_7_ = bf16[256,1024]{1,0:T(8,128)(2,1)} collective-permute-done((bf16[256,1024]{1,0:T(8,128)(2,1)}, bf16[256,1024]{1,0:T(8,128)(2,1)}, u32[]{:S(2)}, u32[]{:S(2)}) %collective-permute-start.7) | collective-permute-done | bytes 524320 | tf_op jit(solution)/shard_map/ppermute | solution.py:145
  97.3 13.3 %shard_map.65 = bf16[128,8192]{1,0:T(8,128)(2,1)} custom-call(s32[4]{0:T(128)S(1)} %pad_add_fusion.1.meta_ref, s32[128,1]{1,0:T(8,128)S(1)} %copy.18.seg_q_ref, s32[1,1024]{1,0:T(1,128)S(1)} %bitcast.43, f32[1,256]{1,0:T(1,128)S(1)} %select_n.75.prefix_bias_ref, bf16[128,8192]{1,0:T(8,128)(2,1)S(1)} %bitcast.41, ...), custom_call_target="tpu_custom_call", output_to_operand_aliasing={{}: (15, {})} | custom-call | tf_op jit(solution)/shard_map/pallas_call | solution.py:106
  (23 shorter events, 0.4 us)
Async XLA Ops:
  6.5 26.8 %copy-start.3 = (s32[1,128]{1,0:T(1,128)S(1)}, s32[1,128]{1,0:T(1,128)}, u32[]{:S(2)}) copy-start(s32[1,128]{1,0:T(1,128)} %param.8) | copy-start | bytes 1540
  6.5 73.5 %all-gather.2.cloned.1.call-start = ((), (), s32[]{:S(2)}) async-start(), calls=%async_computation.2 | async-start | bytes 1179648 | tf_op jit(solution)/shard_map/all_gather | solution.py:183
  7.7 72.4 %copy-start.2 = (bf16[1,128,8192]{2,1,0:T(8,128)(2,1)S(1)}, bf16[1,128,8192]{2,1,0:T(8,128)(2,1)}, u32[]{:S(2)}) copy-start(bf16[1,128,8192]{2,1,0:T(8,128)(2,1)} %param.6) | copy-start | bytes 6291460
  7.7 8.2 %collective-permute-start.1 = (bf16[128,1024]{1,0:T(8,128)(2,1)S(1)}, bf16[128,1024]{1,0:T(8,128)(2,1)}, u32[]{:S(2)}, u32[]{:S(2)}) collective-permute-start(bf16[128,1024]{1,0:T(8,128)(2,1)S(1)} %pad_maximum_fusion), channel_id=1, source_target_pairs={{0,1},{1,0},{2,3},{3,2},{4,5},{5,4},{6,7},{7,6},{8,9},{9,8},{10,11... | collective-permute-start | bytes 786440 | tf_op jit(solution)/shard_map/ppermute | solution.py:145
  17.1 14.8 %collective-permute-start.2 = (bf16[256,1024]{1,0:T(8,128)(2,1)S(1)}, bf16[256,1024]{1,0:T(8,128)(2,1)}, u32[]{:S(2)}, u32[]{:S(2)}) collective-permute-start(bf16[256,1024]{1,0:T(8,128)(2,1)S(1)} %maximum_select_fusion.1.rest_0_.rest_4_), channel_id=1, source_target_pairs={{0,2},{1,3},{2,4},{3,5},{4,6},{5,7},{8,10},{9,11},{10,12},{11,13},... | collective-permute-start | bytes 1572872 | tf_op jit(solution)/shard_map/ppermute | solution.py:160
  31.9 18.6 %collective-permute-start.4 = (bf16[256,1024]{1,0:T(8,128)(2,1)}, bf16[256,1024]{1,0:T(8,128)(2,1)}, u32[]{:S(2)}, u32[]{:S(2)}) collective-permute-start(bf16[256,1024]{1,0:T(8,128)(2,1)} %collective-permute-done.2.rest_1_.rest_5_), channel_id=1, source_target_pairs={{2,4},{3,5},{4,6},{5,7},{10,12},{11,13},{12,14},{13,15},{18,20},{1... | collective-permute-start | bytes 1572872 | tf_op jit(solution)/shard_map/ppermute | solution.py:160
  34.0 22.8 %all-to-all-start = ((s32[32,1,132]{2,1,0:T(1,128)}), s32[32,1,132]{2,1,0:T(1,128)S(1)}, u32[]{:S(2)}, u32[]{:S(2)}) async-start(s32[32,1,132]{2,1,0:T(1,128)} %broadcast_in_dim.61), calls=%async_computation | async-start | bytes 65536 | tf_op jit(solution)/shard_map/all_to_all | solution.py:180
  50.6 21.0 %collective-permute-start.6 = (bf16[256,1024]{1,0:T(8,128)(2,1)}, bf16[256,1024]{1,0:T(8,128)(2,1)}, u32[]{:S(2)}, u32[]{:S(2)}) collective-permute-start(bf16[256,1024]{1,0:T(8,128)(2,1)} %collective-permute-done.4.rest_2_.rest_6_), channel_id=1, source_target_pairs={{4,6},{5,7},{12,14},{13,15},{20,22},{21,23},{28,30},{29,31}} | collective-permute-start | bytes 1572872 | tf_op jit(solution)/shard_map/ppermute | solution.py:160
  51.9 27.0 %collective-permute-start = (bf16[128,1024]{1,0:T(8,128)(2,1)S(1)}, bf16[128,1024]{1,0:T(8,128)(2,1)}, u32[]{:S(2)}, u32[]{:S(2)}) collective-permute-start(bf16[128,1024]{1,0:T(8,128)(2,1)S(1)} %pad_maximum_fusion.1), channel_id=1, source_target_pairs={{0,1},{2,3},{4,5},{6,7},{8,9},{10,11},{12,13},{14,15},{16,17},{18,... | collective-permute-start | bytes 786440 | tf_op jit(solution)/shard_map/ppermute | solution.py:156
  57.2 37.5 %collective-permute-start.3 = (bf16[256,1024]{1,0:T(8,128)(2,1)}, bf16[256,1024]{1,0:T(8,128)(2,1)}, u32[]{:S(2)}, u32[]{:S(2)}) collective-permute-start(bf16[256,1024]{1,0:T(8,128)(2,1)} %collective-permute-done.2.rest_1_.rest_5_), channel_id=1, source_target_pairs={{2,3},{3,2},{4,5},{5,4},{6,7},{7,6},{10,11},{11,10},{12,13},{13,12... | collective-permute-start | bytes 1572872 | tf_op jit(solution)/shard_map/ppermute | solution.py:145
  59.1 35.5 %collective-permute-start.5 = (bf16[256,1024]{1,0:T(8,128)(2,1)}, bf16[256,1024]{1,0:T(8,128)(2,1)}, u32[]{:S(2)}, u32[]{:S(2)}) collective-permute-start(bf16[256,1024]{1,0:T(8,128)(2,1)} %collective-permute-done.4.rest_2_.rest_6_), channel_id=1, source_target_pairs={{4,5},{5,4},{6,7},{7,6},{12,13},{13,12},{14,15},{15,14},{20,21},{2... | collective-permute-start | bytes 1572872 | tf_op jit(solution)/shard_map/ppermute | solution.py:145
  71.6 25.7 %collective-permute-start.7 = (bf16[256,1024]{1,0:T(8,128)(2,1)}, bf16[256,1024]{1,0:T(8,128)(2,1)}, u32[]{:S(2)}, u32[]{:S(2)}) collective-permute-start(bf16[256,1024]{1,0:T(8,128)(2,1)} %collective-permute-done.6.rest_3_.rest_7_), channel_id=1, source_target_pairs={{6,7},{7,6},{14,15},{15,14},{22,23},{23,22},{30,31},{31,30}} | collective-permute-start | bytes 1572872 | tf_op jit(solution)/shard_map/ppermute | solution.py:145
  80.1 1.2 %copy-start = (bf16[32,8,2048]{2,1,0:T(8,128)(2,1)S(1)}, bf16[32,8,2048]{2,1,0:T(8,128)(2,1)}, u32[]{:S(2)}) copy-start(bf16[32,8,2048]{2,1,0:T(8,128)(2,1)} %all-gather.2.cloned.1.call-done) | copy-start | bytes 3145732
  81.3 16.0 %copy-start.1 = (bf16[32,8,2048]{2,1,0:T(8,128)(2,1)S(1)}, bf16[32,8,2048]{2,1,0:T(8,128)(2,1)}, u32[]{:S(2)}) copy-start(bf16[32,8,2048]{2,1,0:T(8,128)(2,1)} %all-gather.2.cloned.1.call-done) | copy-start | bytes 3145732
Sparse Core Ops, SparseCore 0:
  26.4 43.1 all-gather.1

commit v2 on v1

v2 whole, which is shorter than its diff:
```python
import functools
import math

import jax
import jax.numpy as jnp
from jax import lax
from jax.experimental import pallas as pl
from jax.experimental.pallas import tpu as pltpu
from jax.sharding import PartitionSpec as P

H = 64
KVH = 8
HD = 128
GQ = H // KVH
REACH = 7
SLAB = 2
FILL = -1e30


def attend_kernel(pairs, meta_ref, seg_q_ref, seg_k_ref, prefix_bias_ref, q_ref, pk_ref, pv_ref, *rest):
    k_refs, v_refs = rest[: 2 * pairs], rest[2 * pairs : 4 * pairs]
    o_ref, s_ref, top_ref, bias_ref = rest[-4:]
    rows = q_ref.shape[0]
    step = 2 * rows
    prefix_steps = pk_ref.shape[0] // step
    block, reach = meta_ref[0], meta_ref[1]
    scale = math.log2(math.e) / math.sqrt(HD)
    nt = (((1,), (1,)), ((), ()))

    @pl.when(pl.program_id(0) == 0)
    def _():
        row_pos = block * rows + lax.broadcasted_iota(jnp.int32, (rows, rows), 0)
        lane = lax.broadcasted_iota(jnp.int32, (rows, rows), 1)
        for k in range(pairs):
            for part, first in enumerate((block, block + 1 - 2 * lax.rem(block, 2))):
                key_block = jnp.maximum(first - 2 * k, 0)
                seen = (seg_k_ref[key_block] == seg_q_ref[...]) & (
                    key_block * rows + lane <= row_pos
                )
                bias_ref[k, :, part * rows : (part + 1) * rows] = jnp.where(seen, 0.0, FILL)

    def body(near):
        keys = [pk_ref[i * step : (i + 1) * step, :] for i in range(prefix_steps)]
        values = [pv_ref[i * step : (i + 1) * step, :] for i in range(prefix_steps)]
        for k in range(near + 1):
            keys.append(jnp.concatenate([k_refs[2 * k][...], k_refs[2 * k + 1][...]]))
            values.append(jnp.concatenate([v_refs[2 * k][...], v_refs[2 * k + 1][...]]))
        values = jnp.concatenate(values)
        values = jnp.concatenate([values, jnp.ones_like(values)], axis=1)

        def score(slab):
            heads = range(slab * SLAB, (slab + 1) * SLAB)
            q = jnp.concatenate([q_ref[:, g * HD : (g + 1) * HD] for g in heads])
            top = None
            for i, key in enumerate(keys):
                s = lax.dot_general(q, key, nt, preferred_element_type=jnp.float32)
                if i < prefix_steps:
                    bias = prefix_bias_ref[:, i * step : (i + 1) * step]
                else:
                    bias = bias_ref[i - prefix_steps]
                s = (s.reshape(SLAB, rows, step) + bias[None]).reshape(SLAB * rows, step)
                s_ref[slab % 2, :, i * step : (i + 1) * step] = s
                high = jnp.maximum(s[:, :rows], s[:, rows:])
                top = high if top is None else jnp.maximum(top, high)
            top = jnp.max(top, axis=1, keepdims=True)
            top_ref[slab % 2] = jnp.broadcast_to(top, (SLAB * rows, HD))

        def weigh(slab):
            top = top_ref[slab % 2]
            weights = [
                jnp.exp2((s_ref[slab % 2, :, i * HD : (i + 1) * HD] - top) * scale).astype(
                    jnp.bfloat16
                )
                for i in range(len(keys) * step // HD)
            ]
            acc = jnp.dot(
                jnp.concatenate(weights, axis=1), values, preferred_element_type=jnp.float32
            )
            out = (acc[:, :HD] / acc[:, HD:]).astype(o_ref.dtype)
            for j in range(SLAB):
                g = slab * SLAB + j
                o_ref[:, g * HD : (g + 1) * HD] = out[j * rows : (j + 1) * rows]

        score(0)
        for slab in range(GQ // SLAB):
            if slab + 1 < GQ // SLAB:
                score(slab + 1)
            weigh(slab)

    for near in range(pairs):
        pl.when(reach == near)(functools.partial(body, near))


def attend(meta, seg_q, seg_k, prefix_bias, queries, pieces, prefix, out):
    rows = queries.shape[0]
    prefix_keys = prefix.shape[0]
    pairs = len(pieces) // 2
    heads = pieces[0].shape[1] // (2 * HD)
    wide = (rows, GQ * HD)
    in_specs = [
        pl.BlockSpec((rows, 1), lambda i, m: (0, 0)),
        pl.BlockSpec(seg_k.shape, lambda i, m: (0, 0, 0)),
        pl.BlockSpec((1, prefix_keys), lambda i, m: (0, 0)),
        pl.BlockSpec(wide, lambda i, m: (0, m[2] + i)),
        pl.BlockSpec((prefix_keys, HD), lambda i, m: (0, i)),
        pl.BlockSpec((prefix_keys, HD), lambda i, m: (0, heads + i)),
        *[pl.BlockSpec((rows, HD), lambda i, m: (0, i))] * len(pieces),
        *[pl.BlockSpec((rows, HD), lambda i, m: (0, heads + i))] * len(pieces),
    ]
    args = [meta, seg_q, seg_k, prefix_bias, queries, prefix, prefix, *pieces, *pieces]
    aliases = {}
    if out is not None:
        in_specs.append(pl.BlockSpec(memory_space=pl.ANY))
        args.append(out)
        aliases = {len(args) - 1: 0}
    all_keys = 2 * rows * pairs + prefix_keys
    return pl.pallas_call(
        functools.partial(attend_kernel, pairs),
        grid_spec=pltpu.PrefetchScalarGridSpec(
            num_scalar_prefetch=1,
            grid=(heads,),
            in_specs=in_specs,
            out_specs=pl.BlockSpec(wide, lambda i, m: (0, m[2] + i)),
            scratch_shapes=[
                pltpu.VMEM((2, SLAB * rows, all_keys), jnp.float32),
                pltpu.VMEM((2, SLAB * rows, HD), jnp.float32),
                pltpu.VMEM((pairs, rows, 2 * rows), jnp.float32),
            ],
        ),
        out_shape=jax.ShapeDtypeStruct(queries.shape, queries.dtype),
        input_output_aliases=aliases,
        compiler_params=pltpu.CompilerParams(vmem_limit_bytes=40 * 1024 * 1024),
    )(*args)


def on_device(queries, resp_kv, resp_segments, prefix_kv, tile_plan, prompt_lengths):
    rows = queries.shape[1]
    half = KVH * HD // 2
    tiles, tile = prefix_kv.shape[:2]
    groups, count = lax.axis_size("prompt"), lax.axis_size("resp")
    per = tiles // groups
    group = lax.axis_index("prompt")
    block = lax.axis_index("resp")
    side = block % 2
    steps = min(count // 2 - 1, (REACH + 1) // 2)

    def part(owner):
        kv = resp_kv[0].reshape(rows, 2, 2, half)
        return lax.dynamic_index_in_dim(kv, owner, 2, keepdims=False).reshape(rows, 2 * half)

    def swap(value, first):
        return lax.ppermute(value, "resp", [(r, r ^ 1) for r in range(2 * first, count)])

    def climb(value, step):
        pairs = [(r, r + 2) for r in range(2 * step - 2, count - 2)]
        return lax.ppermute(value, "resp", pairs)

    mine, theirs = part(side), part(1 - side)
    straight = [mine, swap(theirs, 0)]
    upper = lax.ppermute(mine, "resp", [(r, r + 1) for r in range(0, count, 2)])
    crossed = [theirs, upper]

    owner, place = tile_plan[:, 0], tile_plan[:, 1]
    index = jnp.arange(tiles, dtype=jnp.int32)
    ahead = (owner[None, :] < owner[:, None]) | (
        (owner[None, :] == owner[:, None]) & (index[None, :] < index[:, None])
    )
    pick = jnp.sum(ahead, axis=1, dtype=jnp.int32)[None, :] == index[:, None]
    own_place = jnp.sum(jnp.where(pick, place[None, :], 0), axis=1, dtype=jnp.int32)
    own_tiles = jnp.sum(
        jnp.where(pick[:, :, None, None], prefix_kv[None], 0).astype(jnp.float32), axis=1
    )
    own_tiles = own_tiles.reshape(groups, per, tile, 2, 2, half).transpose(0, 4, 1, 2, 3, 5)
    own_tiles = own_tiles.reshape(groups, 2, per, tile, 2 * half)
    row = jnp.arange(tile, dtype=jnp.int32)[:, None]
    extra = jnp.where(
        row == 0, resp_segments[0], own_place.reshape(groups, 1, per, 1, 1)
    ).astype(jnp.float32)
    extra = jnp.broadcast_to(extra, (groups, 2, per, tile, rows))
    out_tiles = jnp.concatenate([own_tiles, extra], axis=-1).astype(prefix_kv.dtype)
    out_tiles = jnp.broadcast_to(
        out_tiles[:, None], (groups, count // 2, *out_tiles.shape[1:])
    ).reshape(groups * count, per * tile, 2 * half + rows)
    came = lax.all_to_all(
        out_tiles, ("prompt", "resp"), split_axis=0, concat_axis=0, tiled=True
    )
    prefix = came.reshape(-1, 2 * half + rows)
    prefix_crossed = swap(prefix, 0)

    for step in range(1, steps + 1):
        for k in range(2):
            straight.append(climb(straight[-2], step))
        crossed += [swap(straight[-1], step), swap(straight[-2], step)]

    ints = came.reshape(groups, count, per, tile, -1)[..., 2 * half :].astype(jnp.int32)
    seg_k = lax.dynamic_index_in_dim(ints[:, :, 0, 0], group, 0, keepdims=False)
    places = ints[:, :, :, 1, :1].reshape(-1, 1) * tile + row.reshape(1, -1)
    prefix_bias = jnp.where(places < prompt_lengths[0], 0.0, FILL).reshape(1, -1)
    seg_q = resp_segments[0][:, None]
    before = jnp.sum(seg_k < resp_segments[0, 0], dtype=jnp.int32)
    reach = block // 2 - before // (2 * rows)
    seg_k = seg_k[:, None, :]

    out = None
    for first, pieces, tiles_of in (
        (side, straight, prefix),
        (1 - side, crossed, prefix_crossed),
    ):
        meta = jnp.stack([block, reach, first * (KVH // 2)])
        out = attend(meta, seg_q, seg_k, prefix_bias, queries[0], pieces, tiles_of, out)
    return out[None]


def solution(mesh):
    return jax.shard_map(
        on_device,
        mesh=mesh,
        in_specs=(
            P("prompt", "resp", None),
            P("prompt", "resp", None),
            P("prompt", "resp"),
            P(("prompt", "resp"), None, None),
            P(("prompt", "resp"), None),
            P("prompt"),
        ),
        out_specs=P("prompt", "resp", None),
        check_vma=False,
    )
```

time: 119 us -> 102 us (0.86); the launches traced: 118 us -> 102 us
  between operations: 16.8 us -> 3.7 us
  starting transfers between devices: 26.2 us -> 36.3 us
  local copies, waits for them, and re-layouts: 4.19 us -> 14.2 us
  waiting for transfers between devices: 32.4 us -> 22.9 us
  Pallas kernels: 26.7 us -> 19.9 us
  blocking collectives: 6.54 us -> 0 us
    ppermute x3 -> x6, waiting for transfers between devices: 23.8 us -> 7.96 us  [climb(): return lax.ppermute(value, 'resp', pairs)]
    ppermute x4 -> x8, starting transfers between devices: 11.1 us -> 19.3 us  [swap(): lax.ppermute(value, 'resp', [(r, r ^ 1) for r in range(2 * first, count)])]
    pallas_call x2, Pallas kernels: 26.7 us -> 19.9 us  [attend(): pl.pallas_call(functools.partial(attend_kernel, pairs), grid_spec=pltpu.P...]
    all_to_all x1 -> x0, blocking collectives: 6.54 us -> none  [on_device(): lax.all_to_all(sorted_tiles, 'prompt', split_axis=0, concat_axis=0, tiled...]
    ppermute x4 -> x8, waiting for transfers between devices: 8.56 us -> 14.9 us  [swap(): lax.ppermute(value, 'resp', [(r, r ^ 1) for r in range(2 * first, count)])]
    unnamed x9 -> x24, local copies, waits for them, and re-layouts: 1.24 us -> 5.56 us
    ppermute x3 -> x6, starting transfers between devices: 3.85 us -> 7.72 us  [climb(): return lax.ppermute(value, 'resp', pairs)]
    dynamic_slice x1, local copies, waits for them, and re-layouts: 1.14 us -> 3.61 us  [part(): lax.dynamic_index_in_dim(kv, owner, 2, keepdims=False)]
  transfers between devices with their start and end apart: 10 -> 16, of which waited for: 5 -> 5; matrix products, arithmetic and copies ran while one was open for 5% -> 10% of each run, Pallas kernels for 11% -> 10%
where the time goes in v2:
time: 102 us
  starting transfers between devices  36.3 us (36%)
  waiting for transfers between devices  22.9 us (22%)
  Pallas kernels  19.9 us (20%)
  local copies, waits for them, and re-layouts  14.2 us (14%)
  other arithmetic  5.17 us (5%)
  between operations  3.7 us (4%)
    pallas_call x2, Pallas kernels, attend(): pl.pallas_call(functools.partial(attend_kernel, pairs), grid_spec=pltpu.P...  19.9 us
    ppermute x8, starting transfers between devices, swap(): lax.ppermute(value, 'resp', [(r, r ^ 1) for r in range(2 * first, count)])  19.3 us
    ppermute x8, waiting for transfers between devices, swap(): lax.ppermute(value, 'resp', [(r, r ^ 1) for r in range(2 * first, count)])  14.9 us
    ppermute x6, waiting for transfers between devices, climb(): return lax.ppermute(value, 'resp', pairs)  7.96 us
    ppermute x6, starting transfers between devices, climb(): return lax.ppermute(value, 'resp', pairs)  7.72 us
    all_to_all x1, starting transfers between devices, on_device(): lax.all_to_all(out_tiles, ('prompt', 'resp'), split_axis=0, concat_axis=0...  5.86 us
    unnamed x24, local copies, waits for them, and re-layouts  5.56 us
    dynamic_slice x1, local copies, waits for them, and re-layouts, part(): lax.dynamic_index_in_dim(kv, owner, 2, keepdims=False)  3.61 us
  transfers between devices with their start and end apart: 16, of which 5 were waited for; matrix products, arithmetic and copies ran while one was open for 10% of the time, Pallas kernels for 10%

profile of v2, /device:TPU:26, one launch (start us, length us, event | category | flops | bytes accessed | tf_op | source)
XLA Modules:
  0.0 102.2 jit_solution(3326574592888769220)
XLA Ops:
  0.0 0.8 slice_bitcast_fusion.1
  1.1 1.0 %select_reduce_fusion = bf16[4,8,2048]{2,1,0:T(8,128)(2,1)S(1)} fusion(pred[4,4]{1,0:T(4,128)(4,1)S(1)} %iota_compare_fusion, bf16[4,8,2048]{2,1,0:T(8,128)(2,1)} %param.9), kind=kLoop, calls=%fused_computation.2 | loop fusion | flops 458752 | bytes 262160 | tf_op jit(solution)/shard_map/reduce_sum | solution.py:170
  3.1 0.9 broadcast_in_dim.98
  4.0 5.9 %all-to-all-start = ((bf16[32,8,1152]{2,1,0:T(8,128)(2,1)}), bf16[32,8,1152]{2,1,0:T(8,128)(2,1)S(1)}, u32[]{:S(2)}, u32[]{:S(2)}) async-start(bf16[32,8,1152]{2,1,0:T(8,128)(2,1)} %bitcast.5), calls=%async_computation | async-start | bytes 1179648 | tf_op jit(solution)/shard_map/all_to_all | solution.py:184
  9.9 1.6 %reshape_squeeze.2 = bf16[128,2,2,512]{3,2,1,0:T(2,128)(2,1)S(1)} reshape(bf16[1,128,2048]{2,1,0:T(8,128)(2,1)} %param.7) | data formatting | bytes 1048576 | tf_op jit(solution)/shard_map/reshape;squeeze | solution.py:148
  11.5 3.6 %dynamic-slice_reduce_fusion = (bf16[128,2,512]{2,1,0:T(2,128)(2,1)S(1)}, bf16[128,2,512]{2,1,0:T(2,128)(2,1)S(1)}) fusion(bf16[128,2,2,512]{3,2,1,0:T(2,128)(2,1)S(1)} %reshape_squeeze.2, s32[]{:T(128)S(6)} %select_n.66, s32[]{:T(128)S(6)} %select_n.65), kind=kLoop, calls=%fused_computation | loop fusion | bytes 1048584 | tf_op jit(solution)/shard_map/jit(dynamic_index_in_dim)/dynamic_slice | solution.py:149
  15.1 1.6 %collective-permute-start.2 = (bf16[128,1024]{1,0:T(8,128)(2,1)S(1)}, bf16[128,1024]{1,0:T(8,128)(2,1)S(1)}, u32[]{:S(2)}, u32[]{:S(2)}) collective-permute-start(bf16[128,1024]{1,0:T(8,128)(2,1)S(1)} %bitcast.34), channel_id=1, source_target_pairs={{0,1},{1,0},{2,3},{3,2},{4,5},{5,4},{6,7},{7,6},{8,9},{9,8},{10,11... | collective-permute-start | bytes 786440 | tf_op jit(solution)/shard_map/ppermute | solution.py:152
  16.7 1.3 %collective-permute-start.5 = (bf16[128,1024]{1,0:T(8,128)(2,1)S(1)}, bf16[128,1024]{1,0:T(8,128)(2,1)}, u32[]{:S(2)}, u32[]{:S(2)}) collective-permute-start(bf16[128,1024]{1,0:T(8,128)(2,1)S(1)} %bitcast.37), channel_id=1, source_target_pairs={{0,2},{1,3},{2,4},{3,5},{4,6},{5,7},{8,10},{9,11},{10,12},{11,13},... | collective-permute-start | bytes 786440 | tf_op jit(solution)/shard_map/ppermute | solution.py:156
  18.0 7.2 %collective-permute-done.2.rest_1_.rest_9_ = bf16[128,1024]{1,0:T(8,128)(2,1)S(1)} collective-permute-done((bf16[128,1024]{1,0:T(8,128)(2,1)S(1)}, bf16[128,1024]{1,0:T(8,128)(2,1)S(1)}, u32[]{:S(2)}, u32[]{:S(2)}) %collective-permute-start.2) | collective-permute-done | bytes 262176 | tf_op jit(solution)/shard_map/ppermute | solution.py:152
  25.3 1.3 %collective-permute-start.3 = (bf16[128,1024]{1,0:T(8,128)(2,1)S(1)}, bf16[128,1024]{1,0:T(8,128)(2,1)}, u32[]{:S(2)}, u32[]{:S(2)}) collective-permute-start(bf16[128,1024]{1,0:T(8,128)(2,1)S(1)} %collective-permute-done.2.rest_1_.rest_9_), channel_id=1, source_target_pairs={{0,2},{1,3},{2,4},{3,5},{4,6},{5,7},{8,10},{9,11},{10,12},{11,13},... | collective-permute-start | bytes 786440 | tf_op jit(solution)/shard_map/ppermute | solution.py:156
  27.3 1.0 collective-permute-done.5.rest_2_.rest_10_
  28.2 1.3 %collective-permute-start.9 = (bf16[128,1024]{1,0:T(8,128)(2,1)}, bf16[128,1024]{1,0:T(8,128)(2,1)}, u32[]{:S(2)}, u32[]{:S(2)}) collective-permute-start(bf16[128,1024]{1,0:T(8,128)(2,1)} %collective-permute-done.5.rest_2_.rest_10_), channel_id=1, source_target_pairs={{2,4},{3,5},{4,6},{5,7},{10,12},{11,13},{12,14},{13,15},{18,20},{1... | collective-permute-start | bytes 786440 | tf_op jit(solution)/shard_map/ppermute | solution.py:156
  29.5 7.0 %collective-permute-done.3.rest_3_.rest_11_ = bf16[128,1024]{1,0:T(8,128)(2,1)} collective-permute-done((bf16[128,1024]{1,0:T(8,128)(2,1)S(1)}, bf16[128,1024]{1,0:T(8,128)(2,1)}, u32[]{:S(2)}, u32[]{:S(2)}) %collective-permute-start.3) | collective-permute-done | bytes 262176 | tf_op jit(solution)/shard_map/ppermute | solution.py:156
  36.5 1.3 %collective-permute-start.7 = (bf16[128,1024]{1,0:T(8,128)(2,1)}, bf16[128,1024]{1,0:T(8,128)(2,1)}, u32[]{:S(2)}, u32[]{:S(2)}) collective-permute-start(bf16[128,1024]{1,0:T(8,128)(2,1)} %collective-permute-done.3.rest_3_.rest_11_), channel_id=1, source_target_pairs={{2,4},{3,5},{4,6},{5,7},{10,12},{11,13},{12,14},{13,15},{18,20},{1... | collective-permute-start | bytes 786440 | tf_op jit(solution)/shard_map/ppermute | solution.py:156
  37.8 3.4 %collective-permute-start.1 = (bf16[128,1024]{1,0:T(8,128)(2,1)S(1)}, bf16[128,1024]{1,0:T(8,128)(2,1)S(1)}, u32[]{:S(2)}, u32[]{:S(2)}) collective-permute-start(bf16[128,1024]{1,0:T(8,128)(2,1)S(1)} %bitcast.38), channel_id=1, source_target_pairs={{0,1},{2,3},{4,5},{6,7},{8,9},{10,11},{12,13},{14,15},{16,17},{18,... | collective-permute-start | bytes 786440 | tf_op jit(solution)/shard_map/ppermute | solution.py:160
  43.3 1.9 %collective-permute-start.6 = (bf16[128,1024]{1,0:T(8,128)(2,1)}, bf16[128,1024]{1,0:T(8,128)(2,1)}, u32[]{:S(2)}, u32[]{:S(2)}) collective-permute-start(bf16[128,1024]{1,0:T(8,128)(2,1)} %collective-permute-done.5.rest_2_.rest_10_), channel_id=1, source_target_pairs={{2,3},{3,2},{4,5},{5,4},{6,7},{7,6},{10,11},{11,10},{12,13},{13,12... | collective-permute-start | bytes 786440 | tf_op jit(solution)/shard_map/ppermute | solution.py:152
  45.2 1.3 %collective-permute-start.13 = (bf16[128,1024]{1,0:T(8,128)(2,1)}, bf16[128,1024]{1,0:T(8,128)(2,1)}, u32[]{:S(2)}, u32[]{:S(2)}) collective-permute-start(bf16[128,1024]{1,0:T(8,128)(2,1)} %collective-permute-done.9.rest_4_.rest_12_), channel_id=1, source_target_pairs={{4,6},{5,7},{12,14},{13,15},{20,22},{21,23},{28,30},{29,31}} | collective-permute-start | bytes 786440 | tf_op jit(solution)/shard_map/ppermute | solution.py:156
  46.5 3.9 %collective-permute-start.10 = (bf16[128,1024]{1,0:T(8,128)(2,1)}, bf16[128,1024]{1,0:T(8,128)(2,1)}, u32[]{:S(2)}, u32[]{:S(2)}) collective-permute-start(bf16[128,1024]{1,0:T(8,128)(2,1)} %collective-permute-done.9.rest_4_.rest_12_), channel_id=1, source_target_pairs={{4,5},{5,4},{6,7},{7,6},{12,13},{13,12},{14,15},{15,14},{20,21},{2... | collective-permute-start | bytes 786440 | tf_op jit(solution)/shard_map/ppermute | solution.py:152
  50.5 1.3 %collective-permute-start.11 = (bf16[128,1024]{1,0:T(8,128)(2,1)}, bf16[128,1024]{1,0:T(8,128)(2,1)}, u32[]{:S(2)}, u32[]{:S(2)}) collective-permute-start(bf16[128,1024]{1,0:T(8,128)(2,1)} %collective-permute-done.7.rest_5_.rest_13_), channel_id=1, source_target_pairs={{4,6},{5,7},{12,14},{13,15},{20,22},{21,23},{28,30},{29,31}} | collective-permute-start | bytes 786440 | tf_op jit(solution)/shard_map/ppermute | solution.py:156
  56.6 1.6 %fusion = s32[4,8]{1,0:T(4,128)S(1)} fusion(s32[4,8,1,8,128]{4,3,1,0,2:T(8,128)} %copy-done.9), kind=kLoop, calls=%fused_computation.8 | loop fusion | flops 32 | bytes 256 | tf_op jit(solution)/shard_map/mul | solution.py:197
  58.3 3.9 %collective-permute-start.4 = (bf16[128,1024]{1,0:T(8,128)(2,1)}, bf16[128,1024]{1,0:T(8,128)(2,1)}, u32[]{:S(2)}, u32[]{:S(2)}) collective-permute-start(bf16[128,1024]{1,0:T(8,128)(2,1)} %collective-permute-done.3.rest_3_.rest_11_), channel_id=1, source_target_pairs={{2,3},{3,2},{4,5},{5,4},{6,7},{7,6},{10,11},{11,10},{12,13},{13,12... | collective-permute-start | bytes 786440 | tf_op jit(solution)/shard_map/ppermute | solution.py:152
  62.2 1.9 %collective-permute-start.8 = (bf16[128,1024]{1,0:T(8,128)(2,1)}, bf16[128,1024]{1,0:T(8,128)(2,1)}, u32[]{:S(2)}, u32[]{:S(2)}) collective-permute-start(bf16[128,1024]{1,0:T(8,128)(2,1)} %collective-permute-done.7.rest_5_.rest_13_), channel_id=1, source_target_pairs={{4,5},{5,4},{6,7},{7,6},{12,13},{13,12},{14,15},{15,14},{20,21},{2... | collective-permute-start | bytes 786440 | tf_op jit(solution)/shard_map/ppermute | solution.py:152
  64.2 3.9 %collective-permute-start.14 = (bf16[128,1024]{1,0:T(8,128)(2,1)}, bf16[128,1024]{1,0:T(8,128)(2,1)}, u32[]{:S(2)}, u32[]{:S(2)}) collective-permute-start(bf16[128,1024]{1,0:T(8,128)(2,1)} %collective-permute-done.13.rest_6_.rest_14_), channel_id=1, source_target_pairs={{6,7},{7,6},{14,15},{15,14},{22,23},{23,22},{30,31},{31,30}} | collective-permute-start | bytes 786440 | tf_op jit(solution)/shard_map/ppermute | solution.py:152
  68.1 2.1 %collective-permute-start.12 = (bf16[128,1024]{1,0:T(8,128)(2,1)}, bf16[128,1024]{1,0:T(8,128)(2,1)}, u32[]{:S(2)}, u32[]{:S(2)}) collective-permute-start(bf16[128,1024]{1,0:T(8,128)(2,1)} %collective-permute-done.11.rest_7_.rest_15_), channel_id=1, source_target_pairs={{6,7},{7,6},{14,15},{15,14},{22,23},{23,22},{30,31},{31,30}} | collective-permute-start | bytes 786440 | tf_op jit(solution)/shard_map/ppermute | solution.py:152
  70.9 0.8 select_n.64.prefix_bias_ref
  71.8 1.0 copy-done.2
  72.8 0.9 copy-done.4
  73.7 0.8 copy-done.7
  74.6 9.9 %shard_map.64.rest_16_ = bf16[128,8192]{1,0:T(8,128)(2,1)} custom-call(s32[3]{0:T(128)S(1)} %get-tuple-element.12.meta_ref, s32[128,1]{1,0:T(8,128)S(1)} %copy-done.7, s32[8,1,128]{2,1,0:T(1,128)S(1)} %get-tuple-element.7.seg_k_ref, f32[1,256]{1,0:T(1,128)S(1)} %select_n.64.prefix_bias_ref, bf16[128,8192]{1,0:T(8,128)(2,1)S(1)} %bitcast.28, ...), custom_call_target="tpu_custom_call" | custom-call | tf_op jit(solution)/shard_map/pallas_call | solution.py:117
  84.5 4.9 %collective-permute-done.14.rest_7_.rest_15_ = bf16[128,1024]{1,0:T(8,128)(2,1)} collective-permute-done((bf16[128,1024]{1,0:T(8,128)(2,1)}, bf16[128,1024]{1,0:T(8,128)(2,1)}, u32[]{:S(2)}, u32[]{:S(2)}) %collective-permute-start.14) | collective-permute-done | bytes 262176 | tf_op jit(solution)/shard_map/ppermute | solution.py:152
  89.4 2.8 %collective-permute-done.12.rest_6_.rest_14_ = bf16[128,1024]{1,0:T(8,128)(2,1)} collective-permute-done((bf16[128,1024]{1,0:T(8,128)(2,1)}, bf16[128,1024]{1,0:T(8,128)(2,1)}, u32[]{:S(2)}, u32[]{:S(2)}) %collective-permute-start.12) | collective-permute-done | bytes 262176 | tf_op jit(solution)/shard_map/ppermute | solution.py:152
  92.2 10.0 %shard_map.65 = bf16[128,8192]{1,0:T(8,128)(2,1)} custom-call(s32[3]{0:T(128)S(1)} %get-tuple-element.11.meta_ref, s32[128,1]{1,0:T(8,128)S(1)} %copy-done.8, s32[8,1,128]{2,1,0:T(1,128)S(1)} %get-tuple-element.7.seg_k_ref, f32[1,256]{1,0:T(1,128)S(1)} %select_n.64.prefix_bias_ref, bf16[128,8192]{1,0:T(8,128)(2,1)S(1)} %bitcast.29, ...), custom_call_target="tpu_custom_call", output_to_operand_aliasing={{}: (23, {})} | custom-call | tf_op jit(solution)/shard_map/pallas_call | solution.py:117
  (50 shorter events, 6.5 us)
Async XLA Ops:
  4.0 48.5 %all-to-all-start = ((bf16[32,8,1152]{2,1,0:T(8,128)(2,1)}), bf16[32,8,1152]{2,1,0:T(8,128)(2,1)S(1)}, u32[]{:S(2)}, u32[]{:S(2)}) async-start(bf16[32,8,1152]{2,1,0:T(8,128)(2,1)} %bitcast.5), calls=%async_computation | async-start | bytes 1179648 | tf_op jit(solution)/shard_map/all_to_all | solution.py:184
  9.9 32.7 %copy-start.10 = (s32[1,128]{1,0:T(1,128)S(1)}, s32[1,128]{1,0:T(1,128)}, u32[]{:S(2)}) copy-start(s32[1,128]{1,0:T(1,128)} %param.8) | copy-start | bytes 1540
  9.9 61.9 %copy-start = (bf16[1,128,8192]{2,1,0:T(8,128)(2,1)S(1)}, bf16[1,128,8192]{2,1,0:T(8,128)(2,1)}, u32[]{:S(2)}) copy-start(bf16[1,128,8192]{2,1,0:T(8,128)(2,1)} %param.6) | copy-start | bytes 6291460
  15.1 10.1 %collective-permute-start.2 = (bf16[128,1024]{1,0:T(8,128)(2,1)S(1)}, bf16[128,1024]{1,0:T(8,128)(2,1)S(1)}, u32[]{:S(2)}, u32[]{:S(2)}) collective-permute-start(bf16[128,1024]{1,0:T(8,128)(2,1)S(1)} %bitcast.34), channel_id=1, source_target_pairs={{0,1},{1,0},{2,3},{3,2},{4,5},{5,4},{6,7},{7,6},{8,9},{9,8},{10,11... | collective-permute-start | bytes 786440 | tf_op jit(solution)/shard_map/ppermute | solution.py:152
  16.7 11.5 %collective-permute-start.5 = (bf16[128,1024]{1,0:T(8,128)(2,1)S(1)}, bf16[128,1024]{1,0:T(8,128)(2,1)}, u32[]{:S(2)}, u32[]{:S(2)}) collective-permute-start(bf16[128,1024]{1,0:T(8,128)(2,1)S(1)} %bitcast.37), channel_id=1, source_target_pairs={{0,2},{1,3},{2,4},{3,5},{4,6},{5,7},{8,10},{9,11},{10,12},{11,13},... | collective-permute-start | bytes 786440 | tf_op jit(solution)/shard_map/ppermute | solution.py:156
  25.3 11.2 %collective-permute-start.3 = (bf16[128,1024]{1,0:T(8,128)(2,1)S(1)}, bf16[128,1024]{1,0:T(8,128)(2,1)}, u32[]{:S(2)}, u32[]{:S(2)}) collective-permute-start(bf16[128,1024]{1,0:T(8,128)(2,1)S(1)} %collective-permute-done.2.rest_1_.rest_9_), channel_id=1, source_target_pairs={{0,2},{1,3},{2,4},{3,5},{4,6},{5,7},{8,10},{9,11},{10,12},{11,13},... | collective-permute-start | bytes 786440 | tf_op jit(solution)/shard_map/ppermute | solution.py:156
  26.6 0.7 copy-start.3
  28.2 17.0 %collective-permute-start.9 = (bf16[128,1024]{1,0:T(8,128)(2,1)}, bf16[128,1024]{1,0:T(8,128)(2,1)}, u32[]{:S(2)}, u32[]{:S(2)}) collective-permute-start(bf16[128,1024]{1,0:T(8,128)(2,1)} %collective-permute-done.5.rest_2_.rest_10_), channel_id=1, source_target_pairs={{2,4},{3,5},{4,6},{5,7},{10,12},{11,13},{12,14},{13,15},{18,20},{1... | collective-permute-start | bytes 786440 | tf_op jit(solution)/shard_map/ppermute | solution.py:156
  36.5 14.0 %collective-permute-start.7 = (bf16[128,1024]{1,0:T(8,128)(2,1)}, bf16[128,1024]{1,0:T(8,128)(2,1)}, u32[]{:S(2)}, u32[]{:S(2)}) collective-permute-start(bf16[128,1024]{1,0:T(8,128)(2,1)} %collective-permute-done.3.rest_3_.rest_11_), channel_id=1, source_target_pairs={{2,4},{3,5},{4,6},{5,7},{10,12},{11,13},{12,14},{13,15},{18,20},{1... | collective-permute-start | bytes 786440 | tf_op jit(solution)/shard_map/ppermute | solution.py:156
  37.8 14.0 %collective-permute-start.1 = (bf16[128,1024]{1,0:T(8,128)(2,1)S(1)}, bf16[128,1024]{1,0:T(8,128)(2,1)S(1)}, u32[]{:S(2)}, u32[]{:S(2)}) collective-permute-start(bf16[128,1024]{1,0:T(8,128)(2,1)S(1)} %bitcast.38), channel_id=1, source_target_pairs={{0,1},{2,3},{4,5},{6,7},{8,9},{10,11},{12,13},{14,15},{16,17},{18,... | collective-permute-start | bytes 786440 | tf_op jit(solution)/shard_map/ppermute | solution.py:160
  41.2 0.7 copy-start.1
  43.3 15.0 %collective-permute-start.6 = (bf16[128,1024]{1,0:T(8,128)(2,1)}, bf16[128,1024]{1,0:T(8,128)(2,1)}, u32[]{:S(2)}, u32[]{:S(2)}) collective-permute-start(bf16[128,1024]{1,0:T(8,128)(2,1)} %collective-permute-done.5.rest_2_.rest_10_), channel_id=1, source_target_pairs={{2,3},{3,2},{4,5},{5,4},{6,7},{7,6},{10,11},{11,10},{12,13},{13,12... | collective-permute-start | bytes 786440 | tf_op jit(solution)/shard_map/ppermute | solution.py:152
  45.2 17.0 %collective-permute-start.13 = (bf16[128,1024]{1,0:T(8,128)(2,1)}, bf16[128,1024]{1,0:T(8,128)(2,1)}, u32[]{:S(2)}, u32[]{:S(2)}) collective-permute-start(bf16[128,1024]{1,0:T(8,128)(2,1)} %collective-permute-done.9.rest_4_.rest_12_), channel_id=1, source_target_pairs={{4,6},{5,7},{12,14},{13,15},{20,22},{21,23},{28,30},{29,31}} | collective-permute-start | bytes 786440 | tf_op jit(solution)/shard_map/ppermute | solution.py:156
  46.5 17.6 %collective-permute-start.10 = (bf16[128,1024]{1,0:T(8,128)(2,1)}, bf16[128,1024]{1,0:T(8,128)(2,1)}, u32[]{:S(2)}, u32[]{:S(2)}) collective-permute-start(bf16[128,1024]{1,0:T(8,128)(2,1)} %collective-permute-done.9.rest_4_.rest_12_), channel_id=1, source_target_pairs={{4,5},{5,4},{6,7},{7,6},{12,13},{13,12},{14,15},{15,14},{20,21},{2... | collective-permute-start | bytes 786440 | tf_op jit(solution)/shard_map/ppermute | solution.py:152
  50.5 17.6 %collective-permute-start.11 = (bf16[128,1024]{1,0:T(8,128)(2,1)}, bf16[128,1024]{1,0:T(8,128)(2,1)}, u32[]{:S(2)}, u32[]{:S(2)}) collective-permute-start(bf16[128,1024]{1,0:T(8,128)(2,1)} %collective-permute-done.7.rest_5_.rest_13_), channel_id=1, source_target_pairs={{4,6},{5,7},{12,14},{13,15},{20,22},{21,23},{28,30},{29,31}} | collective-permute-start | bytes 786440 | tf_op jit(solution)/shard_map/ppermute | solution.py:156
  51.8 0.7 copy-start.5
  52.5 39.7 %collective-permute-start = (bf16[256,1152]{1,0:T(8,128)(2,1)S(1)}, bf16[256,1152]{1,0:T(8,128)(2,1)S(1)}, u32[]{:S(2)}, u32[]{:S(2)}) collective-permute-start(bf16[256,1152]{1,0:T(8,128)(2,1)S(1)} %bitcast.30), channel_id=1, source_target_pairs={{0,1},{1,0},{2,3},{3,2},{4,5},{5,4},{6,7},{7,6},{8,9},{9,8},{10,11... | collective-permute-start | bytes 1769480 | tf_op jit(solution)/shard_map/ppermute | solution.py:152
  52.5 0.7 copy-start.9
  58.3 26.2 %collective-permute-start.4 = (bf16[128,1024]{1,0:T(8,128)(2,1)}, bf16[128,1024]{1,0:T(8,128)(2,1)}, u32[]{:S(2)}, u32[]{:S(2)}) collective-permute-start(bf16[128,1024]{1,0:T(8,128)(2,1)} %collective-permute-done.3.rest_3_.rest_11_), channel_id=1, source_target_pairs={{2,3},{3,2},{4,5},{5,4},{6,7},{7,6},{10,11},{11,10},{12,13},{13,12... | collective-permute-start | bytes 786440 | tf_op jit(solution)/shard_map/ppermute | solution.py:152
  62.2 27.1 %collective-permute-start.8 = (bf16[128,1024]{1,0:T(8,128)(2,1)}, bf16[128,1024]{1,0:T(8,128)(2,1)}, u32[]{:S(2)}, u32[]{:S(2)}) collective-permute-start(bf16[128,1024]{1,0:T(8,128)(2,1)} %collective-permute-done.7.rest_5_.rest_13_), channel_id=1, source_target_pairs={{4,5},{5,4},{6,7},{7,6},{12,13},{13,12},{14,15},{15,14},{20,21},{2... | collective-permute-start | bytes 786440 | tf_op jit(solution)/shard_map/ppermute | solution.py:152
  64.2 25.2 %collective-permute-start.14 = (bf16[128,1024]{1,0:T(8,128)(2,1)}, bf16[128,1024]{1,0:T(8,128)(2,1)}, u32[]{:S(2)}, u32[]{:S(2)}) collective-permute-start(bf16[128,1024]{1,0:T(8,128)(2,1)} %collective-permute-done.13.rest_6_.rest_14_), channel_id=1, source_target_pairs={{6,7},{7,6},{14,15},{15,14},{22,23},{23,22},{30,31},{31,30}} | collective-permute-start | bytes 786440 | tf_op jit(solution)/shard_map/ppermute | solution.py:152
  68.1 24.1 %collective-permute-start.12 = (bf16[128,1024]{1,0:T(8,128)(2,1)}, bf16[128,1024]{1,0:T(8,128)(2,1)}, u32[]{:S(2)}, u32[]{:S(2)}) collective-permute-start(bf16[128,1024]{1,0:T(8,128)(2,1)} %collective-permute-done.11.rest_7_.rest_15_), channel_id=1, source_target_pairs={{6,7},{7,6},{14,15},{15,14},{22,23},{23,22},{30,31},{31,30}} | collective-permute-start | bytes 786440 | tf_op jit(solution)/shard_map/ppermute | solution.py:152
  71.8 1.0 copy-start.2
  72.8 0.9 copy-start.4
  73.7 0.8 copy-start.7
  74.5 17.6 %copy-start.6 = (bf16[128,1024]{1,0:T(8,128)(2,1)S(1)}, bf16[128,1024]{1,0:T(8,128)(2,1)}, u32[]{:S(2)}) copy-start(bf16[128,1024]{1,0:T(8,128)(2,1)} %copy-done.5) | copy-start | bytes 786436
  74.6 17.6 %copy-start.8 = (s32[128,1]{1,0:T(8,128)S(1)}, s32[128,1]{1,0:T(8,128)}, u32[]{:S(2)}) copy-start(s32[128,1]{1,0:T(8,128)} %copy.27.seg_q_ref) | copy-start | bytes 1540

commit v3 on v2

--- a/solution.py
+++ b/solution.py
@@ -102,8 +102,8 @@
         pl.BlockSpec(seg_k.shape, lambda i, m: (0, 0, 0)),
         pl.BlockSpec((1, prefix_keys), lambda i, m: (0, 0)),
         pl.BlockSpec(wide, lambda i, m: (0, m[2] + i)),
-        pl.BlockSpec((prefix_keys, HD), lambda i, m: (0, i)),
-        pl.BlockSpec((prefix_keys, HD), lambda i, m: (0, heads + i)),
+        pl.BlockSpec((prefix_keys, HD), lambda i, m: (0, m[2] + i)),
+        pl.BlockSpec((prefix_keys, HD), lambda i, m: (0, KVH + m[2] + i)),
         *[pl.BlockSpec((rows, HD), lambda i, m: (0, i))] * len(pieces),
         *[pl.BlockSpec((rows, HD), lambda i, m: (0, heads + i))] * len(pieces),
     ]
@@ -145,8 +145,9 @@
     steps = min(count // 2 - 1, (REACH + 1) // 2)
 
     def part(owner):
-        kv = resp_kv[0].reshape(rows, 2, 2, half)
-        return lax.dynamic_index_in_dim(kv, owner, 2, keepdims=False).reshape(rows, 2 * half)
+        k = lax.dynamic_slice_in_dim(resp_kv[0], owner * half, half, 1)
+        v = lax.dynamic_slice_in_dim(resp_kv[0], (2 + owner) * half, half, 1)
+        return jnp.concatenate([k, v], axis=1)
 
     def swap(value, first):
         return lax.ppermute(value, "resp", [(r, r ^ 1) for r in range(2 * first, count)])
@@ -157,8 +158,7 @@
 
     mine, theirs = part(side), part(1 - side)
     straight = [mine, swap(theirs, 0)]
-    upper = lax.ppermute(mine, "resp", [(r, r + 1) for r in range(0, count, 2)])
-    crossed = [theirs, upper]
+    crossed = [theirs, None]
 
     owner, place = tile_plan[:, 0], tile_plan[:, 1]
     index = jnp.arange(tiles, dtype=jnp.int32)
@@ -170,29 +170,32 @@
     own_tiles = jnp.sum(
         jnp.where(pick[:, :, None, None], prefix_kv[None], 0).astype(jnp.float32), axis=1
     )
-    own_tiles = own_tiles.reshape(groups, per, tile, 2, 2, half).transpose(0, 4, 1, 2, 3, 5)
-    own_tiles = own_tiles.reshape(groups, 2, per, tile, 2 * half)
+    own_tiles = own_tiles.reshape(groups, per, tile, 4 * half)
     row = jnp.arange(tile, dtype=jnp.int32)[:, None]
-    extra = jnp.where(
-        row == 0, resp_segments[0], own_place.reshape(groups, 1, per, 1, 1)
-    ).astype(jnp.float32)
-    extra = jnp.broadcast_to(extra, (groups, 2, per, tile, rows))
+    extra = jnp.where(row == 0, resp_segments[0], own_place.reshape(groups, per, 1, 1))
+    extra = jnp.broadcast_to(extra.astype(jnp.float32), (groups, per, tile, rows))
     out_tiles = jnp.concatenate([own_tiles, extra], axis=-1).astype(prefix_kv.dtype)
     out_tiles = jnp.broadcast_to(
-        out_tiles[:, None], (groups, count // 2, *out_tiles.shape[1:])
-    ).reshape(groups * count, per * tile, 2 * half + rows)
+        out_tiles[:, None], (groups, count, *out_tiles.shape[1:])
+    ).reshape(groups * count, per * tile, 4 * half + rows)
+    out_tiles, straight[1] = lax.optimization_barrier((out_tiles, straight[1]))
     came = lax.all_to_all(
         out_tiles, ("prompt", "resp"), split_axis=0, concat_axis=0, tiled=True
     )
-    prefix = came.reshape(-1, 2 * half + rows)
-    prefix_crossed = swap(prefix, 0)
-
     for step in range(1, steps + 1):
         for k in range(2):
-            straight.append(climb(straight[-2], step))
+            source = straight[-2]
+            if step > 2:
+                late = 2 * (step - 2) + 1 - k
+                source, crossed[late] = lax.optimization_barrier((source, crossed[late]))
+            straight.append(climb(source, step))
         crossed += [swap(straight[-1], step), swap(straight[-2], step)]
 
-    ints = came.reshape(groups, count, per, tile, -1)[..., 2 * half :].astype(jnp.int32)
+    mine, straight[3] = lax.optimization_barrier((mine, straight[3]))
+    crossed[1] = lax.ppermute(mine, "resp", [(r, r + 1) for r in range(0, count, 2)])
+    came, straight[-3] = lax.optimization_barrier((came, straight[-3]))
+    prefix = came.reshape(-1, 4 * half + rows)
+    ints = came.reshape(groups, count, per, tile, -1)[..., 4 * half :].astype(jnp.int32)
     seg_k = lax.dynamic_index_in_dim(ints[:, :, 0, 0], group, 0, keepdims=False)
     places = ints[:, :, :, 1, :1].reshape(-1, 1) * tile + row.reshape(1, -1)
     prefix_bias = jnp.where(places < prompt_lengths[0], 0.0, FILL).reshape(1, -1)
@@ -202,12 +205,9 @@
     seg_k = seg_k[:, None, :]
 
     out = None
-    for first, pieces, tiles_of in (
-        (side, straight, prefix),
-        (1 - side, crossed, prefix_crossed),
-    ):
+    for first, pieces in ((side, straight), (1 - side, crossed)):
         meta = jnp.stack([block, reach, first * (KVH // 2)])
-        out = attend(meta, seg_q, seg_k, prefix_bias, queries[0], pieces, tiles_of, out)
+        out = attend(meta, seg_q, seg_k, prefix_bias, queries[0], pieces, prefix, out)
     return out[None]
 
 

time: 102 us -> 112 us (1.098); the launches traced: 102 us -> 110 us
  waiting for transfers between devices: 22.9 us -> 33.6 us
  Pallas kernels: 19.9 us -> 18 us
  local copies, waits for them, and re-layouts: 14.2 us -> 12.6 us
    ppermute x6, waiting for transfers between devices: 7.96 us -> 29.9 us  [climb(): return lax.ppermute(value, 'resp', pairs)]
    ppermute x8 -> x7, waiting for transfers between devices: 14.9 us -> 3.67 us  [swap(): lax.ppermute(value, 'resp', [(r, r ^ 1) for r in range(2 * first, count)])]
    pallas_call x2, Pallas kernels: 19.9 us -> 18 us  [attend(): pl.pallas_call(functools.partial(attend_kernel, pairs), grid_spec=pltpu.P...]
    dynamic_slice x1, local copies, waits for them, and re-layouts: 3.61 us -> 1.84 us  [part(): k = lax.dynamic_slice_in_dim(resp_kv[0], owner * half, half, 1)]
    unnamed x24 -> x28, local copies, waits for them, and re-layouts: 5.56 us -> 7.32 us
    another operation x1 -> x0, local copies, waits for them, and re-layouts: 1.57 us -> none  [part(): kv = resp_kv[0].reshape(rows, 2, 2, half)]
    ppermute x8 -> x7, starting transfers between devices: 19.3 us -> 19 us  [swap(): lax.ppermute(value, 'resp', [(r, r ^ 1) for r in range(2 * first, count)])]
  transfers between devices with their start and end apart: 16 -> 15, of which waited for: 5 -> 5; matrix products, arithmetic and copies ran while one was open for 10% -> 8% of each run, Pallas kernels for 10% -> 8%
where the time goes in v3:
time: 112 us; the launch traced here: 110 us
  starting transfers between devices  36.5 us (33%)
  waiting for transfers between devices  33.6 us (30%)
  Pallas kernels  18 us (16%)
  local copies, waits for them, and re-layouts  12.6 us (11%)
  other arithmetic  5.98 us (5%)
  between operations  3.43 us (3%)
    ppermute x6, waiting for transfers between devices, climb(): return lax.ppermute(value, 'resp', pairs)  29.9 us
    ppermute x7, starting transfers between devices, swap(): lax.ppermute(value, 'resp', [(r, r ^ 1) for r in range(2 * first, count)])  19 us
    pallas_call x2, Pallas kernels, attend(): pl.pallas_call(functools.partial(attend_kernel, pairs), grid_spec=pltpu.P...  18 us
    ppermute x6, starting transfers between devices, climb(): return lax.ppermute(value, 'resp', pairs)  7.69 us
    unnamed x28, local copies, waits for them, and re-layouts  7.32 us
    all_to_all x1, starting transfers between devices, on_device(): lax.all_to_all(out_tiles, ('prompt', 'resp'), split_axis=0, concat_axis=0...  5.86 us
    ppermute x1, starting transfers between devices, on_device(): lax.ppermute(mine, 'resp', [(r, r + 1) for r in range(0, count, 2)])  3.98 us
    ppermute x7, waiting for transfers between devices, swap(): lax.ppermute(value, 'resp', [(r, r ^ 1) for r in range(2 * first, count)])  3.67 us
  transfers between devices with their start and end apart: 15, of which 5 were waited for; matrix products, arithmetic and copies ran while one was open for 8% of the time, Pallas kernels for 8%

profile of v3, /device:TPU:26, one launch (start us, length us, event | category | flops | bytes accessed | tf_op | source)
XLA Modules:
  0.0 110.1 jit_solution(3871216045837333446)
XLA Ops:
  0.0 1.8 %dynamic-slice_bitcast_fusion.1 = (bf16[128,512]{1,0:T(8,128)(2,1)}, bf16[128,512]{1,0:T(8,128)(2,1)S(1)}, bf16[128,512]{1,0:T(8,128)(2,1)S(1)}, bf16[128,512]{1,0:T(8,128)(2,1)}) fusion(bf16[1,128,2048]{2,1,0:T(8,128)(2,1)} %param.7, s32[]{:T(128)S(6)} %select_n.72, s32[]{:T(128)S(6)} %select_n.67, s32[]{:T(128)S(6)} %select_n.66, s32[]{:T(128)S(6)} %select_n.73), kind=kLoop, calls=%fused_computation.5 | loop fusion | bytes 1048592 | tf_op jit(solution)/shard_map/dynamic_slice | solution.py:148
  1.9 1.6 %collective-permute-start = (bf16[128,1024]{1,0:T(8,128)(2,1)S(1)}, bf16[128,1024]{1,0:T(8,128)(2,1)S(1)}, u32[]{:S(2)}, u32[]{:S(2)}) collective-permute-start(bf16[128,1024]{1,0:T(8,128)(2,1)S(1)} %pad_maximum_fusion.rest_0_.rest_8_), channel_id=1, source_target_pairs={{0,1},{1,0},{2,3},{3,2},{4,5},{5,4},{6,7},{7,6},{8,9},{9,8},{10,11... | collective-permute-start | bytes 786440 | tf_op jit(solution)/shard_map/ppermute | solution.py:153
  4.5 1.0 select_reduce_fusion
  6.3 3.7 %collective-permute-done.rest_1_.rest_9_ = bf16[128,1024]{1,0:T(8,128)(2,1)S(1)} collective-permute-done((bf16[128,1024]{1,0:T(8,128)(2,1)S(1)}, bf16[128,1024]{1,0:T(8,128)(2,1)S(1)}, u32[]{:S(2)}, u32[]{:S(2)}) %collective-permute-start) | collective-permute-done | bytes 262176 | tf_op jit(solution)/shard_map/ppermute | solution.py:153
  10.0 1.1 broadcast_in_dim.92
  11.1 5.9 %all-to-all-start = ((bf16[32,8,2176]{2,1,0:T(8,128)(2,1)}), bf16[32,8,2176]{2,1,0:T(8,128)(2,1)S(1)}, u32[]{:S(2)}, u32[]{:S(2)}) async-start(bf16[32,8,2176]{2,1,0:T(8,128)(2,1)} %bitcast.36), calls=%async_computation | async-start | bytes 2228224 | tf_op jit(solution)/shard_map/all_to_all | solution.py:182
  16.9 1.0 pad_maximum_fusion.1.rest_0_.rest_8_
  18.6 1.3 %collective-permute-start.5 = (bf16[128,1024]{1,0:T(8,128)(2,1)S(1)}, bf16[128,1024]{1,0:T(8,128)(2,1)S(1)}, u32[]{:S(2)}, u32[]{:S(2)}) collective-permute-start(bf16[128,1024]{1,0:T(8,128)(2,1)S(1)} %pad_maximum_fusion.1.rest_0_.rest_8_), channel_id=1, source_target_pairs={{0,2},{1,3},{2,4},{3,5},{4,6},{5,7},{8,10},{9,11},{10,12},{11,13},... | collective-permute-start | bytes 786440 | tf_op jit(solution)/shard_map/ppermute | solution.py:157
  19.9 1.3 %collective-permute-start.1 = (bf16[128,1024]{1,0:T(8,128)(2,1)}, bf16[128,1024]{1,0:T(8,128)(2,1)S(1)}, u32[]{:S(2)}, u32[]{:S(2)}) collective-permute-start(bf16[128,1024]{1,0:T(8,128)(2,1)} %copy-done.7), channel_id=1, source_target_pairs={{0,2},{1,3},{2,4},{3,5},{4,6},{5,7},{8,10},{9,11},{10,12},{11,13},... | collective-permute-start | bytes 786440 | tf_op jit(solution)/shard_map/ppermute | solution.py:157
  21.2 21.2 %collective-permute-done.5.rest_2_.rest_10_ = bf16[128,1024]{1,0:T(8,128)(2,1)S(1)} collective-permute-done((bf16[128,1024]{1,0:T(8,128)(2,1)S(1)}, bf16[128,1024]{1,0:T(8,128)(2,1)S(1)}, u32[]{:S(2)}, u32[]{:S(2)}) %collective-permute-start.5) | collective-permute-done | bytes 262176 | tf_op jit(solution)/shard_map/ppermute | solution.py:157
  42.4 1.3 %collective-permute-start.6 = (bf16[128,1024]{1,0:T(8,128)(2,1)S(1)}, bf16[128,1024]{1,0:T(8,128)(2,1)}, u32[]{:S(2)}, u32[]{:S(2)}) collective-permute-start(bf16[128,1024]{1,0:T(8,128)(2,1)S(1)} %collective-permute-done.5.rest_2_.rest_10_), channel_id=1, source_target_pairs={{2,4},{3,5},{4,6},{5,7},{10,12},{11,13},{12,14},{13,15},{18,20},{1... | collective-permute-start | bytes 786440 | tf_op jit(solution)/shard_map/ppermute | solution.py:157
  43.7 2.4 %collective-permute-start.7 = (bf16[128,1024]{1,0:T(8,128)(2,1)S(1)}, bf16[128,1024]{1,0:T(8,128)(2,1)S(1)}, u32[]{:S(2)}, u32[]{:S(2)}) collective-permute-start(bf16[128,1024]{1,0:T(8,128)(2,1)S(1)} %collective-permute-done.5.rest_2_.rest_10_), channel_id=1, source_target_pairs={{2,3},{3,2},{4,5},{5,4},{6,7},{7,6},{10,11},{11,10},{12,13},{13,12... | collective-permute-start | bytes 786440 | tf_op jit(solution)/shard_map/ppermute | solution.py:153
  46.8 0.9 collective-permute-done.1.rest_3_.rest_11_
  47.7 1.3 %collective-permute-start.2 = (bf16[128,1024]{1,0:T(8,128)(2,1)S(1)}, bf16[128,1024]{1,0:T(8,128)(2,1)}, u32[]{:S(2)}, u32[]{:S(2)}) collective-permute-start(bf16[128,1024]{1,0:T(8,128)(2,1)S(1)} %collective-permute-done.1.rest_3_.rest_11_), channel_id=1, source_target_pairs={{2,4},{3,5},{4,6},{5,7},{10,12},{11,13},{12,14},{13,15},{18,20},{1... | collective-permute-start | bytes 786440 | tf_op jit(solution)/shard_map/ppermute | solution.py:157
  48.9 3.4 %collective-permute-start.4 = (bf16[128,1024]{1,0:T(8,128)(2,1)S(1)}, bf16[128,1024]{1,0:T(8,128)(2,1)S(1)}, u32[]{:S(2)}, u32[]{:S(2)}) collective-permute-start(bf16[128,1024]{1,0:T(8,128)(2,1)S(1)} %collective-permute-done.1.rest_3_.rest_11_), channel_id=1, source_target_pairs={{2,3},{3,2},{4,5},{5,4},{6,7},{7,6},{10,11},{11,10},{12,13},{13,12... | collective-permute-start | bytes 786440 | tf_op jit(solution)/shard_map/ppermute | solution.py:153
  53.0 3.9 %collective-permute-done.6.rest_4_.rest_12_ = bf16[128,1024]{1,0:T(8,128)(2,1)} collective-permute-done((bf16[128,1024]{1,0:T(8,128)(2,1)S(1)}, bf16[128,1024]{1,0:T(8,128)(2,1)}, u32[]{:S(2)}, u32[]{:S(2)}) %collective-permute-start.6) | collective-permute-done | bytes 262176 | tf_op jit(solution)/shard_map/ppermute | solution.py:157
  57.7 1.3 %collective-permute-start.12 = (bf16[128,1024]{1,0:T(8,128)(2,1)}, bf16[128,1024]{1,0:T(8,128)(2,1)}, u32[]{:S(2)}, u32[]{:S(2)}) collective-permute-start(bf16[128,1024]{1,0:T(8,128)(2,1)} %collective-permute-done.6.rest_4_.rest_12_), channel_id=1, source_target_pairs={{4,6},{5,7},{12,14},{13,15},{20,22},{21,23},{28,30},{29,31}} | collective-permute-start | bytes 786440 | tf_op jit(solution)/shard_map/ppermute | solution.py:157
  59.0 3.9 %collective-permute-done.2.rest_5_.rest_13_ = bf16[128,1024]{1,0:T(8,128)(2,1)} collective-permute-done((bf16[128,1024]{1,0:T(8,128)(2,1)S(1)}, bf16[128,1024]{1,0:T(8,128)(2,1)}, u32[]{:S(2)}, u32[]{:S(2)}) %collective-permute-start.2) | collective-permute-done | bytes 262176 | tf_op jit(solution)/shard_map/ppermute | solution.py:157
  63.5 1.3 %collective-permute-start.10 = (bf16[128,1024]{1,0:T(8,128)(2,1)}, bf16[128,1024]{1,0:T(8,128)(2,1)}, u32[]{:S(2)}, u32[]{:S(2)}) collective-permute-start(bf16[128,1024]{1,0:T(8,128)(2,1)} %collective-permute-done.2.rest_5_.rest_13_), channel_id=1, source_target_pairs={{4,6},{5,7},{12,14},{13,15},{20,22},{21,23},{28,30},{29,31}} | collective-permute-start | bytes 786440 | tf_op jit(solution)/shard_map/ppermute | solution.py:157
  65.6 4.0 %collective-permute-start.3 = (bf16[128,1024]{1,0:T(8,128)(2,1)}, bf16[128,1024]{1,0:T(8,128)(2,1)}, u32[]{:S(2)}, u32[]{:S(2)}) collective-permute-start(bf16[128,1024]{1,0:T(8,128)(2,1)} %copy-done.1), channel_id=1, source_target_pairs={{0,1},{2,3},{4,5},{6,7},{8,9},{10,11},{12,13},{14,15},{16,17},{18,... | collective-permute-start | bytes 786440 | tf_op jit(solution)/shard_map/ppermute | solution.py:195
  69.6 1.9 %collective-permute-start.9 = (bf16[128,1024]{1,0:T(8,128)(2,1)}, bf16[128,1024]{1,0:T(8,128)(2,1)}, u32[]{:S(2)}, u32[]{:S(2)}) collective-permute-start(bf16[128,1024]{1,0:T(8,128)(2,1)} %collective-permute-done.6.rest_4_.rest_12_), channel_id=1, source_target_pairs={{4,5},{5,4},{6,7},{7,6},{12,13},{13,12},{14,15},{15,14},{20,21},{2... | collective-permute-start | bytes 786440 | tf_op jit(solution)/shard_map/ppermute | solution.py:153
  71.5 3.9 %collective-permute-start.8 = (bf16[128,1024]{1,0:T(8,128)(2,1)}, bf16[128,1024]{1,0:T(8,128)(2,1)}, u32[]{:S(2)}, u32[]{:S(2)}) collective-permute-start(bf16[128,1024]{1,0:T(8,128)(2,1)} %collective-permute-done.2.rest_5_.rest_13_), channel_id=1, source_target_pairs={{4,5},{5,4},{6,7},{7,6},{12,13},{13,12},{14,15},{15,14},{20,21},{2... | collective-permute-start | bytes 786440 | tf_op jit(solution)/shard_map/ppermute | solution.py:153
  75.5 1.9 %collective-permute-start.13 = (bf16[128,1024]{1,0:T(8,128)(2,1)}, bf16[128,1024]{1,0:T(8,128)(2,1)}, u32[]{:S(2)}, u32[]{:S(2)}) collective-permute-start(bf16[128,1024]{1,0:T(8,128)(2,1)} %collective-permute-done.12.rest_6_.rest_14_), channel_id=1, source_target_pairs={{6,7},{7,6},{14,15},{15,14},{22,23},{23,22},{30,31},{31,30}} | collective-permute-start | bytes 786440 | tf_op jit(solution)/shard_map/ppermute | solution.py:153
  77.4 3.9 %collective-permute-start.11 = (bf16[128,1024]{1,0:T(8,128)(2,1)}, bf16[128,1024]{1,0:T(8,128)(2,1)}, u32[]{:S(2)}, u32[]{:S(2)}) collective-permute-start(bf16[128,1024]{1,0:T(8,128)(2,1)} %collective-permute-done.10.rest_7_.rest_15_), channel_id=1, source_target_pairs={{6,7},{7,6},{14,15},{15,14},{22,23},{23,22},{30,31},{31,30}} | collective-permute-start | bytes 786440 | tf_op jit(solution)/shard_map/ppermute | solution.py:153
  83.4 1.4 %dynamic-slice_bitcast_fusion.4 = (s32[8,1,128]{2,1,0:T(1,128)S(1)}, s32[]{:T(128)}) fusion(s32[4,8,1,1,128]{4,3,1,0,2:T(1,128)} %slice.25, s32[]{:T(128)S(6)} %select_n.68, s32[]{:T(128)S(1)} %bitcast.39), kind=kLoop, calls=%fused_computation.22 | loop fusion | flops 3071 | bytes 8204 | tf_op jit(solution)/shard_map/broadcast_in_dim | solution.py:205
  87.3 0.8 select_n.71.prefix_bias_ref
  88.2 1.0 copy-done.2
  89.1 0.9 copy-done.8
  90.1 0.9 copy-done.10
  91.0 0.9 copy-done.12
  92.0 9.0 %shard_map.64.rest_16_ = bf16[128,8192]{1,0:T(8,128)(2,1)} custom-call(s32[3]{0:T(128)S(1)} %pad_add_fusion.2.meta_ref, s32[128,1]{1,0:T(8,128)S(1)} %copy.17.seg_q_ref, s32[8,1,128]{2,1,0:T(1,128)S(1)} %get-tuple-element.29.seg_k_ref, f32[1,256]{1,0:T(1,128)S(1)} %select_n.71.prefix_bias_ref, bf16[128,8192]{1,0:T(8,128)(2,1)S(1)} %bitcast.34, ...), custom_call_target="tpu_custom_call" | custom-call | tf_op jit(solution)/shard_map/pallas_call | solution.py:117
  101.1 9.0 %shard_map.65 = bf16[128,8192]{1,0:T(8,128)(2,1)} custom-call(s32[3]{0:T(128)S(1)} %pad_add_fusion.meta_ref, s32[128,1]{1,0:T(8,128)S(1)} %copy.17.seg_q_ref, s32[8,1,128]{2,1,0:T(1,128)S(1)} %get-tuple-element.29.seg_k_ref, f32[1,256]{1,0:T(1,128)S(1)} %select_n.71.prefix_bias_ref, bf16[128,8192]{1,0:T(8,128)(2,1)S(1)} %bitcast.35, ...), custom_call_target="tpu_custom_call", output_to_operand_aliasing={{}: (23, {})} | custom-call | tf_op jit(solution)/shard_map/pallas_call | solution.py:117
  (50 shorter events, 7.7 us)
Async XLA Ops:
  1.9 8.1 %collective-permute-start = (bf16[128,1024]{1,0:T(8,128)(2,1)S(1)}, bf16[128,1024]{1,0:T(8,128)(2,1)S(1)}, u32[]{:S(2)}, u32[]{:S(2)}) collective-permute-start(bf16[128,1024]{1,0:T(8,128)(2,1)S(1)} %pad_maximum_fusion.rest_0_.rest_8_), channel_id=1, source_target_pairs={{0,1},{1,0},{2,3},{3,2},{4,5},{5,4},{6,7},{7,6},{8,9},{9,8},{10,11... | collective-permute-start | bytes 786440 | tf_op jit(solution)/shard_map/ppermute | solution.py:153
  6.3 59.2 %copy-start.13 = (s32[1,128]{1,0:T(1,128)S(1)}, s32[1,128]{1,0:T(1,128)}, u32[]{:S(2)}) copy-start(s32[1,128]{1,0:T(1,128)} %param.8) | copy-start | bytes 1540
  6.3 81.8 %copy-start = (bf16[1,128,8192]{2,1,0:T(8,128)(2,1)S(1)}, bf16[1,128,8192]{2,1,0:T(8,128)(2,1)}, u32[]{:S(2)}) copy-start(bf16[1,128,8192]{2,1,0:T(8,128)(2,1)} %param.6) | copy-start | bytes 6291460
  10.0 1.1 copy-start.7
  11.1 70.3 %all-to-all-start = ((bf16[32,8,2176]{2,1,0:T(8,128)(2,1)}), bf16[32,8,2176]{2,1,0:T(8,128)(2,1)S(1)}, u32[]{:S(2)}, u32[]{:S(2)}) async-start(bf16[32,8,2176]{2,1,0:T(8,128)(2,1)} %bitcast.36), calls=%async_computation | async-start | bytes 2228224 | tf_op jit(solution)/shard_map/all_to_all | solution.py:182
  17.9 0.7 copy-start.1
  18.6 23.8 %collective-permute-start.5 = (bf16[128,1024]{1,0:T(8,128)(2,1)S(1)}, bf16[128,1024]{1,0:T(8,128)(2,1)S(1)}, u32[]{:S(2)}, u32[]{:S(2)}) collective-permute-start(bf16[128,1024]{1,0:T(8,128)(2,1)S(1)} %pad_maximum_fusion.1.rest_0_.rest_8_), channel_id=1, source_target_pairs={{0,2},{1,3},{2,4},{3,5},{4,6},{5,7},{8,10},{9,11},{10,12},{11,13},... | collective-permute-start | bytes 786440 | tf_op jit(solution)/shard_map/ppermute | solution.py:157
  19.9 27.7 %collective-permute-start.1 = (bf16[128,1024]{1,0:T(8,128)(2,1)}, bf16[128,1024]{1,0:T(8,128)(2,1)S(1)}, u32[]{:S(2)}, u32[]{:S(2)}) collective-permute-start(bf16[128,1024]{1,0:T(8,128)(2,1)} %copy-done.7), channel_id=1, source_target_pairs={{0,2},{1,3},{2,4},{3,5},{4,6},{5,7},{8,10},{9,11},{10,12},{11,13},... | collective-permute-start | bytes 786440 | tf_op jit(solution)/shard_map/ppermute | solution.py:157
  42.4 14.5 %collective-permute-start.6 = (bf16[128,1024]{1,0:T(8,128)(2,1)S(1)}, bf16[128,1024]{1,0:T(8,128)(2,1)}, u32[]{:S(2)}, u32[]{:S(2)}) collective-permute-start(bf16[128,1024]{1,0:T(8,128)(2,1)S(1)} %collective-permute-done.5.rest_2_.rest_10_), channel_id=1, source_target_pairs={{2,4},{3,5},{4,6},{5,7},{10,12},{11,13},{12,14},{13,15},{18,20},{1... | collective-permute-start | bytes 786440 | tf_op jit(solution)/shard_map/ppermute | solution.py:157
  43.7 13.3 %collective-permute-start.7 = (bf16[128,1024]{1,0:T(8,128)(2,1)S(1)}, bf16[128,1024]{1,0:T(8,128)(2,1)S(1)}, u32[]{:S(2)}, u32[]{:S(2)}) collective-permute-start(bf16[128,1024]{1,0:T(8,128)(2,1)S(1)} %collective-permute-done.5.rest_2_.rest_10_), channel_id=1, source_target_pairs={{2,3},{3,2},{4,5},{5,4},{6,7},{7,6},{10,11},{11,10},{12,13},{13,12... | collective-permute-start | bytes 786440 | tf_op jit(solution)/shard_map/ppermute | solution.py:153
  46.1 0.7 copy-start.9
  47.7 15.2 %collective-permute-start.2 = (bf16[128,1024]{1,0:T(8,128)(2,1)S(1)}, bf16[128,1024]{1,0:T(8,128)(2,1)}, u32[]{:S(2)}, u32[]{:S(2)}) collective-permute-start(bf16[128,1024]{1,0:T(8,128)(2,1)S(1)} %collective-permute-done.1.rest_3_.rest_11_), channel_id=1, source_target_pairs={{2,4},{3,5},{4,6},{5,7},{10,12},{11,13},{12,14},{13,15},{18,20},{1... | collective-permute-start | bytes 786440 | tf_op jit(solution)/shard_map/ppermute | solution.py:157
  48.9 13.9 %collective-permute-start.4 = (bf16[128,1024]{1,0:T(8,128)(2,1)S(1)}, bf16[128,1024]{1,0:T(8,128)(2,1)S(1)}, u32[]{:S(2)}, u32[]{:S(2)}) collective-permute-start(bf16[128,1024]{1,0:T(8,128)(2,1)S(1)} %collective-permute-done.1.rest_3_.rest_11_), channel_id=1, source_target_pairs={{2,3},{3,2},{4,5},{5,4},{6,7},{7,6},{10,11},{11,10},{12,13},{13,12... | collective-permute-start | bytes 786440 | tf_op jit(solution)/shard_map/ppermute | solution.py:153
  52.3 0.7 copy-start.11
  57.0 0.7 copy-start.3
  57.7 17.8 %collective-permute-start.12 = (bf16[128,1024]{1,0:T(8,128)(2,1)}, bf16[128,1024]{1,0:T(8,128)(2,1)}, u32[]{:S(2)}, u32[]{:S(2)}) collective-permute-start(bf16[128,1024]{1,0:T(8,128)(2,1)} %collective-permute-done.6.rest_4_.rest_12_), channel_id=1, source_target_pairs={{4,6},{5,7},{12,14},{13,15},{20,22},{21,23},{28,30},{29,31}} | collective-permute-start | bytes 786440 | tf_op jit(solution)/shard_map/ppermute | solution.py:157
  62.8 0.7 copy-start.5
  63.5 13.9 %collective-permute-start.10 = (bf16[128,1024]{1,0:T(8,128)(2,1)}, bf16[128,1024]{1,0:T(8,128)(2,1)}, u32[]{:S(2)}, u32[]{:S(2)}) collective-permute-start(bf16[128,1024]{1,0:T(8,128)(2,1)} %collective-permute-done.2.rest_5_.rest_13_), channel_id=1, source_target_pairs={{4,6},{5,7},{12,14},{13,15},{20,22},{21,23},{28,30},{29,31}} | collective-permute-start | bytes 786440 | tf_op jit(solution)/shard_map/ppermute | solution.py:157
  65.6 35.4 %collective-permute-start.3 = (bf16[128,1024]{1,0:T(8,128)(2,1)}, bf16[128,1024]{1,0:T(8,128)(2,1)}, u32[]{:S(2)}, u32[]{:S(2)}) collective-permute-start(bf16[128,1024]{1,0:T(8,128)(2,1)} %copy-done.1), channel_id=1, source_target_pairs={{0,1},{2,3},{4,5},{6,7},{8,9},{10,11},{12,13},{14,15},{16,17},{18,... | collective-permute-start | bytes 786440 | tf_op jit(solution)/shard_map/ppermute | solution.py:195
  69.6 31.5 %collective-permute-start.9 = (bf16[128,1024]{1,0:T(8,128)(2,1)}, bf16[128,1024]{1,0:T(8,128)(2,1)}, u32[]{:S(2)}, u32[]{:S(2)}) collective-permute-start(bf16[128,1024]{1,0:T(8,128)(2,1)} %collective-permute-done.6.rest_4_.rest_12_), channel_id=1, source_target_pairs={{4,5},{5,4},{6,7},{7,6},{12,13},{13,12},{14,15},{15,14},{20,21},{2... | collective-permute-start | bytes 786440 | tf_op jit(solution)/shard_map/ppermute | solution.py:153
  71.5 29.6 %collective-permute-start.8 = (bf16[128,1024]{1,0:T(8,128)(2,1)}, bf16[128,1024]{1,0:T(8,128)(2,1)}, u32[]{:S(2)}, u32[]{:S(2)}) collective-permute-start(bf16[128,1024]{1,0:T(8,128)(2,1)} %collective-permute-done.2.rest_5_.rest_13_), channel_id=1, source_target_pairs={{4,5},{5,4},{6,7},{7,6},{12,13},{13,12},{14,15},{15,14},{20,21},{2... | collective-permute-start | bytes 786440 | tf_op jit(solution)/shard_map/ppermute | solution.py:153
  75.5 25.6 %collective-permute-start.13 = (bf16[128,1024]{1,0:T(8,128)(2,1)}, bf16[128,1024]{1,0:T(8,128)(2,1)}, u32[]{:S(2)}, u32[]{:S(2)}) collective-permute-start(bf16[128,1024]{1,0:T(8,128)(2,1)} %collective-permute-done.12.rest_6_.rest_14_), channel_id=1, source_target_pairs={{6,7},{7,6},{14,15},{15,14},{22,23},{23,22},{30,31},{31,30}} | collective-permute-start | bytes 786440 | tf_op jit(solution)/shard_map/ppermute | solution.py:153
  77.4 23.7 %collective-permute-start.11 = (bf16[128,1024]{1,0:T(8,128)(2,1)}, bf16[128,1024]{1,0:T(8,128)(2,1)}, u32[]{:S(2)}, u32[]{:S(2)}) collective-permute-start(bf16[128,1024]{1,0:T(8,128)(2,1)} %collective-permute-done.10.rest_7_.rest_15_), channel_id=1, source_target_pairs={{6,7},{7,6},{14,15},{15,14},{22,23},{23,22},{30,31},{31,30}} | collective-permute-start | bytes 786440 | tf_op jit(solution)/shard_map/ppermute | solution.py:153
  88.2 1.0 copy-start.2
  89.1 0.9 copy-start.8
  90.1 0.9 copy-start.10
  91.0 0.9 copy-start.12
  92.0 9.1 %copy-start.4 = (bf16[128,1024]{1,0:T(8,128)(2,1)S(1)}, bf16[128,1024]{1,0:T(8,128)(2,1)}, u32[]{:S(2)}) copy-start(bf16[128,1024]{1,0:T(8,128)(2,1)} %copy-done.3) | copy-start | bytes 786436
  92.0 9.1 %copy-start.6 = (bf16[128,1024]{1,0:T(8,128)(2,1)S(1)}, bf16[128,1024]{1,0:T(8,128)(2,1)}, u32[]{:S(2)}) copy-start(bf16[128,1024]{1,0:T(8,128)(2,1)} %copy-done.5) | copy-start | bytes 786436

commit v4 on v3

v4 whole, which is shorter than its diff:
```python
import functools
import math

import jax
import jax.numpy as jnp
from jax import lax
from jax.experimental import pallas as pl
from jax.experimental.pallas import tpu as pltpu
from jax.sharding import PartitionSpec as P

H = 64
KVH = 8
HD = 128
GQ = H // KVH
REACH = 7
SLAB = 2
FILL = -1e30


def halves_kernel(meta_ref, a_ref, b_ref, mine_ref, theirs_ref):
    mine_ref[...] = a_ref[...]
    theirs_ref[...] = b_ref[...]


def halves(kv, side):
    rows, half = kv.shape[0], kv.shape[1] // 4
    shape = (rows, half)
    return pl.pallas_call(
        halves_kernel,
        grid_spec=pltpu.PrefetchScalarGridSpec(
            num_scalar_prefetch=1,
            grid=(2,),
            in_specs=[
                pl.BlockSpec(shape, lambda i, m: (0, 2 * i + m[0])),
                pl.BlockSpec(shape, lambda i, m: (0, 2 * i + 1 - m[0])),
            ],
            out_specs=[pl.BlockSpec(shape, lambda i, m: (0, i))] * 2,
        ),
        out_shape=[jax.ShapeDtypeStruct((rows, 2 * half), kv.dtype)] * 2,
    )(side.reshape(1), kv, kv)


def attend_kernel(pairs, tile, count, meta_ref, seg_ref, q_ref, prefix_ref, *rest):
    pieces = rest[: 2 * pairs]
    o_ref, k_ref, v_ref, ints_ref, seg_k_ref, bias_ref, s_ref, top_ref, reach_ref, sems, sem = (
        rest[-11:]
    )
    rows = q_ref.shape[0]
    heads = k_ref.shape[0]
    step = 2 * rows
    prefix_keys = prefix_ref.shape[0]
    group, block, head0, limit = meta_ref[0], meta_ref[1], meta_ref[2], meta_ref[3]
    head = pl.program_id(0)
    scale = math.log2(math.e) / math.sqrt(HD)
    nt = (((1,), (1,)), ((), ()))

    def column(index):
        return pl.ds(pl.multiple_of(index * HD, HD), HD)

    def copies(h):
        sources = [(prefix_ref, head0 + h, KVH + head0 + h, 0, prefix_keys)]
        for j, piece in enumerate(pieces):
            sources.append((piece, h, heads + h, prefix_keys + j * rows, rows))
        for j, (ref, k_at, v_at, start, size) in enumerate(sources):
            at = pl.ds(start, size)
            yield pltpu.make_async_copy(
                ref.at[:, column(k_at)], k_ref.at[h, at], sems.at[h, 2 * j]
            )
            yield pltpu.make_async_copy(
                ref.at[:, column(v_at)], v_ref.at[h, at, pl.ds(0, HD)], sems.at[h, 2 * j + 1]
            )

    @pl.when(head == 0)
    def _():
        ints_copy = pltpu.make_async_copy(
            prefix_ref.at[:, pl.ds(2 * KVH * HD, rows)], ints_ref, sem
        )
        ints_copy.start()
        for h in range(heads):
            for copy in copies(h):
                copy.start()
        v_ref[:, :, HD:] = jnp.ones((heads, v_ref.shape[1], HD), v_ref.dtype)
        ints_copy.wait()
        ints = ints_ref[...].astype(jnp.float32)
        seg_k_ref[...] = ints
        part = lax.rem(lax.broadcasted_iota(jnp.int32, ints.shape, 0), tile)
        place = jnp.where(part == 0, pltpu.roll(ints, prefix_keys - 1, 0), ints)
        live = place.astype(jnp.int32) * tile + part < limit
        bias_ref[:, :prefix_keys] = jnp.where(live, 0.0, FILL).T

        own = seg_ref[...].astype(jnp.float32)
        first_key = group * count * tile
        segs = seg_k_ref[pl.ds(pl.multiple_of(first_key, tile), count * tile), :]
        heads_of = lax.rem(lax.broadcasted_iota(jnp.int32, segs.shape, 0), tile) == 0
        earlier = jnp.sum(jnp.where(heads_of & (segs < own[:, :1]), 1.0, 0.0))
        reach_ref[0] = lax.div(block, 2) - lax.div(earlier.astype(jnp.int32), step)

        seg_q = jnp.broadcast_to(own, (rows, rows)).T
        row_pos = block * rows + lax.broadcasted_iota(jnp.int32, (rows, rows), 0)
        lane = lax.broadcasted_iota(jnp.int32, (rows, rows), 1)
        for k in range(pairs):
            for j, first in enumerate((block, block + 1 - 2 * lax.rem(block, 2))):
                key_block = jnp.maximum(first - 2 * k, 0)
                at = pl.multiple_of(first_key + key_block * tile, tile)
                seg_k = seg_k_ref[pl.ds(at, tile), :][:1]
                seen = (seg_k == seg_q) & (key_block * rows + lane <= row_pos)
                at = prefix_keys + (2 * k + j) * rows
                bias_ref[:, at : at + rows] = jnp.where(seen, 0.0, FILL)

    for copy in copies(head):
        copy.wait()

    def body(near):
        steps = prefix_keys // step + near + 1

        def score(slab):
            of = range(slab * SLAB, (slab + 1) * SLAB)
            q = jnp.concatenate([q_ref[:, g * HD : (g + 1) * HD] for g in of])
            top = None
            for i in range(steps):
                at = slice(i * step, (i + 1) * step)
                s = lax.dot_general(q, k_ref[head, at, :], nt, preferred_element_type=jnp.float32)
                s = (s.reshape(SLAB, rows, step) + bias_ref[:, at][None]).reshape(-1, step)
                s_ref[slab % 2, :, at] = s
                high = jnp.maximum(s[:, :rows], s[:, rows:])
                top = high if top is None else jnp.maximum(top, high)
            top = jnp.max(top, axis=1, keepdims=True)
            top_ref[slab % 2] = jnp.broadcast_to(top, (SLAB * rows, HD))

        def weigh(slab):
            top = top_ref[slab % 2]
            weights = [
                jnp.exp2((s_ref[slab % 2, :, i * HD : (i + 1) * HD] - top) * scale).astype(
                    jnp.bfloat16
                )
                for i in range(steps * step // HD)
            ]
            acc = jnp.dot(
                jnp.concatenate(weights, axis=1),
                v_ref[head, : steps * step, :],
                preferred_element_type=jnp.float32,
            )
            out = (acc[:, :HD] / acc[:, HD:]).astype(o_ref.dtype)
            for j in range(SLAB):
                g = slab * SLAB + j
                o_ref[:, g * HD : (g + 1) * HD] = out[j * rows : (j + 1) * rows]

        score(0)
        for slab in range(GQ // SLAB):
            if slab + 1 < GQ // SLAB:
                score(slab + 1)
            weigh(slab)

    for near in range(pairs):
        pl.when(reach_ref[0] == near)(functools.partial(body, near))


def attend(meta, segments, queries, pieces, prefix, tile, count, out):
    rows = queries.shape[0]
    prefix_keys = prefix.shape[0]
    pairs = len(pieces) // 2
    heads = pieces[0].shape[1] // (2 * HD)
    keys = rows * len(pieces) + prefix_keys
    wide = (rows, GQ * HD)
    far = pl.BlockSpec(memory_space=pl.ANY)
    in_specs = [
        pl.BlockSpec((1, rows), lambda i, m: (0, 0)),
        pl.BlockSpec(wide, lambda i, m: (0, m[2] + i)),
        far,
        *[far] * len(pieces),
    ]
    args = [meta, segments, queries, prefix, *pieces]
    aliases = {}
    if out is not None:
        in_specs.append(far)
        args.append(out)
        aliases = {len(args) - 1: 0}
    return pl.pallas_call(
        functools.partial(attend_kernel, pairs, tile, count),
        grid_spec=pltpu.PrefetchScalarGridSpec(
            num_scalar_prefetch=1,
            grid=(heads,),
            in_specs=in_specs,
            out_specs=pl.BlockSpec(wide, lambda i, m: (0, m[2] + i)),
            scratch_shapes=[
                pltpu.VMEM((heads, keys, HD), queries.dtype),
                pltpu.VMEM((heads, keys, 2 * HD), queries.dtype),
                pltpu.VMEM((prefix_keys, rows), queries.dtype),
                pltpu.VMEM((prefix_keys, rows), jnp.float32),
                pltpu.VMEM((rows, keys), jnp.float32),
                pltpu.VMEM((2, SLAB * rows, keys), jnp.float32),
                pltpu.VMEM((2, SLAB * rows, HD), jnp.float32),
                pltpu.SMEM((1,), jnp.int32),
                pltpu.SemaphoreType.DMA((heads, 2 * (len(pieces) + 1))),
                pltpu.SemaphoreType.DMA(()),
            ],
        ),
        out_shape=jax.ShapeDtypeStruct(queries.shape, queries.dtype),
        input_output_aliases=aliases,
        compiler_params=pltpu.CompilerParams(vmem_limit_bytes=40 * 1024 * 1024),
    )(*args)


def on_device(queries, resp_kv, resp_segments, prefix_kv, tile_plan, prompt_lengths):
    rows = queries.shape[1]
    tiles, tile, columns = prefix_kv.shape
    groups, count = lax.axis_size("prompt"), lax.axis_size("resp")
    group = lax.axis_index("prompt")
    block = lax.axis_index("resp")
    side = block % 2
    steps = min(count // 2 - 1, (REACH + 1) // 2)
    assert tiles == groups

    def swap(value, first):
        return lax.ppermute(value, "resp", [(r, r ^ 1) for r in range(2 * first, count)])

    def climb(value, step):
        pairs = [(r, r + 2) for r in range(2 * step - 2, count - 2)]
        return lax.ppermute(value, "resp", pairs)

    mine, theirs = halves(resp_kv[0], side)
    straight = [mine, swap(theirs, 0), climb(mine, 1)]
    crossed = [theirs, lax.ppermute(mine, "resp", [(r, r + 1) for r in range(0, count, 2)])]

    pick = tile_plan[None, :, 0] == jnp.arange(groups, dtype=jnp.int32)[:, None]
    place = jnp.sum(jnp.where(pick, tile_plan[None, :, 1], 0), axis=1, dtype=jnp.int32)
    own_tiles = jnp.sum(
        jnp.where(pick[:, :, None, None], prefix_kv[None], 0).astype(jnp.float32), axis=1
    )
    row = jnp.arange(tile, dtype=jnp.int32)[:, None]
    extra = jnp.where(row == 0, resp_segments[0], place.reshape(groups, 1, 1))
    out_tiles = jnp.concatenate([own_tiles, extra.astype(jnp.float32)], axis=-1)
    out_tiles = jnp.broadcast_to(
        out_tiles.astype(prefix_kv.dtype)[:, None], (groups, count, tile, columns + rows)
    ).reshape(groups * count, tile, columns + rows)
    out_tiles, straight[2] = lax.optimization_barrier((out_tiles, straight[2]))
    came = lax.all_to_all(
        out_tiles, ("prompt", "resp"), split_axis=0, concat_axis=0, tiled=True
    )
    prefix = came.reshape(-1, columns + rows)

    for step in range(1, steps + 1):
        for k in range(2):
            if step + k == 1:
                continue
            source = straight[-2]
            late = 1 if step == 2 else 2 * (step - 2) + 1 - k
            if step > 2 or step + k == 3:
                source, crossed[late] = lax.optimization_barrier((source, crossed[late]))
            straight.append(climb(source, step))
        crossed += [swap(straight[-1], step), swap(straight[-2], step)]

    out = None
    for first, pieces in ((side, straight), (1 - side, crossed)):
        meta = jnp.stack([group, block, first * (KVH // 2), prompt_lengths[0]])
        out = attend(meta, resp_segments, queries[0], pieces, prefix, tile, count, out)
    return out[None]


def solution(mesh):
    return jax.shard_map(
        on_device,
        mesh=mesh,
        in_specs=(
            P("prompt", "resp", None),
            P("prompt", "resp", None),
            P("prompt", "resp"),
            P(("prompt", "resp"), None, None),
            P(("prompt", "resp"), None),
            P("prompt"),
        ),
        out_specs=P("prompt", "resp", None),
        check_vma=False,
    )
```

time: 112 us -> 100 us (0.89); the launches traced: 110 us -> 99.5 us
  Pallas kernels: 18 us -> 23.1 us
  local copies, waits for them, and re-layouts: 12.6 us -> 8.17 us
  other arithmetic: 5.98 us -> 2.05 us
  starting transfers between devices: 36.5 us -> 32.9 us
  between operations: 3.43 us -> 0.9 us
  waiting for transfers between devices: 33.6 us -> 32.4 us
    ppermute x6, waiting for transfers between devices: 29.9 us -> 17.6 us  [climb(): return lax.ppermute(value, 'resp', pairs)]
    ppermute x7, waiting for transfers between devices: 3.67 us -> 14.6 us  [swap(): lax.ppermute(value, 'resp', [(r, r ^ 1) for r in range(2 * first, count)])]
    pallas_call x2 -> x3, Pallas kernels: 18 us -> 23.1 us  [the longest x2 21.3 us: attend(): pl.pallas_call(functools.partial(attend_kernel, pairs, tile, count), grid...]
    ppermute x7, starting transfers between devices: 19 us -> 16.8 us  [swap(): lax.ppermute(value, 'resp', [(r, r ^ 1) for r in range(2 * first, count)])]
    dynamic_slice x1 -> x0, local copies, waits for them, and re-layouts: 1.84 us -> none  [part(): k = lax.dynamic_slice_in_dim(resp_kv[0], owner * half, half, 1)]
    ppermute x1, starting transfers between devices: 3.98 us -> 2.44 us  [on_device(): lax.ppermute(mine, 'resp', [(r, r + 1) for r in range(0, count, 2)])]
    broadcast_in_dim x1 -> x0, other arithmetic: 1.37 us -> none  [on_device(): seg_k = seg_k[:, None, :]]
  transfers between devices with their start and end apart: 15 -> 15, of which waited for: 5 -> 8; matrix products, arithmetic and copies ran while one was open for 8% -> 3% of each run, Pallas kernels for 8% -> 11%
where the time goes in v4:
time: 100 us; the launch traced here: 99.5 us
  starting transfers between devices  32.9 us (33%)
  waiting for transfers between devices  32.4 us (32%)
  Pallas kernels  23.1 us (23%)
  local copies, waits for them, and re-layouts  8.17 us (8%)
  other arithmetic  2.05 us (2%)
    pallas_call x2, Pallas kernels, attend(): pl.pallas_call(functools.partial(attend_kernel, pairs, tile, count), grid...  21.3 us
    ppermute x6, waiting for transfers between devices, climb(): return lax.ppermute(value, 'resp', pairs)  17.6 us
    ppermute x7, starting transfers between devices, swap(): lax.ppermute(value, 'resp', [(r, r ^ 1) for r in range(2 * first, count)])  16.8 us
    ppermute x7, waiting for transfers between devices, swap(): lax.ppermute(value, 'resp', [(r, r ^ 1) for r in range(2 * first, count)])  14.6 us
    ppermute x6, starting transfers between devices, climb(): return lax.ppermute(value, 'resp', pairs)  7.82 us
    unnamed x28, local copies, waits for them, and re-layouts  6.35 us
    all_to_all x1, starting transfers between devices, on_device(): lax.all_to_all(out_tiles, ('prompt', 'resp'), split_axis=0, concat_axis=0...  5.86 us
    ppermute x1, starting transfers between devices, on_device(): lax.ppermute(mine, 'resp', [(r, r + 1) for r in range(0, count, 2)])  2.44 us
  transfers between devices with their start and end apart: 15, of which 8 were waited for; matrix products, arithmetic and copies ran while one was open for 3% of the time, Pallas kernels for 11%

profile of v4, /device:TPU:26, one launch (start us, length us, event | category | flops | bytes accessed | tf_op | source)
XLA Modules:
  0.0 99.5 jit_solution(8569156752931625037)
XLA Ops:
  0.0 1.8 %shard_map.64 = (bf16[128,1024]{1,0:T(8,128)(2,1)}, bf16[128,1024]{1,0:T(8,128)(2,1)}) custom-call(s32[1]{0:T(128)} %bitcast.8.meta_ref, bf16[128,2048]{1,0:T(8,128)(2,1)} %bitcast.21, bf16[128,2048]{1,0:T(8,128)(2,1)} %bitcast.22), custom_call_target="tpu_custom_call" | custom-call | tf_op jit(solution)/shard_map/pallas_call | solution.py:28
  1.8 1.4 %collective-permute-start = (bf16[128,1024]{1,0:T(8,128)(2,1)}, bf16[128,1024]{1,0:T(8,128)(2,1)}, u32[]{:S(2)}, u32[]{:S(2)}) collective-permute-start(bf16[128,1024]{1,0:T(8,128)(2,1)} %get-tuple-element.15.rest_0_), channel_id=1, source_target_pairs={{0,2},{1,3},{2,4},{3,5},{4,6},{5,7},{8,10},{9,11},{10,12},{11,13},... | collective-permute-start | bytes 786440 | tf_op jit(solution)/shard_map/ppermute | solution.py:219
  3.3 0.8 slice_bitcast_fusion.1
  4.2 1.0 %select_reduce_fusion = bf16[4,8,2048]{2,1,0:T(8,128)(2,1)S(1)} fusion(pred[4,4]{1,0:T(4,128)(4,1)S(1)} %iota_compare_fusion, bf16[4,8,2048]{2,1,0:T(8,128)(2,1)} %param.9), kind=kLoop, calls=%fused_computation | loop fusion | flops 458752 | bytes 262160 | tf_op jit(solution)/shard_map/reduce_sum | solution.py:227
  5.2 0.7 convert_convert_fusion
  6.0 6.3 %collective-permute-done.rest_2_ = bf16[128,1024]{1,0:T(8,128)(2,1)} collective-permute-done((bf16[128,1024]{1,0:T(8,128)(2,1)}, bf16[128,1024]{1,0:T(8,128)(2,1)}, u32[]{:S(2)}, u32[]{:S(2)}) %collective-permute-start) | collective-permute-done | bytes 262176 | tf_op jit(solution)/shard_map/ppermute | solution.py:219
  12.2 1.1 %broadcast_in_dim.76 = bf16[4,8,8,2176]{3,2,1,0:T(8,128)(2,1)} broadcast(bf16[4,8,2176]{2,1,0:T(8,128)(2,1)S(1)} %pad_maximum_fusion), dimensions={0,2,3} | broadcast | bytes 1253376 | tf_op jit(solution)/shard_map/broadcast_in_dim | solution.py:233
  13.3 5.9 %all-to-all-start = ((bf16[32,8,2176]{2,1,0:T(8,128)(2,1)}), bf16[32,8,2176]{2,1,0:T(8,128)(2,1)S(1)}, u32[]{:S(2)}, u32[]{:S(2)}) async-start(bf16[32,8,2176]{2,1,0:T(8,128)(2,1)} %bitcast.20), calls=%async_computation | async-start | bytes 2228224 | tf_op jit(solution)/shard_map/all_to_all | solution.py:237
  19.2 1.6 %collective-permute-start.1 = (bf16[128,1024]{1,0:T(8,128)(2,1)S(1)}, bf16[128,1024]{1,0:T(8,128)(2,1)S(1)}, u32[]{:S(2)}, u32[]{:S(2)}) collective-permute-start(bf16[128,1024]{1,0:T(8,128)(2,1)S(1)} %copy-done.1), channel_id=1, source_target_pairs={{0,1},{1,0},{2,3},{3,2},{4,5},{5,4},{6,7},{7,6},{8,9},{9,8},{10,11... | collective-permute-start | bytes 786440 | tf_op jit(solution)/shard_map/ppermute | solution.py:215
  20.7 2.4 %collective-permute-start.3 = (bf16[128,1024]{1,0:T(8,128)(2,1)}, bf16[128,1024]{1,0:T(8,128)(2,1)S(1)}, u32[]{:S(2)}, u32[]{:S(2)}) collective-permute-start(bf16[128,1024]{1,0:T(8,128)(2,1)} %get-tuple-element.15.rest_0_), channel_id=1, source_target_pairs={{0,1},{2,3},{4,5},{6,7},{8,9},{10,11},{12,13},{14,15},{16,17},{18,... | collective-permute-start | bytes 786440 | tf_op jit(solution)/shard_map/ppermute | solution.py:223
  23.2 14.4 %collective-permute-done.1.rest_1_ = bf16[128,1024]{1,0:T(8,128)(2,1)S(1)} collective-permute-done((bf16[128,1024]{1,0:T(8,128)(2,1)S(1)}, bf16[128,1024]{1,0:T(8,128)(2,1)S(1)}, u32[]{:S(2)}, u32[]{:S(2)}) %collective-permute-start.1) | collective-permute-done | bytes 262176 | tf_op jit(solution)/shard_map/ppermute | solution.py:215
  37.6 1.3 %collective-permute-start.2 = (bf16[128,1024]{1,0:T(8,128)(2,1)S(1)}, bf16[128,1024]{1,0:T(8,128)(2,1)S(1)}, u32[]{:S(2)}, u32[]{:S(2)}) collective-permute-start(bf16[128,1024]{1,0:T(8,128)(2,1)S(1)} %collective-permute-done.1.rest_1_), channel_id=1, source_target_pairs={{0,2},{1,3},{2,4},{3,5},{4,6},{5,7},{8,10},{9,11},{10,12},{11,13},... | collective-permute-start | bytes 786440 | tf_op jit(solution)/shard_map/ppermute | solution.py:219
  39.6 1.3 %collective-permute-start.6 = (bf16[128,1024]{1,0:T(8,128)(2,1)}, bf16[128,1024]{1,0:T(8,128)(2,1)}, u32[]{:S(2)}, u32[]{:S(2)}) collective-permute-start(bf16[128,1024]{1,0:T(8,128)(2,1)} %collective-permute-done.rest_2_), channel_id=1, source_target_pairs={{2,4},{3,5},{4,6},{5,7},{10,12},{11,13},{12,14},{13,15},{18,20},{1... | collective-permute-start | bytes 786440 | tf_op jit(solution)/shard_map/ppermute | solution.py:219
  40.9 1.9 %collective-permute-start.7 = (bf16[128,1024]{1,0:T(8,128)(2,1)}, bf16[128,1024]{1,0:T(8,128)(2,1)S(1)}, u32[]{:S(2)}, u32[]{:S(2)}) collective-permute-start(bf16[128,1024]{1,0:T(8,128)(2,1)} %collective-permute-done.rest_2_), channel_id=1, source_target_pairs={{2,3},{3,2},{4,5},{5,4},{6,7},{7,6},{10,11},{11,10},{12,13},{13,12... | collective-permute-start | bytes 786440 | tf_op jit(solution)/shard_map/ppermute | solution.py:215
  43.7 5.7 %collective-permute-done.2.rest_3_ = bf16[128,1024]{1,0:T(8,128)(2,1)S(1)} collective-permute-done((bf16[128,1024]{1,0:T(8,128)(2,1)S(1)}, bf16[128,1024]{1,0:T(8,128)(2,1)S(1)}, u32[]{:S(2)}, u32[]{:S(2)}) %collective-permute-start.2) | collective-permute-done | bytes 262176 | tf_op jit(solution)/shard_map/ppermute | solution.py:219
  49.4 1.3 %collective-permute-start.4 = (bf16[128,1024]{1,0:T(8,128)(2,1)S(1)}, bf16[128,1024]{1,0:T(8,128)(2,1)}, u32[]{:S(2)}, u32[]{:S(2)}) collective-permute-start(bf16[128,1024]{1,0:T(8,128)(2,1)S(1)} %collective-permute-done.2.rest_3_), channel_id=1, source_target_pairs={{2,4},{3,5},{4,6},{5,7},{10,12},{11,13},{12,14},{13,15},{18,20},{1... | collective-permute-start | bytes 786440 | tf_op jit(solution)/shard_map/ppermute | solution.py:219
  50.6 2.1 %collective-permute-start.5 = (bf16[128,1024]{1,0:T(8,128)(2,1)S(1)}, bf16[128,1024]{1,0:T(8,128)(2,1)S(1)}, u32[]{:S(2)}, u32[]{:S(2)}) collective-permute-start(bf16[128,1024]{1,0:T(8,128)(2,1)S(1)} %collective-permute-done.2.rest_3_), channel_id=1, source_target_pairs={{2,3},{3,2},{4,5},{5,4},{6,7},{7,6},{10,11},{11,10},{12,13},{13,12... | collective-permute-start | bytes 786440 | tf_op jit(solution)/shard_map/ppermute | solution.py:215
  53.5 1.6 %collective-permute-done.6.rest_4_ = bf16[128,1024]{1,0:T(8,128)(2,1)} collective-permute-done((bf16[128,1024]{1,0:T(8,128)(2,1)}, bf16[128,1024]{1,0:T(8,128)(2,1)}, u32[]{:S(2)}, u32[]{:S(2)}) %collective-permute-start.6) | collective-permute-done | bytes 262176 | tf_op jit(solution)/shard_map/ppermute | solution.py:219
  55.8 1.3 %collective-permute-start.12 = (bf16[128,1024]{1,0:T(8,128)(2,1)}, bf16[128,1024]{1,0:T(8,128)(2,1)}, u32[]{:S(2)}, u32[]{:S(2)}) collective-permute-start(bf16[128,1024]{1,0:T(8,128)(2,1)} %collective-permute-done.6.rest_4_), channel_id=1, source_target_pairs={{4,6},{5,7},{12,14},{13,15},{20,22},{21,23},{28,30},{29,31}} | collective-permute-start | bytes 786440 | tf_op jit(solution)/shard_map/ppermute | solution.py:219
  57.1 3.3 %collective-permute-done.4.rest_5_ = bf16[128,1024]{1,0:T(8,128)(2,1)} collective-permute-done((bf16[128,1024]{1,0:T(8,128)(2,1)S(1)}, bf16[128,1024]{1,0:T(8,128)(2,1)}, u32[]{:S(2)}, u32[]{:S(2)}) %collective-permute-start.4) | collective-permute-done | bytes 262176 | tf_op jit(solution)/shard_map/ppermute | solution.py:219
  60.4 0.7 copy-done.9
  61.1 1.3 %collective-permute-start.10 = (bf16[128,1024]{1,0:T(8,128)(2,1)}, bf16[128,1024]{1,0:T(8,128)(2,1)}, u32[]{:S(2)}, u32[]{:S(2)}) collective-permute-start(bf16[128,1024]{1,0:T(8,128)(2,1)} %collective-permute-done.4.rest_5_), channel_id=1, source_target_pairs={{4,6},{5,7},{12,14},{13,15},{20,22},{21,23},{28,30},{29,31}} | collective-permute-start | bytes 786440 | tf_op jit(solution)/shard_map/ppermute | solution.py:219
  62.4 2.3 %collective-permute-start.9 = (bf16[128,1024]{1,0:T(8,128)(2,1)}, bf16[128,1024]{1,0:T(8,128)(2,1)}, u32[]{:S(2)}, u32[]{:S(2)}) collective-permute-start(bf16[128,1024]{1,0:T(8,128)(2,1)} %collective-permute-done.6.rest_4_), channel_id=1, source_target_pairs={{4,5},{5,4},{6,7},{7,6},{12,13},{13,12},{14,15},{15,14},{20,21},{2... | collective-permute-start | bytes 786440 | tf_op jit(solution)/shard_map/ppermute | solution.py:215
  64.7 3.5 %collective-permute-start.8 = (bf16[128,1024]{1,0:T(8,128)(2,1)}, bf16[128,1024]{1,0:T(8,128)(2,1)}, u32[]{:S(2)}, u32[]{:S(2)}) collective-permute-start(bf16[128,1024]{1,0:T(8,128)(2,1)} %collective-permute-done.4.rest_5_), channel_id=1, source_target_pairs={{4,5},{5,4},{6,7},{7,6},{12,13},{13,12},{14,15},{15,14},{20,21},{2... | collective-permute-start | bytes 786440 | tf_op jit(solution)/shard_map/ppermute | solution.py:215
  68.3 2.3 %collective-permute-start.13 = (bf16[128,1024]{1,0:T(8,128)(2,1)}, bf16[128,1024]{1,0:T(8,128)(2,1)}, u32[]{:S(2)}, u32[]{:S(2)}) collective-permute-start(bf16[128,1024]{1,0:T(8,128)(2,1)} %collective-permute-done.12.rest_6_), channel_id=1, source_target_pairs={{6,7},{7,6},{14,15},{15,14},{22,23},{23,22},{30,31},{31,30}} | collective-permute-start | bytes 786440 | tf_op jit(solution)/shard_map/ppermute | solution.py:215
  70.6 0.7 collective-permute-done.10.rest_7_
  71.3 3.0 %collective-permute-start.11 = (bf16[128,1024]{1,0:T(8,128)(2,1)}, bf16[128,1024]{1,0:T(8,128)(2,1)}, u32[]{:S(2)}, u32[]{:S(2)}) collective-permute-start(bf16[128,1024]{1,0:T(8,128)(2,1)} %collective-permute-done.10.rest_7_), channel_id=1, source_target_pairs={{6,7},{7,6},{14,15},{15,14},{22,23},{23,22},{30,31},{31,30}} | collective-permute-start | bytes 786440 | tf_op jit(solution)/shard_map/ppermute | solution.py:215
  75.2 0.9 copy-done.2
  76.1 0.9 copy-done.8
  77.1 0.9 copy-done.12
  78.0 10.6 %shard_map.65.rest_8_ = bf16[128,8192]{1,0:T(8,128)(2,1)} custom-call(s32[4]{0:T(128)S(1)} %add_add_fusion.1.meta_ref, s32[1,128]{1,0:T(1,128)S(1)} %copy-done.13, bf16[128,8192]{1,0:T(8,128)(2,1)S(1)} %bitcast.17, bf16[256,2176]{1,0:T(8,128)(2,1)S(1)} %bitcast.15, bf16[128,1024]{1,0:T(8,128)(2,1)S(1)} %copy-done.2, bf16[128,1024]{1,0:T(8,128)(2,1)S(1)} %copy-done.8, ...), custom_call_target="tpu_custom_call" | custom-call | tf_op jit(solution)/shard_map/pallas_call | solution.py:178
  88.9 10.7 %shard_map.66 = bf16[128,8192]{1,0:T(8,128)(2,1)} custom-call(s32[4]{0:T(128)S(1)} %add_add_fusion.meta_ref, s32[1,128]{1,0:T(1,128)S(1)} %copy-done.13, bf16[128,8192]{1,0:T(8,128)(2,1)S(1)} %bitcast.18, bf16[256,2176]{1,0:T(8,128)(2,1)S(1)} %bitcast.16, bf16[128,1024]{1,0:T(8,128)(2,1)S(1)} %copy-done.1, ...), custom_call_target="tpu_custom_call", output_to_operand_aliasing={{}: (12, {})} | custom-call | tf_op jit(solution)/shard_map/pallas_call | solution.py:178
  (39 shorter events, 3.5 us)
Async XLA Ops:
  1.8 17.3 %copy-start.1 = (bf16[128,1024]{1,0:T(8,128)(2,1)S(1)}, bf16[128,1024]{1,0:T(8,128)(2,1)}, u32[]{:S(2)}) copy-start(bf16[128,1024]{1,0:T(8,128)(2,1)} %get-tuple-element.17.rest_0_) | copy-start | bytes 786436
  1.8 73.3 %copy-start = (bf16[1,128,8192]{2,1,0:T(8,128)(2,1)S(1)}, bf16[1,128,8192]{2,1,0:T(8,128)(2,1)}, u32[]{:S(2)}) copy-start(bf16[1,128,8192]{2,1,0:T(8,128)(2,1)} %param.6) | copy-start | bytes 6291460
  1.8 73.3 %copy-start.13 = (s32[1,128]{1,0:T(1,128)S(1)}, s32[1,128]{1,0:T(1,128)}, u32[]{:S(2)}) copy-start(s32[1,128]{1,0:T(1,128)} %seg_ref.3) | copy-start | bytes 1540
  1.8 10.4 %collective-permute-start = (bf16[128,1024]{1,0:T(8,128)(2,1)}, bf16[128,1024]{1,0:T(8,128)(2,1)}, u32[]{:S(2)}, u32[]{:S(2)}) collective-permute-start(bf16[128,1024]{1,0:T(8,128)(2,1)} %get-tuple-element.15.rest_0_), channel_id=1, source_target_pairs={{0,2},{1,3},{2,4},{3,5},{4,6},{5,7},{8,10},{9,11},{10,12},{11,13},... | collective-permute-start | bytes 786440 | tf_op jit(solution)/shard_map/ppermute | solution.py:219
  13.3 61.9 %all-to-all-start = ((bf16[32,8,2176]{2,1,0:T(8,128)(2,1)}), bf16[32,8,2176]{2,1,0:T(8,128)(2,1)S(1)}, u32[]{:S(2)}, u32[]{:S(2)}) async-start(bf16[32,8,2176]{2,1,0:T(8,128)(2,1)} %bitcast.20), calls=%async_computation | async-start | bytes 2228224 | tf_op jit(solution)/shard_map/all_to_all | solution.py:237
  19.2 18.4 %collective-permute-start.1 = (bf16[128,1024]{1,0:T(8,128)(2,1)S(1)}, bf16[128,1024]{1,0:T(8,128)(2,1)S(1)}, u32[]{:S(2)}, u32[]{:S(2)}) collective-permute-start(bf16[128,1024]{1,0:T(8,128)(2,1)S(1)} %copy-done.1), channel_id=1, source_target_pairs={{0,1},{1,0},{2,3},{3,2},{4,5},{5,4},{6,7},{7,6},{8,9},{9,8},{10,11... | collective-permute-start | bytes 786440 | tf_op jit(solution)/shard_map/ppermute | solution.py:215
  20.7 22.2 %collective-permute-start.3 = (bf16[128,1024]{1,0:T(8,128)(2,1)}, bf16[128,1024]{1,0:T(8,128)(2,1)S(1)}, u32[]{:S(2)}, u32[]{:S(2)}) collective-permute-start(bf16[128,1024]{1,0:T(8,128)(2,1)} %get-tuple-element.15.rest_0_), channel_id=1, source_target_pairs={{0,1},{2,3},{4,5},{6,7},{8,9},{10,11},{12,13},{14,15},{16,17},{18,... | collective-permute-start | bytes 786440 | tf_op jit(solution)/shard_map/ppermute | solution.py:223
  37.6 11.8 %collective-permute-start.2 = (bf16[128,1024]{1,0:T(8,128)(2,1)S(1)}, bf16[128,1024]{1,0:T(8,128)(2,1)S(1)}, u32[]{:S(2)}, u32[]{:S(2)}) collective-permute-start(bf16[128,1024]{1,0:T(8,128)(2,1)S(1)} %collective-permute-done.1.rest_1_), channel_id=1, source_target_pairs={{0,2},{1,3},{2,4},{3,5},{4,6},{5,7},{8,10},{9,11},{10,12},{11,13},... | collective-permute-start | bytes 786440 | tf_op jit(solution)/shard_map/ppermute | solution.py:219
  38.9 0.7 copy-start.7
  39.6 15.5 %collective-permute-start.6 = (bf16[128,1024]{1,0:T(8,128)(2,1)}, bf16[128,1024]{1,0:T(8,128)(2,1)}, u32[]{:S(2)}, u32[]{:S(2)}) collective-permute-start(bf16[128,1024]{1,0:T(8,128)(2,1)} %collective-permute-done.rest_2_), channel_id=1, source_target_pairs={{2,4},{3,5},{4,6},{5,7},{10,12},{11,13},{12,14},{13,15},{18,20},{1... | collective-permute-start | bytes 786440 | tf_op jit(solution)/shard_map/ppermute | solution.py:219
  40.9 14.2 %collective-permute-start.7 = (bf16[128,1024]{1,0:T(8,128)(2,1)}, bf16[128,1024]{1,0:T(8,128)(2,1)S(1)}, u32[]{:S(2)}, u32[]{:S(2)}) collective-permute-start(bf16[128,1024]{1,0:T(8,128)(2,1)} %collective-permute-done.rest_2_), channel_id=1, source_target_pairs={{2,3},{3,2},{4,5},{5,4},{6,7},{7,6},{10,11},{11,10},{12,13},{13,12... | collective-permute-start | bytes 786440 | tf_op jit(solution)/shard_map/ppermute | solution.py:215
  43.0 0.7 copy-start.3
  49.4 11.0 %collective-permute-start.4 = (bf16[128,1024]{1,0:T(8,128)(2,1)S(1)}, bf16[128,1024]{1,0:T(8,128)(2,1)}, u32[]{:S(2)}, u32[]{:S(2)}) collective-permute-start(bf16[128,1024]{1,0:T(8,128)(2,1)S(1)} %collective-permute-done.2.rest_3_), channel_id=1, source_target_pairs={{2,4},{3,5},{4,6},{5,7},{10,12},{11,13},{12,14},{13,15},{18,20},{1... | collective-permute-start | bytes 786440 | tf_op jit(solution)/shard_map/ppermute | solution.py:219
  50.6 9.8 %collective-permute-start.5 = (bf16[128,1024]{1,0:T(8,128)(2,1)S(1)}, bf16[128,1024]{1,0:T(8,128)(2,1)S(1)}, u32[]{:S(2)}, u32[]{:S(2)}) collective-permute-start(bf16[128,1024]{1,0:T(8,128)(2,1)S(1)} %collective-permute-done.2.rest_3_), channel_id=1, source_target_pairs={{2,3},{3,2},{4,5},{5,4},{6,7},{7,6},{10,11},{11,10},{12,13},{13,12... | collective-permute-start | bytes 786440 | tf_op jit(solution)/shard_map/ppermute | solution.py:215
  52.8 0.7 copy-start.11
  55.1 0.7 copy-start.5
  55.8 12.5 %collective-permute-start.12 = (bf16[128,1024]{1,0:T(8,128)(2,1)}, bf16[128,1024]{1,0:T(8,128)(2,1)}, u32[]{:S(2)}, u32[]{:S(2)}) collective-permute-start(bf16[128,1024]{1,0:T(8,128)(2,1)} %collective-permute-done.6.rest_4_), channel_id=1, source_target_pairs={{4,6},{5,7},{12,14},{13,15},{20,22},{21,23},{28,30},{29,31}} | collective-permute-start | bytes 786440 | tf_op jit(solution)/shard_map/ppermute | solution.py:219
  60.4 0.7 copy-start.9
  61.1 10.2 %collective-permute-start.10 = (bf16[128,1024]{1,0:T(8,128)(2,1)}, bf16[128,1024]{1,0:T(8,128)(2,1)}, u32[]{:S(2)}, u32[]{:S(2)}) collective-permute-start(bf16[128,1024]{1,0:T(8,128)(2,1)} %collective-permute-done.4.rest_5_), channel_id=1, source_target_pairs={{4,6},{5,7},{12,14},{13,15},{20,22},{21,23},{28,30},{29,31}} | collective-permute-start | bytes 786440 | tf_op jit(solution)/shard_map/ppermute | solution.py:219
  62.4 26.3 %collective-permute-start.9 = (bf16[128,1024]{1,0:T(8,128)(2,1)}, bf16[128,1024]{1,0:T(8,128)(2,1)}, u32[]{:S(2)}, u32[]{:S(2)}) collective-permute-start(bf16[128,1024]{1,0:T(8,128)(2,1)} %collective-permute-done.6.rest_4_), channel_id=1, source_target_pairs={{4,5},{5,4},{6,7},{7,6},{12,13},{13,12},{14,15},{15,14},{20,21},{2... | collective-permute-start | bytes 786440 | tf_op jit(solution)/shard_map/ppermute | solution.py:215
  64.7 24.0 %collective-permute-start.8 = (bf16[128,1024]{1,0:T(8,128)(2,1)}, bf16[128,1024]{1,0:T(8,128)(2,1)}, u32[]{:S(2)}, u32[]{:S(2)}) collective-permute-start(bf16[128,1024]{1,0:T(8,128)(2,1)} %collective-permute-done.4.rest_5_), channel_id=1, source_target_pairs={{4,5},{5,4},{6,7},{7,6},{12,13},{13,12},{14,15},{15,14},{20,21},{2... | collective-permute-start | bytes 786440 | tf_op jit(solution)/shard_map/ppermute | solution.py:215
  68.3 20.4 %collective-permute-start.13 = (bf16[128,1024]{1,0:T(8,128)(2,1)}, bf16[128,1024]{1,0:T(8,128)(2,1)}, u32[]{:S(2)}, u32[]{:S(2)}) collective-permute-start(bf16[128,1024]{1,0:T(8,128)(2,1)} %collective-permute-done.12.rest_6_), channel_id=1, source_target_pairs={{6,7},{7,6},{14,15},{15,14},{22,23},{23,22},{30,31},{31,30}} | collective-permute-start | bytes 786440 | tf_op jit(solution)/shard_map/ppermute | solution.py:215
  71.3 17.6 %collective-permute-start.11 = (bf16[128,1024]{1,0:T(8,128)(2,1)}, bf16[128,1024]{1,0:T(8,128)(2,1)}, u32[]{:S(2)}, u32[]{:S(2)}) collective-permute-start(bf16[128,1024]{1,0:T(8,128)(2,1)} %collective-permute-done.10.rest_7_), channel_id=1, source_target_pairs={{6,7},{7,6},{14,15},{15,14},{22,23},{23,22},{30,31},{31,30}} | collective-permute-start | bytes 786440 | tf_op jit(solution)/shard_map/ppermute | solution.py:215
  75.2 1.0 copy-start.2
  76.1 0.9 copy-start.8
  77.1 0.9 copy-start.12
  78.0 10.9 %copy-start.4 = (bf16[128,1024]{1,0:T(8,128)(2,1)S(1)}, bf16[128,1024]{1,0:T(8,128)(2,1)}, u32[]{:S(2)}) copy-start(bf16[128,1024]{1,0:T(8,128)(2,1)} %copy-done.3) | copy-start | bytes 786436
  78.0 10.9 %copy-start.6 = (bf16[128,1024]{1,0:T(8,128)(2,1)S(1)}, bf16[128,1024]{1,0:T(8,128)(2,1)}, u32[]{:S(2)}) copy-start(bf16[128,1024]{1,0:T(8,128)(2,1)} %copy-done.5) | copy-start | bytes 786436
  78.0 10.9 %copy-start.10 = (bf16[128,1024]{1,0:T(8,128)(2,1)S(1)}, bf16[128,1024]{1,0:T(8,128)(2,1)}, u32[]{:S(2)}) copy-start(bf16[128,1024]{1,0:T(8,128)(2,1)} %copy-done.9) | copy-start | bytes 786436

commit v5 on v4

--- a/solution.py
+++ b/solution.py
@@ -197,7 +197,7 @@
         ),
         out_shape=jax.ShapeDtypeStruct(queries.shape, queries.dtype),
         input_output_aliases=aliases,
-        compiler_params=pltpu.CompilerParams(vmem_limit_bytes=40 * 1024 * 1024),
+        compiler_params=pltpu.CompilerParams(vmem_limit_bytes=20 * 1024 * 1024),
     )(*args)
 
 
@@ -214,13 +214,22 @@
     def swap(value, first):
         return lax.ppermute(value, "resp", [(r, r ^ 1) for r in range(2 * first, count)])
 
-    def climb(value, step):
-        pairs = [(r, r + 2) for r in range(2 * step - 2, count - 2)]
+    def climb(value, step, by):
+        pairs = [(r, r + 2 * by) for r in range(2 * (step - by), count - 2 * by)]
         return lax.ppermute(value, "resp", pairs)
 
+    def after(value, *others):
+        return lax.optimization_barrier((value, *others))[0]
+
     mine, theirs = halves(resp_kv[0], side)
-    straight = [mine, swap(theirs, 0), climb(mine, 1)]
-    crossed = [theirs, lax.ppermute(mine, "resp", [(r, r + 1) for r in range(0, count, 2)])]
+    near, far = climb(mine, 1, 1), climb(mine, 2, 2)
+    partner = swap(theirs, 0)
+    upper = [(r, r + 1) for r in range(0, count, 2)]
+    upper = lax.ppermute(after(mine, partner), "resp", upper)
+    near2, far2 = climb(partner, 1, 1), climb(partner, 2, 2)
+    straight = [mine, partner, near, near2, far, far2]
+    swapped, swapped_far = swap(near, 1), swap(far, 2)
+    crossed = [theirs, upper, swap(near2, 1), swapped, swap(far2, 2), swapped_far]
 
     pick = tile_plan[None, :, 0] == jnp.arange(groups, dtype=jnp.int32)[:, None]
     place = jnp.sum(jnp.where(pick, tile_plan[None, :, 1], 0), axis=1, dtype=jnp.int32)
@@ -233,22 +242,17 @@
     out_tiles = jnp.broadcast_to(
         out_tiles.astype(prefix_kv.dtype)[:, None], (groups, count, tile, columns + rows)
     ).reshape(groups * count, tile, columns + rows)
-    out_tiles, straight[2] = lax.optimization_barrier((out_tiles, straight[2]))
+    out_tiles = after(out_tiles, near, far, near2)
     came = lax.all_to_all(
         out_tiles, ("prompt", "resp"), split_axis=0, concat_axis=0, tiled=True
     )
     prefix = came.reshape(-1, columns + rows)
 
-    for step in range(1, steps + 1):
-        for k in range(2):
-            if step + k == 1:
-                continue
-            source = straight[-2]
-            late = 1 if step == 2 else 2 * (step - 2) + 1 - k
-            if step > 2 or step + k == 3:
-                source, crossed[late] = lax.optimization_barrier((source, crossed[late]))
-            straight.append(climb(source, step))
-        crossed += [swap(straight[-1], step), swap(straight[-2], step)]
+    for step in range(3, steps + 1):
+        one = climb(far, step, step - 2)
+        two = climb(after(far2, swapped, swapped_far, upper), step, step - 2)
+        straight += [one, two]
+        crossed += [swap(two, step), swap(one, step)]
 
     out = None
     for first, pieces in ((side, straight), (1 - side, crossed)):

time: 100 us -> 112 us (1.12)
  the two profiles are of different devices: /device:TPU:26 before, /device:TPU:28 now
where the time goes in v5:
time: 112 us; the launch traced here: 111 us
  waiting for transfers between devices  48.7 us (43%)
  starting transfers between devices  32.7 us (29%)
  Pallas kernels  20.9 us (19%)
  local copies, waits for them, and re-layouts  5.59 us (5%)
  other arithmetic  1.98 us (2%)
    ppermute x6, waiting for transfers between devices, climb(): return lax.ppermute(value, 'resp', pairs)  27.6 us
    pallas_call x2, Pallas kernels, attend(): pl.pallas_call(functools.partial(attend_kernel, pairs, tile, count), grid...  19 us
    ppermute x7, starting transfers between devices, swap(): lax.ppermute(value, 'resp', [(r, r ^ 1) for r in range(2 * first, count)])  17.7 us
    ppermute x7, waiting for transfers between devices, swap(): lax.ppermute(value, 'resp', [(r, r ^ 1) for r in range(2 * first, count)])  14.7 us
    ppermute x6, starting transfers between devices, climb(): return lax.ppermute(value, 'resp', pairs)  7.86 us
    ppermute x1, waiting for transfers between devices, on_device(): upper = lax.ppermute(after(mine, partner), 'resp', upper)  6.47 us
    all_to_all x1, starting transfers between devices, on_device(): lax.all_to_all(out_tiles, ('prompt', 'resp'), split_axis=0, concat_axis=0...  5.84 us
    unnamed x24, local copies, waits for them, and re-layouts  3.77 us
  transfers between devices with their start and end apart: 15, of which 8 were waited for; matrix products, arithmetic and copies ran while one was open for 2% of the time, Pallas kernels for 9%

profile of v5, /device:TPU:28, one launch (start us, length us, event | category | flops | bytes accessed | tf_op | source)
XLA Modules:
  0.0 110.8 jit_solution(15124249765070143667)
XLA Ops:
  0.0 1.8 %shard_map.64 = (bf16[128,1024]{1,0:T(8,128)(2,1)}, bf16[128,1024]{1,0:T(8,128)(2,1)}) custom-call(s32[1]{0:T(128)} %bitcast.8.meta_ref, bf16[128,2048]{1,0:T(8,128)(2,1)} %bitcast.21, bf16[128,2048]{1,0:T(8,128)(2,1)} %bitcast.22), custom_call_target="tpu_custom_call" | custom-call | tf_op jit(solution)/shard_map/pallas_call | solution.py:28
  1.9 1.4 %collective-permute-start = (bf16[128,1024]{1,0:T(8,128)(2,1)}, bf16[128,1024]{1,0:T(8,128)(2,1)}, u32[]{:S(2)}, u32[]{:S(2)}) collective-permute-start(bf16[128,1024]{1,0:T(8,128)(2,1)} %get-tuple-element.13.rest_0_), channel_id=1, source_target_pairs={{0,2},{1,3},{2,4},{3,5},{4,6},{5,7},{8,10},{9,11},{10,12},{11,13},... | collective-permute-start | bytes 786440 | tf_op jit(solution)/shard_map/ppermute | solution.py:219
  3.3 1.3 %collective-permute-start.1 = (bf16[128,1024]{1,0:T(8,128)(2,1)}, bf16[128,1024]{1,0:T(8,128)(2,1)}, u32[]{:S(2)}, u32[]{:S(2)}) collective-permute-start(bf16[128,1024]{1,0:T(8,128)(2,1)} %get-tuple-element.13.rest_0_), channel_id=1, source_target_pairs={{0,4},{1,5},{2,6},{3,7},{8,12},{9,13},{10,14},{11,15},{16,20},{17,... | collective-permute-start | bytes 786440 | tf_op jit(solution)/shard_map/ppermute | solution.py:219
  5.2 0.8 slice_bitcast_fusion.1
  6.0 1.0 select_reduce_fusion
  7.1 0.7 convert_convert_fusion
  7.8 5.1 %collective-permute-done.2.rest_1_ = bf16[128,1024]{1,0:T(8,128)(2,1)S(1)} collective-permute-done((bf16[128,1024]{1,0:T(8,128)(2,1)}, bf16[128,1024]{1,0:T(8,128)(2,1)S(1)}, u32[]{:S(2)}, u32[]{:S(2)}) %collective-permute-start.2) | collective-permute-done | bytes 262176 | tf_op jit(solution)/shard_map/ppermute | solution.py:215
  13.6 1.3 %collective-permute-start.3 = (bf16[128,1024]{1,0:T(8,128)(2,1)S(1)}, bf16[128,1024]{1,0:T(8,128)(2,1)}, u32[]{:S(2)}, u32[]{:S(2)}) collective-permute-start(bf16[128,1024]{1,0:T(8,128)(2,1)S(1)} %collective-permute-done.2.rest_1_), channel_id=1, source_target_pairs={{0,2},{1,3},{2,4},{3,5},{4,6},{5,7},{8,10},{9,11},{10,12},{11,13},... | collective-permute-start | bytes 786440 | tf_op jit(solution)/shard_map/ppermute | solution.py:219
  14.9 9.6 %collective-permute-done.1.rest_4_ = bf16[128,1024]{1,0:T(8,128)(2,1)} collective-permute-done((bf16[128,1024]{1,0:T(8,128)(2,1)}, bf16[128,1024]{1,0:T(8,128)(2,1)}, u32[]{:S(2)}, u32[]{:S(2)}) %collective-permute-start.1) | collective-permute-done | bytes 262176 | tf_op jit(solution)/shard_map/ppermute | solution.py:219
  24.6 3.7 %collective-permute-done.3.rest_3_ = bf16[128,1024]{1,0:T(8,128)(2,1)} collective-permute-done((bf16[128,1024]{1,0:T(8,128)(2,1)S(1)}, bf16[128,1024]{1,0:T(8,128)(2,1)}, u32[]{:S(2)}, u32[]{:S(2)}) %collective-permute-start.3) | collective-permute-done | bytes 262176 | tf_op jit(solution)/shard_map/ppermute | solution.py:219
  28.2 1.1 broadcast_in_dim.76
  29.3 5.8 %all-to-all-start = ((bf16[32,8,2176]{2,1,0:T(8,128)(2,1)}), bf16[32,8,2176]{2,1,0:T(8,128)(2,1)S(1)}, u32[]{:S(2)}, u32[]{:S(2)}) async-start(bf16[32,8,2176]{2,1,0:T(8,128)(2,1)} %bitcast.20), calls=%async_computation | async-start | bytes 2228224 | tf_op jit(solution)/shard_map/all_to_all | solution.py:246
  35.2 1.3 %collective-permute-start.4 = (bf16[128,1024]{1,0:T(8,128)(2,1)S(1)}, bf16[128,1024]{1,0:T(8,128)(2,1)S(1)}, u32[]{:S(2)}, u32[]{:S(2)}) collective-permute-start(bf16[128,1024]{1,0:T(8,128)(2,1)S(1)} %copy-done.2), channel_id=1, source_target_pairs={{0,1},{2,3},{4,5},{6,7},{8,9},{10,11},{12,13},{14,15},{16,17},{18,... | collective-permute-start | bytes 786440 | tf_op jit(solution)/shard_map/ppermute | solution.py:228
  36.5 4.6 %collective-permute-start.6 = (bf16[128,1024]{1,0:T(8,128)(2,1)}, bf16[128,1024]{1,0:T(8,128)(2,1)S(1)}, u32[]{:S(2)}, u32[]{:S(2)}) collective-permute-start(bf16[128,1024]{1,0:T(8,128)(2,1)} %collective-permute-done.rest_2_), channel_id=1, source_target_pairs={{2,3},{3,2},{4,5},{5,4},{6,7},{7,6},{10,11},{11,10},{12,13},{13,12... | collective-permute-start | bytes 786440 | tf_op jit(solution)/shard_map/ppermute | solution.py:215
  41.0 1.3 %collective-permute-start.7 = (bf16[128,1024]{1,0:T(8,128)(2,1)}, bf16[128,1024]{1,0:T(8,128)(2,1)}, u32[]{:S(2)}, u32[]{:S(2)}) collective-permute-start(bf16[128,1024]{1,0:T(8,128)(2,1)} %copy-done.3), channel_id=1, source_target_pairs={{0,4},{1,5},{2,6},{3,7},{8,12},{9,13},{10,14},{11,15},{16,20},{17,... | collective-permute-start | bytes 786440 | tf_op jit(solution)/shard_map/ppermute | solution.py:219
  42.3 1.9 %collective-permute-start.9 = (bf16[128,1024]{1,0:T(8,128)(2,1)}, bf16[128,1024]{1,0:T(8,128)(2,1)S(1)}, u32[]{:S(2)}, u32[]{:S(2)}) collective-permute-start(bf16[128,1024]{1,0:T(8,128)(2,1)} %collective-permute-done.1.rest_4_), channel_id=1, source_target_pairs={{4,5},{5,4},{6,7},{7,6},{12,13},{13,12},{14,15},{15,14},{20,21},{2... | collective-permute-start | bytes 786440 | tf_op jit(solution)/shard_map/ppermute | solution.py:215
  44.3 1.3 %collective-permute-start.12 = (bf16[128,1024]{1,0:T(8,128)(2,1)}, bf16[128,1024]{1,0:T(8,128)(2,1)}, u32[]{:S(2)}, u32[]{:S(2)}) collective-permute-start(bf16[128,1024]{1,0:T(8,128)(2,1)} %collective-permute-done.1.rest_4_), channel_id=1, source_target_pairs={{4,6},{5,7},{12,14},{13,15},{20,22},{21,23},{28,30},{29,31}} | collective-permute-start | bytes 786440 | tf_op jit(solution)/shard_map/ppermute | solution.py:219
  45.6 6.5 %collective-permute-done.4.rest_1_ = bf16[128,1024]{1,0:T(8,128)(2,1)S(1)} collective-permute-done((bf16[128,1024]{1,0:T(8,128)(2,1)S(1)}, bf16[128,1024]{1,0:T(8,128)(2,1)S(1)}, u32[]{:S(2)}, u32[]{:S(2)}) %collective-permute-start.4) | collective-permute-done | bytes 262176 | tf_op jit(solution)/shard_map/ppermute | solution.py:228
  52.0 0.7 copy-done.5
  52.7 5.3 %collective-permute-done.6.rest_3_ = bf16[128,1024]{1,0:T(8,128)(2,1)S(1)} collective-permute-done((bf16[128,1024]{1,0:T(8,128)(2,1)}, bf16[128,1024]{1,0:T(8,128)(2,1)S(1)}, u32[]{:S(2)}, u32[]{:S(2)}) %collective-permute-start.6) | collective-permute-done | bytes 262176 | tf_op jit(solution)/shard_map/ppermute | solution.py:215
  58.7 13.2 %collective-permute-done.7.rest_5_ = bf16[128,1024]{1,0:T(8,128)(2,1)} collective-permute-done((bf16[128,1024]{1,0:T(8,128)(2,1)}, bf16[128,1024]{1,0:T(8,128)(2,1)}, u32[]{:S(2)}, u32[]{:S(2)}) %collective-permute-start.7) | collective-permute-done | bytes 262176 | tf_op jit(solution)/shard_map/ppermute | solution.py:219
  71.9 0.7 copy-done.9
  72.6 1.3 %collective-permute-start.10 = (bf16[128,1024]{1,0:T(8,128)(2,1)}, bf16[128,1024]{1,0:T(8,128)(2,1)}, u32[]{:S(2)}, u32[]{:S(2)}) collective-permute-start(bf16[128,1024]{1,0:T(8,128)(2,1)} %collective-permute-done.7.rest_5_), channel_id=1, source_target_pairs={{4,6},{5,7},{12,14},{13,15},{20,22},{21,23},{28,30},{29,31}} | collective-permute-start | bytes 786440 | tf_op jit(solution)/shard_map/ppermute | solution.py:219
  73.9 2.3 %collective-permute-start.5 = (bf16[128,1024]{1,0:T(8,128)(2,1)}, bf16[128,1024]{1,0:T(8,128)(2,1)}, u32[]{:S(2)}, u32[]{:S(2)}) collective-permute-start(bf16[128,1024]{1,0:T(8,128)(2,1)} %collective-permute-done.3.rest_3_), channel_id=1, source_target_pairs={{2,3},{3,2},{4,5},{5,4},{6,7},{7,6},{10,11},{11,10},{12,13},{13,12... | collective-permute-start | bytes 786440 | tf_op jit(solution)/shard_map/ppermute | solution.py:215
  76.2 3.6 %collective-permute-start.13 = (bf16[128,1024]{1,0:T(8,128)(2,1)}, bf16[128,1024]{1,0:T(8,128)(2,1)}, u32[]{:S(2)}, u32[]{:S(2)}) collective-permute-start(bf16[128,1024]{1,0:T(8,128)(2,1)} %collective-permute-done.12.rest_6_), channel_id=1, source_target_pairs={{6,7},{7,6},{14,15},{15,14},{22,23},{23,22},{30,31},{31,30}} | collective-permute-start | bytes 786440 | tf_op jit(solution)/shard_map/ppermute | solution.py:215
  79.8 2.3 %collective-permute-start.8 = (bf16[128,1024]{1,0:T(8,128)(2,1)}, bf16[128,1024]{1,0:T(8,128)(2,1)}, u32[]{:S(2)}, u32[]{:S(2)}) collective-permute-start(bf16[128,1024]{1,0:T(8,128)(2,1)} %collective-permute-done.7.rest_5_), channel_id=1, source_target_pairs={{4,5},{5,4},{6,7},{7,6},{12,13},{13,12},{14,15},{15,14},{20,21},{2... | collective-permute-start | bytes 786440 | tf_op jit(solution)/shard_map/ppermute | solution.py:215
  82.1 1.0 collective-permute-done.10.rest_7_
  83.1 2.5 %collective-permute-start.11 = (bf16[128,1024]{1,0:T(8,128)(2,1)}, bf16[128,1024]{1,0:T(8,128)(2,1)}, u32[]{:S(2)}, u32[]{:S(2)}) collective-permute-start(bf16[128,1024]{1,0:T(8,128)(2,1)} %collective-permute-done.10.rest_7_), channel_id=1, source_target_pairs={{6,7},{7,6},{14,15},{15,14},{22,23},{23,22},{30,31},{31,30}} | collective-permute-start | bytes 786440 | tf_op jit(solution)/shard_map/ppermute | solution.py:215
  86.4 0.9 copy-done.4
  87.4 9.5 %shard_map.65.rest_8_ = bf16[128,8192]{1,0:T(8,128)(2,1)} custom-call(s32[4]{0:T(128)S(1)} %get-tuple-element.18.meta_ref, s32[1,128]{1,0:T(1,128)S(1)} %copy-done.11, bf16[128,8192]{1,0:T(8,128)(2,1)S(1)} %bitcast.17, bf16[256,2176]{1,0:T(8,128)(2,1)S(1)} %bitcast.15, bf16[128,1024]{1,0:T(8,128)(2,1)S(1)} %copy-done.2, bf16[128,1024]{1,0:T(8,128)(2,1)S(1)} %copy-done.4, ...), custom_call_target="tpu_custom_call" | custom-call | tf_op jit(solution)/shard_map/pallas_call | solution.py:178
  97.0 4.3 %collective-permute-done.11.rest_6_ = bf16[128,1024]{1,0:T(8,128)(2,1)} collective-permute-done((bf16[128,1024]{1,0:T(8,128)(2,1)}, bf16[128,1024]{1,0:T(8,128)(2,1)}, u32[]{:S(2)}, u32[]{:S(2)}) %collective-permute-start.11) | collective-permute-done | bytes 262176 | tf_op jit(solution)/shard_map/ppermute | solution.py:215
  101.3 9.5 %shard_map.66 = bf16[128,8192]{1,0:T(8,128)(2,1)} custom-call(s32[4]{0:T(128)S(1)} %get-tuple-element.17.meta_ref, s32[1,128]{1,0:T(1,128)S(1)} %copy-done.11, bf16[128,8192]{1,0:T(8,128)(2,1)S(1)} %bitcast.18, bf16[256,2176]{1,0:T(8,128)(2,1)S(1)} %bitcast.16, bf16[128,1024]{1,0:T(8,128)(2,1)S(1)} %copy-done.1, ...), custom_call_target="tpu_custom_call", output_to_operand_aliasing={{}: (12, {})} | custom-call | tf_op jit(solution)/shard_map/pallas_call | solution.py:178
  (34 shorter events, 2.2 us)
Async XLA Ops:
  1.8 33.3 %copy-start.2 = (bf16[128,1024]{1,0:T(8,128)(2,1)S(1)}, bf16[128,1024]{1,0:T(8,128)(2,1)}, u32[]{:S(2)}) copy-start(bf16[128,1024]{1,0:T(8,128)(2,1)} %get-tuple-element.13.rest_0_) | copy-start | bytes 786436
  1.8 84.6 %copy-start = (bf16[1,128,8192]{2,1,0:T(8,128)(2,1)S(1)}, bf16[1,128,8192]{2,1,0:T(8,128)(2,1)}, u32[]{:S(2)}) copy-start(bf16[1,128,8192]{2,1,0:T(8,128)(2,1)} %param.6) | copy-start | bytes 6291460
  1.8 84.6 %copy-start.11 = (s32[1,128]{1,0:T(1,128)S(1)}, s32[1,128]{1,0:T(1,128)}, u32[]{:S(2)}) copy-start(s32[1,128]{1,0:T(1,128)} %seg_ref.3) | copy-start | bytes 1540
  1.9 13.1 %collective-permute-start = (bf16[128,1024]{1,0:T(8,128)(2,1)}, bf16[128,1024]{1,0:T(8,128)(2,1)}, u32[]{:S(2)}, u32[]{:S(2)}) collective-permute-start(bf16[128,1024]{1,0:T(8,128)(2,1)} %get-tuple-element.13.rest_0_), channel_id=1, source_target_pairs={{0,2},{1,3},{2,4},{3,5},{4,6},{5,7},{8,10},{9,11},{10,12},{11,13},... | collective-permute-start | bytes 786440 | tf_op jit(solution)/shard_map/ppermute | solution.py:219
  3.3 21.3 %collective-permute-start.1 = (bf16[128,1024]{1,0:T(8,128)(2,1)}, bf16[128,1024]{1,0:T(8,128)(2,1)}, u32[]{:S(2)}, u32[]{:S(2)}) collective-permute-start(bf16[128,1024]{1,0:T(8,128)(2,1)} %get-tuple-element.13.rest_0_), channel_id=1, source_target_pairs={{0,4},{1,5},{2,6},{3,7},{8,12},{9,13},{10,14},{11,15},{16,20},{17,... | collective-permute-start | bytes 786440 | tf_op jit(solution)/shard_map/ppermute | solution.py:219
  4.6 8.3 %collective-permute-start.2 = (bf16[128,1024]{1,0:T(8,128)(2,1)}, bf16[128,1024]{1,0:T(8,128)(2,1)S(1)}, u32[]{:S(2)}, u32[]{:S(2)}) collective-permute-start(bf16[128,1024]{1,0:T(8,128)(2,1)} %get-tuple-element.11.rest_0_), channel_id=1, source_target_pairs={{0,1},{1,0},{2,3},{3,2},{4,5},{5,4},{6,7},{7,6},{8,9},{9,8},{10,11... | collective-permute-start | bytes 786440 | tf_op jit(solution)/shard_map/ppermute | solution.py:215
  12.9 0.7 copy-start.3
  13.6 14.6 %collective-permute-start.3 = (bf16[128,1024]{1,0:T(8,128)(2,1)S(1)}, bf16[128,1024]{1,0:T(8,128)(2,1)}, u32[]{:S(2)}, u32[]{:S(2)}) collective-permute-start(bf16[128,1024]{1,0:T(8,128)(2,1)S(1)} %collective-permute-done.2.rest_1_), channel_id=1, source_target_pairs={{0,2},{1,3},{2,4},{3,5},{4,6},{5,7},{8,10},{9,11},{10,12},{11,13},... | collective-permute-start | bytes 786440 | tf_op jit(solution)/shard_map/ppermute | solution.py:219
  29.3 57.1 %all-to-all-start = ((bf16[32,8,2176]{2,1,0:T(8,128)(2,1)}), bf16[32,8,2176]{2,1,0:T(8,128)(2,1)S(1)}, u32[]{:S(2)}, u32[]{:S(2)}) async-start(bf16[32,8,2176]{2,1,0:T(8,128)(2,1)} %bitcast.20), calls=%async_computation | async-start | bytes 2228224 | tf_op jit(solution)/shard_map/all_to_all | solution.py:246
  35.2 16.9 %collective-permute-start.4 = (bf16[128,1024]{1,0:T(8,128)(2,1)S(1)}, bf16[128,1024]{1,0:T(8,128)(2,1)S(1)}, u32[]{:S(2)}, u32[]{:S(2)}) collective-permute-start(bf16[128,1024]{1,0:T(8,128)(2,1)S(1)} %copy-done.2), channel_id=1, source_target_pairs={{0,1},{2,3},{4,5},{6,7},{8,9},{10,11},{12,13},{14,15},{16,17},{18,... | collective-permute-start | bytes 786440 | tf_op jit(solution)/shard_map/ppermute | solution.py:228
  36.5 21.6 %collective-permute-start.6 = (bf16[128,1024]{1,0:T(8,128)(2,1)}, bf16[128,1024]{1,0:T(8,128)(2,1)S(1)}, u32[]{:S(2)}, u32[]{:S(2)}) collective-permute-start(bf16[128,1024]{1,0:T(8,128)(2,1)} %collective-permute-done.rest_2_), channel_id=1, source_target_pairs={{2,3},{3,2},{4,5},{5,4},{6,7},{7,6},{10,11},{11,10},{12,13},{13,12... | collective-permute-start | bytes 786440 | tf_op jit(solution)/shard_map/ppermute | solution.py:215
  41.0 30.9 %collective-permute-start.7 = (bf16[128,1024]{1,0:T(8,128)(2,1)}, bf16[128,1024]{1,0:T(8,128)(2,1)}, u32[]{:S(2)}, u32[]{:S(2)}) collective-permute-start(bf16[128,1024]{1,0:T(8,128)(2,1)} %copy-done.3), channel_id=1, source_target_pairs={{0,4},{1,5},{2,6},{3,7},{8,12},{9,13},{10,14},{11,15},{16,20},{17,... | collective-permute-start | bytes 786440 | tf_op jit(solution)/shard_map/ppermute | solution.py:219
  42.3 29.6 %collective-permute-start.9 = (bf16[128,1024]{1,0:T(8,128)(2,1)}, bf16[128,1024]{1,0:T(8,128)(2,1)S(1)}, u32[]{:S(2)}, u32[]{:S(2)}) collective-permute-start(bf16[128,1024]{1,0:T(8,128)(2,1)} %collective-permute-done.1.rest_4_), channel_id=1, source_target_pairs={{4,5},{5,4},{6,7},{7,6},{12,13},{13,12},{14,15},{15,14},{20,21},{2... | collective-permute-start | bytes 786440 | tf_op jit(solution)/shard_map/ppermute | solution.py:215
  44.3 32.0 %collective-permute-start.12 = (bf16[128,1024]{1,0:T(8,128)(2,1)}, bf16[128,1024]{1,0:T(8,128)(2,1)}, u32[]{:S(2)}, u32[]{:S(2)}) collective-permute-start(bf16[128,1024]{1,0:T(8,128)(2,1)} %collective-permute-done.1.rest_4_), channel_id=1, source_target_pairs={{4,6},{5,7},{12,14},{13,15},{20,22},{21,23},{28,30},{29,31}} | collective-permute-start | bytes 786440 | tf_op jit(solution)/shard_map/ppermute | solution.py:219
  52.0 0.7 copy-start.5
  58.0 0.7 copy-start.7
  71.9 0.7 copy-start.9
  72.6 10.5 %collective-permute-start.10 = (bf16[128,1024]{1,0:T(8,128)(2,1)}, bf16[128,1024]{1,0:T(8,128)(2,1)}, u32[]{:S(2)}, u32[]{:S(2)}) collective-permute-start(bf16[128,1024]{1,0:T(8,128)(2,1)} %collective-permute-done.7.rest_5_), channel_id=1, source_target_pairs={{4,6},{5,7},{12,14},{13,15},{20,22},{21,23},{28,30},{29,31}} | collective-permute-start | bytes 786440 | tf_op jit(solution)/shard_map/ppermute | solution.py:219
  73.9 23.0 %collective-permute-start.5 = (bf16[128,1024]{1,0:T(8,128)(2,1)}, bf16[128,1024]{1,0:T(8,128)(2,1)}, u32[]{:S(2)}, u32[]{:S(2)}) collective-permute-start(bf16[128,1024]{1,0:T(8,128)(2,1)} %collective-permute-done.3.rest_3_), channel_id=1, source_target_pairs={{2,3},{3,2},{4,5},{5,4},{6,7},{7,6},{10,11},{11,10},{12,13},{13,12... | collective-permute-start | bytes 786440 | tf_op jit(solution)/shard_map/ppermute | solution.py:215
  76.2 20.7 %collective-permute-start.13 = (bf16[128,1024]{1,0:T(8,128)(2,1)}, bf16[128,1024]{1,0:T(8,128)(2,1)}, u32[]{:S(2)}, u32[]{:S(2)}) collective-permute-start(bf16[128,1024]{1,0:T(8,128)(2,1)} %collective-permute-done.12.rest_6_), channel_id=1, source_target_pairs={{6,7},{7,6},{14,15},{15,14},{22,23},{23,22},{30,31},{31,30}} | collective-permute-start | bytes 786440 | tf_op jit(solution)/shard_map/ppermute | solution.py:215
  79.8 17.1 %collective-permute-start.8 = (bf16[128,1024]{1,0:T(8,128)(2,1)}, bf16[128,1024]{1,0:T(8,128)(2,1)}, u32[]{:S(2)}, u32[]{:S(2)}) collective-permute-start(bf16[128,1024]{1,0:T(8,128)(2,1)} %collective-permute-done.7.rest_5_), channel_id=1, source_target_pairs={{4,5},{5,4},{6,7},{7,6},{12,13},{13,12},{14,15},{15,14},{20,21},{2... | collective-permute-start | bytes 786440 | tf_op jit(solution)/shard_map/ppermute | solution.py:215
  83.1 18.2 %collective-permute-start.11 = (bf16[128,1024]{1,0:T(8,128)(2,1)}, bf16[128,1024]{1,0:T(8,128)(2,1)}, u32[]{:S(2)}, u32[]{:S(2)}) collective-permute-start(bf16[128,1024]{1,0:T(8,128)(2,1)} %collective-permute-done.10.rest_7_), channel_id=1, source_target_pairs={{6,7},{7,6},{14,15},{15,14},{22,23},{23,22},{30,31},{31,30}} | collective-permute-start | bytes 786440 | tf_op jit(solution)/shard_map/ppermute | solution.py:215
  86.4 1.0 copy-start.4
  87.4 13.9 %copy-start.1 = (bf16[128,1024]{1,0:T(8,128)(2,1)S(1)}, bf16[128,1024]{1,0:T(8,128)(2,1)}, u32[]{:S(2)}) copy-start(bf16[128,1024]{1,0:T(8,128)(2,1)} %get-tuple-element.11.rest_0_) | copy-start | bytes 786436
  87.4 13.9 %copy-start.6 = (bf16[128,1024]{1,0:T(8,128)(2,1)S(1)}, bf16[128,1024]{1,0:T(8,128)(2,1)}, u32[]{:S(2)}) copy-start(bf16[128,1024]{1,0:T(8,128)(2,1)} %copy-done.5) | copy-start | bytes 786436
  87.4 13.9 %copy-start.8 = (bf16[128,1024]{1,0:T(8,128)(2,1)S(1)}, bf16[128,1024]{1,0:T(8,128)(2,1)}, u32[]{:S(2)}) copy-start(bf16[128,1024]{1,0:T(8,128)(2,1)} %copy-done.7) | copy-start | bytes 786436
  87.4 13.9 %copy-start.10 = (bf16[128,1024]{1,0:T(8,128)(2,1)S(1)}, bf16[128,1024]{1,0:T(8,128)(2,1)}, u32[]{:S(2)}) copy-start(bf16[128,1024]{1,0:T(8,128)(2,1)} %copy-done.9) | copy-start | bytes 786436

commit v6 on v4

v6 whole, which is shorter than its diff:
```python
import functools
import math

import jax
import jax.numpy as jnp
from jax import lax
from jax.experimental import pallas as pl
from jax.experimental.pallas import tpu as pltpu
from jax.sharding import PartitionSpec as P

H = 64
KVH = 8
HD = 128
GQ = H // KVH
REACH = 7
SLAB = 2
FILL = -1e30


def halves_kernel(meta_ref, a_ref, b_ref, mine_ref, theirs_ref):
    mine_ref[...] = a_ref[...]
    theirs_ref[...] = b_ref[...]


def halves(kv, side):
    rows, half = kv.shape[0], kv.shape[1] // 4
    shape = (rows, half)
    return pl.pallas_call(
        halves_kernel,
        grid_spec=pltpu.PrefetchScalarGridSpec(
            num_scalar_prefetch=1,
            grid=(2,),
            in_specs=[
                pl.BlockSpec(shape, lambda i, m: (0, 2 * i + m[0])),
                pl.BlockSpec(shape, lambda i, m: (0, 2 * i + 1 - m[0])),
            ],
            out_specs=[pl.BlockSpec(shape, lambda i, m: (0, i))] * 2,
        ),
        out_shape=[jax.ShapeDtypeStruct((rows, 2 * half), kv.dtype)] * 2,
    )(side.reshape(1), kv, kv)


def attend_kernel(pairs, tile, count, fresh, meta_ref, *refs):
    kv_ref, s_ref, top_ref, sems = refs[-4:]
    if fresh:
        seg_ref, q_ref, prefix_ref, *pieces = refs[: 3 + 2 * pairs]
        o_ref, bias_ref, reach_ref, ints_ref, seg_k_ref = refs[3 + 2 * pairs : -4]
    else:
        bias_ref, reach_ref, q_ref, prefix_ref, *pieces = refs[: 4 + 2 * pairs]
        o_ref = refs[-5]
    rows = q_ref.shape[0]
    heads = kv_ref.shape[1] // (2 * HD)
    step = 2 * rows
    prefix_keys = prefix_ref.shape[0]
    group, block, head0, limit = meta_ref[0], meta_ref[1], meta_ref[2], meta_ref[3]
    head = pl.program_id(0)
    scale = math.log2(math.e) / math.sqrt(HD)
    nt = (((1,), (1,)), ((), ()))

    def column(index, width=HD):
        return pl.ds(pl.multiple_of(index * HD, HD), width)

    def masks():
        ints_copy = pltpu.make_async_copy(
            prefix_ref.at[:, pl.ds(2 * KVH * HD, rows)], ints_ref, sems.at[2 * pairs + 2]
        )
        ints_copy.start()
        ints_copy.wait()
        ints = ints_ref[...].astype(jnp.float32)
        seg_k_ref[...] = ints
        part = lax.rem(lax.broadcasted_iota(jnp.int32, ints.shape, 0), tile)
        place = jnp.where(part == 0, pltpu.roll(ints, prefix_keys - 1, 0), ints)
        live = place.astype(jnp.int32) * tile + part < limit
        bias_ref[:, :prefix_keys] = jnp.where(live, 0.0, FILL).T

        own = seg_ref[...].astype(jnp.float32)
        first_key = group * count * tile
        segs = seg_k_ref[pl.ds(pl.multiple_of(first_key, tile), count * tile), :]
        heads_of = lax.rem(lax.broadcasted_iota(jnp.int32, segs.shape, 0), tile) == 0
        earlier = jnp.sum(jnp.where(heads_of & (segs < own[:, :1]), 1.0, 0.0))
        reach_ref[0] = lax.div(block, 2) - lax.div(earlier.astype(jnp.int32), step)

        seg_q = jnp.broadcast_to(own, (rows, rows)).T
        row_pos = block * rows + lax.broadcasted_iota(jnp.int32, (rows, rows), 0)
        lane = lax.broadcasted_iota(jnp.int32, (rows, rows), 1)
        for k in range(pairs):
            for j, first in enumerate((block, block + 1 - 2 * lax.rem(block, 2))):
                key_block = jnp.maximum(first - 2 * k, 0)
                at = pl.multiple_of(first_key + key_block * tile, tile)
                seg_k = seg_k_ref[pl.ds(at, tile), :][:1]
                seen = (seg_k == seg_q) & (key_block * rows + lane <= row_pos)
                at = prefix_keys + (2 * k + j) * rows
                bias_ref[:, at : at + rows] = jnp.where(seen, 0.0, FILL)

    @pl.when(head == 0)
    def _():
        copies = []
        for j, first in enumerate((head0, KVH + head0)):
            copies.append(
                pltpu.make_async_copy(
                    prefix_ref.at[:, column(first, heads * HD)],
                    kv_ref.at[pl.ds(0, prefix_keys), pl.ds(j * heads * HD, heads * HD)],
                    sems.at[j],
                )
            )
        for j, piece in enumerate(pieces):
            at = pl.ds(prefix_keys + j * rows, rows)
            copies.append(pltpu.make_async_copy(piece, kv_ref.at[at], sems.at[2 + j]))
        for copy in copies:
            copy.start()
        if fresh:
            masks()
        for copy in copies:
            copy.wait()

    def body(near):
        steps = prefix_keys // step + near + 1
        values = kv_ref[: steps * step, column(heads + head)]
        values = jnp.concatenate([values, jnp.ones_like(values)], axis=1)

        def score(slab):
            of = range(slab * SLAB, (slab + 1) * SLAB)
            q = jnp.concatenate([q_ref[:, g * HD : (g + 1) * HD] for g in of])
            top = None
            for i in range(steps):
                at = slice(i * step, (i + 1) * step)
                s = lax.dot_general(
                    q, kv_ref[at, column(head)], nt, preferred_element_type=jnp.float32
                )
                s = (s.reshape(SLAB, rows, step) + bias_ref[:, at][None]).reshape(-1, step)
                s_ref[slab % 2, :, at] = s
                high = jnp.maximum(s[:, :rows], s[:, rows:])
                top = high if top is None else jnp.maximum(top, high)
            top = jnp.max(top, axis=1, keepdims=True)
            top_ref[slab % 2] = jnp.broadcast_to(top, (SLAB * rows, HD))

        def weigh(slab):
            top = top_ref[slab % 2]
            weights = [
                jnp.exp2((s_ref[slab % 2, :, i * HD : (i + 1) * HD] - top) * scale).astype(
                    jnp.bfloat16
                )
                for i in range(steps * step // HD)
            ]
            acc = jnp.dot(
                jnp.concatenate(weights, axis=1), values, preferred_element_type=jnp.float32
            )
            out = (acc[:, :HD] / acc[:, HD:]).astype(o_ref.dtype)
            for j in range(SLAB):
                g = slab * SLAB + j
                o_ref[:, g * HD : (g + 1) * HD] = out[j * rows : (j + 1) * rows]

        score(0)
        for slab in range(GQ // SLAB):
            if slab + 1 < GQ // SLAB:
                score(slab + 1)
            weigh(slab)

    for near in range(pairs):
        pl.when(reach_ref[0] == near)(functools.partial(body, near))


def attend(meta, queries, pieces, prefix, tile, count, segments=None, before=None):
    rows = queries.shape[0]
    prefix_keys = prefix.shape[0]
    pairs = len(pieces) // 2
    heads = pieces[0].shape[1] // (2 * HD)
    keys = rows * len(pieces) + prefix_keys
    far = pl.BlockSpec(memory_space=pltpu.HBM)
    whole = pl.BlockSpec((rows, keys), lambda i, m: (0, 0))
    scalar = pl.BlockSpec(memory_space=pltpu.SMEM)
    wide = pl.BlockSpec((rows, GQ * HD), lambda i, m: (0, m[2] + i))
    fresh = before is None
    args = [meta, *([segments] if fresh else before[1:]), queries, prefix, *pieces]
    in_specs = [pl.BlockSpec((1, rows), lambda i, m: (0, 0))] if fresh else [whole, scalar]
    in_specs += [wide, far, *[far] * len(pieces)]
    out_specs = [wide]
    out_shape = [jax.ShapeDtypeStruct(queries.shape, queries.dtype)]
    scratch = []
    aliases = {}
    if fresh:
        out_specs += [whole, scalar]
        out_shape += [
            jax.ShapeDtypeStruct((rows, keys), jnp.float32),
            jax.ShapeDtypeStruct((1,), jnp.int32),
        ]
        scratch = [
            pltpu.VMEM((prefix_keys, rows), queries.dtype),
            pltpu.VMEM((prefix_keys, rows), jnp.float32),
        ]
    else:
        args.append(before[0])
        in_specs.append(far)
        aliases = {len(args) - 1: 0}
    return pl.pallas_call(
        functools.partial(attend_kernel, pairs, tile, count, fresh),
        grid_spec=pltpu.PrefetchScalarGridSpec(
            num_scalar_prefetch=1,
            grid=(heads,),
            in_specs=in_specs,
            out_specs=out_specs,
            scratch_shapes=[
                *scratch,
                pltpu.VMEM((keys, 2 * heads * HD), queries.dtype),
                pltpu.VMEM((2, SLAB * rows, keys), jnp.float32),
                pltpu.VMEM((2, SLAB * rows, HD), jnp.float32),
                pltpu.SemaphoreType.DMA((len(pieces) + 3,)),
            ],
        ),
        out_shape=out_shape,
        input_output_aliases=aliases,
        compiler_params=pltpu.CompilerParams(vmem_limit_bytes=24 * 1024 * 1024),
    )(*args)


def on_device(queries, resp_kv, resp_segments, prefix_kv, tile_plan, prompt_lengths):
    rows = queries.shape[1]
    tiles, tile, columns = prefix_kv.shape
    groups, count = lax.axis_size("prompt"), lax.axis_size("resp")
    group = lax.axis_index("prompt")
    block = lax.axis_index("resp")
    side = block % 2
    steps = min(count // 2 - 1, (REACH + 1) // 2)
    assert tiles == groups

    pick = tile_plan[None, :, 0] == jnp.arange(groups, dtype=jnp.int32)[:, None]
    place = jnp.sum(jnp.where(pick, tile_plan[None, :, 1], 0), axis=1, dtype=jnp.int32)
    own_tiles = jnp.sum(
        jnp.where(pick[:, :, None, None], prefix_kv[None], 0).astype(jnp.float32), axis=1
    )
    row = jnp.arange(tile, dtype=jnp.int32)[:, None]
    extra = jnp.where(row == 0, resp_segments[0], place.reshape(groups, 1, 1))
    out_tiles = jnp.concatenate([own_tiles, extra.astype(jnp.float32)], axis=-1)
    out_tiles = jnp.broadcast_to(
        out_tiles.astype(prefix_kv.dtype)[:, None], (groups, count, tile, columns + rows)
    ).reshape(groups * count, tile, columns + rows)
    came = lax.all_to_all(
        out_tiles, ("prompt", "resp"), split_axis=0, concat_axis=0, tiled=True
    )
    prefix = came.reshape(-1, columns + rows)

    def swap(value, first):
        return lax.ppermute(value, "resp", [(r, r ^ 1) for r in range(2 * first, count)])

    def climb(value, step):
        pairs = [(r, r + 2) for r in range(2 * step - 2, count - 2)]
        return lax.ppermute(value, "resp", pairs)

    def after(value, *others):
        return lax.optimization_barrier((value, *others))[0]

    mine, theirs = halves(resp_kv[0], side)
    partner = swap(theirs, 0)
    upper = [(r, r + 1) for r in range(0, count, 2)]
    upper = lax.ppermute(after(mine, partner), "resp", upper)
    straight, crossed = [mine, partner], [theirs, upper]
    for step in range(1, steps + 1):
        one, two = straight[-2:]
        if step > 2:
            one = after(one, upper, crossed[-3])
            two = after(two, crossed[-4], crossed[-1])
        one, two = climb(one, step), climb(two, step)
        straight += [one, two]
        crossed += [swap(two, step), swap(one, step)]

    def meta(first):
        return jnp.stack([group, block, first * (KVH // 2), prompt_lengths[0]])

    done = attend(
        meta(side), queries[0], straight, prefix, tile, count, segments=resp_segments
    )
    done = attend(meta(1 - side), queries[0], crossed, prefix, tile, count, before=done)
    return done[0][None]


def solution(mesh):
    return jax.shard_map(
        on_device,
        mesh=mesh,
        in_specs=(
            P("prompt", "resp", None),
            P("prompt", "resp", None),
            P("prompt", "resp"),
            P(("prompt", "resp"), None, None),
            P(("prompt", "resp"), None),
            P("prompt"),
        ),
        out_specs=P("prompt", "resp", None),
        check_vma=False,
    )
```

time: 100 us -> 108 us (1.080); the launches traced: 99.5 us -> 106 us
  starting transfers between devices: 32.9 us -> 38.1 us
  local copies, waits for them, and re-layouts: 8.17 us -> 10.6 us
  Pallas kernels: 23.1 us -> 20.9 us
    ppermute x7, starting transfers between devices: 16.8 us -> 22.2 us  [swap(): lax.ppermute(value, 'resp', [(r, r ^ 1) for r in range(2 * first, count)])]
    unnamed x28 -> x36, local copies, waits for them, and re-layouts: 6.35 us -> 8.75 us
    ppermute x7, waiting for transfers between devices: 14.6 us -> 16.9 us  [swap(): lax.ppermute(value, 'resp', [(r, r ^ 1) for r in range(2 * first, count)])]
    pallas_call x2, Pallas kernels: 21.3 us -> 19 us  [attend(): pl.pallas_call(functools.partial(attend_kernel, pairs, tile, count, fresh...]
    ppermute x6, waiting for transfers between devices: 17.6 us -> 16 us  [climb(): return lax.ppermute(value, 'resp', pairs)]
  transfers between devices with their start and end apart: 15 -> 15, of which waited for: 8 -> 6; matrix products, arithmetic and copies ran while one was open for 3% -> 0% of each run, Pallas kernels for 11% -> 11%
where the time goes in v6:
time: 108 us; the launch traced here: 106 us
  starting transfers between devices  38.1 us (35%)
  waiting for transfers between devices  32.9 us (30%)
  Pallas kernels  20.9 us (19%)
  local copies, waits for them, and re-layouts  10.6 us (10%)
  other arithmetic  2.05 us (2%)
    ppermute x7, starting transfers between devices, swap(): lax.ppermute(value, 'resp', [(r, r ^ 1) for r in range(2 * first, count)])  22.2 us
    pallas_call x2, Pallas kernels, attend(): pl.pallas_call(functools.partial(attend_kernel, pairs, tile, count, fresh...  19 us
    ppermute x7, waiting for transfers between devices, swap(): lax.ppermute(value, 'resp', [(r, r ^ 1) for r in range(2 * first, count)])  16.9 us
    ppermute x6, waiting for transfers between devices, climb(): return lax.ppermute(value, 'resp', pairs)  16 us
    unnamed x36, local copies, waits for them, and re-layouts  8.75 us
    ppermute x6, starting transfers between devices, climb(): return lax.ppermute(value, 'resp', pairs)  7.68 us
    all_to_all x1, starting transfers between devices, on_device(): lax.all_to_all(out_tiles, ('prompt', 'resp'), split_axis=0, concat_axis=0...  5.86 us
    ppermute x1, starting transfers between devices, on_device(): upper = lax.ppermute(after(mine, partner), 'resp', upper)  2.38 us
  transfers between devices with their start and end apart: 15, of which 6 were waited for; matrix products, arithmetic and copies ran while one was open for 0% of the time, Pallas kernels for 11%

profile of v6, /device:TPU:26, one launch (start us, length us, event | category | flops | bytes accessed | tf_op | source)
XLA Modules:
  0.0 105.5 jit_solution(11044100708679100096)
XLA Ops:
  0.0 0.8 slice_bitcast_fusion.1
  0.9 1.0 select_reduce_fusion
  1.9 0.7 convert_convert_fusion
  2.7 1.1 %broadcast_in_dim.76 = bf16[4,8,8,2176]{3,2,1,0:T(8,128)(2,1)} broadcast(bf16[4,8,2176]{2,1,0:T(8,128)(2,1)S(1)} %pad_maximum_fusion), dimensions={0,2,3} | broadcast | bytes 1253376 | tf_op jit(solution)/shard_map/broadcast_in_dim | solution.py:234
  3.8 5.9 %all-to-all-start = ((bf16[32,8,2176]{2,1,0:T(8,128)(2,1)}), bf16[32,8,2176]{2,1,0:T(8,128)(2,1)S(1)}, u32[]{:S(2)}, u32[]{:S(2)}) async-start(bf16[32,8,2176]{2,1,0:T(8,128)(2,1)} %bitcast.20), calls=%async_computation | async-start | bytes 2228224 | tf_op jit(solution)/shard_map/all_to_all | solution.py:237
  9.6 1.9 %shard_map.64 = (bf16[128,1024]{1,0:T(8,128)(2,1)}, bf16[128,1024]{1,0:T(8,128)(2,1)}) custom-call(s32[1]{0:T(128)} %bitcast.10.meta_ref, bf16[128,2048]{1,0:T(8,128)(2,1)} %bitcast.21, bf16[128,2048]{1,0:T(8,128)(2,1)} %bitcast.22), custom_call_target="tpu_custom_call" | custom-call | tf_op jit(solution)/shard_map/pallas_call | solution.py:28
  11.5 1.5 %collective-permute-start = (bf16[128,1024]{1,0:T(8,128)(2,1)}, bf16[128,1024]{1,0:T(8,128)(2,1)S(1)}, u32[]{:S(2)}, u32[]{:S(2)}) collective-permute-start(bf16[128,1024]{1,0:T(8,128)(2,1)} %get-tuple-element.14.refs_4_), channel_id=1, source_target_pairs={{0,1},{1,0},{2,3},{3,2},{4,5},{5,4},{6,7},{7,6},{8,9},{9,8},{10,11... | collective-permute-start | bytes 786440 | tf_op jit(solution)/shard_map/ppermute | solution.py:243
  13.0 1.3 %collective-permute-start.1 = (bf16[128,1024]{1,0:T(8,128)(2,1)}, bf16[128,1024]{1,0:T(8,128)(2,1)S(1)}, u32[]{:S(2)}, u32[]{:S(2)}) collective-permute-start(bf16[128,1024]{1,0:T(8,128)(2,1)} %get-tuple-element.15.refs_3_), channel_id=1, source_target_pairs={{0,2},{1,3},{2,4},{3,5},{4,6},{5,7},{8,10},{9,11},{10,12},{11,13},... | collective-permute-start | bytes 786440 | tf_op jit(solution)/shard_map/ppermute | solution.py:247
  14.3 13.7 %collective-permute-done.refs_4_ = bf16[128,1024]{1,0:T(8,128)(2,1)S(1)} collective-permute-done((bf16[128,1024]{1,0:T(8,128)(2,1)}, bf16[128,1024]{1,0:T(8,128)(2,1)S(1)}, u32[]{:S(2)}, u32[]{:S(2)}) %collective-permute-start) | collective-permute-done | bytes 262176 | tf_op jit(solution)/shard_map/ppermute | solution.py:243
  28.0 1.3 %collective-permute-start.2 = (bf16[128,1024]{1,0:T(8,128)(2,1)S(1)}, bf16[128,1024]{1,0:T(8,128)(2,1)S(1)}, u32[]{:S(2)}, u32[]{:S(2)}) collective-permute-start(bf16[128,1024]{1,0:T(8,128)(2,1)S(1)} %collective-permute-done.refs_4_), channel_id=1, source_target_pairs={{0,2},{1,3},{2,4},{3,5},{4,6},{5,7},{8,10},{9,11},{10,12},{11,13},... | collective-permute-start | bytes 786440 | tf_op jit(solution)/shard_map/ppermute | solution.py:247
  29.3 5.8 %collective-permute-done.1.refs_5_ = bf16[128,1024]{1,0:T(8,128)(2,1)S(1)} collective-permute-done((bf16[128,1024]{1,0:T(8,128)(2,1)}, bf16[128,1024]{1,0:T(8,128)(2,1)S(1)}, u32[]{:S(2)}, u32[]{:S(2)}) %collective-permute-start.1) | collective-permute-done | bytes 262176 | tf_op jit(solution)/shard_map/ppermute | solution.py:247
  35.1 1.3 %collective-permute-start.3 = (bf16[128,1024]{1,0:T(8,128)(2,1)S(1)}, bf16[128,1024]{1,0:T(8,128)(2,1)S(1)}, u32[]{:S(2)}, u32[]{:S(2)}) collective-permute-start(bf16[128,1024]{1,0:T(8,128)(2,1)S(1)} %collective-permute-done.1.refs_5_), channel_id=1, source_target_pairs={{2,4},{3,5},{4,6},{5,7},{10,12},{11,13},{12,14},{13,15},{18,20},{1... | collective-permute-start | bytes 786440 | tf_op jit(solution)/shard_map/ppermute | solution.py:247
  36.4 2.4 %collective-permute-start.5 = (bf16[128,1024]{1,0:T(8,128)(2,1)}, bf16[128,1024]{1,0:T(8,128)(2,1)S(1)}, u32[]{:S(2)}, u32[]{:S(2)}) collective-permute-start(bf16[128,1024]{1,0:T(8,128)(2,1)} %get-tuple-element.15.refs_3_), channel_id=1, source_target_pairs={{0,1},{2,3},{4,5},{6,7},{8,9},{10,11},{12,13},{14,15},{16,17},{18,... | collective-permute-start | bytes 786440 | tf_op jit(solution)/shard_map/ppermute | solution.py:255
  38.8 1.9 %collective-permute-start.6 = (bf16[128,1024]{1,0:T(8,128)(2,1)S(1)}, bf16[128,1024]{1,0:T(8,128)(2,1)S(1)}, u32[]{:S(2)}, u32[]{:S(2)}) collective-permute-start(bf16[128,1024]{1,0:T(8,128)(2,1)S(1)} %collective-permute-done.1.refs_5_), channel_id=1, source_target_pairs={{2,3},{3,2},{4,5},{5,4},{6,7},{7,6},{10,11},{11,10},{12,13},{13,12... | collective-permute-start | bytes 786440 | tf_op jit(solution)/shard_map/ppermute | solution.py:243
  41.5 1.3 %collective-permute-start.4 = (bf16[128,1024]{1,0:T(8,128)(2,1)S(1)}, bf16[128,1024]{1,0:T(8,128)(2,1)}, u32[]{:S(2)}, u32[]{:S(2)}) collective-permute-start(bf16[128,1024]{1,0:T(8,128)(2,1)S(1)} %collective-permute-done.2.refs_6_), channel_id=1, source_target_pairs={{2,4},{3,5},{4,6},{5,7},{10,12},{11,13},{12,14},{13,15},{18,20},{1... | collective-permute-start | bytes 786440 | tf_op jit(solution)/shard_map/ppermute | solution.py:247
  42.8 3.9 %collective-permute-start.8 = (bf16[128,1024]{1,0:T(8,128)(2,1)S(1)}, bf16[128,1024]{1,0:T(8,128)(2,1)S(1)}, u32[]{:S(2)}, u32[]{:S(2)}) collective-permute-start(bf16[128,1024]{1,0:T(8,128)(2,1)S(1)} %collective-permute-done.2.refs_6_), channel_id=1, source_target_pairs={{2,3},{3,2},{4,5},{5,4},{6,7},{7,6},{10,11},{11,10},{12,13},{13,12... | collective-permute-start | bytes 786440 | tf_op jit(solution)/shard_map/ppermute | solution.py:243
  47.4 2.2 %collective-permute-done.3.refs_7_ = bf16[128,1024]{1,0:T(8,128)(2,1)S(1)} collective-permute-done((bf16[128,1024]{1,0:T(8,128)(2,1)S(1)}, bf16[128,1024]{1,0:T(8,128)(2,1)S(1)}, u32[]{:S(2)}, u32[]{:S(2)}) %collective-permute-start.3) | collective-permute-done | bytes 262176 | tf_op jit(solution)/shard_map/ppermute | solution.py:247
  49.6 3.5 %collective-permute-start.9 = (bf16[128,1024]{1,0:T(8,128)(2,1)S(1)}, bf16[128,1024]{1,0:T(8,128)(2,1)S(1)}, u32[]{:S(2)}, u32[]{:S(2)}) collective-permute-start(bf16[128,1024]{1,0:T(8,128)(2,1)S(1)} %collective-permute-done.3.refs_7_), channel_id=1, source_target_pairs={{4,5},{5,4},{6,7},{7,6},{12,13},{13,12},{14,15},{15,14},{20,21},{2... | collective-permute-start | bytes 786440 | tf_op jit(solution)/shard_map/ppermute | solution.py:243
  54.5 1.3 %collective-permute-start.7 = (bf16[128,1024]{1,0:T(8,128)(2,1)S(1)}, bf16[128,1024]{1,0:T(8,128)(2,1)}, u32[]{:S(2)}, u32[]{:S(2)}) collective-permute-start(bf16[128,1024]{1,0:T(8,128)(2,1)S(1)} %collective-permute-done.3.refs_7_), channel_id=1, source_target_pairs={{4,6},{5,7},{12,14},{13,15},{20,22},{21,23},{28,30},{29,31}} | collective-permute-start | bytes 786440 | tf_op jit(solution)/shard_map/ppermute | solution.py:247
  56.5 1.0 collective-permute-done.4.refs_8_
  58.2 3.2 %collective-permute-done.9.refs_9_ = bf16[128,1024]{1,0:T(8,128)(2,1)S(1)} collective-permute-done((bf16[128,1024]{1,0:T(8,128)(2,1)S(1)}, bf16[128,1024]{1,0:T(8,128)(2,1)S(1)}, u32[]{:S(2)}, u32[]{:S(2)}) %collective-permute-start.9) | collective-permute-done | bytes 262176 | tf_op jit(solution)/shard_map/ppermute | solution.py:243
  62.1 1.3 %collective-permute-start.10 = (bf16[128,1024]{1,0:T(8,128)(2,1)}, bf16[128,1024]{1,0:T(8,128)(2,1)}, u32[]{:S(2)}, u32[]{:S(2)}) collective-permute-start(bf16[128,1024]{1,0:T(8,128)(2,1)} %collective-permute-done.4.refs_8_), channel_id=1, source_target_pairs={{4,6},{5,7},{12,14},{13,15},{20,22},{21,23},{28,30},{29,31}} | collective-permute-start | bytes 786440 | tf_op jit(solution)/shard_map/ppermute | solution.py:247
  63.4 4.4 %collective-permute-start.11 = (bf16[128,1024]{1,0:T(8,128)(2,1)}, bf16[128,1024]{1,0:T(8,128)(2,1)}, u32[]{:S(2)}, u32[]{:S(2)}) collective-permute-start(bf16[128,1024]{1,0:T(8,128)(2,1)} %collective-permute-done.4.refs_8_), channel_id=1, source_target_pairs={{4,5},{5,4},{6,7},{7,6},{12,13},{13,12},{14,15},{15,14},{20,21},{2... | collective-permute-start | bytes 786440 | tf_op jit(solution)/shard_map/ppermute | solution.py:243
  67.8 2.6 %collective-permute-start.13 = (bf16[128,1024]{1,0:T(8,128)(2,1)}, bf16[128,1024]{1,0:T(8,128)(2,1)}, u32[]{:S(2)}, u32[]{:S(2)}) collective-permute-start(bf16[128,1024]{1,0:T(8,128)(2,1)} %collective-permute-done.7.refs_9_), channel_id=1, source_target_pairs={{6,7},{7,6},{14,15},{15,14},{22,23},{23,22},{30,31},{31,30}} | collective-permute-start | bytes 786440 | tf_op jit(solution)/shard_map/ppermute | solution.py:243
  70.4 6.9 %collective-permute-done.10.refs_10_ = bf16[128,1024]{1,0:T(8,128)(2,1)} collective-permute-done((bf16[128,1024]{1,0:T(8,128)(2,1)}, bf16[128,1024]{1,0:T(8,128)(2,1)}, u32[]{:S(2)}, u32[]{:S(2)}) %collective-permute-start.10) | collective-permute-done | bytes 262176 | tf_op jit(solution)/shard_map/ppermute | solution.py:247
  77.3 4.4 %collective-permute-start.12 = (bf16[128,1024]{1,0:T(8,128)(2,1)}, bf16[128,1024]{1,0:T(8,128)(2,1)}, u32[]{:S(2)}, u32[]{:S(2)}) collective-permute-start(bf16[128,1024]{1,0:T(8,128)(2,1)} %collective-permute-done.10.refs_10_), channel_id=1, source_target_pairs={{6,7},{7,6},{14,15},{15,14},{22,23},{23,22},{30,31},{31,30}} | collective-permute-start | bytes 786440 | tf_op jit(solution)/shard_map/ppermute | solution.py:243
  82.6 0.9 copy-done.1
  83.5 0.9 copy-done.3
  84.5 0.9 copy-done.5
  85.4 0.9 copy-done.7
  86.4 9.2 %shard_map.65 = (bf16[128,8192]{1,0:T(8,128)(2,1)}, f32[128,1280]{1,0:T(8,128)S(1)}, s32[1]{0:T(128)}) custom-call(s32[4]{0:T(128)S(1)} %add_add_fusion.1.meta_ref, s32[1,128]{1,0:T(1,128)S(1)} %copy-done.17, bf16[128,8192]{1,0:T(8,128)(2,1)S(1)} %bitcast.17, bf16[256,2176]{1,0:T(8,128)(2,1)S(1)} %bitcast.15, bf16[128,1024]{1,0:T(8,128)(2,1)S(1)} %copy-done.1, ...), custom_call_target="tpu_custom_call" | custom-call | tf_op jit(solution)/shard_map/pallas_call | solution.py:195
  95.7 9.8 %shard_map.66 = bf16[128,8192]{1,0:T(8,128)(2,1)} custom-call(s32[4]{0:T(128)S(1)} %add_add_fusion.meta_ref, f32[128,1280]{1,0:T(8,128)S(1)} %get-tuple-element.18.refs_0_, s32[1]{0:T(128)} %get-tuple-element.19.refs_1_, bf16[128,8192]{1,0:T(8,128)(2,1)S(1)} %bitcast.18, bf16[256,2176]{1,0:T(8,128)(2,1)S(1)} %bitcast.16, ...), custom_call_target="tpu_custom_call", output_to_operand_aliasing={{}: (13, {})} | custom-call | tf_op jit(solution)/shard_map/pallas_call | solution.py:195
  (47 shorter events, 5.3 us)
Async XLA Ops:
  2.7 79.9 %copy-start = (bf16[1,128,8192]{2,1,0:T(8,128)(2,1)S(1)}, bf16[1,128,8192]{2,1,0:T(8,128)(2,1)}, u32[]{:S(2)}) copy-start(bf16[1,128,8192]{2,1,0:T(8,128)(2,1)} %param.6) | copy-start | bytes 6291460
  2.7 79.9 %copy-start.17 = (s32[1,128]{1,0:T(1,128)S(1)}, s32[1,128]{1,0:T(1,128)}, u32[]{:S(2)}) copy-start(s32[1,128]{1,0:T(1,128)} %refs_0_.1) | copy-start | bytes 1540
  3.8 78.8 %all-to-all-start = ((bf16[32,8,2176]{2,1,0:T(8,128)(2,1)}), bf16[32,8,2176]{2,1,0:T(8,128)(2,1)S(1)}, u32[]{:S(2)}, u32[]{:S(2)}) async-start(bf16[32,8,2176]{2,1,0:T(8,128)(2,1)} %bitcast.20), calls=%async_computation | async-start | bytes 2228224 | tf_op jit(solution)/shard_map/all_to_all | solution.py:237
  11.5 16.5 %collective-permute-start = (bf16[128,1024]{1,0:T(8,128)(2,1)}, bf16[128,1024]{1,0:T(8,128)(2,1)S(1)}, u32[]{:S(2)}, u32[]{:S(2)}) collective-permute-start(bf16[128,1024]{1,0:T(8,128)(2,1)} %get-tuple-element.14.refs_4_), channel_id=1, source_target_pairs={{0,1},{1,0},{2,3},{3,2},{4,5},{5,4},{6,7},{7,6},{8,9},{9,8},{10,11... | collective-permute-start | bytes 786440 | tf_op jit(solution)/shard_map/ppermute | solution.py:243
  13.0 22.1 %collective-permute-start.1 = (bf16[128,1024]{1,0:T(8,128)(2,1)}, bf16[128,1024]{1,0:T(8,128)(2,1)S(1)}, u32[]{:S(2)}, u32[]{:S(2)}) collective-permute-start(bf16[128,1024]{1,0:T(8,128)(2,1)} %get-tuple-element.15.refs_3_), channel_id=1, source_target_pairs={{0,2},{1,3},{2,4},{3,5},{4,6},{5,7},{8,10},{9,11},{10,12},{11,13},... | collective-permute-start | bytes 786440 | tf_op jit(solution)/shard_map/ppermute | solution.py:247
  28.0 13.5 %collective-permute-start.2 = (bf16[128,1024]{1,0:T(8,128)(2,1)S(1)}, bf16[128,1024]{1,0:T(8,128)(2,1)S(1)}, u32[]{:S(2)}, u32[]{:S(2)}) collective-permute-start(bf16[128,1024]{1,0:T(8,128)(2,1)S(1)} %collective-permute-done.refs_4_), channel_id=1, source_target_pairs={{0,2},{1,3},{2,4},{3,5},{4,6},{5,7},{8,10},{9,11},{10,12},{11,13},... | collective-permute-start | bytes 786440 | tf_op jit(solution)/shard_map/ppermute | solution.py:247
  35.1 14.4 %collective-permute-start.3 = (bf16[128,1024]{1,0:T(8,128)(2,1)S(1)}, bf16[128,1024]{1,0:T(8,128)(2,1)S(1)}, u32[]{:S(2)}, u32[]{:S(2)}) collective-permute-start(bf16[128,1024]{1,0:T(8,128)(2,1)S(1)} %collective-permute-done.1.refs_5_), channel_id=1, source_target_pairs={{2,4},{3,5},{4,6},{5,7},{10,12},{11,13},{12,14},{13,15},{18,20},{1... | collective-permute-start | bytes 786440 | tf_op jit(solution)/shard_map/ppermute | solution.py:247
  36.4 16.6 %collective-permute-start.5 = (bf16[128,1024]{1,0:T(8,128)(2,1)}, bf16[128,1024]{1,0:T(8,128)(2,1)S(1)}, u32[]{:S(2)}, u32[]{:S(2)}) collective-permute-start(bf16[128,1024]{1,0:T(8,128)(2,1)} %get-tuple-element.15.refs_3_), channel_id=1, source_target_pairs={{0,1},{2,3},{4,5},{6,7},{8,9},{10,11},{12,13},{14,15},{16,17},{18,... | collective-permute-start | bytes 786440 | tf_op jit(solution)/shard_map/ppermute | solution.py:255
  38.8 15.0 %collective-permute-start.6 = (bf16[128,1024]{1,0:T(8,128)(2,1)S(1)}, bf16[128,1024]{1,0:T(8,128)(2,1)S(1)}, u32[]{:S(2)}, u32[]{:S(2)}) collective-permute-start(bf16[128,1024]{1,0:T(8,128)(2,1)S(1)} %collective-permute-done.1.refs_5_), channel_id=1, source_target_pairs={{2,3},{3,2},{4,5},{5,4},{6,7},{7,6},{10,11},{11,10},{12,13},{13,12... | collective-permute-start | bytes 786440 | tf_op jit(solution)/shard_map/ppermute | solution.py:243
  40.8 0.7 copy-start.2
  41.5 16.0 %collective-permute-start.4 = (bf16[128,1024]{1,0:T(8,128)(2,1)S(1)}, bf16[128,1024]{1,0:T(8,128)(2,1)}, u32[]{:S(2)}, u32[]{:S(2)}) collective-permute-start(bf16[128,1024]{1,0:T(8,128)(2,1)S(1)} %collective-permute-done.2.refs_6_), channel_id=1, source_target_pairs={{2,4},{3,5},{4,6},{5,7},{10,12},{11,13},{12,14},{13,15},{18,20},{1... | collective-permute-start | bytes 786440 | tf_op jit(solution)/shard_map/ppermute | solution.py:247
  42.8 14.7 %collective-permute-start.8 = (bf16[128,1024]{1,0:T(8,128)(2,1)S(1)}, bf16[128,1024]{1,0:T(8,128)(2,1)S(1)}, u32[]{:S(2)}, u32[]{:S(2)}) collective-permute-start(bf16[128,1024]{1,0:T(8,128)(2,1)S(1)} %collective-permute-done.2.refs_6_), channel_id=1, source_target_pairs={{2,3},{3,2},{4,5},{5,4},{6,7},{7,6},{10,11},{11,10},{12,13},{13,12... | collective-permute-start | bytes 786440 | tf_op jit(solution)/shard_map/ppermute | solution.py:243
  46.7 0.7 copy-start.4
  49.6 11.8 %collective-permute-start.9 = (bf16[128,1024]{1,0:T(8,128)(2,1)S(1)}, bf16[128,1024]{1,0:T(8,128)(2,1)S(1)}, u32[]{:S(2)}, u32[]{:S(2)}) collective-permute-start(bf16[128,1024]{1,0:T(8,128)(2,1)S(1)} %collective-permute-done.3.refs_7_), channel_id=1, source_target_pairs={{4,5},{5,4},{6,7},{7,6},{12,13},{13,12},{14,15},{15,14},{20,21},{2... | collective-permute-start | bytes 786440 | tf_op jit(solution)/shard_map/ppermute | solution.py:243
  53.1 0.7 copy-start.9
  53.8 0.7 copy-start.11
  54.5 13.3 %collective-permute-start.7 = (bf16[128,1024]{1,0:T(8,128)(2,1)S(1)}, bf16[128,1024]{1,0:T(8,128)(2,1)}, u32[]{:S(2)}, u32[]{:S(2)}) collective-permute-start(bf16[128,1024]{1,0:T(8,128)(2,1)S(1)} %collective-permute-done.3.refs_7_), channel_id=1, source_target_pairs={{4,6},{5,7},{12,14},{13,15},{20,22},{21,23},{28,30},{29,31}} | collective-permute-start | bytes 786440 | tf_op jit(solution)/shard_map/ppermute | solution.py:247
  57.5 0.7 copy-start.13
  61.4 0.7 copy-start.15
  62.1 15.2 %collective-permute-start.10 = (bf16[128,1024]{1,0:T(8,128)(2,1)}, bf16[128,1024]{1,0:T(8,128)(2,1)}, u32[]{:S(2)}, u32[]{:S(2)}) collective-permute-start(bf16[128,1024]{1,0:T(8,128)(2,1)} %collective-permute-done.4.refs_8_), channel_id=1, source_target_pairs={{4,6},{5,7},{12,14},{13,15},{20,22},{21,23},{28,30},{29,31}} | collective-permute-start | bytes 786440 | tf_op jit(solution)/shard_map/ppermute | solution.py:247
  63.4 32.2 %collective-permute-start.11 = (bf16[128,1024]{1,0:T(8,128)(2,1)}, bf16[128,1024]{1,0:T(8,128)(2,1)}, u32[]{:S(2)}, u32[]{:S(2)}) collective-permute-start(bf16[128,1024]{1,0:T(8,128)(2,1)} %collective-permute-done.4.refs_8_), channel_id=1, source_target_pairs={{4,5},{5,4},{6,7},{7,6},{12,13},{13,12},{14,15},{15,14},{20,21},{2... | collective-permute-start | bytes 786440 | tf_op jit(solution)/shard_map/ppermute | solution.py:243
  67.8 27.8 %collective-permute-start.13 = (bf16[128,1024]{1,0:T(8,128)(2,1)}, bf16[128,1024]{1,0:T(8,128)(2,1)}, u32[]{:S(2)}, u32[]{:S(2)}) collective-permute-start(bf16[128,1024]{1,0:T(8,128)(2,1)} %collective-permute-done.7.refs_9_), channel_id=1, source_target_pairs={{6,7},{7,6},{14,15},{15,14},{22,23},{23,22},{30,31},{31,30}} | collective-permute-start | bytes 786440 | tf_op jit(solution)/shard_map/ppermute | solution.py:243
  77.3 18.3 %collective-permute-start.12 = (bf16[128,1024]{1,0:T(8,128)(2,1)}, bf16[128,1024]{1,0:T(8,128)(2,1)}, u32[]{:S(2)}, u32[]{:S(2)}) collective-permute-start(bf16[128,1024]{1,0:T(8,128)(2,1)} %collective-permute-done.10.refs_10_), channel_id=1, source_target_pairs={{6,7},{7,6},{14,15},{15,14},{22,23},{23,22},{30,31},{31,30}} | collective-permute-start | bytes 786440 | tf_op jit(solution)/shard_map/ppermute | solution.py:243
  82.6 1.0 copy-start.1
  83.5 0.9 copy-start.3
  84.5 0.9 copy-start.5
  85.4 0.9 copy-start.7
  86.4 9.3 %copy-start.8 = (bf16[128,1024]{1,0:T(8,128)(2,1)S(1)}, bf16[128,1024]{1,0:T(8,128)(2,1)}, u32[]{:S(2)}) copy-start(bf16[128,1024]{1,0:T(8,128)(2,1)} %get-tuple-element.14.refs_4_) | copy-start | bytes 786436
  86.4 9.3 %copy-start.10 = (bf16[128,1024]{1,0:T(8,128)(2,1)S(1)}, bf16[128,1024]{1,0:T(8,128)(2,1)}, u32[]{:S(2)}) copy-start(bf16[128,1024]{1,0:T(8,128)(2,1)} %copy-done.9) | copy-start | bytes 786436
  86.4 9.3 %copy-start.12 = (bf16[128,1024]{1,0:T(8,128)(2,1)S(1)}, bf16[128,1024]{1,0:T(8,128)(2,1)}, u32[]{:S(2)}) copy-start(bf16[128,1024]{1,0:T(8,128)(2,1)} %copy-done.11) | copy-start | bytes 786436
  86.4 9.3 %copy-start.14 = (bf16[128,1024]{1,0:T(8,128)(2,1)S(1)}, bf16[128,1024]{1,0:T(8,128)(2,1)}, u32[]{:S(2)}) copy-start(bf16[128,1024]{1,0:T(8,128)(2,1)} %copy-done.13) | copy-start | bytes 786436
  86.4 9.3 %copy-start.16 = (bf16[128,1024]{1,0:T(8,128)(2,1)S(1)}, bf16[128,1024]{1,0:T(8,128)(2,1)}, u32[]{:S(2)}) copy-start(bf16[128,1024]{1,0:T(8,128)(2,1)} %copy-done.15) | copy-start | bytes 786436
  (1 other events, 0.7 us)

commit v7 on v6

--- a/solution.py
+++ b/solution.py
@@ -41,31 +41,23 @@
 
 
 def attend_kernel(pairs, tile, count, fresh, meta_ref, *refs):
-    kv_ref, s_ref, top_ref, sems = refs[-4:]
+    s_ref, top_ref = refs[-2:]
     if fresh:
-        seg_ref, q_ref, prefix_ref, *pieces = refs[: 3 + 2 * pairs]
-        o_ref, bias_ref, reach_ref, ints_ref, seg_k_ref = refs[3 + 2 * pairs : -4]
+        seg_ref, ints_ref, q_ref, *inputs = refs[: 5 + 4 * pairs]
+        o_ref, bias_ref, reach_ref, seg_k_ref = refs[5 + 4 * pairs : -2]
     else:
-        bias_ref, reach_ref, q_ref, prefix_ref, *pieces = refs[: 4 + 2 * pairs]
-        o_ref = refs[-5]
+        bias_ref, reach_ref, q_ref, *inputs = refs[: 5 + 4 * pairs]
+        o_ref = refs[-3]
+    pk_ref, pv_ref, *inputs = inputs
+    k_refs, v_refs = inputs[: 2 * pairs], inputs[2 * pairs :]
     rows = q_ref.shape[0]
-    heads = kv_ref.shape[1] // (2 * HD)
     step = 2 * rows
-    prefix_keys = prefix_ref.shape[0]
-    group, block, head0, limit = meta_ref[0], meta_ref[1], meta_ref[2], meta_ref[3]
-    head = pl.program_id(0)
+    prefix_keys = pk_ref.shape[0]
+    group, block, limit = meta_ref[0], meta_ref[1], meta_ref[3]
     scale = math.log2(math.e) / math.sqrt(HD)
     nt = (((1,), (1,)), ((), ()))
 
-    def column(index, width=HD):
-        return pl.ds(pl.multiple_of(index * HD, HD), width)
-
     def masks():
-        ints_copy = pltpu.make_async_copy(
-            prefix_ref.at[:, pl.ds(2 * KVH * HD, rows)], ints_ref, sems.at[2 * pairs + 2]
-        )
-        ints_copy.start()
-        ints_copy.wait()
         ints = ints_ref[...].astype(jnp.float32)
         seg_k_ref[...] = ints
         part = lax.rem(lax.broadcasted_iota(jnp.int32, ints.shape, 0), tile)
@@ -92,30 +84,15 @@
                 at = prefix_keys + (2 * k + j) * rows
                 bias_ref[:, at : at + rows] = jnp.where(seen, 0.0, FILL)
 
-    @pl.when(head == 0)
-    def _():
-        copies = []
-        for j, first in enumerate((head0, KVH + head0)):
-            copies.append(
-                pltpu.make_async_copy(
-                    prefix_ref.at[:, column(first, heads * HD)],
-                    kv_ref.at[pl.ds(0, prefix_keys), pl.ds(j * heads * HD, heads * HD)],
-                    sems.at[j],
-                )
-            )
-        for j, piece in enumerate(pieces):
-            at = pl.ds(prefix_keys + j * rows, rows)
-            copies.append(pltpu.make_async_copy(piece, kv_ref.at[at], sems.at[2 + j]))
-        for copy in copies:
-            copy.start()
-        if fresh:
-            masks()
-        for copy in copies:
-            copy.wait()
+    if fresh:
+        pl.when(pl.program_id(0) == 0)(masks)
 
     def body(near):
         steps = prefix_keys // step + near + 1
-        values = kv_ref[: steps * step, column(heads + head)]
+        keys = [pk_ref[at : at + step, :] for at in range(0, prefix_keys, step)]
+        for k in range(near + 1):
+            keys.append(jnp.concatenate([k_refs[2 * k][...], k_refs[2 * k + 1][...]]))
+        values = jnp.concatenate([pv_ref[...]] + [ref[...] for ref in v_refs[: 2 * near + 2]])
         values = jnp.concatenate([values, jnp.ones_like(values)], axis=1)
 
         def score(slab):
@@ -124,9 +101,7 @@
             top = None
             for i in range(steps):
                 at = slice(i * step, (i + 1) * step)
-                s = lax.dot_general(
-                    q, kv_ref[at, column(head)], nt, preferred_element_type=jnp.float32
-                )
+                s = lax.dot_general(q, keys[i], nt, preferred_element_type=jnp.float32)
                 s = (s.reshape(SLAB, rows, step) + bias_ref[:, at][None]).reshape(-1, step)
                 s_ref[slab % 2, :, at] = s
                 high = jnp.maximum(s[:, :rows], s[:, rows:])
@@ -166,14 +141,24 @@
     pairs = len(pieces) // 2
     heads = pieces[0].shape[1] // (2 * HD)
     keys = rows * len(pieces) + prefix_keys
-    far = pl.BlockSpec(memory_space=pltpu.HBM)
     whole = pl.BlockSpec((rows, keys), lambda i, m: (0, 0))
     scalar = pl.BlockSpec(memory_space=pltpu.SMEM)
     wide = pl.BlockSpec((rows, GQ * HD), lambda i, m: (0, m[2] + i))
     fresh = before is None
-    args = [meta, *([segments] if fresh else before[1:]), queries, prefix, *pieces]
-    in_specs = [pl.BlockSpec((1, rows), lambda i, m: (0, 0))] if fresh else [whole, scalar]
-    in_specs += [wide, far, *[far] * len(pieces)]
+    queries, prefix, *pieces = [
+        pltpu.with_memory_space_constraint(array, pltpu.HBM) for array in (queries, prefix, *pieces)
+    ]
+    args = [meta, *([segments, prefix] if fresh else before[1:])]
+    args += [queries, prefix, prefix, *pieces, *pieces]
+    ints = pl.BlockSpec((prefix_keys, rows), lambda i, m: (0, 2 * KVH))
+    in_specs = [pl.BlockSpec((1, rows), lambda i, m: (0, 0)), ints] if fresh else [whole, scalar]
+    in_specs += [
+        wide,
+        pl.BlockSpec((prefix_keys, HD), lambda i, m: (0, m[2] + i)),
+        pl.BlockSpec((prefix_keys, HD), lambda i, m: (0, KVH + m[2] + i)),
+        *[pl.BlockSpec((rows, HD), lambda i, m: (0, i))] * len(pieces),
+        *[pl.BlockSpec((rows, HD), lambda i, m: (0, heads + i))] * len(pieces),
+    ]
     out_specs = [wide]
     out_shape = [jax.ShapeDtypeStruct(queries.shape, queries.dtype)]
     scratch = []
@@ -184,13 +169,10 @@
             jax.ShapeDtypeStruct((rows, keys), jnp.float32),
             jax.ShapeDtypeStruct((1,), jnp.int32),
         ]
-        scratch = [
-            pltpu.VMEM((prefix_keys, rows), queries.dtype),
-            pltpu.VMEM((prefix_keys, rows), jnp.float32),
-        ]
+        scratch = [pltpu.VMEM((prefix_keys, rows), jnp.float32)]
     else:
         args.append(before[0])
-        in_specs.append(far)
+        in_specs.append(pl.BlockSpec(memory_space=pl.ANY))
         aliases = {len(args) - 1: 0}
     return pl.pallas_call(
         functools.partial(attend_kernel, pairs, tile, count, fresh),
@@ -201,10 +183,8 @@
             out_specs=out_specs,
             scratch_shapes=[
                 *scratch,
-                pltpu.VMEM((keys, 2 * heads * HD), queries.dtype),
                 pltpu.VMEM((2, SLAB * rows, keys), jnp.float32),
                 pltpu.VMEM((2, SLAB * rows, HD), jnp.float32),
-                pltpu.SemaphoreType.DMA((len(pieces) + 3,)),
             ],
         ),
         out_shape=out_shape,
@@ -234,11 +214,6 @@
     out_tiles = jnp.broadcast_to(
         out_tiles.astype(prefix_kv.dtype)[:, None], (groups, count, tile, columns + rows)
     ).reshape(groups * count, tile, columns + rows)
-    came = lax.all_to_all(
-        out_tiles, ("prompt", "resp"), split_axis=0, concat_axis=0, tiled=True
-    )
-    prefix = came.reshape(-1, columns + rows)
-
     def swap(value, first):
         return lax.ppermute(value, "resp", [(r, r ^ 1) for r in range(2 * first, count)])
 
@@ -259,9 +234,16 @@
         if step > 2:
             one = after(one, upper, crossed[-3])
             two = after(two, crossed[-4], crossed[-1])
-        one, two = climb(one, step), climb(two, step)
+        one = climb(one, step)
+        if step == 1:
+            out_tiles = after(out_tiles, one, two)
+        two = climb(two, step)
         straight += [one, two]
         crossed += [swap(two, step), swap(one, step)]
+    came = lax.all_to_all(
+        out_tiles, ("prompt", "resp"), split_axis=0, concat_axis=0, tiled=True
+    )
+    prefix = came.reshape(-1, columns + rows)
 
     def meta(first):
         return jnp.stack([group, block, first * (KVH // 2), prompt_lengths[0]])

time: 108 us -> 102 us (0.944)
  the two profiles are of different devices: /device:TPU:26 before, /device:TPU:24 now
where the time goes in v7:
time: 102 us; the launch traced here: 103 us
  waiting for transfers between devices  39.3 us (39%)
  starting transfers between devices  34.2 us (34%)
  Pallas kernels  23 us (23%)
  local copies, waits for them, and re-layouts  3.51 us (3%)
  other arithmetic  2.06 us (2%)
    ppermute x6, waiting for transfers between devices, climb(): return lax.ppermute(value, 'resp', pairs)  34.5 us
    pallas_call x2, Pallas kernels, attend(): pl.pallas_call(functools.partial(attend_kernel, pairs, tile, count, fresh...  21.1 us
    ppermute x7, starting transfers between devices, swap(): lax.ppermute(value, 'resp', [(r, r ^ 1) for r in range(2 * first, count)])  18.1 us
    ppermute x6, starting transfers between devices, climb(): return lax.ppermute(value, 'resp', pairs)  7.72 us
    all_to_all x1, starting transfers between devices, on_device(): lax.all_to_all(out_tiles, ('prompt', 'resp'), split_axis=0, concat_axis=0...  4.91 us
    ppermute x7, waiting for transfers between devices, swap(): lax.ppermute(value, 'resp', [(r, r ^ 1) for r in range(2 * first, count)])  4.84 us
    ppermute x1, starting transfers between devices, on_device(): upper = lax.ppermute(after(mine, partner), 'resp', upper)  3.42 us
  transfers between devices with their start and end apart: 15, of which 8 were waited for; matrix products, arithmetic and copies ran while one was open for 3% of the time, Pallas kernels for 10%

profile of v7, /device:TPU:24, one launch (start us, length us, event | category | flops | bytes accessed | tf_op | source)
XLA Modules:
  0.0 103.0 jit_solution(16697907240297460878)
XLA Ops:
  0.0 1.8 %shard_map.64 = (bf16[128,1024]{1,0:T(8,128)(2,1)}, bf16[128,1024]{1,0:T(8,128)(2,1)}) custom-call(s32[1]{0:T(128)} %bitcast.8.meta_ref, bf16[128,2048]{1,0:T(8,128)(2,1)} %bitcast.23, bf16[128,2048]{1,0:T(8,128)(2,1)} %bitcast.24), custom_call_target="tpu_custom_call" | custom-call | tf_op jit(solution)/shard_map/pallas_call | solution.py:28
  1.9 1.6 %collective-permute-start.1 = (bf16[128,1024]{1,0:T(8,128)(2,1)}, bf16[128,1024]{1,0:T(8,128)(2,1)S(1)}, u32[]{:S(2)}, u32[]{:S(2)}) collective-permute-start(bf16[128,1024]{1,0:T(8,128)(2,1)} %get-tuple-element.15.refs_5_.refs_13_), channel_id=1, source_target_pairs={{0,1},{1,0},{2,3},{3,2},{4,5},{5,4},{6,7},{7,6},{8,9},{9,8},{10,11... | collective-permute-start | bytes 786440 | tf_op jit(solution)/shard_map/ppermute | solution.py:218
  3.4 1.3 %collective-permute-start = (bf16[128,1024]{1,0:T(8,128)(2,1)}, bf16[128,1024]{1,0:T(8,128)(2,1)S(1)}, u32[]{:S(2)}, u32[]{:S(2)}) collective-permute-start(bf16[128,1024]{1,0:T(8,128)(2,1)} %get-tuple-element.17.refs_5_.refs_13_), channel_id=1, source_target_pairs={{0,2},{1,3},{2,4},{3,5},{4,6},{5,7},{8,10},{9,11},{10,12},{11,13},... | collective-permute-start | bytes 786440 | tf_op jit(solution)/shard_map/ppermute | solution.py:222
  4.7 0.8 slice_bitcast_fusion.1
  5.6 1.0 %select_reduce_fusion = bf16[4,8,2048]{2,1,0:T(8,128)(2,1)S(1)} fusion(pred[4,4]{1,0:T(4,128)(4,1)S(1)} %iota_compare_fusion, bf16[4,8,2048]{2,1,0:T(8,128)(2,1)} %param.9), kind=kLoop, calls=%fused_computation | loop fusion | flops 458752 | bytes 262160 | tf_op jit(solution)/shard_map/reduce_sum | solution.py:208
  6.7 0.7 convert_convert_fusion
  7.4 2.8 %collective-permute-done.1.refs_6_.refs_14_ = bf16[128,1024]{1,0:T(8,128)(2,1)S(1)} collective-permute-done((bf16[128,1024]{1,0:T(8,128)(2,1)}, bf16[128,1024]{1,0:T(8,128)(2,1)S(1)}, u32[]{:S(2)}, u32[]{:S(2)}) %collective-permute-start.1) | collective-permute-done | bytes 262176 | tf_op jit(solution)/shard_map/ppermute | solution.py:218
  10.2 3.1 %collective-permute-done.refs_7_.refs_15_ = bf16[128,1024]{1,0:T(8,128)(2,1)S(1)} collective-permute-done((bf16[128,1024]{1,0:T(8,128)(2,1)}, bf16[128,1024]{1,0:T(8,128)(2,1)S(1)}, u32[]{:S(2)}, u32[]{:S(2)}) %collective-permute-start) | collective-permute-done | bytes 262176 | tf_op jit(solution)/shard_map/ppermute | solution.py:222
  13.3 1.1 %broadcast_in_dim.76 = bf16[4,8,8,2176]{3,2,1,0:T(8,128)(2,1)} broadcast(bf16[4,8,2176]{2,1,0:T(8,128)(2,1)S(1)} %pad_maximum_fusion), dimensions={0,2,3} | broadcast | bytes 1253376 | tf_op jit(solution)/shard_map/broadcast_in_dim | solution.py:214
  14.4 4.9 %all-to-all-start = ((bf16[32,8,2176]{2,1,0:T(8,128)(2,1)}), bf16[32,8,2176]{2,1,0:T(8,128)(2,1)S(1)}, u32[]{:S(2)}, u32[]{:S(2)}) async-start(bf16[32,8,2176]{2,1,0:T(8,128)(2,1)} %bitcast.7), calls=%async_computation | async-start | bytes 2228224 | tf_op jit(solution)/shard_map/all_to_all | solution.py:243
  19.3 1.3 %collective-permute-start.2 = (bf16[128,1024]{1,0:T(8,128)(2,1)S(1)}, bf16[128,1024]{1,0:T(8,128)(2,1)S(1)}, u32[]{:S(2)}, u32[]{:S(2)}) collective-permute-start(bf16[128,1024]{1,0:T(8,128)(2,1)S(1)} %collective-permute-done.1.refs_6_.refs_14_), channel_id=1, source_target_pairs={{0,2},{1,3},{2,4},{3,5},{4,6},{5,7},{8,10},{9,11},{10,12},{11,13},... | collective-permute-start | bytes 786440 | tf_op jit(solution)/shard_map/ppermute | solution.py:222
  20.6 1.3 %collective-permute-start.3 = (bf16[128,1024]{1,0:T(8,128)(2,1)S(1)}, bf16[128,1024]{1,0:T(8,128)(2,1)S(1)}, u32[]{:S(2)}, u32[]{:S(2)}) collective-permute-start(bf16[128,1024]{1,0:T(8,128)(2,1)S(1)} %collective-permute-done.refs_7_.refs_15_), channel_id=1, source_target_pairs={{2,4},{3,5},{4,6},{5,7},{10,12},{11,13},{12,14},{13,15},{18,20},{1... | collective-permute-start | bytes 786440 | tf_op jit(solution)/shard_map/ppermute | solution.py:222
  21.9 3.4 %collective-permute-start.5 = (bf16[128,1024]{1,0:T(8,128)(2,1)S(1)}, bf16[128,1024]{1,0:T(8,128)(2,1)S(1)}, u32[]{:S(2)}, u32[]{:S(2)}) collective-permute-start(bf16[128,1024]{1,0:T(8,128)(2,1)S(1)} %copy-done.2), channel_id=1, source_target_pairs={{0,1},{2,3},{4,5},{6,7},{8,9},{10,11},{12,13},{14,15},{16,17},{18,... | collective-permute-start | bytes 786440 | tf_op jit(solution)/shard_map/ppermute | solution.py:230
  25.3 1.9 %collective-permute-start.6 = (bf16[128,1024]{1,0:T(8,128)(2,1)S(1)}, bf16[128,1024]{1,0:T(8,128)(2,1)S(1)}, u32[]{:S(2)}, u32[]{:S(2)}) collective-permute-start(bf16[128,1024]{1,0:T(8,128)(2,1)S(1)} %collective-permute-done.refs_7_.refs_15_), channel_id=1, source_target_pairs={{2,3},{3,2},{4,5},{5,4},{6,7},{7,6},{10,11},{11,10},{12,13},{13,12... | collective-permute-start | bytes 786440 | tf_op jit(solution)/shard_map/ppermute | solution.py:218
  27.3 17.5 %collective-permute-done.2.refs_8_.refs_16_ = bf16[128,1024]{1,0:T(8,128)(2,1)S(1)} collective-permute-done((bf16[128,1024]{1,0:T(8,128)(2,1)S(1)}, bf16[128,1024]{1,0:T(8,128)(2,1)S(1)}, u32[]{:S(2)}, u32[]{:S(2)}) %collective-permute-start.2) | collective-permute-done | bytes 262176 | tf_op jit(solution)/shard_map/ppermute | solution.py:222
  44.7 1.3 %collective-permute-start.4 = (bf16[128,1024]{1,0:T(8,128)(2,1)S(1)}, bf16[128,1024]{1,0:T(8,128)(2,1)}, u32[]{:S(2)}, u32[]{:S(2)}) collective-permute-start(bf16[128,1024]{1,0:T(8,128)(2,1)S(1)} %collective-permute-done.2.refs_8_.refs_16_), channel_id=1, source_target_pairs={{2,4},{3,5},{4,6},{5,7},{10,12},{11,13},{12,14},{13,15},{18,20},{1... | collective-permute-start | bytes 786440 | tf_op jit(solution)/shard_map/ppermute | solution.py:222
  46.0 2.4 %collective-permute-start.8 = (bf16[128,1024]{1,0:T(8,128)(2,1)S(1)}, bf16[128,1024]{1,0:T(8,128)(2,1)S(1)}, u32[]{:S(2)}, u32[]{:S(2)}) collective-permute-start(bf16[128,1024]{1,0:T(8,128)(2,1)S(1)} %collective-permute-done.2.refs_8_.refs_16_), channel_id=1, source_target_pairs={{2,3},{3,2},{4,5},{5,4},{6,7},{7,6},{10,11},{11,10},{12,13},{13,12... | collective-permute-start | bytes 786440 | tf_op jit(solution)/shard_map/ppermute | solution.py:218
  48.5 1.6 %collective-permute-done.3.refs_9_.refs_17_ = bf16[128,1024]{1,0:T(8,128)(2,1)S(1)} collective-permute-done((bf16[128,1024]{1,0:T(8,128)(2,1)S(1)}, bf16[128,1024]{1,0:T(8,128)(2,1)S(1)}, u32[]{:S(2)}, u32[]{:S(2)}) %collective-permute-start.3) | collective-permute-done | bytes 262176 | tf_op jit(solution)/shard_map/ppermute | solution.py:222
  50.0 3.4 %collective-permute-start.9 = (bf16[128,1024]{1,0:T(8,128)(2,1)S(1)}, bf16[128,1024]{1,0:T(8,128)(2,1)S(1)}, u32[]{:S(2)}, u32[]{:S(2)}) collective-permute-start(bf16[128,1024]{1,0:T(8,128)(2,1)S(1)} %collective-permute-done.3.refs_9_.refs_17_), channel_id=1, source_target_pairs={{4,5},{5,4},{6,7},{7,6},{12,13},{13,12},{14,15},{15,14},{20,21},{2... | collective-permute-start | bytes 786440 | tf_op jit(solution)/shard_map/ppermute | solution.py:218
  53.4 1.3 %collective-permute-start.7 = (bf16[128,1024]{1,0:T(8,128)(2,1)S(1)}, bf16[128,1024]{1,0:T(8,128)(2,1)}, u32[]{:S(2)}, u32[]{:S(2)}) collective-permute-start(bf16[128,1024]{1,0:T(8,128)(2,1)S(1)} %collective-permute-done.3.refs_9_.refs_17_), channel_id=1, source_target_pairs={{4,6},{5,7},{12,14},{13,15},{20,22},{21,23},{28,30},{29,31}} | collective-permute-start | bytes 786440 | tf_op jit(solution)/shard_map/ppermute | solution.py:222
  54.7 4.4 %collective-permute-done.4.refs_10_.refs_18_ = bf16[128,1024]{1,0:T(8,128)(2,1)} collective-permute-done((bf16[128,1024]{1,0:T(8,128)(2,1)S(1)}, bf16[128,1024]{1,0:T(8,128)(2,1)}, u32[]{:S(2)}, u32[]{:S(2)}) %collective-permute-start.4) | collective-permute-done | bytes 262176 | tf_op jit(solution)/shard_map/ppermute | solution.py:222
  59.2 2.1 %collective-permute-done.9.refs_10_.refs_18_ = bf16[128,1024]{1,0:T(8,128)(2,1)S(1)} collective-permute-done((bf16[128,1024]{1,0:T(8,128)(2,1)S(1)}, bf16[128,1024]{1,0:T(8,128)(2,1)S(1)}, u32[]{:S(2)}, u32[]{:S(2)}) %collective-permute-start.9) | collective-permute-done | bytes 262176 | tf_op jit(solution)/shard_map/ppermute | solution.py:218
  61.2 1.3 %collective-permute-start.10 = (bf16[128,1024]{1,0:T(8,128)(2,1)}, bf16[128,1024]{1,0:T(8,128)(2,1)}, u32[]{:S(2)}, u32[]{:S(2)}) collective-permute-start(bf16[128,1024]{1,0:T(8,128)(2,1)} %collective-permute-done.4.refs_10_.refs_18_), channel_id=1, source_target_pairs={{4,6},{5,7},{12,14},{13,15},{20,22},{21,23},{28,30},{29,31}} | collective-permute-start | bytes 786440 | tf_op jit(solution)/shard_map/ppermute | solution.py:222
  62.5 2.8 %collective-permute-start.11 = (bf16[128,1024]{1,0:T(8,128)(2,1)}, bf16[128,1024]{1,0:T(8,128)(2,1)S(1)}, u32[]{:S(2)}, u32[]{:S(2)}) collective-permute-start(bf16[128,1024]{1,0:T(8,128)(2,1)} %collective-permute-done.4.refs_10_.refs_18_), channel_id=1, source_target_pairs={{4,5},{5,4},{6,7},{7,6},{12,13},{13,12},{14,15},{15,14},{20,21},{2... | collective-permute-start | bytes 786440 | tf_op jit(solution)/shard_map/ppermute | solution.py:218
  65.3 2.3 %collective-permute-done.7.refs_11_.refs_19_ = bf16[128,1024]{1,0:T(8,128)(2,1)} collective-permute-done((bf16[128,1024]{1,0:T(8,128)(2,1)S(1)}, bf16[128,1024]{1,0:T(8,128)(2,1)}, u32[]{:S(2)}, u32[]{:S(2)}) %collective-permute-start.7) | collective-permute-done | bytes 262176 | tf_op jit(solution)/shard_map/ppermute | solution.py:222
  67.6 2.2 %collective-permute-start.13 = (bf16[128,1024]{1,0:T(8,128)(2,1)}, bf16[128,1024]{1,0:T(8,128)(2,1)}, u32[]{:S(2)}, u32[]{:S(2)}) collective-permute-start(bf16[128,1024]{1,0:T(8,128)(2,1)} %collective-permute-done.7.refs_11_.refs_19_), channel_id=1, source_target_pairs={{6,7},{7,6},{14,15},{15,14},{22,23},{23,22},{30,31},{31,30}} | collective-permute-start | bytes 786440 | tf_op jit(solution)/shard_map/ppermute | solution.py:218
  69.8 5.6 %collective-permute-done.10.refs_12_.refs_20_ = bf16[128,1024]{1,0:T(8,128)(2,1)} collective-permute-done((bf16[128,1024]{1,0:T(8,128)(2,1)}, bf16[128,1024]{1,0:T(8,128)(2,1)}, u32[]{:S(2)}, u32[]{:S(2)}) %collective-permute-start.10) | collective-permute-done | bytes 262176 | tf_op jit(solution)/shard_map/ppermute | solution.py:222
  75.4 3.8 %collective-permute-start.12 = (bf16[128,1024]{1,0:T(8,128)(2,1)}, bf16[128,1024]{1,0:T(8,128)(2,1)}, u32[]{:S(2)}, u32[]{:S(2)}) collective-permute-start(bf16[128,1024]{1,0:T(8,128)(2,1)} %collective-permute-done.10.refs_12_.refs_20_), channel_id=1, source_target_pairs={{6,7},{7,6},{14,15},{15,14},{22,23},{23,22},{30,31},{31,30}} | collective-permute-start | bytes 786440 | tf_op jit(solution)/shard_map/ppermute | solution.py:218
  80.1 1.0 copy-done.1
  81.1 10.4 %shard_map.65 = (bf16[128,8192]{1,0:T(8,128)(2,1)}, f32[128,1280]{1,0:T(8,128)S(1)}, s32[1]{0:T(128)}) custom-call(s32[4]{0:T(128)S(1)} %add_add_fusion.1.meta_ref, s32[1,128]{1,0:T(1,128)S(1)} %copy-done, bf16[256,2176]{1,0:T(8,128)(2,1)} %bitcast.16, bf16[128,8192]{1,0:T(8,128)(2,1)} %bitcast.21, bf16[256,2176]{1,0:T(8,128)(2,1)} %bitcast.17, ...), custom_call_target="tpu_custom_call" | custom-call | tf_op jit(solution)/shard_map/pallas_call | solution.py:177
  91.6 0.7 copy-done.11
  92.3 10.7 %shard_map.66 = bf16[128,8192]{1,0:T(8,128)(2,1)} custom-call(s32[4]{0:T(128)S(1)} %add_add_fusion.meta_ref, f32[128,1280]{1,0:T(8,128)S(1)} %get-tuple-element.20.refs_0_, s32[1]{0:T(128)} %get-tuple-element.21.refs_1_, bf16[128,8192]{1,0:T(8,128)(2,1)} %bitcast.22, bf16[256,2176]{1,0:T(8,128)(2,1)} %bitcast.19, ...), custom_call_target="tpu_custom_call", output_to_operand_aliasing={{}: (22, {})} | custom-call | tf_op jit(solution)/shard_map/pallas_call | solution.py:177
  (35 shorter events, 0.4 us)
Async XLA Ops:
  1.9 20.0 %copy-start.2 = (bf16[128,1024]{1,0:T(8,128)(2,1)S(1)}, bf16[128,1024]{1,0:T(8,128)(2,1)}, u32[]{:S(2)}) copy-start(bf16[128,1024]{1,0:T(8,128)(2,1)} %get-tuple-element.17.refs_5_.refs_13_) | copy-start | bytes 786436
  1.9 79.2 %copy-start = (s32[1,128]{1,0:T(1,128)S(1)}, s32[1,128]{1,0:T(1,128)}, u32[]{:S(2)}) copy-start(s32[1,128]{1,0:T(1,128)} %refs_0_.1) | copy-start | bytes 1540
  1.9 8.3 %collective-permute-start.1 = (bf16[128,1024]{1,0:T(8,128)(2,1)}, bf16[128,1024]{1,0:T(8,128)(2,1)S(1)}, u32[]{:S(2)}, u32[]{:S(2)}) collective-permute-start(bf16[128,1024]{1,0:T(8,128)(2,1)} %get-tuple-element.15.refs_5_.refs_13_), channel_id=1, source_target_pairs={{0,1},{1,0},{2,3},{3,2},{4,5},{5,4},{6,7},{7,6},{8,9},{9,8},{10,11... | collective-permute-start | bytes 786440 | tf_op jit(solution)/shard_map/ppermute | solution.py:218
  3.4 9.9 %collective-permute-start = (bf16[128,1024]{1,0:T(8,128)(2,1)}, bf16[128,1024]{1,0:T(8,128)(2,1)S(1)}, u32[]{:S(2)}, u32[]{:S(2)}) collective-permute-start(bf16[128,1024]{1,0:T(8,128)(2,1)} %get-tuple-element.17.refs_5_.refs_13_), channel_id=1, source_target_pairs={{0,2},{1,3},{2,4},{3,5},{4,6},{5,7},{8,10},{9,11},{10,12},{11,13},... | collective-permute-start | bytes 786440 | tf_op jit(solution)/shard_map/ppermute | solution.py:222
  10.2 69.9 %copy-start.3 = (bf16[128,1024]{1,0:T(8,128)(2,1)}, bf16[128,1024]{1,0:T(8,128)(2,1)S(1)}, u32[]{:S(2)}) copy-start(bf16[128,1024]{1,0:T(8,128)(2,1)S(1)} %collective-permute-done.1.refs_6_.refs_14_) | copy-start | bytes 786436
  13.3 66.8 %copy-start.4 = (bf16[128,1024]{1,0:T(8,128)(2,1)}, bf16[128,1024]{1,0:T(8,128)(2,1)S(1)}, u32[]{:S(2)}) copy-start(bf16[128,1024]{1,0:T(8,128)(2,1)S(1)} %collective-permute-done.refs_7_.refs_15_) | copy-start | bytes 786436
  14.4 65.7 %all-to-all-start = ((bf16[32,8,2176]{2,1,0:T(8,128)(2,1)}), bf16[32,8,2176]{2,1,0:T(8,128)(2,1)S(1)}, u32[]{:S(2)}, u32[]{:S(2)}) async-start(bf16[32,8,2176]{2,1,0:T(8,128)(2,1)} %bitcast.7), calls=%async_computation | async-start | bytes 2228224 | tf_op jit(solution)/shard_map/all_to_all | solution.py:243
  19.3 25.4 %collective-permute-start.2 = (bf16[128,1024]{1,0:T(8,128)(2,1)S(1)}, bf16[128,1024]{1,0:T(8,128)(2,1)S(1)}, u32[]{:S(2)}, u32[]{:S(2)}) collective-permute-start(bf16[128,1024]{1,0:T(8,128)(2,1)S(1)} %collective-permute-done.1.refs_6_.refs_14_), channel_id=1, source_target_pairs={{0,2},{1,3},{2,4},{3,5},{4,6},{5,7},{8,10},{9,11},{10,12},{11,13},... | collective-permute-start | bytes 786440 | tf_op jit(solution)/shard_map/ppermute | solution.py:222
  20.6 29.5 %collective-permute-start.3 = (bf16[128,1024]{1,0:T(8,128)(2,1)S(1)}, bf16[128,1024]{1,0:T(8,128)(2,1)S(1)}, u32[]{:S(2)}, u32[]{:S(2)}) collective-permute-start(bf16[128,1024]{1,0:T(8,128)(2,1)S(1)} %collective-permute-done.refs_7_.refs_15_), channel_id=1, source_target_pairs={{2,4},{3,5},{4,6},{5,7},{10,12},{11,13},{12,14},{13,15},{18,20},{1... | collective-permute-start | bytes 786440 | tf_op jit(solution)/shard_map/ppermute | solution.py:222
  21.9 31.5 %collective-permute-start.5 = (bf16[128,1024]{1,0:T(8,128)(2,1)S(1)}, bf16[128,1024]{1,0:T(8,128)(2,1)S(1)}, u32[]{:S(2)}, u32[]{:S(2)}) collective-permute-start(bf16[128,1024]{1,0:T(8,128)(2,1)S(1)} %copy-done.2), channel_id=1, source_target_pairs={{0,1},{2,3},{4,5},{6,7},{8,9},{10,11},{12,13},{14,15},{16,17},{18,... | collective-permute-start | bytes 786440 | tf_op jit(solution)/shard_map/ppermute | solution.py:230
  25.3 28.1 %collective-permute-start.6 = (bf16[128,1024]{1,0:T(8,128)(2,1)S(1)}, bf16[128,1024]{1,0:T(8,128)(2,1)S(1)}, u32[]{:S(2)}, u32[]{:S(2)}) collective-permute-start(bf16[128,1024]{1,0:T(8,128)(2,1)S(1)} %collective-permute-done.refs_7_.refs_15_), channel_id=1, source_target_pairs={{2,3},{3,2},{4,5},{5,4},{6,7},{7,6},{10,11},{11,10},{12,13},{13,12... | collective-permute-start | bytes 786440 | tf_op jit(solution)/shard_map/ppermute | solution.py:218
  44.7 35.4 %copy-start.7 = (bf16[128,1024]{1,0:T(8,128)(2,1)}, bf16[128,1024]{1,0:T(8,128)(2,1)S(1)}, u32[]{:S(2)}) copy-start(bf16[128,1024]{1,0:T(8,128)(2,1)S(1)} %collective-permute-done.2.refs_8_.refs_16_) | copy-start | bytes 786436
  44.7 14.4 %collective-permute-start.4 = (bf16[128,1024]{1,0:T(8,128)(2,1)S(1)}, bf16[128,1024]{1,0:T(8,128)(2,1)}, u32[]{:S(2)}, u32[]{:S(2)}) collective-permute-start(bf16[128,1024]{1,0:T(8,128)(2,1)S(1)} %collective-permute-done.2.refs_8_.refs_16_), channel_id=1, source_target_pairs={{2,4},{3,5},{4,6},{5,7},{10,12},{11,13},{12,14},{13,15},{18,20},{1... | collective-permute-start | bytes 786440 | tf_op jit(solution)/shard_map/ppermute | solution.py:222
  46.0 13.1 %collective-permute-start.8 = (bf16[128,1024]{1,0:T(8,128)(2,1)S(1)}, bf16[128,1024]{1,0:T(8,128)(2,1)S(1)}, u32[]{:S(2)}, u32[]{:S(2)}) collective-permute-start(bf16[128,1024]{1,0:T(8,128)(2,1)S(1)} %collective-permute-done.2.refs_8_.refs_16_), channel_id=1, source_target_pairs={{2,3},{3,2},{4,5},{5,4},{6,7},{7,6},{10,11},{11,10},{12,13},{13,12... | collective-permute-start | bytes 786440 | tf_op jit(solution)/shard_map/ppermute | solution.py:218
  50.0 30.1 %copy-start.9 = (bf16[128,1024]{1,0:T(8,128)(2,1)}, bf16[128,1024]{1,0:T(8,128)(2,1)S(1)}, u32[]{:S(2)}) copy-start(bf16[128,1024]{1,0:T(8,128)(2,1)S(1)} %collective-permute-done.3.refs_9_.refs_17_) | copy-start | bytes 786436
  50.0 11.2 %collective-permute-start.9 = (bf16[128,1024]{1,0:T(8,128)(2,1)S(1)}, bf16[128,1024]{1,0:T(8,128)(2,1)S(1)}, u32[]{:S(2)}, u32[]{:S(2)}) collective-permute-start(bf16[128,1024]{1,0:T(8,128)(2,1)S(1)} %collective-permute-done.3.refs_9_.refs_17_), channel_id=1, source_target_pairs={{4,5},{5,4},{6,7},{7,6},{12,13},{13,12},{14,15},{15,14},{20,21},{2... | collective-permute-start | bytes 786440 | tf_op jit(solution)/shard_map/ppermute | solution.py:218
  53.4 38.2 %copy-start.5 = (bf16[128,1024]{1,0:T(8,128)(2,1)}, bf16[128,1024]{1,0:T(8,128)(2,1)S(1)}, u32[]{:S(2)}) copy-start(bf16[128,1024]{1,0:T(8,128)(2,1)S(1)} %collective-permute-done.5.refs_6_.refs_14_) | copy-start | bytes 786436
  53.4 38.2 %copy-start.6 = (bf16[128,1024]{1,0:T(8,128)(2,1)}, bf16[128,1024]{1,0:T(8,128)(2,1)S(1)}, u32[]{:S(2)}) copy-start(bf16[128,1024]{1,0:T(8,128)(2,1)S(1)} %collective-permute-done.6.refs_8_.refs_16_) | copy-start | bytes 786436
  53.4 14.2 %collective-permute-start.7 = (bf16[128,1024]{1,0:T(8,128)(2,1)S(1)}, bf16[128,1024]{1,0:T(8,128)(2,1)}, u32[]{:S(2)}, u32[]{:S(2)}) collective-permute-start(bf16[128,1024]{1,0:T(8,128)(2,1)S(1)} %collective-permute-done.3.refs_9_.refs_17_), channel_id=1, source_target_pairs={{4,6},{5,7},{12,14},{13,15},{20,22},{21,23},{28,30},{29,31}} | collective-permute-start | bytes 786440 | tf_op jit(solution)/shard_map/ppermute | solution.py:222
  59.2 32.4 %copy-start.8 = (bf16[128,1024]{1,0:T(8,128)(2,1)}, bf16[128,1024]{1,0:T(8,128)(2,1)S(1)}, u32[]{:S(2)}) copy-start(bf16[128,1024]{1,0:T(8,128)(2,1)S(1)} %collective-permute-done.8.refs_7_.refs_15_) | copy-start | bytes 786436
  61.2 30.4 %copy-start.10 = (bf16[128,1024]{1,0:T(8,128)(2,1)}, bf16[128,1024]{1,0:T(8,128)(2,1)S(1)}, u32[]{:S(2)}) copy-start(bf16[128,1024]{1,0:T(8,128)(2,1)S(1)} %collective-permute-done.9.refs_10_.refs_18_) | copy-start | bytes 786436
  61.2 14.2 %collective-permute-start.10 = (bf16[128,1024]{1,0:T(8,128)(2,1)}, bf16[128,1024]{1,0:T(8,128)(2,1)}, u32[]{:S(2)}, u32[]{:S(2)}) collective-permute-start(bf16[128,1024]{1,0:T(8,128)(2,1)} %collective-permute-done.4.refs_10_.refs_18_), channel_id=1, source_target_pairs={{4,6},{5,7},{12,14},{13,15},{20,22},{21,23},{28,30},{29,31}} | collective-permute-start | bytes 786440 | tf_op jit(solution)/shard_map/ppermute | solution.py:222
  62.5 29.0 %collective-permute-start.11 = (bf16[128,1024]{1,0:T(8,128)(2,1)}, bf16[128,1024]{1,0:T(8,128)(2,1)S(1)}, u32[]{:S(2)}, u32[]{:S(2)}) collective-permute-start(bf16[128,1024]{1,0:T(8,128)(2,1)} %collective-permute-done.4.refs_10_.refs_18_), channel_id=1, source_target_pairs={{4,5},{5,4},{6,7},{7,6},{12,13},{13,12},{14,15},{15,14},{20,21},{2... | collective-permute-start | bytes 786440 | tf_op jit(solution)/shard_map/ppermute | solution.py:218
  67.6 23.9 %collective-permute-start.13 = (bf16[128,1024]{1,0:T(8,128)(2,1)}, bf16[128,1024]{1,0:T(8,128)(2,1)}, u32[]{:S(2)}, u32[]{:S(2)}) collective-permute-start(bf16[128,1024]{1,0:T(8,128)(2,1)} %collective-permute-done.7.refs_11_.refs_19_), channel_id=1, source_target_pairs={{6,7},{7,6},{14,15},{15,14},{22,23},{23,22},{30,31},{31,30}} | collective-permute-start | bytes 786440 | tf_op jit(solution)/shard_map/ppermute | solution.py:218
  75.4 16.2 %collective-permute-start.12 = (bf16[128,1024]{1,0:T(8,128)(2,1)}, bf16[128,1024]{1,0:T(8,128)(2,1)}, u32[]{:S(2)}, u32[]{:S(2)}) collective-permute-start(bf16[128,1024]{1,0:T(8,128)(2,1)} %collective-permute-done.10.refs_12_.refs_20_), channel_id=1, source_target_pairs={{6,7},{7,6},{14,15},{15,14},{22,23},{23,22},{30,31},{31,30}} | collective-permute-start | bytes 786440 | tf_op jit(solution)/shard_map/ppermute | solution.py:218
  80.1 1.0 copy-start.1
  91.6 0.7 copy-start.11

commit v8 on v7

--- a/solution.py
+++ b/solution.py
@@ -150,12 +150,12 @@
     ]
     args = [meta, *([segments, prefix] if fresh else before[1:])]
     args += [queries, prefix, prefix, *pieces, *pieces]
-    ints = pl.BlockSpec((prefix_keys, rows), lambda i, m: (0, 2 * KVH))
+    ints = pl.BlockSpec((prefix_keys, rows), lambda i, m: (0, 2 * heads))
     in_specs = [pl.BlockSpec((1, rows), lambda i, m: (0, 0)), ints] if fresh else [whole, scalar]
     in_specs += [
         wide,
-        pl.BlockSpec((prefix_keys, HD), lambda i, m: (0, m[2] + i)),
-        pl.BlockSpec((prefix_keys, HD), lambda i, m: (0, KVH + m[2] + i)),
+        pl.BlockSpec((prefix_keys, HD), lambda i, m: (0, i)),
+        pl.BlockSpec((prefix_keys, HD), lambda i, m: (0, heads + i)),
         *[pl.BlockSpec((rows, HD), lambda i, m: (0, i))] * len(pieces),
         *[pl.BlockSpec((rows, HD), lambda i, m: (0, heads + i))] * len(pieces),
     ]
@@ -208,12 +208,21 @@
     own_tiles = jnp.sum(
         jnp.where(pick[:, :, None, None], prefix_kv[None], 0).astype(jnp.float32), axis=1
     )
+    own_tiles = own_tiles.astype(prefix_kv.dtype)
+    half = columns // 4
     row = jnp.arange(tile, dtype=jnp.int32)[:, None]
     extra = jnp.where(row == 0, resp_segments[0], place.reshape(groups, 1, 1))
-    out_tiles = jnp.concatenate([own_tiles, extra.astype(jnp.float32)], axis=-1)
+    extra = extra.astype(prefix_kv.dtype)
+    out_tiles = [
+        jnp.concatenate(
+            [own_tiles[..., at : at + half], own_tiles[..., at + 2 * half :][..., :half], extra],
+            axis=-1,
+        )
+        for at in (0, half)
+    ]
     out_tiles = jnp.broadcast_to(
-        out_tiles.astype(prefix_kv.dtype)[:, None], (groups, count, tile, columns + rows)
-    ).reshape(groups * count, tile, columns + rows)
+        jnp.stack(out_tiles, axis=1)[:, None], (groups, count // 2, 2, tile, 2 * half + rows)
+    ).reshape(groups * count, tile, 2 * half + rows)
     def swap(value, first):
         return lax.ppermute(value, "resp", [(r, r ^ 1) for r in range(2 * first, count)])
 
@@ -231,19 +240,18 @@
     straight, crossed = [mine, partner], [theirs, upper]
     for step in range(1, steps + 1):
         one, two = straight[-2:]
-        if step > 2:
-            one = after(one, upper, crossed[-3])
-            two = after(two, crossed[-4], crossed[-1])
         one = climb(one, step)
         if step == 1:
             out_tiles = after(out_tiles, one, two)
+            prefix = lax.all_to_all(
+                out_tiles, ("prompt", "resp"), split_axis=0, concat_axis=0, tiled=True
+            ).reshape(-1, 2 * half + rows)
+            prefix_crossed = swap(prefix, 0)
+        if step > 2:
+            two = after(two, upper, prefix_crossed, *crossed[-4:-2], crossed[-1])
         two = climb(two, step)
         straight += [one, two]
         crossed += [swap(two, step), swap(one, step)]
-    came = lax.all_to_all(
-        out_tiles, ("prompt", "resp"), split_axis=0, concat_axis=0, tiled=True
-    )
-    prefix = came.reshape(-1, columns + rows)
 
     def meta(first):
         return jnp.stack([group, block, first * (KVH // 2), prompt_lengths[0]])
@@ -251,7 +259,7 @@
     done = attend(
         meta(side), queries[0], straight, prefix, tile, count, segments=resp_segments
     )
-    done = attend(meta(1 - side), queries[0], crossed, prefix, tile, count, before=done)
+    done = attend(meta(1 - side), queries[0], crossed, prefix_crossed, tile, count, before=done)
     return done[0][None]
 
 

time: 102 us -> 104 us (1.020)
  the two profiles are of different devices: /device:TPU:24 before, /device:TPU:26 now
where the time goes in v8:
time: 104 us; the launch traced here: 103 us
  starting transfers between devices  34.1 us (33%)
  waiting for transfers between devices  22.8 us (22%)
  blocking collectives  21.2 us (20%)
  Pallas kernels  20.6 us (20%)
  other arithmetic  2.07 us (2%)
    ppermute x8, starting transfers between devices, swap(): lax.ppermute(value, 'resp', [(r, r ^ 1) for r in range(2 * first, count)])  22.5 us
    all_to_all x1, blocking collectives, on_device(): lax.all_to_all(out_tiles, ('prompt', 'resp'), split_axis=0, concat_axis=0...  21.2 us
    pallas_call x2, Pallas kernels, attend(): pl.pallas_call(functools.partial(attend_kernel, pairs, tile, count, fresh...  18.8 us
    ppermute x8, waiting for transfers between devices, swap(): lax.ppermute(value, 'resp', [(r, r ^ 1) for r in range(2 * first, count)])  10.4 us
    ppermute x6, waiting for transfers between devices, climb(): return lax.ppermute(value, 'resp', pairs)  9.97 us
    ppermute x6, starting transfers between devices, climb(): return lax.ppermute(value, 'resp', pairs)  7.83 us
    ppermute x1, starting transfers between devices, on_device(): upper = lax.ppermute(after(mine, partner), 'resp', upper)  3.78 us
    ppermute x1, waiting for transfers between devices, on_device(): upper = lax.ppermute(after(mine, partner), 'resp', upper)  2.4 us
  transfers between devices with their start and end apart: 15, of which 8 were waited for; matrix products, arithmetic and copies ran while one was open for 3% of the time, Pallas kernels for 9%

profile of v8, /device:TPU:26, one launch (start us, length us, event | category | flops | bytes accessed | tf_op | source)
XLA Modules:
  0.0 102.6 jit_solution(11949669425580685537)
XLA Ops:
  0.0 1.9 %shard_map.64 = (bf16[128,1024]{1,0:T(8,128)(2,1)}, bf16[128,1024]{1,0:T(8,128)(2,1)}) custom-call(s32[1]{0:T(128)} %bitcast.10.meta_ref, bf16[128,2048]{1,0:T(8,128)(2,1)} %bitcast.27, bf16[128,2048]{1,0:T(8,128)(2,1)} %bitcast.28), custom_call_target="tpu_custom_call" | custom-call | tf_op jit(solution)/shard_map/pallas_call | solution.py:28
  1.9 1.4 %collective-permute-start = (bf16[128,1024]{1,0:T(8,128)(2,1)}, bf16[128,1024]{1,0:T(8,128)(2,1)S(1)}, u32[]{:S(2)}, u32[]{:S(2)}) collective-permute-start(bf16[128,1024]{1,0:T(8,128)(2,1)} %get-tuple-element.16.refs_5_.refs_13_), channel_id=1, source_target_pairs={{0,2},{1,3},{2,4},{3,5},{4,6},{5,7},{8,10},{9,11},{10,12},{11,13},... | collective-permute-start | bytes 786440 | tf_op jit(solution)/shard_map/ppermute | solution.py:231
  3.3 1.6 %collective-permute-start.1 = (bf16[128,1024]{1,0:T(8,128)(2,1)}, bf16[128,1024]{1,0:T(8,128)(2,1)S(1)}, u32[]{:S(2)}, u32[]{:S(2)}) collective-permute-start(bf16[128,1024]{1,0:T(8,128)(2,1)} %get-tuple-element.14.refs_5_.refs_13_), channel_id=1, source_target_pairs={{0,1},{1,0},{2,3},{3,2},{4,5},{5,4},{6,7},{7,6},{8,9},{9,8},{10,11... | collective-permute-start | bytes 786440 | tf_op jit(solution)/shard_map/ppermute | solution.py:227
  4.9 0.8 slice_bitcast_fusion.1
  5.6 1.0 %select_reduce_fusion = bf16[4,8,2048]{2,1,0:T(8,128)(2,1)S(1)} fusion(pred[4,4]{1,0:T(4,128)(4,1)S(1)} %iota_compare_fusion, bf16[4,8,2048]{2,1,0:T(8,128)(2,1)} %param.9), kind=kLoop, calls=%fused_computation | loop fusion | flops 458752 | bytes 262160 | tf_op jit(solution)/shard_map/reduce_sum | solution.py:208
  6.7 0.1 select_reduce_fusion.1
  6.8 0.7 select_convert_fusion
  7.6 4.5 %collective-permute-done.refs_7_.refs_15_ = bf16[128,1024]{1,0:T(8,128)(2,1)S(1)} collective-permute-done((bf16[128,1024]{1,0:T(8,128)(2,1)}, bf16[128,1024]{1,0:T(8,128)(2,1)S(1)}, u32[]{:S(2)}, u32[]{:S(2)}) %collective-permute-start) | collective-permute-done | bytes 262176 | tf_op jit(solution)/shard_map/ppermute | solution.py:231
  12.2 21.2 %all_to_all.5 = bf16[32,8,1152]{2,1,0:T(8,128)(2,1)S(1)} all-to-all(bf16[32,8,1152]{2,1,0:T(8,128)(2,1)S(1)} %bitcast.26), channel_id=1, replica_groups=mesh['prompt'=4,'resp'=8] {'prompt','resp'}, dimensions={0} | all-to-all | bytes 1179648 | tf_op jit(solution)/shard_map/all_to_all | solution.py:246
  33.3 0.2 collective-permute-start.7
  33.5 1.3 %collective-permute-start.3 = (bf16[128,1024]{1,0:T(8,128)(2,1)S(1)}, bf16[128,1024]{1,0:T(8,128)(2,1)S(1)}, u32[]{:S(2)}, u32[]{:S(2)}) collective-permute-start(bf16[128,1024]{1,0:T(8,128)(2,1)S(1)} %collective-permute-done.refs_7_.refs_15_), channel_id=1, source_target_pairs={{2,4},{3,5},{4,6},{5,7},{10,12},{11,13},{12,14},{13,15},{18,20},{1... | collective-permute-start | bytes 786440 | tf_op jit(solution)/shard_map/ppermute | solution.py:231
  34.8 1.3 %collective-permute-start.2 = (bf16[128,1024]{1,0:T(8,128)(2,1)S(1)}, bf16[128,1024]{1,0:T(8,128)(2,1)S(1)}, u32[]{:S(2)}, u32[]{:S(2)}) collective-permute-start(bf16[128,1024]{1,0:T(8,128)(2,1)S(1)} %collective-permute-done.1.refs_6_.refs_14_), channel_id=1, source_target_pairs={{0,2},{1,3},{2,4},{3,5},{4,6},{5,7},{8,10},{9,11},{10,12},{11,13},... | collective-permute-start | bytes 786440 | tf_op jit(solution)/shard_map/ppermute | solution.py:231
  36.1 3.8 %collective-permute-start.6 = (bf16[128,1024]{1,0:T(8,128)(2,1)S(1)}, bf16[128,1024]{1,0:T(8,128)(2,1)S(1)}, u32[]{:S(2)}, u32[]{:S(2)}) collective-permute-start(bf16[128,1024]{1,0:T(8,128)(2,1)S(1)} %copy-done.3), channel_id=1, source_target_pairs={{0,1},{2,3},{4,5},{6,7},{8,9},{10,11},{12,13},{14,15},{16,17},{18,... | collective-permute-start | bytes 786440 | tf_op jit(solution)/shard_map/ppermute | solution.py:239
  39.9 1.9 %collective-permute-start.9 = (bf16[128,1024]{1,0:T(8,128)(2,1)S(1)}, bf16[128,1024]{1,0:T(8,128)(2,1)S(1)}, u32[]{:S(2)}, u32[]{:S(2)}) collective-permute-start(bf16[128,1024]{1,0:T(8,128)(2,1)S(1)} %collective-permute-done.refs_7_.refs_15_), channel_id=1, source_target_pairs={{2,3},{3,2},{4,5},{5,4},{6,7},{7,6},{10,11},{11,10},{12,13},{13,12... | collective-permute-start | bytes 786440 | tf_op jit(solution)/shard_map/ppermute | solution.py:227
  41.8 2.8 %collective-permute-done.3.refs_9_.refs_17_ = bf16[128,1024]{1,0:T(8,128)(2,1)S(1)} collective-permute-done((bf16[128,1024]{1,0:T(8,128)(2,1)S(1)}, bf16[128,1024]{1,0:T(8,128)(2,1)S(1)}, u32[]{:S(2)}, u32[]{:S(2)}) %collective-permute-start.3) | collective-permute-done | bytes 262176 | tf_op jit(solution)/shard_map/ppermute | solution.py:231
  44.6 3.8 %collective-permute-start.10 = (bf16[128,1024]{1,0:T(8,128)(2,1)S(1)}, bf16[128,1024]{1,0:T(8,128)(2,1)S(1)}, u32[]{:S(2)}, u32[]{:S(2)}) collective-permute-start(bf16[128,1024]{1,0:T(8,128)(2,1)S(1)} %collective-permute-done.3.refs_9_.refs_17_), channel_id=1, source_target_pairs={{4,5},{5,4},{6,7},{7,6},{12,13},{13,12},{14,15},{15,14},{20,21},{2... | collective-permute-start | bytes 786440 | tf_op jit(solution)/shard_map/ppermute | solution.py:227
  48.4 0.8 collective-permute-done.2.refs_8_.refs_16_
  49.1 1.3 %collective-permute-start.4 = (bf16[128,1024]{1,0:T(8,128)(2,1)S(1)}, bf16[128,1024]{1,0:T(8,128)(2,1)S(1)}, u32[]{:S(2)}, u32[]{:S(2)}) collective-permute-start(bf16[128,1024]{1,0:T(8,128)(2,1)S(1)} %collective-permute-done.2.refs_8_.refs_16_), channel_id=1, source_target_pairs={{2,4},{3,5},{4,6},{5,7},{10,12},{11,13},{12,14},{13,15},{18,20},{1... | collective-permute-start | bytes 786440 | tf_op jit(solution)/shard_map/ppermute | solution.py:231
  50.4 2.4 %collective-permute-done.6.refs_6_.refs_14_ = bf16[128,1024]{1,0:T(8,128)(2,1)S(1)} collective-permute-done((bf16[128,1024]{1,0:T(8,128)(2,1)S(1)}, bf16[128,1024]{1,0:T(8,128)(2,1)S(1)}, u32[]{:S(2)}, u32[]{:S(2)}) %collective-permute-start.6) | collective-permute-done | bytes 262176 | tf_op jit(solution)/shard_map/ppermute | solution.py:239
  52.8 4.4 %collective-permute-start.8 = (bf16[128,1024]{1,0:T(8,128)(2,1)S(1)}, bf16[128,1024]{1,0:T(8,128)(2,1)S(1)}, u32[]{:S(2)}, u32[]{:S(2)}) collective-permute-start(bf16[128,1024]{1,0:T(8,128)(2,1)S(1)} %collective-permute-done.2.refs_8_.refs_16_), channel_id=1, source_target_pairs={{2,3},{3,2},{4,5},{5,4},{6,7},{7,6},{10,11},{11,10},{12,13},{13,12... | collective-permute-start | bytes 786440 | tf_op jit(solution)/shard_map/ppermute | solution.py:227
  57.2 1.2 %collective-permute-done.9.refs_8_.refs_16_ = bf16[128,1024]{1,0:T(8,128)(2,1)S(1)} collective-permute-done((bf16[128,1024]{1,0:T(8,128)(2,1)S(1)}, bf16[128,1024]{1,0:T(8,128)(2,1)S(1)}, u32[]{:S(2)}, u32[]{:S(2)}) %collective-permute-start.9) | collective-permute-done | bytes 262176 | tf_op jit(solution)/shard_map/ppermute | solution.py:227
  58.4 1.3 %collective-permute-start.5 = (bf16[128,1024]{1,0:T(8,128)(2,1)S(1)}, bf16[128,1024]{1,0:T(8,128)(2,1)}, u32[]{:S(2)}, u32[]{:S(2)}) collective-permute-start(bf16[128,1024]{1,0:T(8,128)(2,1)S(1)} %collective-permute-done.3.refs_9_.refs_17_), channel_id=1, source_target_pairs={{4,6},{5,7},{12,14},{13,15},{20,22},{21,23},{28,30},{29,31}} | collective-permute-start | bytes 786440 | tf_op jit(solution)/shard_map/ppermute | solution.py:231
  59.7 4.3 %collective-permute-done.10.refs_10_.refs_18_ = bf16[128,1024]{1,0:T(8,128)(2,1)S(1)} collective-permute-done((bf16[128,1024]{1,0:T(8,128)(2,1)S(1)}, bf16[128,1024]{1,0:T(8,128)(2,1)S(1)}, u32[]{:S(2)}, u32[]{:S(2)}) %collective-permute-start.10) | collective-permute-done | bytes 262176 | tf_op jit(solution)/shard_map/ppermute | solution.py:227
  64.1 4.9 %collective-permute-done.8.refs_7_.refs_15_ = bf16[128,1024]{1,0:T(8,128)(2,1)S(1)} collective-permute-done((bf16[128,1024]{1,0:T(8,128)(2,1)S(1)}, bf16[128,1024]{1,0:T(8,128)(2,1)S(1)}, u32[]{:S(2)}, u32[]{:S(2)}) %collective-permute-start.8) | collective-permute-done | bytes 262176 | tf_op jit(solution)/shard_map/ppermute | solution.py:227
  68.9 1.3 %collective-permute-start.11 = (bf16[128,1024]{1,0:T(8,128)(2,1)S(1)}, bf16[128,1024]{1,0:T(8,128)(2,1)}, u32[]{:S(2)}, u32[]{:S(2)}) collective-permute-start(bf16[128,1024]{1,0:T(8,128)(2,1)S(1)} %collective-permute-done.4.refs_10_.refs_18_), channel_id=1, source_target_pairs={{4,6},{5,7},{12,14},{13,15},{20,22},{21,23},{28,30},{29,31}} | collective-permute-start | bytes 786440 | tf_op jit(solution)/shard_map/ppermute | solution.py:231
  70.2 4.4 %collective-permute-start.12 = (bf16[128,1024]{1,0:T(8,128)(2,1)S(1)}, bf16[128,1024]{1,0:T(8,128)(2,1)}, u32[]{:S(2)}, u32[]{:S(2)}) collective-permute-start(bf16[128,1024]{1,0:T(8,128)(2,1)S(1)} %collective-permute-done.4.refs_10_.refs_18_), channel_id=1, source_target_pairs={{4,5},{5,4},{6,7},{7,6},{12,13},{13,12},{14,15},{15,14},{20,21},{2... | collective-permute-start | bytes 786440 | tf_op jit(solution)/shard_map/ppermute | solution.py:227
  74.6 1.9 %collective-permute-start.14 = (bf16[128,1024]{1,0:T(8,128)(2,1)}, bf16[128,1024]{1,0:T(8,128)(2,1)}, u32[]{:S(2)}, u32[]{:S(2)}) collective-permute-start(bf16[128,1024]{1,0:T(8,128)(2,1)} %collective-permute-done.5.refs_11_.refs_19_), channel_id=1, source_target_pairs={{6,7},{7,6},{14,15},{15,14},{22,23},{23,22},{30,31},{31,30}} | collective-permute-start | bytes 786440 | tf_op jit(solution)/shard_map/ppermute | solution.py:227
  76.6 1.9 %collective-permute-done.11.refs_12_.refs_20_ = bf16[128,1024]{1,0:T(8,128)(2,1)} collective-permute-done((bf16[128,1024]{1,0:T(8,128)(2,1)S(1)}, bf16[128,1024]{1,0:T(8,128)(2,1)}, u32[]{:S(2)}, u32[]{:S(2)}) %collective-permute-start.11) | collective-permute-done | bytes 262176 | tf_op jit(solution)/shard_map/ppermute | solution.py:231
  78.5 4.4 %collective-permute-start.13 = (bf16[128,1024]{1,0:T(8,128)(2,1)}, bf16[128,1024]{1,0:T(8,128)(2,1)}, u32[]{:S(2)}, u32[]{:S(2)}) collective-permute-start(bf16[128,1024]{1,0:T(8,128)(2,1)} %collective-permute-done.11.refs_12_.refs_20_), channel_id=1, source_target_pairs={{6,7},{7,6},{14,15},{15,14},{22,23},{23,22},{30,31},{31,30}} | collective-permute-start | bytes 786440 | tf_op jit(solution)/shard_map/ppermute | solution.py:227
  83.5 0.1 add_add_fusion.1.meta_ref
  83.7 9.3 %shard_map.65 = (bf16[128,8192]{1,0:T(8,128)(2,1)}, f32[128,1280]{1,0:T(8,128)S(1)}, s32[1]{0:T(128)}) custom-call(s32[4]{0:T(128)S(1)} %add_add_fusion.1.meta_ref, s32[1,128]{1,0:T(1,128)S(1)} %copy-done, bf16[256,1152]{1,0:T(8,128)(2,1)} %bitcast.21, bf16[128,8192]{1,0:T(8,128)(2,1)} %bitcast.24, bf16[256,1152]{1,0:T(8,128)(2,1)} %bitcast.22, ...), custom_call_target="tpu_custom_call" | custom-call | tf_op jit(solution)/shard_map/pallas_call | solution.py:177
  93.1 9.5 %shard_map.66 = bf16[128,8192]{1,0:T(8,128)(2,1)} custom-call(s32[4]{0:T(128)S(1)} %add_add_fusion.meta_ref, f32[128,1280]{1,0:T(8,128)S(1)} %get-tuple-element.18.refs_0_, s32[1]{0:T(128)} %get-tuple-element.19.refs_1_, bf16[128,8192]{1,0:T(8,128)(2,1)} %bitcast.25, bf16[256,1152]{1,0:T(8,128)(2,1)} %copy-done.2, ...), custom_call_target="tpu_custom_call", output_to_operand_aliasing={{}: (22, {})} | custom-call | tf_op jit(solution)/shard_map/pallas_call | solution.py:177
  (41 shorter events, 0.3 us)
Async XLA Ops:
  0.0 83.7 %copy-start = (s32[1,128]{1,0:T(1,128)S(1)}, s32[1,128]{1,0:T(1,128)}, u32[]{:S(2)}) copy-start(s32[1,128]{1,0:T(1,128)} %refs_0_.1) | copy-start | bytes 1540
  1.9 34.2 %copy-start.3 = (bf16[128,1024]{1,0:T(8,128)(2,1)S(1)}, bf16[128,1024]{1,0:T(8,128)(2,1)}, u32[]{:S(2)}) copy-start(bf16[128,1024]{1,0:T(8,128)(2,1)} %get-tuple-element.16.refs_5_.refs_13_) | copy-start | bytes 786436
  1.9 10.3 %collective-permute-start = (bf16[128,1024]{1,0:T(8,128)(2,1)}, bf16[128,1024]{1,0:T(8,128)(2,1)S(1)}, u32[]{:S(2)}, u32[]{:S(2)}) collective-permute-start(bf16[128,1024]{1,0:T(8,128)(2,1)} %get-tuple-element.16.refs_5_.refs_13_), channel_id=1, source_target_pairs={{0,2},{1,3},{2,4},{3,5},{4,6},{5,7},{8,10},{9,11},{10,12},{11,13},... | collective-permute-start | bytes 786440 | tf_op jit(solution)/shard_map/ppermute | solution.py:231
  3.3 8.9 %collective-permute-start.1 = (bf16[128,1024]{1,0:T(8,128)(2,1)}, bf16[128,1024]{1,0:T(8,128)(2,1)S(1)}, u32[]{:S(2)}, u32[]{:S(2)}) collective-permute-start(bf16[128,1024]{1,0:T(8,128)(2,1)} %get-tuple-element.14.refs_5_.refs_13_), channel_id=1, source_target_pairs={{0,1},{1,0},{2,3},{3,2},{4,5},{5,4},{6,7},{7,6},{8,9},{9,8},{10,11... | collective-permute-start | bytes 786440 | tf_op jit(solution)/shard_map/ppermute | solution.py:227
  12.1 71.6 %copy-start.4 = (bf16[128,1024]{1,0:T(8,128)(2,1)}, bf16[128,1024]{1,0:T(8,128)(2,1)S(1)}, u32[]{:S(2)}) copy-start(bf16[128,1024]{1,0:T(8,128)(2,1)S(1)} %collective-permute-done.refs_7_.refs_15_) | copy-start | bytes 786436
  12.1 71.5 %copy-start.5 = (bf16[128,1024]{1,0:T(8,128)(2,1)}, bf16[128,1024]{1,0:T(8,128)(2,1)S(1)}, u32[]{:S(2)}) copy-start(bf16[128,1024]{1,0:T(8,128)(2,1)S(1)} %collective-permute-done.1.refs_6_.refs_14_) | copy-start | bytes 786436
  33.3 50.3 %copy-start.1 = (bf16[32,8,1152]{2,1,0:T(8,128)(2,1)}, bf16[32,8,1152]{2,1,0:T(8,128)(2,1)S(1)}, u32[]{:S(2)}) copy-start(bf16[32,8,1152]{2,1,0:T(8,128)(2,1)S(1)} %all_to_all.5) | copy-start | bytes 1769476
  33.3 35.6 %collective-permute-start.7 = (bf16[256,1152]{1,0:T(8,128)(2,1)S(1)}, bf16[256,1152]{1,0:T(8,128)(2,1)S(1)}, u32[]{:S(2)}, u32[]{:S(2)}) collective-permute-start(bf16[256,1152]{1,0:T(8,128)(2,1)S(1)} %bitcast.20), channel_id=1, source_target_pairs={{0,1},{1,0},{2,3},{3,2},{4,5},{5,4},{6,7},{7,6},{8,9},{9,8},{10,11... | collective-permute-start | bytes 1769480 | tf_op jit(solution)/shard_map/ppermute | solution.py:227
  33.5 11.1 %collective-permute-start.3 = (bf16[128,1024]{1,0:T(8,128)(2,1)S(1)}, bf16[128,1024]{1,0:T(8,128)(2,1)S(1)}, u32[]{:S(2)}, u32[]{:S(2)}) collective-permute-start(bf16[128,1024]{1,0:T(8,128)(2,1)S(1)} %collective-permute-done.refs_7_.refs_15_), channel_id=1, source_target_pairs={{2,4},{3,5},{4,6},{5,7},{10,12},{11,13},{12,14},{13,15},{18,20},{1... | collective-permute-start | bytes 786440 | tf_op jit(solution)/shard_map/ppermute | solution.py:231
  34.8 14.3 %collective-permute-start.2 = (bf16[128,1024]{1,0:T(8,128)(2,1)S(1)}, bf16[128,1024]{1,0:T(8,128)(2,1)S(1)}, u32[]{:S(2)}, u32[]{:S(2)}) collective-permute-start(bf16[128,1024]{1,0:T(8,128)(2,1)S(1)} %collective-permute-done.1.refs_6_.refs_14_), channel_id=1, source_target_pairs={{0,2},{1,3},{2,4},{3,5},{4,6},{5,7},{8,10},{9,11},{10,12},{11,13},... | collective-permute-start | bytes 786440 | tf_op jit(solution)/shard_map/ppermute | solution.py:231
  36.1 16.7 %collective-permute-start.6 = (bf16[128,1024]{1,0:T(8,128)(2,1)S(1)}, bf16[128,1024]{1,0:T(8,128)(2,1)S(1)}, u32[]{:S(2)}, u32[]{:S(2)}) collective-permute-start(bf16[128,1024]{1,0:T(8,128)(2,1)S(1)} %copy-done.3), channel_id=1, source_target_pairs={{0,1},{2,3},{4,5},{6,7},{8,9},{10,11},{12,13},{14,15},{16,17},{18,... | collective-permute-start | bytes 786440 | tf_op jit(solution)/shard_map/ppermute | solution.py:239
  39.9 18.5 %collective-permute-start.9 = (bf16[128,1024]{1,0:T(8,128)(2,1)S(1)}, bf16[128,1024]{1,0:T(8,128)(2,1)S(1)}, u32[]{:S(2)}, u32[]{:S(2)}) collective-permute-start(bf16[128,1024]{1,0:T(8,128)(2,1)S(1)} %collective-permute-done.refs_7_.refs_15_), channel_id=1, source_target_pairs={{2,3},{3,2},{4,5},{5,4},{6,7},{7,6},{10,11},{11,10},{12,13},{13,12... | collective-permute-start | bytes 786440 | tf_op jit(solution)/shard_map/ppermute | solution.py:227
  44.6 39.1 %copy-start.9 = (bf16[128,1024]{1,0:T(8,128)(2,1)}, bf16[128,1024]{1,0:T(8,128)(2,1)S(1)}, u32[]{:S(2)}) copy-start(bf16[128,1024]{1,0:T(8,128)(2,1)S(1)} %collective-permute-done.3.refs_9_.refs_17_) | copy-start | bytes 786436
  44.6 19.5 %collective-permute-start.10 = (bf16[128,1024]{1,0:T(8,128)(2,1)S(1)}, bf16[128,1024]{1,0:T(8,128)(2,1)S(1)}, u32[]{:S(2)}, u32[]{:S(2)}) collective-permute-start(bf16[128,1024]{1,0:T(8,128)(2,1)S(1)} %collective-permute-done.3.refs_9_.refs_17_), channel_id=1, source_target_pairs={{4,5},{5,4},{6,7},{7,6},{12,13},{13,12},{14,15},{15,14},{20,21},{2... | collective-permute-start | bytes 786440 | tf_op jit(solution)/shard_map/ppermute | solution.py:227
  49.1 34.6 %copy-start.10 = (bf16[128,1024]{1,0:T(8,128)(2,1)}, bf16[128,1024]{1,0:T(8,128)(2,1)S(1)}, u32[]{:S(2)}) copy-start(bf16[128,1024]{1,0:T(8,128)(2,1)S(1)} %collective-permute-done.2.refs_8_.refs_16_) | copy-start | bytes 786436
  49.1 14.9 %collective-permute-start.4 = (bf16[128,1024]{1,0:T(8,128)(2,1)S(1)}, bf16[128,1024]{1,0:T(8,128)(2,1)S(1)}, u32[]{:S(2)}, u32[]{:S(2)}) collective-permute-start(bf16[128,1024]{1,0:T(8,128)(2,1)S(1)} %collective-permute-done.2.refs_8_.refs_16_), channel_id=1, source_target_pairs={{2,4},{3,5},{4,6},{5,7},{10,12},{11,13},{12,14},{13,15},{18,20},{1... | collective-permute-start | bytes 786440 | tf_op jit(solution)/shard_map/ppermute | solution.py:231
  52.8 40.2 %copy-start.6 = (bf16[128,1024]{1,0:T(8,128)(2,1)}, bf16[128,1024]{1,0:T(8,128)(2,1)S(1)}, u32[]{:S(2)}) copy-start(bf16[128,1024]{1,0:T(8,128)(2,1)S(1)} %collective-permute-done.6.refs_6_.refs_14_) | copy-start | bytes 786436
  52.8 16.1 %collective-permute-start.8 = (bf16[128,1024]{1,0:T(8,128)(2,1)S(1)}, bf16[128,1024]{1,0:T(8,128)(2,1)S(1)}, u32[]{:S(2)}, u32[]{:S(2)}) collective-permute-start(bf16[128,1024]{1,0:T(8,128)(2,1)S(1)} %collective-permute-done.2.refs_8_.refs_16_), channel_id=1, source_target_pairs={{2,3},{3,2},{4,5},{5,4},{6,7},{7,6},{10,11},{11,10},{12,13},{13,12... | collective-permute-start | bytes 786440 | tf_op jit(solution)/shard_map/ppermute | solution.py:227
  58.4 34.6 %copy-start.7 = (bf16[128,1024]{1,0:T(8,128)(2,1)}, bf16[128,1024]{1,0:T(8,128)(2,1)S(1)}, u32[]{:S(2)}) copy-start(bf16[128,1024]{1,0:T(8,128)(2,1)S(1)} %collective-permute-done.9.refs_8_.refs_16_) | copy-start | bytes 786436
  58.4 16.2 %collective-permute-start.5 = (bf16[128,1024]{1,0:T(8,128)(2,1)S(1)}, bf16[128,1024]{1,0:T(8,128)(2,1)}, u32[]{:S(2)}, u32[]{:S(2)}) collective-permute-start(bf16[128,1024]{1,0:T(8,128)(2,1)S(1)} %collective-permute-done.3.refs_9_.refs_17_), channel_id=1, source_target_pairs={{4,6},{5,7},{12,14},{13,15},{20,22},{21,23},{28,30},{29,31}} | collective-permute-start | bytes 786440 | tf_op jit(solution)/shard_map/ppermute | solution.py:231
  64.1 29.0 %copy-start.8 = (bf16[128,1024]{1,0:T(8,128)(2,1)}, bf16[128,1024]{1,0:T(8,128)(2,1)S(1)}, u32[]{:S(2)}) copy-start(bf16[128,1024]{1,0:T(8,128)(2,1)S(1)} %collective-permute-done.10.refs_10_.refs_18_) | copy-start | bytes 786436
  64.1 19.7 %copy-start.12 = (bf16[128,1024]{1,0:T(8,128)(2,1)}, bf16[128,1024]{1,0:T(8,128)(2,1)S(1)}, u32[]{:S(2)}) copy-start(bf16[128,1024]{1,0:T(8,128)(2,1)S(1)} %collective-permute-done.4.refs_10_.refs_18_) | copy-start | bytes 786436
  68.9 24.1 %copy-start.11 = (bf16[128,1024]{1,0:T(8,128)(2,1)}, bf16[128,1024]{1,0:T(8,128)(2,1)S(1)}, u32[]{:S(2)}) copy-start(bf16[128,1024]{1,0:T(8,128)(2,1)S(1)} %collective-permute-done.8.refs_7_.refs_15_) | copy-start | bytes 786436
  68.9 24.1 %copy-start.2 = (bf16[256,1152]{1,0:T(8,128)(2,1)}, bf16[256,1152]{1,0:T(8,128)(2,1)S(1)}, u32[]{:S(2)}) copy-start(bf16[256,1152]{1,0:T(8,128)(2,1)S(1)} %collective-permute-done.7.refs_3_.refs_4_) | copy-start | bytes 1769476
  68.9 9.6 %collective-permute-start.11 = (bf16[128,1024]{1,0:T(8,128)(2,1)S(1)}, bf16[128,1024]{1,0:T(8,128)(2,1)}, u32[]{:S(2)}, u32[]{:S(2)}) collective-permute-start(bf16[128,1024]{1,0:T(8,128)(2,1)S(1)} %collective-permute-done.4.refs_10_.refs_18_), channel_id=1, source_target_pairs={{4,6},{5,7},{12,14},{13,15},{20,22},{21,23},{28,30},{29,31}} | collective-permute-start | bytes 786440 | tf_op jit(solution)/shard_map/ppermute | solution.py:231
  70.2 22.8 %collective-permute-start.12 = (bf16[128,1024]{1,0:T(8,128)(2,1)S(1)}, bf16[128,1024]{1,0:T(8,128)(2,1)}, u32[]{:S(2)}, u32[]{:S(2)}) collective-permute-start(bf16[128,1024]{1,0:T(8,128)(2,1)S(1)} %collective-permute-done.4.refs_10_.refs_18_), channel_id=1, source_target_pairs={{4,5},{5,4},{6,7},{7,6},{12,13},{13,12},{14,15},{15,14},{20,21},{2... | collective-permute-start | bytes 786440 | tf_op jit(solution)/shard_map/ppermute | solution.py:227
  74.6 18.4 %collective-permute-start.14 = (bf16[128,1024]{1,0:T(8,128)(2,1)}, bf16[128,1024]{1,0:T(8,128)(2,1)}, u32[]{:S(2)}, u32[]{:S(2)}) collective-permute-start(bf16[128,1024]{1,0:T(8,128)(2,1)} %collective-permute-done.5.refs_11_.refs_19_), channel_id=1, source_target_pairs={{6,7},{7,6},{14,15},{15,14},{22,23},{23,22},{30,31},{31,30}} | collective-permute-start | bytes 786440 | tf_op jit(solution)/shard_map/ppermute | solution.py:227
  78.5 14.6 %collective-permute-start.13 = (bf16[128,1024]{1,0:T(8,128)(2,1)}, bf16[128,1024]{1,0:T(8,128)(2,1)}, u32[]{:S(2)}, u32[]{:S(2)}) collective-permute-start(bf16[128,1024]{1,0:T(8,128)(2,1)} %collective-permute-done.11.refs_12_.refs_20_), channel_id=1, source_target_pairs={{6,7},{7,6},{14,15},{15,14},{22,23},{23,22},{30,31},{31,30}} | collective-permute-start | bytes 786440 | tf_op jit(solution)/shard_map/ppermute | solution.py:227

commit v9 on v7

v9 whole, which is shorter than its diff:
```python
import functools
import math

import jax
import jax.numpy as jnp
from jax import lax
from jax.experimental import pallas as pl
from jax.experimental.pallas import tpu as pltpu
from jax.sharding import PartitionSpec as P

H = 64
KVH = 8
HD = 128
GQ = H // KVH
REACH = 7
SLAB = 2
FILL = -1e30


def halves_kernel(meta_ref, a_ref, b_ref, mine_ref, theirs_ref):
    mine_ref[...] = a_ref[...]
    theirs_ref[...] = b_ref[...]


def halves(kv, side):
    rows, half = kv.shape[0], kv.shape[1] // 4
    shape = (rows, half)
    return pl.pallas_call(
        halves_kernel,
        grid_spec=pltpu.PrefetchScalarGridSpec(
            num_scalar_prefetch=1,
            grid=(2,),
            in_specs=[
                pl.BlockSpec(shape, lambda i, m: (0, 2 * i + m[0])),
                pl.BlockSpec(shape, lambda i, m: (0, 2 * i + 1 - m[0])),
            ],
            out_specs=[pl.BlockSpec(shape, lambda i, m: (0, i))] * 2,
        ),
        out_shape=[jax.ShapeDtypeStruct((rows, 2 * half), kv.dtype)] * 2,
    )(side.reshape(1), kv, kv)


def attend_kernel(pairs, parts, tile, tiles, fresh, meta_ref, *refs):
    s_ref, top_ref = refs[-2:]
    inputs = 2 * parts + 4 * pairs
    if fresh:
        seg_ref, *ints_refs = refs[: 1 + parts]
        q_ref, *inputs = refs[1 + parts : 2 + parts + inputs]
        o_ref, bias_ref, reach_ref = refs[-5:-2]
    else:
        bias_ref, reach_ref, q_ref, *inputs = refs[: 3 + inputs]
        o_ref = refs[-3]
    pk_refs, pv_refs = inputs[:parts], inputs[parts : 2 * parts]
    k_refs, v_refs = inputs[2 * parts :][: 2 * pairs], inputs[2 * parts + 2 * pairs :]
    rows = q_ref.shape[0]
    step = 2 * rows
    span = pk_refs[0].shape[0]
    prefix_keys = parts * span
    block, limit = meta_ref[0], meta_ref[2]
    scale = math.log2(math.e) / math.sqrt(HD)
    nt = (((1,), (1,)), ((), ()))

    def masks():
        ints = jnp.concatenate([ref[...].astype(jnp.float32) for ref in ints_refs])
        row = lax.broadcasted_iota(jnp.int32, ints.shape, 0)
        part = lax.rem(row, tile)
        place = jnp.where(part == 0, pltpu.roll(ints, prefix_keys - 1, 0), ints)
        live = place.astype(jnp.int32) * tile + part < limit
        bias_ref[:, :prefix_keys] = jnp.where(live, 0.0, FILL).T

        own = seg_ref[...].astype(jnp.float32)
        has_segs = lax.rem(row, tiles * tile) == 0
        earlier = jnp.sum(jnp.where(has_segs & (ints < own[:, :1]), 1.0, 0.0))
        reach_ref[0] = lax.div(block, 2) - lax.div(earlier.astype(jnp.int32), step)

        seg_q = jnp.broadcast_to(own, (rows, rows)).T
        row_pos = block * rows + lax.broadcasted_iota(jnp.int32, (rows, rows), 0)
        lane = lax.broadcasted_iota(jnp.int32, (rows, rows), 1)
        for k in range(pairs):
            for j, first in enumerate((block, block + 1 - 2 * lax.rem(block, 2))):
                at = (2 * k + j) * tiles * tile
                seen = (ints[at : at + 1] == seg_q) & ((first - 2 * k) * rows + lane <= row_pos)
                at = prefix_keys + (2 * k + j) * rows
                bias_ref[:, at : at + rows] = jnp.where(seen, 0.0, FILL)

    if fresh:
        pl.when(pl.program_id(0) == 0)(masks)

    def body(near):
        steps = prefix_keys // step + near + 1
        each = step // span
        keys = [
            jnp.concatenate([ref[...] for ref in pk_refs[at : at + each]])
            for at in range(0, parts, each)
        ]
        for k in range(near + 1):
            keys.append(jnp.concatenate([k_refs[2 * k][...], k_refs[2 * k + 1][...]]))
        values = jnp.concatenate([ref[...] for ref in (*pv_refs, *v_refs[: 2 * near + 2])])
        values = jnp.concatenate([values, jnp.ones_like(values)], axis=1)

        def score(slab):
            of = range(slab * SLAB, (slab + 1) * SLAB)
            q = jnp.concatenate([q_ref[:, g * HD : (g + 1) * HD] for g in of])
            top = None
            for i in range(steps):
                at = slice(i * step, (i + 1) * step)
                s = lax.dot_general(q, keys[i], nt, preferred_element_type=jnp.float32)
                s = (s.reshape(SLAB, rows, step) + bias_ref[:, at][None]).reshape(-1, step)
                s_ref[slab % 2, :, at] = s
                high = jnp.maximum(s[:, :rows], s[:, rows:])
                top = high if top is None else jnp.maximum(top, high)
            top = jnp.max(top, axis=1, keepdims=True)
            top_ref[slab % 2] = jnp.broadcast_to(top, (SLAB * rows, HD))

        def weigh(slab):
            top = top_ref[slab % 2]
            weights = [
                jnp.exp2((s_ref[slab % 2, :, i * HD : (i + 1) * HD] - top) * scale).astype(
                    jnp.bfloat16
                )
                for i in range(steps * step // HD)
            ]
            acc = jnp.dot(
                jnp.concatenate(weights, axis=1), values, preferred_element_type=jnp.float32
            )
            out = (acc[:, :HD] / acc[:, HD:]).astype(o_ref.dtype)
            for j in range(SLAB):
                g = slab * SLAB + j
                o_ref[:, g * HD : (g + 1) * HD] = out[j * rows : (j + 1) * rows]

        score(0)
        for slab in range(GQ // SLAB):
            if slab + 1 < GQ // SLAB:
                score(slab + 1)
            weigh(slab)

    for near in range(pairs):
        pl.when(reach_ref[0] == near)(functools.partial(body, near))


def attend(meta, queries, pieces, prefix, tile, tiles, segments=None, before=None):
    rows = queries.shape[0]
    span = prefix[0].shape[0]
    pairs, parts = len(pieces) // 2, len(prefix)
    heads = pieces[0].shape[1] // (2 * HD)
    keys = rows * len(pieces) + span * parts
    whole = pl.BlockSpec((rows, keys), lambda i, m: (0, 0))
    scalar = pl.BlockSpec(memory_space=pltpu.SMEM)
    wide = pl.BlockSpec((rows, GQ * HD), lambda i, m: (0, m[1] + i))
    fresh = before is None
    queries, *arrays = [
        pltpu.with_memory_space_constraint(array, pltpu.HBM)
        for array in (queries, *prefix, *pieces)
    ]
    prefix, pieces = arrays[:parts], arrays[parts:]
    args = [meta, *([segments, *prefix] if fresh else before[1:])]
    args += [queries, *prefix, *prefix, *pieces, *pieces]
    if fresh:
        ints = pl.BlockSpec((span, rows), lambda i, m: (0, 2 * KVH))
        in_specs = [pl.BlockSpec((1, rows), lambda i, m: (0, 0)), *[ints] * parts]
    else:
        in_specs = [whole, scalar]
    in_specs += [
        wide,
        *[pl.BlockSpec((span, HD), lambda i, m: (0, m[1] + i))] * parts,
        *[pl.BlockSpec((span, HD), lambda i, m: (0, KVH + m[1] + i))] * parts,
        *[pl.BlockSpec((rows, HD), lambda i, m: (0, i))] * len(pieces),
        *[pl.BlockSpec((rows, HD), lambda i, m: (0, heads + i))] * len(pieces),
    ]
    out_specs = [wide]
    out_shape = [jax.ShapeDtypeStruct(queries.shape, queries.dtype)]
    aliases = {}
    if fresh:
        out_specs += [whole, scalar]
        out_shape += [
            jax.ShapeDtypeStruct((rows, keys), jnp.float32),
            jax.ShapeDtypeStruct((1,), jnp.int32),
        ]
    else:
        args.append(before[0])
        in_specs.append(pl.BlockSpec(memory_space=pl.ANY))
        aliases = {len(args) - 1: 0}
    return pl.pallas_call(
        functools.partial(attend_kernel, pairs, parts, tile, tiles, fresh),
        grid_spec=pltpu.PrefetchScalarGridSpec(
            num_scalar_prefetch=1,
            grid=(heads,),
            in_specs=in_specs,
            out_specs=out_specs,
            scratch_shapes=[
                pltpu.VMEM((2, SLAB * rows, keys), jnp.float32),
                pltpu.VMEM((2, SLAB * rows, HD), jnp.float32),
            ],
        ),
        out_shape=out_shape,
        input_output_aliases=aliases,
        compiler_params=pltpu.CompilerParams(vmem_limit_bytes=24 * 1024 * 1024),
    )(*args)


def on_device(queries, resp_kv, resp_segments, prefix_kv, tile_plan, prompt_lengths):
    rows = queries.shape[1]
    tiles, tile, columns = prefix_kv.shape
    groups, count = lax.axis_size("prompt"), lax.axis_size("resp")
    group = lax.axis_index("prompt")
    block = lax.axis_index("resp")
    side = block % 2
    steps = min(count // 2 - 1, (REACH + 1) // 2)
    assert tiles == groups

    def swap(value, first):
        return lax.ppermute(value, "resp", [(r, r ^ 1) for r in range(2 * first, count)])

    def climb(value, step):
        pairs = [(r, r + 2) for r in range(2 * step - 2, count - 2)]
        return lax.ppermute(value, "resp", pairs)

    def shift(value, axis, by):
        size = lax.axis_size(axis)
        return lax.ppermute(value, axis, [(r, (r + by) % size) for r in range(size)])

    def after(value, *others):
        return lax.optimization_barrier((value, *others))[0]

    mine, theirs = halves(resp_kv[0], side)
    partner = swap(theirs, 0)
    upper = [(r, r + 1) for r in range(0, count, 2)]
    upper = lax.ppermute(after(mine, partner), "resp", upper)
    straight, crossed = [mine, partner], [theirs, upper]
    for step in range(1, steps + 1):
        one, two = straight[-2:]
        if step > 2:
            one, two = after(one, crossed[-3]), after(two, crossed[-4], upper)
        one, two = climb(one, step), climb(two, step)
        straight += [one, two]
        crossed += [swap(two, step), swap(one, step)]

    owners = (group + jnp.arange(groups, dtype=jnp.int32)) % groups
    pick = tile_plan[None, :, 0] == owners[:, None]
    place = jnp.sum(jnp.where(pick, tile_plan[None, :, 1], 0), axis=1, dtype=jnp.int32)
    own_tiles = jnp.sum(
        jnp.where(pick[:, :, None, None], prefix_kv[None], 0).astype(jnp.float32), axis=1
    )
    row = jnp.arange(tile, dtype=jnp.int32)[:, None]
    extra = jnp.where(row == 0, resp_segments[0], place.reshape(groups, 1, 1))
    own_tiles = jnp.concatenate([own_tiles, extra.astype(jnp.float32)], axis=-1)
    own_tiles = own_tiles.astype(prefix_kv.dtype)
    came = [own_tiles[0]] + [shift(own_tiles[by], "prompt", by) for by in range(1, groups)]
    came = jnp.concatenate(came)
    prefix = [jnp.concatenate([came, swap(came, 0)])]
    prefix += [shift(prefix[0], "resp", 2 * by) for by in range(1, count // 2)]

    def meta(first):
        return jnp.stack([block, first * (KVH // 2), prompt_lengths[0]])

    done = attend(
        meta(side), queries[0], straight, prefix, tile, tiles, segments=resp_segments
    )
    done = attend(meta(1 - side), queries[0], crossed, prefix, tile, tiles, before=done)
    return done[0][None]


def solution(mesh):
    return jax.shard_map(
        on_device,
        mesh=mesh,
        in_specs=(
            P("prompt", "resp", None),
            P("prompt", "resp", None),
            P("prompt", "resp"),
            P(("prompt", "resp"), None, None),
            P(("prompt", "resp"), None),
            P("prompt"),
        ),
        out_specs=P("prompt", "resp", None),
        check_vma=False,
    )
```

time: 102 us -> 93.8 us (0.920)
  the two profiles are of different devices: /device:TPU:24 before, /device:TPU:26 now
where the time goes in v9:
time: 93.8 us; the launch traced here: 92 us
  starting transfers between devices  43.2 us (46%)
  waiting for transfers between devices  22.5 us (24%)
  Pallas kernels  21.6 us (23%)
  other arithmetic  2.14 us (2%)
  local copies, waits for them, and re-layouts  1.48 us (2%)
  between operations  1.18 us (1%)
    ppermute x8, starting transfers between devices, swap(): lax.ppermute(value, 'resp', [(r, r ^ 1) for r in range(2 * first, count)])  20.7 us
    pallas_call x2, Pallas kernels, attend(): pl.pallas_call(functools.partial(attend_kernel, pairs, parts, tile, tiles...  19.7 us
    ppermute x6, waiting for transfers between devices, shift(): lax.ppermute(value, axis, [(r, (r + by) % size) for r in range(size)])  17.4 us
    ppermute x6, starting transfers between devices, shift(): lax.ppermute(value, axis, [(r, (r + by) % size) for r in range(size)])  11.4 us
    ppermute x6, starting transfers between devices, climb(): return lax.ppermute(value, 'resp', pairs)  7.72 us
    ppermute x6, waiting for transfers between devices, climb(): return lax.ppermute(value, 'resp', pairs)  4.41 us
    ppermute x1, starting transfers between devices, on_device(): upper = lax.ppermute(after(mine, partner), 'resp', upper)  3.44 us
  transfers between devices with their start and end apart: 21, of which 6 were waited for; matrix products, arithmetic and copies ran while one was open for 3% of the time, Pallas kernels for 10%

profile of v9, /device:TPU:26, one launch (start us, length us, event | category | flops | bytes accessed | tf_op | source)
XLA Modules:
  0.0 92.0 jit_solution(15477907729925461328)
XLA Ops:
  0.0 1.9 %shard_map.64 = (bf16[128,1024]{1,0:T(8,128)(2,1)}, bf16[128,1024]{1,0:T(8,128)(2,1)}) custom-call(s32[1]{0:T(128)} %bitcast.11.meta_ref, bf16[128,2048]{1,0:T(8,128)(2,1)} %bitcast.24, bf16[128,2048]{1,0:T(8,128)(2,1)} %bitcast.25), custom_call_target="tpu_custom_call" | custom-call | tf_op jit(solution)/shard_map/pallas_call | solution.py:28
  1.9 1.5 %collective-permute-start.7 = (bf16[128,1024]{1,0:T(8,128)(2,1)}, bf16[128,1024]{1,0:T(8,128)(2,1)S(1)}, u32[]{:S(2)}, u32[]{:S(2)}) collective-permute-start(bf16[128,1024]{1,0:T(8,128)(2,1)} %get-tuple-element.14.refs_11_.refs_19_), channel_id=1, source_target_pairs={{0,1},{1,0},{2,3},{3,2},{4,5},{5,4},{6,7},{7,6},{8,9},{9,8},{10,11... | collective-permute-start | bytes 786440 | tf_op jit(solution)/shard_map/ppermute | solution.py:212
  3.4 1.3 %collective-permute-start.8 = (bf16[128,1024]{1,0:T(8,128)(2,1)}, bf16[128,1024]{1,0:T(8,128)(2,1)S(1)}, u32[]{:S(2)}, u32[]{:S(2)}) collective-permute-start(bf16[128,1024]{1,0:T(8,128)(2,1)} %get-tuple-element.16.refs_14_.refs_22_), channel_id=1, source_target_pairs={{0,2},{1,3},{2,4},{3,5},{4,6},{5,7},{8,10},{9,11},{10,12},{11,13},... | collective-permute-start | bytes 786440 | tf_op jit(solution)/shard_map/ppermute | solution.py:216
  4.7 0.8 slice_bitcast_fusion.1
  5.6 1.0 %select_reduce_fusion = bf16[4,8,2048]{2,1,0:T(8,128)(2,1)S(1)} fusion(pred[4,4]{1,0:T(4,128)(4,1)S(1)} %get-tuple-element.24, bf16[4,8,2048]{2,1,0:T(8,128)(2,1)} %param.9), kind=kLoop, calls=%fused_computation | loop fusion | flops 458752 | bytes 262160 | tf_op jit(solution)/shard_map/reduce_sum | solution.py:241
  6.7 0.7 convert_convert_fusion
  7.5 0.6 collective-permute-start.1
  8.1 1.4 %collective-permute-start.2 = (bf16[8,2176]{1,0:T(8,128)(2,1)S(1)}, bf16[8,2176]{1,0:T(8,128)(2,1)S(1)}, u32[]{:S(2)}, u32[]{:S(2)}) collective-permute-start(bf16[8,2176]{1,0:T(8,128)(2,1)S(1)} %get-tuple-element.25), channel_id=1, source_target_pairs={{0,24},{8,0},{16,8},{24,16},{1,25},{9,1},{17,9},{25,17},{2,26},{10... | collective-permute-start | bytes 104456 | tf_op jit(solution)/shard_map/ppermute | solution.py:220
  9.5 1.4 %collective-permute-done = bf16[8,2176]{1,0:T(8,128)(2,1)S(1)} collective-permute-done((bf16[8,2176]{1,0:T(8,128)(2,1)S(1)}, bf16[8,2176]{1,0:T(8,128)(2,1)S(1)}, u32[]{:S(2)}, u32[]{:S(2)}) %collective-permute-start) | collective-permute-done | bytes 34848 | tf_op jit(solution)/shard_map/ppermute | solution.py:220
  10.8 0.7 collective-permute-done.1
  11.6 0.6 collective-permute-start.3
  12.2 1.3 %collective-permute-start.9 = (bf16[128,1024]{1,0:T(8,128)(2,1)S(1)}, bf16[128,1024]{1,0:T(8,128)(2,1)S(1)}, u32[]{:S(2)}, u32[]{:S(2)}) collective-permute-start(bf16[128,1024]{1,0:T(8,128)(2,1)S(1)} %collective-permute-done.7.refs_15_.refs_23_), channel_id=1, source_target_pairs={{0,2},{1,3},{2,4},{3,5},{4,6},{5,7},{8,10},{9,11},{10,12},{11,13},... | collective-permute-start | bytes 786440 | tf_op jit(solution)/shard_map/ppermute | solution.py:216
  13.5 3.4 %collective-permute-start.15 = (bf16[128,1024]{1,0:T(8,128)(2,1)}, bf16[128,1024]{1,0:T(8,128)(2,1)S(1)}, u32[]{:S(2)}, u32[]{:S(2)}) collective-permute-start(bf16[128,1024]{1,0:T(8,128)(2,1)} %get-tuple-element.16.refs_14_.refs_22_), channel_id=1, source_target_pairs={{0,1},{2,3},{4,5},{6,7},{8,9},{10,11},{12,13},{14,15},{16,17},{18,... | collective-permute-start | bytes 786440 | tf_op jit(solution)/shard_map/ppermute | solution.py:228
  17.0 1.3 %collective-permute-start.10 = (bf16[128,1024]{1,0:T(8,128)(2,1)S(1)}, bf16[128,1024]{1,0:T(8,128)(2,1)S(1)}, u32[]{:S(2)}, u32[]{:S(2)}) collective-permute-start(bf16[128,1024]{1,0:T(8,128)(2,1)S(1)} %collective-permute-done.8.refs_16_.refs_24_), channel_id=1, source_target_pairs={{2,4},{3,5},{4,6},{5,7},{10,12},{11,13},{12,14},{13,15},{18,20},{1... | collective-permute-start | bytes 786440 | tf_op jit(solution)/shard_map/ppermute | solution.py:216
  18.3 1.9 %collective-permute-start.12 = (bf16[128,1024]{1,0:T(8,128)(2,1)S(1)}, bf16[128,1024]{1,0:T(8,128)(2,1)S(1)}, u32[]{:S(2)}, u32[]{:S(2)}) collective-permute-start(bf16[128,1024]{1,0:T(8,128)(2,1)S(1)} %collective-permute-done.8.refs_16_.refs_24_), channel_id=1, source_target_pairs={{2,3},{3,2},{4,5},{5,4},{6,7},{7,6},{10,11},{11,10},{12,13},{13,12... | collective-permute-start | bytes 786440 | tf_op jit(solution)/shard_map/ppermute | solution.py:212
  20.2 3.5 %collective-permute-done.9.refs_17_.refs_25_ = bf16[128,1024]{1,0:T(8,128)(2,1)S(1)} collective-permute-done((bf16[128,1024]{1,0:T(8,128)(2,1)S(1)}, bf16[128,1024]{1,0:T(8,128)(2,1)S(1)}, u32[]{:S(2)}, u32[]{:S(2)}) %collective-permute-start.9) | collective-permute-done | bytes 262176 | tf_op jit(solution)/shard_map/ppermute | solution.py:216
  23.8 1.3 %collective-permute-start.11 = (bf16[128,1024]{1,0:T(8,128)(2,1)S(1)}, bf16[128,1024]{1,0:T(8,128)(2,1)S(1)}, u32[]{:S(2)}, u32[]{:S(2)}) collective-permute-start(bf16[128,1024]{1,0:T(8,128)(2,1)S(1)} %collective-permute-done.9.refs_17_.refs_25_), channel_id=1, source_target_pairs={{2,4},{3,5},{4,6},{5,7},{10,12},{11,13},{12,14},{13,15},{18,20},{1... | collective-permute-start | bytes 786440 | tf_op jit(solution)/shard_map/ppermute | solution.py:216
  25.1 3.4 %collective-permute-start.14 = (bf16[128,1024]{1,0:T(8,128)(2,1)S(1)}, bf16[128,1024]{1,0:T(8,128)(2,1)S(1)}, u32[]{:S(2)}, u32[]{:S(2)}) collective-permute-start(bf16[128,1024]{1,0:T(8,128)(2,1)S(1)} %collective-permute-done.9.refs_17_.refs_25_), channel_id=1, source_target_pairs={{2,3},{3,2},{4,5},{5,4},{6,7},{7,6},{10,11},{11,10},{12,13},{13,12... | collective-permute-start | bytes 786440 | tf_op jit(solution)/shard_map/ppermute | solution.py:212
  28.5 0.8 collective-permute-done.10.refs_18_.refs_26_
  29.4 5.3 %collective-permute-start.5 = (bf16[64,2176]{1,0:T(8,128)(2,1)S(1)}, bf16[64,2176]{1,0:T(8,128)(2,1)S(1)}, u32[]{:S(2)}, u32[]{:S(2)}) collective-permute-start(bf16[64,2176]{1,0:T(8,128)(2,1)S(1)} %constant_dynamic-update-slice_fusion.refs_1_.refs_6_.refs_10_.refs_3_.refs_7_), channel_id=1, source_target_pairs={{0,4},{1,5},{2,6},{3,7},{4,0},{5,1},{6,2},{7,3},{8,12},{9,13},{10,... | collective-permute-start | bytes 835592 | tf_op jit(solution)/shard_map/ppermute | solution.py:220
  34.7 1.3 %collective-permute-start.13 = (bf16[128,1024]{1,0:T(8,128)(2,1)S(1)}, bf16[128,1024]{1,0:T(8,128)(2,1)}, u32[]{:S(2)}, u32[]{:S(2)}) collective-permute-start(bf16[128,1024]{1,0:T(8,128)(2,1)S(1)} %collective-permute-done.10.refs_18_.refs_26_), channel_id=1, source_target_pairs={{4,6},{5,7},{12,14},{13,15},{20,22},{21,23},{28,30},{29,31}} | collective-permute-start | bytes 786440 | tf_op jit(solution)/shard_map/ppermute | solution.py:216
  36.0 1.3 %collective-permute-start.16 = (bf16[128,1024]{1,0:T(8,128)(2,1)S(1)}, bf16[128,1024]{1,0:T(8,128)(2,1)}, u32[]{:S(2)}, u32[]{:S(2)}) collective-permute-start(bf16[128,1024]{1,0:T(8,128)(2,1)S(1)} %collective-permute-done.11.refs_19_.refs_27_), channel_id=1, source_target_pairs={{4,6},{5,7},{12,14},{13,15},{20,22},{21,23},{28,30},{29,31}} | collective-permute-start | bytes 786440 | tf_op jit(solution)/shard_map/ppermute | solution.py:216
  37.3 4.0 %collective-permute-start.6 = (bf16[64,2176]{1,0:T(8,128)(2,1)S(1)}, bf16[64,2176]{1,0:T(8,128)(2,1)S(1)}, u32[]{:S(2)}, u32[]{:S(2)}) collective-permute-start(bf16[64,2176]{1,0:T(8,128)(2,1)S(1)} %constant_dynamic-update-slice_fusion.refs_1_.refs_6_.refs_10_.refs_3_.refs_7_), channel_id=1, source_target_pairs={{0,6},{1,7},{2,0},{3,1},{4,2},{5,3},{6,4},{7,5},{8,14},{9,15},{10,... | collective-permute-start | bytes 835592 | tf_op jit(solution)/shard_map/ppermute | solution.py:220
  41.4 3.8 %collective-permute-start.18 = (bf16[128,1024]{1,0:T(8,128)(2,1)S(1)}, bf16[128,1024]{1,0:T(8,128)(2,1)S(1)}, u32[]{:S(2)}, u32[]{:S(2)}) collective-permute-start(bf16[128,1024]{1,0:T(8,128)(2,1)S(1)} %collective-permute-done.10.refs_18_.refs_26_), channel_id=1, source_target_pairs={{4,5},{5,4},{6,7},{7,6},{12,13},{13,12},{14,15},{15,14},{20,21},{2... | collective-permute-start | bytes 786440 | tf_op jit(solution)/shard_map/ppermute | solution.py:212
  45.2 15.3 %collective-permute-done.5.refs_3_.refs_8_.refs_12_.refs_5_.refs_9_ = bf16[64,2176]{1,0:T(8,128)(2,1)S(1)} collective-permute-done((bf16[64,2176]{1,0:T(8,128)(2,1)S(1)}, bf16[64,2176]{1,0:T(8,128)(2,1)S(1)}, u32[]{:S(2)}, u32[]{:S(2)}) %collective-permute-start.5) | collective-permute-done | bytes 278560 | tf_op jit(solution)/shard_map/ppermute | solution.py:220
  60.4 3.4 %collective-permute-start.17 = (bf16[128,1024]{1,0:T(8,128)(2,1)S(1)}, bf16[128,1024]{1,0:T(8,128)(2,1)}, u32[]{:S(2)}, u32[]{:S(2)}) collective-permute-start(bf16[128,1024]{1,0:T(8,128)(2,1)S(1)} %collective-permute-done.11.refs_19_.refs_27_), channel_id=1, source_target_pairs={{4,5},{5,4},{6,7},{7,6},{12,13},{13,12},{14,15},{15,14},{20,21},{2... | collective-permute-start | bytes 786440 | tf_op jit(solution)/shard_map/ppermute | solution.py:212
  63.9 2.4 %collective-permute-start.20 = (bf16[128,1024]{1,0:T(8,128)(2,1)}, bf16[128,1024]{1,0:T(8,128)(2,1)}, u32[]{:S(2)}, u32[]{:S(2)}) collective-permute-start(bf16[128,1024]{1,0:T(8,128)(2,1)} %collective-permute-done.13.refs_20_.refs_28_), channel_id=1, source_target_pairs={{6,7},{7,6},{14,15},{15,14},{22,23},{23,22},{30,31},{31,30}} | collective-permute-start | bytes 786440 | tf_op jit(solution)/shard_map/ppermute | solution.py:212
  66.3 3.6 %collective-permute-start.19 = (bf16[128,1024]{1,0:T(8,128)(2,1)}, bf16[128,1024]{1,0:T(8,128)(2,1)}, u32[]{:S(2)}, u32[]{:S(2)}) collective-permute-start(bf16[128,1024]{1,0:T(8,128)(2,1)} %collective-permute-done.16.refs_21_.refs_29_), channel_id=1, source_target_pairs={{6,7},{7,6},{14,15},{15,14},{22,23},{23,22},{30,31},{31,30}} | collective-permute-start | bytes 786440 | tf_op jit(solution)/shard_map/ppermute | solution.py:212
  70.8 0.6 copy-done.4
  71.4 9.7 %shard_map.65 = (bf16[128,8192]{1,0:T(8,128)(2,1)}, f32[128,1280]{1,0:T(8,128)S(1)}, s32[1]{0:T(128)}) custom-call(s32[3]{0:T(128)S(1)} %add_add_fusion.1.meta_ref, s32[1,128]{1,0:T(1,128)S(1)} %copy-done, bf16[64,2176]{1,0:T(8,128)(2,1)} %copy-done.1, bf16[64,2176]{1,0:T(8,128)(2,1)} %copy-done.2, bf16[64,2176]{1,0:T(8,128)(2,1)} %copy-done.3, ...), custom_call_target="tpu_custom_call" | custom-call | tf_op jit(solution)/shard_map/pallas_call | solution.py:183
  81.1 0.6 collective-permute-done.19.refs_17_.refs_25_
  81.8 10.0 %shard_map.66 = bf16[128,8192]{1,0:T(8,128)(2,1)} custom-call(s32[3]{0:T(128)S(1)} %add_add_fusion.meta_ref, f32[128,1280]{1,0:T(8,128)S(1)} %get-tuple-element.18.refs_0_, s32[1]{0:T(128)} %get-tuple-element.19.refs_1_, bf16[128,8192]{1,0:T(8,128)(2,1)} %bitcast.23, bf16[64,2176]{1,0:T(8,128)(2,1)} %copy-done.1, ...), custom_call_target="tpu_custom_call", output_to_operand_aliasing={{}: (28, {})} | custom-call | tf_op jit(solution)/shard_map/pallas_call | solution.py:183
  (56 shorter events, 0.6 us)
Async XLA Ops:
  0.0 71.4 %copy-start = (s32[1,128]{1,0:T(1,128)S(1)}, s32[1,128]{1,0:T(1,128)}, u32[]{:S(2)}) copy-start(s32[1,128]{1,0:T(1,128)} %refs_0_.1) | copy-start | bytes 1540
  1.9 10.3 %collective-permute-start.7 = (bf16[128,1024]{1,0:T(8,128)(2,1)}, bf16[128,1024]{1,0:T(8,128)(2,1)S(1)}, u32[]{:S(2)}, u32[]{:S(2)}) collective-permute-start(bf16[128,1024]{1,0:T(8,128)(2,1)} %get-tuple-element.14.refs_11_.refs_19_), channel_id=1, source_target_pairs={{0,1},{1,0},{2,3},{3,2},{4,5},{5,4},{6,7},{7,6},{8,9},{9,8},{10,11... | collective-permute-start | bytes 786440 | tf_op jit(solution)/shard_map/ppermute | solution.py:212
  3.4 13.6 %collective-permute-start.8 = (bf16[128,1024]{1,0:T(8,128)(2,1)}, bf16[128,1024]{1,0:T(8,128)(2,1)S(1)}, u32[]{:S(2)}, u32[]{:S(2)}) collective-permute-start(bf16[128,1024]{1,0:T(8,128)(2,1)} %get-tuple-element.16.refs_14_.refs_22_), channel_id=1, source_target_pairs={{0,2},{1,3},{2,4},{3,5},{4,6},{5,7},{8,10},{9,11},{10,12},{11,13},... | collective-permute-start | bytes 786440 | tf_op jit(solution)/shard_map/ppermute | solution.py:216
  7.4 3.4 %collective-permute-start = (bf16[8,2176]{1,0:T(8,128)(2,1)S(1)}, bf16[8,2176]{1,0:T(8,128)(2,1)S(1)}, u32[]{:S(2)}, u32[]{:S(2)}) collective-permute-start(bf16[8,2176]{1,0:T(8,128)(2,1)S(1)} %get-tuple-element.26), channel_id=1, source_target_pairs={{0,8},{8,16},{16,24},{24,0},{1,9},{9,17},{17,25},{25,1},{2,10},{10... | collective-permute-start | bytes 104456 | tf_op jit(solution)/shard_map/ppermute | solution.py:220
  7.5 4.1 %collective-permute-start.1 = (bf16[8,2176]{1,0:T(8,128)(2,1)S(1)}, bf16[8,2176]{1,0:T(8,128)(2,1)S(1)}, u32[]{:S(2)}, u32[]{:S(2)}) collective-permute-start(bf16[8,2176]{1,0:T(8,128)(2,1)S(1)} %get-tuple-element.27), channel_id=1, source_target_pairs={{0,16},{8,24},{16,0},{24,8},{1,17},{9,25},{17,1},{25,9},{2,18},{10... | collective-permute-start | bytes 104456 | tf_op jit(solution)/shard_map/ppermute | solution.py:220
  8.1 3.5 %collective-permute-start.2 = (bf16[8,2176]{1,0:T(8,128)(2,1)S(1)}, bf16[8,2176]{1,0:T(8,128)(2,1)S(1)}, u32[]{:S(2)}, u32[]{:S(2)}) collective-permute-start(bf16[8,2176]{1,0:T(8,128)(2,1)S(1)} %get-tuple-element.25), channel_id=1, source_target_pairs={{0,24},{8,0},{16,8},{24,16},{1,25},{9,1},{17,9},{25,17},{2,26},{10... | collective-permute-start | bytes 104456 | tf_op jit(solution)/shard_map/ppermute | solution.py:220
  11.6 13.5 %collective-permute-start.3 = (bf16[32,2176]{1,0:T(8,128)(2,1)S(1)}, bf16[32,2176]{1,0:T(8,128)(2,1)S(1)}, u32[]{:S(2)}, u32[]{:S(2)}) collective-permute-start(bf16[32,2176]{1,0:T(8,128)(2,1)S(1)} %pad_maximum_fusion), channel_id=1, source_target_pairs={{0,1},{1,0},{2,3},{3,2},{4,5},{5,4},{6,7},{7,6},{8,9},{9,8},{10,11... | collective-permute-start | bytes 417800 | tf_op jit(solution)/shard_map/ppermute | solution.py:212
  12.2 58.5 %copy-start.5 = (bf16[128,1024]{1,0:T(8,128)(2,1)}, bf16[128,1024]{1,0:T(8,128)(2,1)S(1)}, u32[]{:S(2)}) copy-start(bf16[128,1024]{1,0:T(8,128)(2,1)S(1)} %collective-permute-done.7.refs_15_.refs_23_) | copy-start | bytes 786436
  12.2 11.6 %collective-permute-start.9 = (bf16[128,1024]{1,0:T(8,128)(2,1)S(1)}, bf16[128,1024]{1,0:T(8,128)(2,1)S(1)}, u32[]{:S(2)}, u32[]{:S(2)}) collective-permute-start(bf16[128,1024]{1,0:T(8,128)(2,1)S(1)} %collective-permute-done.7.refs_15_.refs_23_), channel_id=1, source_target_pairs={{0,2},{1,3},{2,4},{3,5},{4,6},{5,7},{8,10},{9,11},{10,12},{11,13},... | collective-permute-start | bytes 786440 | tf_op jit(solution)/shard_map/ppermute | solution.py:216
  13.5 21.2 %collective-permute-start.15 = (bf16[128,1024]{1,0:T(8,128)(2,1)}, bf16[128,1024]{1,0:T(8,128)(2,1)S(1)}, u32[]{:S(2)}, u32[]{:S(2)}) collective-permute-start(bf16[128,1024]{1,0:T(8,128)(2,1)} %get-tuple-element.16.refs_14_.refs_22_), channel_id=1, source_target_pairs={{0,1},{2,3},{4,5},{6,7},{8,9},{10,11},{12,13},{14,15},{16,17},{18,... | collective-permute-start | bytes 786440 | tf_op jit(solution)/shard_map/ppermute | solution.py:228
  17.0 53.8 %copy-start.6 = (bf16[128,1024]{1,0:T(8,128)(2,1)}, bf16[128,1024]{1,0:T(8,128)(2,1)S(1)}, u32[]{:S(2)}) copy-start(bf16[128,1024]{1,0:T(8,128)(2,1)S(1)} %collective-permute-done.8.refs_16_.refs_24_) | copy-start | bytes 786436
  17.0 12.4 %collective-permute-start.10 = (bf16[128,1024]{1,0:T(8,128)(2,1)S(1)}, bf16[128,1024]{1,0:T(8,128)(2,1)S(1)}, u32[]{:S(2)}, u32[]{:S(2)}) collective-permute-start(bf16[128,1024]{1,0:T(8,128)(2,1)S(1)} %collective-permute-done.8.refs_16_.refs_24_), channel_id=1, source_target_pairs={{2,4},{3,5},{4,6},{5,7},{10,12},{11,13},{12,14},{13,15},{18,20},{1... | collective-permute-start | bytes 786440 | tf_op jit(solution)/shard_map/ppermute | solution.py:216
  18.3 11.1 %collective-permute-start.12 = (bf16[128,1024]{1,0:T(8,128)(2,1)S(1)}, bf16[128,1024]{1,0:T(8,128)(2,1)S(1)}, u32[]{:S(2)}, u32[]{:S(2)}) collective-permute-start(bf16[128,1024]{1,0:T(8,128)(2,1)S(1)} %collective-permute-done.8.refs_16_.refs_24_), channel_id=1, source_target_pairs={{2,3},{3,2},{4,5},{5,4},{6,7},{7,6},{10,11},{11,10},{12,13},{13,12... | collective-permute-start | bytes 786440 | tf_op jit(solution)/shard_map/ppermute | solution.py:212
  23.8 47.0 %copy-start.9 = (bf16[128,1024]{1,0:T(8,128)(2,1)}, bf16[128,1024]{1,0:T(8,128)(2,1)S(1)}, u32[]{:S(2)}) copy-start(bf16[128,1024]{1,0:T(8,128)(2,1)S(1)} %collective-permute-done.9.refs_17_.refs_25_) | copy-start | bytes 786436
  23.8 12.2 %collective-permute-start.11 = (bf16[128,1024]{1,0:T(8,128)(2,1)S(1)}, bf16[128,1024]{1,0:T(8,128)(2,1)S(1)}, u32[]{:S(2)}, u32[]{:S(2)}) collective-permute-start(bf16[128,1024]{1,0:T(8,128)(2,1)S(1)} %collective-permute-done.9.refs_17_.refs_25_), channel_id=1, source_target_pairs={{2,4},{3,5},{4,6},{5,7},{10,12},{11,13},{12,14},{13,15},{18,20},{1... | collective-permute-start | bytes 786440 | tf_op jit(solution)/shard_map/ppermute | solution.py:216
  25.1 10.9 %collective-permute-start.14 = (bf16[128,1024]{1,0:T(8,128)(2,1)S(1)}, bf16[128,1024]{1,0:T(8,128)(2,1)S(1)}, u32[]{:S(2)}, u32[]{:S(2)}) collective-permute-start(bf16[128,1024]{1,0:T(8,128)(2,1)S(1)} %collective-permute-done.9.refs_17_.refs_25_), channel_id=1, source_target_pairs={{2,3},{3,2},{4,5},{5,4},{6,7},{7,6},{10,11},{11,10},{12,13},{13,12... | collective-permute-start | bytes 786440 | tf_op jit(solution)/shard_map/ppermute | solution.py:212
  28.5 42.2 %copy-start.1 = (bf16[64,2176]{1,0:T(8,128)(2,1)}, bf16[64,2176]{1,0:T(8,128)(2,1)S(1)}, u32[]{:S(2)}) copy-start(bf16[64,2176]{1,0:T(8,128)(2,1)S(1)} %constant_dynamic-update-slice_fusion.refs_1_.refs_6_.refs_10_.refs_3_.refs_7_) | copy-start | bytes 835588
  29.4 41.4 %copy-start.11 = (bf16[128,1024]{1,0:T(8,128)(2,1)}, bf16[128,1024]{1,0:T(8,128)(2,1)S(1)}, u32[]{:S(2)}) copy-start(bf16[128,1024]{1,0:T(8,128)(2,1)S(1)} %collective-permute-done.10.refs_18_.refs_26_) | copy-start | bytes 786436
  29.4 12.0 %collective-permute-start.4 = (bf16[64,2176]{1,0:T(8,128)(2,1)S(1)}, bf16[64,2176]{1,0:T(8,128)(2,1)S(1)}, u32[]{:S(2)}, u32[]{:S(2)}) collective-permute-start(bf16[64,2176]{1,0:T(8,128)(2,1)S(1)} %constant_dynamic-update-slice_fusion.refs_1_.refs_6_.refs_10_.refs_3_.refs_7_), channel_id=1, source_target_pairs={{0,2},{1,3},{2,4},{3,5},{4,6},{5,7},{6,0},{7,1},{8,10},{9,11},{10,... | collective-permute-start | bytes 835592 | tf_op jit(solution)/shard_map/ppermute | solution.py:220
  29.4 52.4 %copy-start.8 = (bf16[128,1024]{1,0:T(8,128)(2,1)}, bf16[128,1024]{1,0:T(8,128)(2,1)S(1)}, u32[]{:S(2)}) copy-start(bf16[128,1024]{1,0:T(8,128)(2,1)S(1)} %collective-permute-done.12.refs_14_.refs_22_) | copy-start | bytes 786436
  29.4 31.0 %collective-permute-start.5 = (bf16[64,2176]{1,0:T(8,128)(2,1)S(1)}, bf16[64,2176]{1,0:T(8,128)(2,1)S(1)}, u32[]{:S(2)}, u32[]{:S(2)}) collective-permute-start(bf16[64,2176]{1,0:T(8,128)(2,1)S(1)} %constant_dynamic-update-slice_fusion.refs_1_.refs_6_.refs_10_.refs_3_.refs_7_), channel_id=1, source_target_pairs={{0,4},{1,5},{2,6},{3,7},{4,0},{5,1},{6,2},{7,3},{8,12},{9,13},{10,... | collective-permute-start | bytes 835592 | tf_op jit(solution)/shard_map/ppermute | solution.py:220
  34.7 47.1 %copy-start.7 = (bf16[128,1024]{1,0:T(8,128)(2,1)}, bf16[128,1024]{1,0:T(8,128)(2,1)S(1)}, u32[]{:S(2)}) copy-start(bf16[128,1024]{1,0:T(8,128)(2,1)S(1)} %collective-permute-done.15.refs_12_.refs_20_) | copy-start | bytes 786436
  34.7 29.2 %collective-permute-start.13 = (bf16[128,1024]{1,0:T(8,128)(2,1)S(1)}, bf16[128,1024]{1,0:T(8,128)(2,1)}, u32[]{:S(2)}, u32[]{:S(2)}) collective-permute-start(bf16[128,1024]{1,0:T(8,128)(2,1)S(1)} %collective-permute-done.10.refs_18_.refs_26_), channel_id=1, source_target_pairs={{4,6},{5,7},{12,14},{13,15},{20,22},{21,23},{28,30},{29,31}} | collective-permute-start | bytes 786440 | tf_op jit(solution)/shard_map/ppermute | solution.py:216
  36.0 34.8 %copy-start.12 = (bf16[128,1024]{1,0:T(8,128)(2,1)}, bf16[128,1024]{1,0:T(8,128)(2,1)S(1)}, u32[]{:S(2)}) copy-start(bf16[128,1024]{1,0:T(8,128)(2,1)S(1)} %collective-permute-done.11.refs_19_.refs_27_) | copy-start | bytes 786436
  36.0 45.8 %copy-start.10 = (bf16[128,1024]{1,0:T(8,128)(2,1)}, bf16[128,1024]{1,0:T(8,128)(2,1)S(1)}, u32[]{:S(2)}) copy-start(bf16[128,1024]{1,0:T(8,128)(2,1)S(1)} %collective-permute-done.14.refs_13_.refs_21_) | copy-start | bytes 786436
  36.0 30.3 %collective-permute-start.16 = (bf16[128,1024]{1,0:T(8,128)(2,1)S(1)}, bf16[128,1024]{1,0:T(8,128)(2,1)}, u32[]{:S(2)}, u32[]{:S(2)}) collective-permute-start(bf16[128,1024]{1,0:T(8,128)(2,1)S(1)} %collective-permute-done.11.refs_19_.refs_27_), channel_id=1, source_target_pairs={{4,6},{5,7},{12,14},{13,15},{20,22},{21,23},{28,30},{29,31}} | collective-permute-start | bytes 786440 | tf_op jit(solution)/shard_map/ppermute | solution.py:216
  37.3 33.4 %collective-permute-start.6 = (bf16[64,2176]{1,0:T(8,128)(2,1)S(1)}, bf16[64,2176]{1,0:T(8,128)(2,1)S(1)}, u32[]{:S(2)}, u32[]{:S(2)}) collective-permute-start(bf16[64,2176]{1,0:T(8,128)(2,1)S(1)} %constant_dynamic-update-slice_fusion.refs_1_.refs_6_.refs_10_.refs_3_.refs_7_), channel_id=1, source_target_pairs={{0,6},{1,7},{2,0},{3,1},{4,2},{5,3},{6,4},{7,5},{8,14},{9,15},{10,... | collective-permute-start | bytes 835592 | tf_op jit(solution)/shard_map/ppermute | solution.py:220
  41.4 29.4 %copy-start.2 = (bf16[64,2176]{1,0:T(8,128)(2,1)}, bf16[64,2176]{1,0:T(8,128)(2,1)S(1)}, u32[]{:S(2)}) copy-start(bf16[64,2176]{1,0:T(8,128)(2,1)S(1)} %collective-permute-done.4.refs_2_.refs_7_.refs_11_.refs_4_.refs_8_) | copy-start | bytes 835588
  41.4 39.7 %collective-permute-start.18 = (bf16[128,1024]{1,0:T(8,128)(2,1)S(1)}, bf16[128,1024]{1,0:T(8,128)(2,1)S(1)}, u32[]{:S(2)}, u32[]{:S(2)}) collective-permute-start(bf16[128,1024]{1,0:T(8,128)(2,1)S(1)} %collective-permute-done.10.refs_18_.refs_26_), channel_id=1, source_target_pairs={{4,5},{5,4},{6,7},{7,6},{12,13},{13,12},{14,15},{15,14},{20,21},{2... | collective-permute-start | bytes 786440 | tf_op jit(solution)/shard_map/ppermute | solution.py:212
  60.4 20.7 %collective-permute-start.17 = (bf16[128,1024]{1,0:T(8,128)(2,1)S(1)}, bf16[128,1024]{1,0:T(8,128)(2,1)}, u32[]{:S(2)}, u32[]{:S(2)}) collective-permute-start(bf16[128,1024]{1,0:T(8,128)(2,1)S(1)} %collective-permute-done.11.refs_19_.refs_27_), channel_id=1, source_target_pairs={{4,5},{5,4},{6,7},{7,6},{12,13},{13,12},{14,15},{15,14},{20,21},{2... | collective-permute-start | bytes 786440 | tf_op jit(solution)/shard_map/ppermute | solution.py:212
  63.9 17.2 %collective-permute-start.20 = (bf16[128,1024]{1,0:T(8,128)(2,1)}, bf16[128,1024]{1,0:T(8,128)(2,1)}, u32[]{:S(2)}, u32[]{:S(2)}) collective-permute-start(bf16[128,1024]{1,0:T(8,128)(2,1)} %collective-permute-done.13.refs_20_.refs_28_), channel_id=1, source_target_pairs={{6,7},{7,6},{14,15},{15,14},{22,23},{23,22},{30,31},{31,30}} | collective-permute-start | bytes 786440 | tf_op jit(solution)/shard_map/ppermute | solution.py:212
  66.3 15.5 %collective-permute-start.19 = (bf16[128,1024]{1,0:T(8,128)(2,1)}, bf16[128,1024]{1,0:T(8,128)(2,1)}, u32[]{:S(2)}, u32[]{:S(2)}) collective-permute-start(bf16[128,1024]{1,0:T(8,128)(2,1)} %collective-permute-done.16.refs_21_.refs_29_), channel_id=1, source_target_pairs={{6,7},{7,6},{14,15},{15,14},{22,23},{23,22},{30,31},{31,30}} | collective-permute-start | bytes 786440 | tf_op jit(solution)/shard_map/ppermute | solution.py:212
  (3 other events, 11.8 us)

commit v10 on v9

--- a/solution.py
+++ b/solution.py
@@ -14,6 +14,7 @@
 GQ = H // KVH
 REACH = 7
 SLAB = 2
+BOTH = 2
 FILL = -1e30
 
 
@@ -40,28 +41,26 @@
     )(side.reshape(1), kv, kv)
 
 
-def attend_kernel(pairs, parts, tile, tiles, fresh, meta_ref, *refs):
+def attend_kernel(pairs, tile, tiles, fresh, meta_ref, *refs):
     s_ref, top_ref = refs[-2:]
-    inputs = 2 * parts + 4 * pairs
     if fresh:
-        seg_ref, *ints_refs = refs[: 1 + parts]
-        q_ref, *inputs = refs[1 + parts : 2 + parts + inputs]
-        o_ref, bias_ref, reach_ref = refs[-5:-2]
+        seg_ref, ints_ref, q_ref, *inputs = refs[: 5 + 4 * pairs]
+        o_ref, bias_ref, reach_ref, seg_k_ref = refs[5 + 4 * pairs : -2]
     else:
-        bias_ref, reach_ref, q_ref, *inputs = refs[: 3 + inputs]
+        bias_ref, reach_ref, q_ref, *inputs = refs[: 5 + 4 * pairs]
         o_ref = refs[-3]
-    pk_refs, pv_refs = inputs[:parts], inputs[parts : 2 * parts]
-    k_refs, v_refs = inputs[2 * parts :][: 2 * pairs], inputs[2 * parts + 2 * pairs :]
+    pk_ref, pv_ref, *inputs = inputs
+    k_refs, v_refs = inputs[: 2 * pairs], inputs[2 * pairs :]
     rows = q_ref.shape[0]
     step = 2 * rows
-    span = pk_refs[0].shape[0]
-    prefix_keys = parts * span
+    prefix_keys = pk_ref.shape[0]
     block, limit = meta_ref[0], meta_ref[2]
     scale = math.log2(math.e) / math.sqrt(HD)
     nt = (((1,), (1,)), ((), ()))
 
     def masks():
-        ints = jnp.concatenate([ref[...].astype(jnp.float32) for ref in ints_refs])
+        ints = ints_ref[...].astype(jnp.float32)
+        seg_k_ref[...] = ints
         row = lax.broadcasted_iota(jnp.int32, ints.shape, 0)
         part = lax.rem(row, tile)
         place = jnp.where(part == 0, pltpu.roll(ints, prefix_keys - 1, 0), ints)
@@ -71,15 +70,18 @@
         own = seg_ref[...].astype(jnp.float32)
         has_segs = lax.rem(row, tiles * tile) == 0
         earlier = jnp.sum(jnp.where(has_segs & (ints < own[:, :1]), 1.0, 0.0))
-        reach_ref[0] = lax.div(block, 2) - lax.div(earlier.astype(jnp.int32), step)
+        own_pair = lax.div(block, 2)
+        reach_ref[0] = own_pair - lax.div(earlier.astype(jnp.int32), step)
 
         seg_q = jnp.broadcast_to(own, (rows, rows)).T
         row_pos = block * rows + lax.broadcasted_iota(jnp.int32, (rows, rows), 0)
         lane = lax.broadcasted_iota(jnp.int32, (rows, rows), 1)
         for k in range(pairs):
+            pair = jnp.maximum(own_pair - k, 0)
             for j, first in enumerate((block, block + 1 - 2 * lax.rem(block, 2))):
-                at = (2 * k + j) * tiles * tile
-                seen = (ints[at : at + 1] == seg_q) & ((first - 2 * k) * rows + lane <= row_pos)
+                at = pl.multiple_of((2 * pair + j) * tiles * tile, tile)
+                seg_k = seg_k_ref[pl.ds(at, tile), :][:1]
+                seen = (seg_k == seg_q) & ((first - 2 * k) * rows + lane <= row_pos)
                 at = prefix_keys + (2 * k + j) * rows
                 bias_ref[:, at : at + rows] = jnp.where(seen, 0.0, FILL)
 
@@ -88,23 +90,20 @@
 
     def body(near):
         steps = prefix_keys // step + near + 1
-        each = step // span
-        keys = [
-            jnp.concatenate([ref[...] for ref in pk_refs[at : at + each]])
-            for at in range(0, parts, each)
-        ]
-        for k in range(near + 1):
-            keys.append(jnp.concatenate([k_refs[2 * k][...], k_refs[2 * k + 1][...]]))
-        values = jnp.concatenate([ref[...] for ref in (*pv_refs, *v_refs[: 2 * near + 2])])
-        values = jnp.concatenate([values, jnp.ones_like(values)], axis=1)
 
         def score(slab):
+            head = pl.ds(slab // (GQ // SLAB) * HD, HD)
             of = range(slab * SLAB, (slab + 1) * SLAB)
             q = jnp.concatenate([q_ref[:, g * HD : (g + 1) * HD] for g in of])
             top = None
             for i in range(steps):
                 at = slice(i * step, (i + 1) * step)
-                s = lax.dot_general(q, keys[i], nt, preferred_element_type=jnp.float32)
+                if i < prefix_keys // step:
+                    keys = pk_ref[at, head]
+                else:
+                    j = 2 * (i - prefix_keys // step)
+                    keys = jnp.concatenate([ref[:, head] for ref in k_refs[j : j + 2]])
+                s = lax.dot_general(q, keys, nt, preferred_element_type=jnp.float32)
                 s = (s.reshape(SLAB, rows, step) + bias_ref[:, at][None]).reshape(-1, step)
                 s_ref[slab % 2, :, at] = s
                 high = jnp.maximum(s[:, :rows], s[:, rows:])
@@ -113,6 +112,10 @@
             top_ref[slab % 2] = jnp.broadcast_to(top, (SLAB * rows, HD))
 
         def weigh(slab):
+            head = pl.ds(slab // (GQ // SLAB) * HD, HD)
+            values = [ref[:, head] for ref in (pv_ref, *v_refs[: 2 * near + 2])]
+            values = jnp.concatenate(values)
+            values = jnp.concatenate([values, jnp.ones_like(values)], axis=1)
             top = top_ref[slab % 2]
             weights = [
                 jnp.exp2((s_ref[slab % 2, :, i * HD : (i + 1) * HD] - top) * scale).astype(
@@ -128,9 +131,10 @@
                 g = slab * SLAB + j
                 o_ref[:, g * HD : (g + 1) * HD] = out[j * rows : (j + 1) * rows]
 
+        slabs = BOTH * GQ // SLAB
         score(0)
-        for slab in range(GQ // SLAB):
-            if slab + 1 < GQ // SLAB:
+        for slab in range(slabs):
+            if slab + 1 < slabs:
                 score(slab + 1)
             weigh(slab)
 
@@ -140,34 +144,32 @@
 
 def attend(meta, queries, pieces, prefix, tile, tiles, segments=None, before=None):
     rows = queries.shape[0]
-    span = prefix[0].shape[0]
-    pairs, parts = len(pieces) // 2, len(prefix)
+    prefix_keys = prefix.shape[0]
+    pairs = len(pieces) // 2
+    pieces, places = zip(*[piece if isinstance(piece, tuple) else (piece, 0) for piece in pieces])
     heads = pieces[0].shape[1] // (2 * HD)
-    keys = rows * len(pieces) + span * parts
+    blocks = heads // BOTH
+    keys = rows * len(pieces) + prefix_keys
     whole = pl.BlockSpec((rows, keys), lambda i, m: (0, 0))
     scalar = pl.BlockSpec(memory_space=pltpu.SMEM)
-    wide = pl.BlockSpec((rows, GQ * HD), lambda i, m: (0, m[1] + i))
+    wide = pl.BlockSpec((rows, BOTH * GQ * HD), lambda i, m: (0, m[1] + i))
     fresh = before is None
-    queries, *arrays = [
-        pltpu.with_memory_space_constraint(array, pltpu.HBM)
-        for array in (queries, *prefix, *pieces)
+    queries, prefix, *pieces = [
+        pltpu.with_memory_space_constraint(array, pltpu.HBM) for array in (queries, prefix, *pieces)
     ]
-    prefix, pieces = arrays[:parts], arrays[parts:]
-    args = [meta, *([segments, *prefix] if fresh else before[1:])]
-    args += [queries, *prefix, *prefix, *pieces, *pieces]
-    if fresh:
-        ints = pl.BlockSpec((span, rows), lambda i, m: (0, 2 * KVH))
-        in_specs = [pl.BlockSpec((1, rows), lambda i, m: (0, 0)), *[ints] * parts]
-    else:
-        in_specs = [whole, scalar]
+    args = [meta, *([segments, prefix] if fresh else before[1:])]
+    args += [queries, prefix, prefix, *pieces, *pieces]
+    ints = pl.BlockSpec((prefix_keys, rows), lambda i, m: (0, 2 * KVH))
+    in_specs = [pl.BlockSpec((1, rows), lambda i, m: (0, 0)), ints] if fresh else [whole, scalar]
     in_specs += [
         wide,
-        *[pl.BlockSpec((span, HD), lambda i, m: (0, m[1] + i))] * parts,
-        *[pl.BlockSpec((span, HD), lambda i, m: (0, KVH + m[1] + i))] * parts,
-        *[pl.BlockSpec((rows, HD), lambda i, m: (0, i))] * len(pieces),
-        *[pl.BlockSpec((rows, HD), lambda i, m: (0, heads + i))] * len(pieces),
+        pl.BlockSpec((prefix_keys, BOTH * HD), lambda i, m: (0, m[1] + i)),
+        pl.BlockSpec((prefix_keys, BOTH * HD), lambda i, m: (0, KVH // BOTH + m[1] + i)),
+        *[pl.BlockSpec((rows, BOTH * HD), lambda i, m, at=at: (at, i)) for at in places],
+        *[pl.BlockSpec((rows, BOTH * HD), lambda i, m, at=at: (at, blocks + i)) for at in places],
     ]
     out_specs = [wide]
+    scratch = []
     out_shape = [jax.ShapeDtypeStruct(queries.shape, queries.dtype)]
     aliases = {}
     if fresh:
@@ -176,18 +178,20 @@
             jax.ShapeDtypeStruct((rows, keys), jnp.float32),
             jax.ShapeDtypeStruct((1,), jnp.int32),
         ]
+        scratch = [pltpu.VMEM((prefix_keys, rows), jnp.float32)]
     else:
         args.append(before[0])
         in_specs.append(pl.BlockSpec(memory_space=pl.ANY))
         aliases = {len(args) - 1: 0}
     return pl.pallas_call(
-        functools.partial(attend_kernel, pairs, parts, tile, tiles, fresh),
+        functools.partial(attend_kernel, pairs, tile, tiles, fresh),
         grid_spec=pltpu.PrefetchScalarGridSpec(
             num_scalar_prefetch=1,
-            grid=(heads,),
+            grid=(blocks,),
             in_specs=in_specs,
             out_specs=out_specs,
             scratch_shapes=[
+                *scratch,
                 pltpu.VMEM((2, SLAB * rows, keys), jnp.float32),
                 pltpu.VMEM((2, SLAB * rows, HD), jnp.float32),
             ],
@@ -230,10 +234,14 @@
     for step in range(1, steps + 1):
         one, two = straight[-2:]
         if step > 2:
-            one, two = after(one, crossed[-3]), after(two, crossed[-4], upper)
+            two = after(two, crossed[2][0], upper)
         one, two = climb(one, step), climb(two, step)
         straight += [one, two]
-        crossed += [swap(two, step), swap(one, step)]
+        if step < steps:
+            both = swap(jnp.concatenate([two, one]), step)
+            crossed += [(both, 0), (both, 1)]
+        else:
+            crossed += [swap(two, step), swap(one, step)]
 
     owners = (group + jnp.arange(groups, dtype=jnp.int32)) % groups
     pick = tile_plan[None, :, 0] == owners[:, None]
@@ -247,11 +255,15 @@
     own_tiles = own_tiles.astype(prefix_kv.dtype)
     came = [own_tiles[0]] + [shift(own_tiles[by], "prompt", by) for by in range(1, groups)]
     came = jnp.concatenate(came)
-    prefix = [jnp.concatenate([came, swap(came, 0)])]
-    prefix += [shift(prefix[0], "resp", 2 * by) for by in range(1, count // 2)]
+    came = jnp.concatenate([came, swap(came, 0)])
+    came = jnp.broadcast_to(after(came, *straight[2:4])[None], (count // 2, *came.shape))
+    columns_of = [list(range(first, count, 2)) for first in range(2)]
+    prefix = lax.all_to_all(
+        came, "resp", split_axis=0, concat_axis=0, axis_index_groups=columns_of, tiled=True
+    ).reshape(-1, columns + rows)
 
     def meta(first):
-        return jnp.stack([block, first * (KVH // 2), prompt_lengths[0]])
+        return jnp.stack([block, first * (KVH // 2 // BOTH), prompt_lengths[0]])
 
     done = attend(
         meta(side), queries[0], straight, prefix, tile, tiles, segments=resp_segments

time: 93.8 us -> 102 us (1.087)
  waiting for transfers between devices: 22.5 us -> 40.9 us
  starting transfers between devices: 43.2 us -> 32.7 us
  local copies, waits for them, and re-layouts: 1.48 us -> 3.85 us
  Pallas kernels: 21.6 us -> 19.5 us
    ppermute x6, waiting for transfers between devices: 4.41 us -> 34.5 us  [climb(): return lax.ppermute(value, 'resp', pairs)]
    ppermute x6 -> x3, waiting for transfers between devices: 17.4 us -> 2.1 us  [shift(): lax.ppermute(value, axis, [(r, (r + by) % size) for r in range(size)])]
    ppermute x6 -> x3, starting transfers between devices: 11.4 us -> 2.05 us  [shift(): lax.ppermute(value, axis, [(r, (r + by) % size) for r in range(size)])]
    ppermute x8 -> x6, starting transfers between devices: 20.7 us -> 14.8 us  [swap(): lax.ppermute(value, 'resp', [(r, r ^ 1) for r in range(2 * first, count)])]
    all_to_all x0 -> x1, starting transfers between devices: none -> 5.78 us  [on_device(): lax.all_to_all(came, 'resp', split_axis=0, concat_axis=0, axis_index_grou...]
    ppermute x8 -> x6, waiting for transfers between devices: 0.66 us -> 4.35 us  [swap(): lax.ppermute(value, 'resp', [(r, r ^ 1) for r in range(2 * first, count)])]
    pallas_call x2, Pallas kernels: 19.7 us -> 17.6 us  [attend(): pl.pallas_call(functools.partial(attend_kernel, pairs, tile, tiles, fresh...]
    unnamed x31 -> x27, local copies, waits for them, and re-layouts: 0.71 us -> 2 us
  transfers between devices with their start and end apart: 21 -> 17, of which waited for: 6 -> 8; matrix products, arithmetic and copies ran while one was open for 3% -> 4% of each run, Pallas kernels for 10% -> 8%
where the time goes in v10:
time: 102 us; the launch traced here: 101 us
  waiting for transfers between devices  40.9 us (40%)
  starting transfers between devices  32.7 us (32%)
  Pallas kernels  19.5 us (19%)
  local copies, waits for them, and re-layouts  3.85 us (4%)
  other arithmetic  3.06 us (3%)
  between operations  1.11 us (1%)
    ppermute x6, waiting for transfers between devices, climb(): return lax.ppermute(value, 'resp', pairs)  34.5 us
    pallas_call x2, Pallas kernels, attend(): pl.pallas_call(functools.partial(attend_kernel, pairs, tile, tiles, fresh...  17.6 us
    ppermute x6, starting transfers between devices, swap(): lax.ppermute(value, 'resp', [(r, r ^ 1) for r in range(2 * first, count)])  14.8 us
    ppermute x6, starting transfers between devices, climb(): return lax.ppermute(value, 'resp', pairs)  7.73 us
    all_to_all x1, starting transfers between devices, on_device(): lax.all_to_all(came, 'resp', split_axis=0, concat_axis=0, axis_index_grou...  5.78 us
    ppermute x6, waiting for transfers between devices, swap(): lax.ppermute(value, 'resp', [(r, r ^ 1) for r in range(2 * first, count)])  4.35 us
    ppermute x1, starting transfers between devices, on_device(): upper = lax.ppermute(after(mine, partner), 'resp', upper)  2.43 us
    ppermute x3, waiting for transfers between devices, shift(): lax.ppermute(value, axis, [(r, (r + by) % size) for r in range(size)])  2.1 us
  transfers between devices with their start and end apart: 17, of which 8 were waited for; matrix products, arithmetic and copies ran while one was open for 4% of the time, Pallas kernels for 8%

profile of v10, /device:TPU:26, one launch (start us, length us, event | category | flops | bytes accessed | tf_op | source)
XLA Modules:
  0.0 101.1 jit_solution(8761445352462126321)
XLA Ops:
  0.0 1.9 %shard_map.64 = (bf16[128,1024]{1,0:T(8,128)(2,1)}, bf16[128,1024]{1,0:T(8,128)(2,1)}) custom-call(s32[1]{0:T(128)} %bitcast.10.meta_ref, bf16[128,2048]{1,0:T(8,128)(2,1)} %bitcast.30, bf16[128,2048]{1,0:T(8,128)(2,1)} %bitcast.31), custom_call_target="tpu_custom_call" | custom-call | tf_op jit(solution)/shard_map/pallas_call | solution.py:29
  1.9 1.5 %collective-permute-start.5 = (bf16[128,1024]{1,0:T(8,128)(2,1)}, bf16[128,1024]{1,0:T(8,128)(2,1)S(1)}, u32[]{:S(2)}, u32[]{:S(2)}) collective-permute-start(bf16[128,1024]{1,0:T(8,128)(2,1)} %get-tuple-element.14.refs_5_.refs_13_), channel_id=1, source_target_pairs={{0,1},{1,0},{2,3},{3,2},{4,5},{5,4},{6,7},{7,6},{8,9},{9,8},{10,11... | collective-permute-start | bytes 786440 | tf_op jit(solution)/shard_map/ppermute | solution.py:216
  3.4 1.3 %collective-permute-start.4 = (bf16[128,1024]{1,0:T(8,128)(2,1)}, bf16[128,1024]{1,0:T(8,128)(2,1)S(1)}, u32[]{:S(2)}, u32[]{:S(2)}) collective-permute-start(bf16[128,1024]{1,0:T(8,128)(2,1)} %get-tuple-element.16.refs_5_.refs_13_), channel_id=1, source_target_pairs={{0,2},{1,3},{2,4},{3,5},{4,6},{5,7},{8,10},{9,11},{10,12},{11,13},... | collective-permute-start | bytes 786440 | tf_op jit(solution)/shard_map/ppermute | solution.py:220
  4.7 0.8 slice_bitcast_fusion.1
  5.6 1.0 %select_reduce_fusion = bf16[4,8,2048]{2,1,0:T(8,128)(2,1)S(1)} fusion(pred[4,4]{1,0:T(4,128)(4,1)S(1)} %get-tuple-element.24, bf16[4,8,2048]{2,1,0:T(8,128)(2,1)} %param.9), kind=kLoop, calls=%fused_computation.2 | loop fusion | flops 458752 | bytes 262160 | tf_op jit(solution)/shard_map/reduce_sum | solution.py:249
  6.7 0.7 convert_convert_fusion
  8.1 1.4 %collective-permute-start.2 = (bf16[8,2176]{1,0:T(8,128)(2,1)S(1)}, bf16[8,2176]{1,0:T(8,128)(2,1)S(1)}, u32[]{:S(2)}, u32[]{:S(2)}) collective-permute-start(bf16[8,2176]{1,0:T(8,128)(2,1)S(1)} %get-tuple-element.25), channel_id=1, source_target_pairs={{0,24},{8,0},{16,8},{24,16},{1,25},{9,1},{17,9},{25,17},{2,26},{10... | collective-permute-start | bytes 104456 | tf_op jit(solution)/shard_map/ppermute | solution.py:224
  9.5 1.4 %collective-permute-done = bf16[8,2176]{1,0:T(8,128)(2,1)S(1)} collective-permute-done((bf16[8,2176]{1,0:T(8,128)(2,1)S(1)}, bf16[8,2176]{1,0:T(8,128)(2,1)S(1)}, u32[]{:S(2)}, u32[]{:S(2)}) %collective-permute-start) | collective-permute-done | bytes 34848 | tf_op jit(solution)/shard_map/ppermute | solution.py:224
  10.8 0.7 collective-permute-done.1
  12.2 1.3 %collective-permute-start.6 = (bf16[128,1024]{1,0:T(8,128)(2,1)S(1)}, bf16[128,1024]{1,0:T(8,128)(2,1)S(1)}, u32[]{:S(2)}, u32[]{:S(2)}) collective-permute-start(bf16[128,1024]{1,0:T(8,128)(2,1)S(1)} %collective-permute-done.5.refs_6_.refs_14_), channel_id=1, source_target_pairs={{0,2},{1,3},{2,4},{3,5},{4,6},{5,7},{8,10},{9,11},{10,12},{11,13},... | collective-permute-start | bytes 786440 | tf_op jit(solution)/shard_map/ppermute | solution.py:220
  13.5 4.3 %collective-permute-done.3 = bf16[32,2176]{1,0:T(8,128)(2,1)S(1)} collective-permute-done((bf16[32,2176]{1,0:T(8,128)(2,1)S(1)}, bf16[32,2176]{1,0:T(8,128)(2,1)S(1)}, u32[]{:S(2)}, u32[]{:S(2)}) %collective-permute-start.3) | collective-permute-done | bytes 139296 | tf_op jit(solution)/shard_map/ppermute | solution.py:216
  17.9 5.9 %collective-permute-done.6.refs_8_.refs_16_ = bf16[128,1024]{1,0:T(8,128)(2,1)S(1)} collective-permute-done((bf16[128,1024]{1,0:T(8,128)(2,1)S(1)}, bf16[128,1024]{1,0:T(8,128)(2,1)S(1)}, u32[]{:S(2)}, u32[]{:S(2)}) %collective-permute-start.6) | collective-permute-done | bytes 262176 | tf_op jit(solution)/shard_map/ppermute | solution.py:220
  23.8 1.1 %broadcast_in_dim.76 = bf16[4,64,2176]{2,1,0:T(8,128)(2,1)} broadcast(bf16[64,2176]{1,0:T(8,128)(2,1)S(1)} %constant_dynamic-update-slice_fusion), dimensions={1,2} | broadcast | bytes 1392640 | tf_op jit(solution)/shard_map/broadcast_in_dim | solution.py:259
  24.9 5.8 %all-to-all-start = ((bf16[4,64,2176]{2,1,0:T(8,128)(2,1)}), bf16[4,64,2176]{2,1,0:T(8,128)(2,1)S(1)}, u32[]{:S(2)}, u32[]{:S(2)}) async-start(bf16[4,64,2176]{2,1,0:T(8,128)(2,1)} %broadcast_in_dim.76), calls=%async_computation | async-start | bytes 2228224 | tf_op jit(solution)/shard_map/all_to_all | solution.py:261
  30.7 3.4 %collective-permute-start.10 = (bf16[256,1024]{1,0:T(8,128)(2,1)S(1)}, bf16[256,1024]{1,0:T(8,128)(2,1)S(1)}, u32[]{:S(2)}, u32[]{:S(2)}) collective-permute-start(bf16[256,1024]{1,0:T(8,128)(2,1)S(1)} %pad_maximum_fusion), channel_id=1, source_target_pairs={{2,3},{3,2},{4,5},{5,4},{6,7},{7,6},{10,11},{11,10},{12,13},{13,12... | collective-permute-start | bytes 1572872 | tf_op jit(solution)/shard_map/ppermute | solution.py:216
  34.1 1.3 %collective-permute-start.7 = (bf16[128,1024]{1,0:T(8,128)(2,1)S(1)}, bf16[128,1024]{1,0:T(8,128)(2,1)S(1)}, u32[]{:S(2)}, u32[]{:S(2)}) collective-permute-start(bf16[128,1024]{1,0:T(8,128)(2,1)S(1)} %collective-permute-done.4.refs_7_.refs_15_), channel_id=1, source_target_pairs={{2,4},{3,5},{4,6},{5,7},{10,12},{11,13},{12,14},{13,15},{18,20},{1... | collective-permute-start | bytes 786440 | tf_op jit(solution)/shard_map/ppermute | solution.py:220
  35.4 1.3 %collective-permute-start.8 = (bf16[128,1024]{1,0:T(8,128)(2,1)S(1)}, bf16[128,1024]{1,0:T(8,128)(2,1)S(1)}, u32[]{:S(2)}, u32[]{:S(2)}) collective-permute-start(bf16[128,1024]{1,0:T(8,128)(2,1)S(1)} %collective-permute-done.6.refs_8_.refs_16_), channel_id=1, source_target_pairs={{2,4},{3,5},{4,6},{5,7},{10,12},{11,13},{12,14},{13,15},{18,20},{1... | collective-permute-start | bytes 786440 | tf_op jit(solution)/shard_map/ppermute | solution.py:220
  36.7 2.4 %collective-permute-start.11 = (bf16[128,1024]{1,0:T(8,128)(2,1)}, bf16[128,1024]{1,0:T(8,128)(2,1)S(1)}, u32[]{:S(2)}, u32[]{:S(2)}) collective-permute-start(bf16[128,1024]{1,0:T(8,128)(2,1)} %get-tuple-element.16.refs_5_.refs_13_), channel_id=1, source_target_pairs={{0,1},{2,3},{4,5},{6,7},{8,9},{10,11},{12,13},{14,15},{16,17},{18,... | collective-permute-start | bytes 786440 | tf_op jit(solution)/shard_map/ppermute | solution.py:232
  39.2 16.1 %collective-permute-done.7.refs_9_.refs_17_ = bf16[128,1024]{1,0:T(8,128)(2,1)S(1)} collective-permute-done((bf16[128,1024]{1,0:T(8,128)(2,1)S(1)}, bf16[128,1024]{1,0:T(8,128)(2,1)S(1)}, u32[]{:S(2)}, u32[]{:S(2)}) %collective-permute-start.7) | collective-permute-done | bytes 262176 | tf_op jit(solution)/shard_map/ppermute | solution.py:220
  55.3 1.3 %collective-permute-start.9 = (bf16[128,1024]{1,0:T(8,128)(2,1)S(1)}, bf16[128,1024]{1,0:T(8,128)(2,1)}, u32[]{:S(2)}, u32[]{:S(2)}) collective-permute-start(bf16[128,1024]{1,0:T(8,128)(2,1)S(1)} %collective-permute-done.7.refs_9_.refs_17_), channel_id=1, source_target_pairs={{4,6},{5,7},{12,14},{13,15},{20,22},{21,23},{28,30},{29,31}} | collective-permute-start | bytes 786440 | tf_op jit(solution)/shard_map/ppermute | solution.py:220
  56.5 4.3 %collective-permute-done.8.refs_10_.refs_18_ = bf16[128,1024]{1,0:T(8,128)(2,1)S(1)} collective-permute-done((bf16[128,1024]{1,0:T(8,128)(2,1)S(1)}, bf16[128,1024]{1,0:T(8,128)(2,1)S(1)}, u32[]{:S(2)}, u32[]{:S(2)}) %collective-permute-start.8) | collective-permute-done | bytes 262176 | tf_op jit(solution)/shard_map/ppermute | solution.py:220
  60.8 0.9 pad_maximum_fusion.1
  61.7 3.4 %collective-permute-start.13 = (bf16[256,1024]{1,0:T(8,128)(2,1)}, bf16[256,1024]{1,0:T(8,128)(2,1)S(1)}, u32[]{:S(2)}, u32[]{:S(2)}) collective-permute-start(bf16[256,1024]{1,0:T(8,128)(2,1)} %pad_maximum_fusion.1), channel_id=1, source_target_pairs={{4,5},{5,4},{6,7},{7,6},{12,13},{13,12},{14,15},{15,14},{20,21},{2... | collective-permute-start | bytes 1572872 | tf_op jit(solution)/shard_map/ppermute | solution.py:216
  65.2 1.3 %collective-permute-start.12 = (bf16[128,1024]{1,0:T(8,128)(2,1)S(1)}, bf16[128,1024]{1,0:T(8,128)(2,1)}, u32[]{:S(2)}, u32[]{:S(2)}) collective-permute-start(bf16[128,1024]{1,0:T(8,128)(2,1)S(1)} %collective-permute-done.8.refs_10_.refs_18_), channel_id=1, source_target_pairs={{4,6},{5,7},{12,14},{13,15},{20,22},{21,23},{28,30},{29,31}} | collective-permute-start | bytes 786440 | tf_op jit(solution)/shard_map/ppermute | solution.py:220
  66.5 2.3 %collective-permute-done.9.refs_11_.refs_19_ = bf16[128,1024]{1,0:T(8,128)(2,1)} collective-permute-done((bf16[128,1024]{1,0:T(8,128)(2,1)S(1)}, bf16[128,1024]{1,0:T(8,128)(2,1)}, u32[]{:S(2)}, u32[]{:S(2)}) %collective-permute-start.9) | collective-permute-done | bytes 262176 | tf_op jit(solution)/shard_map/ppermute | solution.py:220
  68.8 3.4 %collective-permute-start.15 = (bf16[128,1024]{1,0:T(8,128)(2,1)}, bf16[128,1024]{1,0:T(8,128)(2,1)S(1)}, u32[]{:S(2)}, u32[]{:S(2)}) collective-permute-start(bf16[128,1024]{1,0:T(8,128)(2,1)} %collective-permute-done.9.refs_11_.refs_19_), channel_id=1, source_target_pairs={{6,7},{7,6},{14,15},{15,14},{22,23},{23,22},{30,31},{31,30}} | collective-permute-start | bytes 786440 | tf_op jit(solution)/shard_map/ppermute | solution.py:216
  72.2 5.9 %collective-permute-done.12.refs_12_.refs_20_ = bf16[128,1024]{1,0:T(8,128)(2,1)} collective-permute-done((bf16[128,1024]{1,0:T(8,128)(2,1)S(1)}, bf16[128,1024]{1,0:T(8,128)(2,1)}, u32[]{:S(2)}, u32[]{:S(2)}) %collective-permute-start.12) | collective-permute-done | bytes 262176 | tf_op jit(solution)/shard_map/ppermute | solution.py:220
  78.1 2.4 %collective-permute-start.14 = (bf16[128,1024]{1,0:T(8,128)(2,1)}, bf16[128,1024]{1,0:T(8,128)(2,1)S(1)}, u32[]{:S(2)}, u32[]{:S(2)}) collective-permute-start(bf16[128,1024]{1,0:T(8,128)(2,1)} %collective-permute-done.12.refs_12_.refs_20_), channel_id=1, source_target_pairs={{6,7},{7,6},{14,15},{15,14},{22,23},{23,22},{30,31},{31,30}} | collective-permute-start | bytes 786440 | tf_op jit(solution)/shard_map/ppermute | solution.py:216
  81.4 1.0 copy-done.1
  82.4 8.6 %shard_map.65 = (bf16[128,8192]{1,0:T(8,128)(2,1)}, f32[128,1280]{1,0:T(8,128)S(1)}, s32[1]{0:T(128)}) custom-call(s32[3]{0:T(128)S(1)} %add_add_fusion.1.meta_ref, s32[1,128]{1,0:T(1,128)S(1)} %copy-done, bf16[256,2176]{1,0:T(8,128)(2,1)} %bitcast.23, bf16[128,8192]{1,0:T(8,128)(2,1)} %bitcast.28, bf16[256,2176]{1,0:T(8,128)(2,1)} %bitcast.24, ...), custom_call_target="tpu_custom_call" | custom-call | tf_op jit(solution)/shard_map/pallas_call | solution.py:186
  91.0 0.6 copy-done.9
  92.0 9.0 %shard_map.66 = bf16[128,8192]{1,0:T(8,128)(2,1)} custom-call(s32[3]{0:T(128)S(1)} %add_add_fusion.meta_ref, f32[128,1280]{1,0:T(8,128)S(1)} %get-tuple-element.18.refs_0_, s32[1]{0:T(128)} %get-tuple-element.19.refs_1_, bf16[128,8192]{1,0:T(8,128)(2,1)} %bitcast.29, bf16[256,2176]{1,0:T(8,128)(2,1)} %bitcast.26, ...), custom_call_target="tpu_custom_call", output_to_operand_aliasing={{}: (22, {})} | custom-call | tf_op jit(solution)/shard_map/pallas_call | solution.py:186
  (47 shorter events, 2.0 us)
Async XLA Ops:
  1.9 10.3 %collective-permute-start.5 = (bf16[128,1024]{1,0:T(8,128)(2,1)}, bf16[128,1024]{1,0:T(8,128)(2,1)S(1)}, u32[]{:S(2)}, u32[]{:S(2)}) collective-permute-start(bf16[128,1024]{1,0:T(8,128)(2,1)} %get-tuple-element.14.refs_5_.refs_13_), channel_id=1, source_target_pairs={{0,1},{1,0},{2,3},{3,2},{4,5},{5,4},{6,7},{7,6},{8,9},{9,8},{10,11... | collective-permute-start | bytes 786440 | tf_op jit(solution)/shard_map/ppermute | solution.py:216
  3.4 14.5 %collective-permute-start.4 = (bf16[128,1024]{1,0:T(8,128)(2,1)}, bf16[128,1024]{1,0:T(8,128)(2,1)S(1)}, u32[]{:S(2)}, u32[]{:S(2)}) collective-permute-start(bf16[128,1024]{1,0:T(8,128)(2,1)} %get-tuple-element.16.refs_5_.refs_13_), channel_id=1, source_target_pairs={{0,2},{1,3},{2,4},{3,5},{4,6},{5,7},{8,10},{9,11},{10,12},{11,13},... | collective-permute-start | bytes 786440 | tf_op jit(solution)/shard_map/ppermute | solution.py:220
  7.4 3.4 %collective-permute-start = (bf16[8,2176]{1,0:T(8,128)(2,1)S(1)}, bf16[8,2176]{1,0:T(8,128)(2,1)S(1)}, u32[]{:S(2)}, u32[]{:S(2)}) collective-permute-start(bf16[8,2176]{1,0:T(8,128)(2,1)S(1)} %get-tuple-element.26), channel_id=1, source_target_pairs={{0,8},{8,16},{16,24},{24,0},{1,9},{9,17},{17,25},{25,1},{2,10},{10... | collective-permute-start | bytes 104456 | tf_op jit(solution)/shard_map/ppermute | solution.py:224
  7.5 4.1 %collective-permute-start.1 = (bf16[8,2176]{1,0:T(8,128)(2,1)S(1)}, bf16[8,2176]{1,0:T(8,128)(2,1)S(1)}, u32[]{:S(2)}, u32[]{:S(2)}) collective-permute-start(bf16[8,2176]{1,0:T(8,128)(2,1)S(1)} %get-tuple-element.27), channel_id=1, source_target_pairs={{0,16},{8,24},{16,0},{24,8},{1,17},{9,25},{17,1},{25,9},{2,18},{10... | collective-permute-start | bytes 104456 | tf_op jit(solution)/shard_map/ppermute | solution.py:224
  8.1 3.5 %collective-permute-start.2 = (bf16[8,2176]{1,0:T(8,128)(2,1)S(1)}, bf16[8,2176]{1,0:T(8,128)(2,1)S(1)}, u32[]{:S(2)}, u32[]{:S(2)}) collective-permute-start(bf16[8,2176]{1,0:T(8,128)(2,1)S(1)} %get-tuple-element.25), channel_id=1, source_target_pairs={{0,24},{8,0},{16,8},{24,16},{1,25},{9,1},{17,9},{25,17},{2,26},{10... | collective-permute-start | bytes 104456 | tf_op jit(solution)/shard_map/ppermute | solution.py:224
  11.6 6.3 %collective-permute-start.3 = (bf16[32,2176]{1,0:T(8,128)(2,1)S(1)}, bf16[32,2176]{1,0:T(8,128)(2,1)S(1)}, u32[]{:S(2)}, u32[]{:S(2)}) collective-permute-start(bf16[32,2176]{1,0:T(8,128)(2,1)S(1)} %pad_maximum_fusion.2), channel_id=1, source_target_pairs={{0,1},{1,0},{2,3},{3,2},{4,5},{5,4},{6,7},{7,6},{8,9},{9,8},{10,11... | collective-permute-start | bytes 417800 | tf_op jit(solution)/shard_map/ppermute | solution.py:216
  12.2 11.6 %copy-start.11 = (bf16[128,1024]{1,0:T(8,128)(2,1)}, bf16[128,1024]{1,0:T(8,128)(2,1)S(1)}, u32[]{:S(2)}) copy-start(bf16[128,1024]{1,0:T(8,128)(2,1)S(1)} %collective-permute-done.5.refs_6_.refs_14_) | copy-start | bytes 786436
  12.2 11.6 %collective-permute-start.6 = (bf16[128,1024]{1,0:T(8,128)(2,1)S(1)}, bf16[128,1024]{1,0:T(8,128)(2,1)S(1)}, u32[]{:S(2)}, u32[]{:S(2)}) collective-permute-start(bf16[128,1024]{1,0:T(8,128)(2,1)S(1)} %collective-permute-done.5.refs_6_.refs_14_), channel_id=1, source_target_pairs={{0,2},{1,3},{2,4},{3,5},{4,6},{5,7},{8,10},{9,11},{10,12},{11,13},... | collective-permute-start | bytes 786440 | tf_op jit(solution)/shard_map/ppermute | solution.py:220
  17.9 16.2 %copy-start.4 = (bf16[128,1024]{1,0:T(8,128)(2,1)}, bf16[128,1024]{1,0:T(8,128)(2,1)S(1)}, u32[]{:S(2)}) copy-start(bf16[128,1024]{1,0:T(8,128)(2,1)S(1)} %collective-permute-done.4.refs_7_.refs_15_) | copy-start | bytes 786436
  23.8 11.6 %copy-start.5 = (bf16[128,1024]{1,0:T(8,128)(2,1)}, bf16[128,1024]{1,0:T(8,128)(2,1)S(1)}, u32[]{:S(2)}) copy-start(bf16[128,1024]{1,0:T(8,128)(2,1)S(1)} %collective-permute-done.6.refs_8_.refs_16_) | copy-start | bytes 786436
  24.9 57.5 %copy-start = (s32[1,128]{1,0:T(1,128)S(1)}, s32[1,128]{1,0:T(1,128)}, u32[]{:S(2)}) copy-start(s32[1,128]{1,0:T(1,128)} %refs_0_.1) | copy-start | bytes 1540
  24.9 56.5 %all-to-all-start = ((bf16[4,64,2176]{2,1,0:T(8,128)(2,1)}), bf16[4,64,2176]{2,1,0:T(8,128)(2,1)S(1)}, u32[]{:S(2)}, u32[]{:S(2)}) async-start(bf16[4,64,2176]{2,1,0:T(8,128)(2,1)} %broadcast_in_dim.76), calls=%async_computation | async-start | bytes 2228224 | tf_op jit(solution)/shard_map/all_to_all | solution.py:261
  30.7 34.5 %collective-permute-start.10 = (bf16[256,1024]{1,0:T(8,128)(2,1)S(1)}, bf16[256,1024]{1,0:T(8,128)(2,1)S(1)}, u32[]{:S(2)}, u32[]{:S(2)}) collective-permute-start(bf16[256,1024]{1,0:T(8,128)(2,1)S(1)} %pad_maximum_fusion), channel_id=1, source_target_pairs={{2,3},{3,2},{4,5},{5,4},{6,7},{7,6},{10,11},{11,10},{12,13},{13,12... | collective-permute-start | bytes 1572872 | tf_op jit(solution)/shard_map/ppermute | solution.py:216
  34.1 21.1 %collective-permute-start.7 = (bf16[128,1024]{1,0:T(8,128)(2,1)S(1)}, bf16[128,1024]{1,0:T(8,128)(2,1)S(1)}, u32[]{:S(2)}, u32[]{:S(2)}) collective-permute-start(bf16[128,1024]{1,0:T(8,128)(2,1)S(1)} %collective-permute-done.4.refs_7_.refs_15_), channel_id=1, source_target_pairs={{2,4},{3,5},{4,6},{5,7},{10,12},{11,13},{12,14},{13,15},{18,20},{1... | collective-permute-start | bytes 786440 | tf_op jit(solution)/shard_map/ppermute | solution.py:220
  35.4 25.4 %collective-permute-start.8 = (bf16[128,1024]{1,0:T(8,128)(2,1)S(1)}, bf16[128,1024]{1,0:T(8,128)(2,1)S(1)}, u32[]{:S(2)}, u32[]{:S(2)}) collective-permute-start(bf16[128,1024]{1,0:T(8,128)(2,1)S(1)} %collective-permute-done.6.refs_8_.refs_16_), channel_id=1, source_target_pairs={{2,4},{3,5},{4,6},{5,7},{10,12},{11,13},{12,14},{13,15},{18,20},{1... | collective-permute-start | bytes 786440 | tf_op jit(solution)/shard_map/ppermute | solution.py:220
  36.7 28.4 %collective-permute-start.11 = (bf16[128,1024]{1,0:T(8,128)(2,1)}, bf16[128,1024]{1,0:T(8,128)(2,1)S(1)}, u32[]{:S(2)}, u32[]{:S(2)}) collective-permute-start(bf16[128,1024]{1,0:T(8,128)(2,1)} %get-tuple-element.16.refs_5_.refs_13_), channel_id=1, source_target_pairs={{0,1},{2,3},{4,5},{6,7},{8,9},{10,11},{12,13},{14,15},{16,17},{18,... | collective-permute-start | bytes 786440 | tf_op jit(solution)/shard_map/ppermute | solution.py:232
  55.3 26.1 %copy-start.6 = (bf16[128,1024]{1,0:T(8,128)(2,1)}, bf16[128,1024]{1,0:T(8,128)(2,1)S(1)}, u32[]{:S(2)}) copy-start(bf16[128,1024]{1,0:T(8,128)(2,1)S(1)} %collective-permute-done.7.refs_9_.refs_17_) | copy-start | bytes 786436
  55.3 13.6 %collective-permute-start.9 = (bf16[128,1024]{1,0:T(8,128)(2,1)S(1)}, bf16[128,1024]{1,0:T(8,128)(2,1)}, u32[]{:S(2)}, u32[]{:S(2)}) collective-permute-start(bf16[128,1024]{1,0:T(8,128)(2,1)S(1)} %collective-permute-done.7.refs_9_.refs_17_), channel_id=1, source_target_pairs={{4,6},{5,7},{12,14},{13,15},{20,22},{21,23},{28,30},{29,31}} | collective-permute-start | bytes 786440 | tf_op jit(solution)/shard_map/ppermute | solution.py:220
  60.8 20.5 %copy-start.7 = (bf16[128,1024]{1,0:T(8,128)(2,1)}, bf16[128,1024]{1,0:T(8,128)(2,1)S(1)}, u32[]{:S(2)}) copy-start(bf16[128,1024]{1,0:T(8,128)(2,1)S(1)} %collective-permute-done.8.refs_10_.refs_18_) | copy-start | bytes 786436
  61.7 29.3 %collective-permute-start.13 = (bf16[256,1024]{1,0:T(8,128)(2,1)}, bf16[256,1024]{1,0:T(8,128)(2,1)S(1)}, u32[]{:S(2)}, u32[]{:S(2)}) collective-permute-start(bf16[256,1024]{1,0:T(8,128)(2,1)} %pad_maximum_fusion.1), channel_id=1, source_target_pairs={{4,5},{5,4},{6,7},{7,6},{12,13},{13,12},{14,15},{15,14},{20,21},{2... | collective-permute-start | bytes 1572872 | tf_op jit(solution)/shard_map/ppermute | solution.py:216
  65.1 25.9 %copy-start.8 = (bf16[128,1024]{1,0:T(8,128)(2,1)}, bf16[128,1024]{1,0:T(8,128)(2,1)S(1)}, u32[]{:S(2)}) copy-start(bf16[128,1024]{1,0:T(8,128)(2,1)S(1)} %collective-permute-done.11.refs_6_.refs_14_) | copy-start | bytes 786436
  65.2 25.9 %copy-start.2 = (bf16[256,1024]{1,0:T(8,128)(2,1)}, bf16[256,1024]{1,0:T(8,128)(2,1)S(1)}, u32[]{:S(2)}) copy-start(bf16[256,1024]{1,0:T(8,128)(2,1)S(1)} %collective-permute-done.10.refs_7_.refs_8_.refs_15_.refs_16_) | copy-start | bytes 1572868
  65.2 12.9 %collective-permute-start.12 = (bf16[128,1024]{1,0:T(8,128)(2,1)S(1)}, bf16[128,1024]{1,0:T(8,128)(2,1)}, u32[]{:S(2)}, u32[]{:S(2)}) collective-permute-start(bf16[128,1024]{1,0:T(8,128)(2,1)S(1)} %collective-permute-done.8.refs_10_.refs_18_), channel_id=1, source_target_pairs={{4,6},{5,7},{12,14},{13,15},{20,22},{21,23},{28,30},{29,31}} | collective-permute-start | bytes 786440 | tf_op jit(solution)/shard_map/ppermute | solution.py:220
  68.8 22.1 %collective-permute-start.15 = (bf16[128,1024]{1,0:T(8,128)(2,1)}, bf16[128,1024]{1,0:T(8,128)(2,1)S(1)}, u32[]{:S(2)}, u32[]{:S(2)}) collective-permute-start(bf16[128,1024]{1,0:T(8,128)(2,1)} %collective-permute-done.9.refs_11_.refs_19_), channel_id=1, source_target_pairs={{6,7},{7,6},{14,15},{15,14},{22,23},{23,22},{30,31},{31,30}} | collective-permute-start | bytes 786440 | tf_op jit(solution)/shard_map/ppermute | solution.py:216
  78.1 12.9 %collective-permute-start.14 = (bf16[128,1024]{1,0:T(8,128)(2,1)}, bf16[128,1024]{1,0:T(8,128)(2,1)S(1)}, u32[]{:S(2)}, u32[]{:S(2)}) collective-permute-start(bf16[128,1024]{1,0:T(8,128)(2,1)} %collective-permute-done.12.refs_12_.refs_20_), channel_id=1, source_target_pairs={{6,7},{7,6},{14,15},{15,14},{22,23},{23,22},{30,31},{31,30}} | collective-permute-start | bytes 786440 | tf_op jit(solution)/shard_map/ppermute | solution.py:216
  81.3 1.0 %copy-start.1 = (bf16[4,64,2176]{2,1,0:T(8,128)(2,1)}, bf16[4,64,2176]{2,1,0:T(8,128)(2,1)S(1)}, u32[]{:S(2)}) copy-start(bf16[4,64,2176]{2,1,0:T(8,128)(2,1)S(1)} %all-to-all-done) | copy-start | bytes 3342340
  91.0 0.7 copy-start.9
  91.0 0.9 copy-start.3
  91.0 1.0 copy-start.10

commit v11 on v9

--- a/solution.py
+++ b/solution.py
@@ -14,6 +14,7 @@
 GQ = H // KVH
 REACH = 7
 SLAB = 2
+BOTH = 2
 FILL = -1e30
 
 
@@ -87,24 +88,20 @@
         pl.when(pl.program_id(0) == 0)(masks)
 
     def body(near):
+        each = step // span
         steps = prefix_keys // step + near + 1
-        each = step // span
-        keys = [
-            jnp.concatenate([ref[...] for ref in pk_refs[at : at + each]])
-            for at in range(0, parts, each)
-        ]
-        for k in range(near + 1):
-            keys.append(jnp.concatenate([k_refs[2 * k][...], k_refs[2 * k + 1][...]]))
-        values = jnp.concatenate([ref[...] for ref in (*pv_refs, *v_refs[: 2 * near + 2])])
-        values = jnp.concatenate([values, jnp.ones_like(values)], axis=1)
 
         def score(slab):
+            head = pl.ds(slab // (GQ // SLAB) * HD, HD)
             of = range(slab * SLAB, (slab + 1) * SLAB)
             q = jnp.concatenate([q_ref[:, g * HD : (g + 1) * HD] for g in of])
+            refs_of = [pk_refs[at : at + each] for at in range(0, parts, each)]
+            refs_of += [k_refs[2 * k : 2 * k + 2] for k in range(near + 1)]
             top = None
             for i in range(steps):
                 at = slice(i * step, (i + 1) * step)
-                s = lax.dot_general(q, keys[i], nt, preferred_element_type=jnp.float32)
+                keys = jnp.concatenate([ref[:, head] for ref in refs_of[i]])
+                s = lax.dot_general(q, keys, nt, preferred_element_type=jnp.float32)
                 s = (s.reshape(SLAB, rows, step) + bias_ref[:, at][None]).reshape(-1, step)
                 s_ref[slab % 2, :, at] = s
                 high = jnp.maximum(s[:, :rows], s[:, rows:])
@@ -113,6 +110,10 @@
             top_ref[slab % 2] = jnp.broadcast_to(top, (SLAB * rows, HD))
 
         def weigh(slab):
+            head = pl.ds(slab // (GQ // SLAB) * HD, HD)
+            values = [ref[:, head] for ref in (*pv_refs, *v_refs[: 2 * near + 2])]
+            values = jnp.concatenate(values)
+            values = jnp.concatenate([values, jnp.ones_like(values)], axis=1)
             top = top_ref[slab % 2]
             weights = [
                 jnp.exp2((s_ref[slab % 2, :, i * HD : (i + 1) * HD] - top) * scale).astype(
@@ -128,9 +129,10 @@
                 g = slab * SLAB + j
                 o_ref[:, g * HD : (g + 1) * HD] = out[j * rows : (j + 1) * rows]
 
+        slabs = BOTH * GQ // SLAB
         score(0)
-        for slab in range(GQ // SLAB):
-            if slab + 1 < GQ // SLAB:
+        for slab in range(slabs):
+            if slab + 1 < slabs:
                 score(slab + 1)
             weigh(slab)
 
@@ -142,11 +144,13 @@
     rows = queries.shape[0]
     span = prefix[0].shape[0]
     pairs, parts = len(pieces) // 2, len(prefix)
+    pieces, places = zip(*[piece if isinstance(piece, tuple) else (piece, 0) for piece in pieces])
     heads = pieces[0].shape[1] // (2 * HD)
+    blocks = heads // BOTH
     keys = rows * len(pieces) + span * parts
     whole = pl.BlockSpec((rows, keys), lambda i, m: (0, 0))
     scalar = pl.BlockSpec(memory_space=pltpu.SMEM)
-    wide = pl.BlockSpec((rows, GQ * HD), lambda i, m: (0, m[1] + i))
+    wide = pl.BlockSpec((rows, BOTH * GQ * HD), lambda i, m: (0, m[1] + i))
     fresh = before is None
     queries, *arrays = [
         pltpu.with_memory_space_constraint(array, pltpu.HBM)
@@ -162,10 +166,10 @@
         in_specs = [whole, scalar]
     in_specs += [
         wide,
-        *[pl.BlockSpec((span, HD), lambda i, m: (0, m[1] + i))] * parts,
-        *[pl.BlockSpec((span, HD), lambda i, m: (0, KVH + m[1] + i))] * parts,
-        *[pl.BlockSpec((rows, HD), lambda i, m: (0, i))] * len(pieces),
-        *[pl.BlockSpec((rows, HD), lambda i, m: (0, heads + i))] * len(pieces),
+        *[pl.BlockSpec((span, BOTH * HD), lambda i, m: (0, m[1] + i))] * parts,
+        *[pl.BlockSpec((span, BOTH * HD), lambda i, m: (0, KVH // BOTH + m[1] + i))] * parts,
+        *[pl.BlockSpec((rows, BOTH * HD), lambda i, m, at=at: (at, i)) for at in places],
+        *[pl.BlockSpec((rows, BOTH * HD), lambda i, m, at=at: (at, blocks + i)) for at in places],
     ]
     out_specs = [wide]
     out_shape = [jax.ShapeDtypeStruct(queries.shape, queries.dtype)]
@@ -184,7 +188,7 @@
         functools.partial(attend_kernel, pairs, parts, tile, tiles, fresh),
         grid_spec=pltpu.PrefetchScalarGridSpec(
             num_scalar_prefetch=1,
-            grid=(heads,),
+            grid=(blocks,),
             in_specs=in_specs,
             out_specs=out_specs,
             scratch_shapes=[
@@ -230,10 +234,14 @@
     for step in range(1, steps + 1):
         one, two = straight[-2:]
         if step > 2:
-            one, two = after(one, crossed[-3]), after(two, crossed[-4], upper)
+            two = after(two, crossed[2][0], upper)
         one, two = climb(one, step), climb(two, step)
         straight += [one, two]
-        crossed += [swap(two, step), swap(one, step)]
+        if step < steps:
+            both = swap(jnp.concatenate([two, one]), step)
+            crossed += [(both, 0), (both, 1)]
+        else:
+            crossed += [swap(two, step), swap(one, step)]
 
     owners = (group + jnp.arange(groups, dtype=jnp.int32)) % groups
     pick = tile_plan[None, :, 0] == owners[:, None]
@@ -248,10 +256,12 @@
     came = [own_tiles[0]] + [shift(own_tiles[by], "prompt", by) for by in range(1, groups)]
     came = jnp.concatenate(came)
     prefix = [jnp.concatenate([came, swap(came, 0)])]
-    prefix += [shift(prefix[0], "resp", 2 * by) for by in range(1, count // 2)]
+    for by in range(1, count // 2):
+        source = after(prefix[0], straight[min(2 * by + 1, len(straight) - 2)])
+        prefix.append(shift(source, "resp", 2 * by))
 
     def meta(first):
-        return jnp.stack([block, first * (KVH // 2), prompt_lengths[0]])
+        return jnp.stack([block, first * (KVH // 2 // BOTH), prompt_lengths[0]])
 
     done = attend(
         meta(side), queries[0], straight, prefix, tile, tiles, segments=resp_segments

time: 93.8 us -> 99 us (1.055); the launches traced: 92 us -> 99.3 us
  waiting for transfers between devices: 22.5 us -> 46.9 us
  starting transfers between devices: 43.2 us -> 23.5 us
    ppermute x6, waiting for transfers between devices: 4.41 us -> 39.8 us  [climb(): return lax.ppermute(value, 'resp', pairs)]
    ppermute x6, waiting for transfers between devices: 17.4 us -> 7.04 us  [shift(): lax.ppermute(value, axis, [(r, (r + by) % size) for r in range(size)])]
    ppermute x8 -> x6, starting transfers between devices: 20.7 us -> 11.3 us  [swap(): lax.ppermute(value, 'resp', [(r, r ^ 1) for r in range(2 * first, count)])]
    ppermute x6, starting transfers between devices: 11.4 us -> 2.11 us  [shift(): lax.ppermute(value, axis, [(r, (r + by) % size) for r in range(size)])]
    ppermute x1, starting transfers between devices: 3.44 us -> 2.43 us  [on_device(): upper = lax.ppermute(after(mine, partner), 'resp', upper)]
  transfers between devices with their start and end apart: 21 -> 19, of which waited for: 6 -> 8; matrix products, arithmetic and copies ran while one was open for 3% -> 4% of each run, Pallas kernels for 10% -> 10%
where the time goes in v11:
time: 99 us; the launch traced here: 99.3 us
  waiting for transfers between devices  46.9 us (47%)
  starting transfers between devices  23.5 us (24%)
  Pallas kernels  22.4 us (23%)
  other arithmetic  3.07 us (3%)
  local copies, waits for them, and re-layouts  2.3 us (2%)
  between operations  1.16 us (1%)
    ppermute x6, waiting for transfers between devices, climb(): return lax.ppermute(value, 'resp', pairs)  39.8 us
    pallas_call x2, Pallas kernels, attend(): pl.pallas_call(functools.partial(attend_kernel, pairs, parts, tile, tiles...  20.5 us
    ppermute x6, starting transfers between devices, swap(): lax.ppermute(value, 'resp', [(r, r ^ 1) for r in range(2 * first, count)])  11.3 us
    ppermute x6, starting transfers between devices, climb(): return lax.ppermute(value, 'resp', pairs)  7.73 us
    ppermute x6, waiting for transfers between devices, shift(): lax.ppermute(value, axis, [(r, (r + by) % size) for r in range(size)])  7.04 us
    ppermute x1, starting transfers between devices, on_device(): upper = lax.ppermute(after(mine, partner), 'resp', upper)  2.43 us
    ppermute x6, starting transfers between devices, shift(): lax.ppermute(value, axis, [(r, (r + by) % size) for r in range(size)])  2.11 us
  transfers between devices with their start and end apart: 19, of which 8 were waited for; matrix products, arithmetic and copies ran while one was open for 4% of the time, Pallas kernels for 10%

profile of v11, /device:TPU:26, one launch (start us, length us, event | category | flops | bytes accessed | tf_op | source)
XLA Modules:
  0.0 99.3 jit_solution(4166066965773592324)
XLA Ops:
  0.0 1.9 %shard_map.64 = (bf16[128,1024]{1,0:T(8,128)(2,1)}, bf16[128,1024]{1,0:T(8,128)(2,1)}) custom-call(s32[1]{0:T(128)} %bitcast.10.meta_ref, bf16[128,2048]{1,0:T(8,128)(2,1)} %bitcast.24, bf16[128,2048]{1,0:T(8,128)(2,1)} %bitcast.25), custom_call_target="tpu_custom_call" | custom-call | tf_op jit(solution)/shard_map/pallas_call | solution.py:29
  1.9 1.5 %collective-permute-start.4 = (bf16[128,1024]{1,0:T(8,128)(2,1)}, bf16[128,1024]{1,0:T(8,128)(2,1)S(1)}, u32[]{:S(2)}, u32[]{:S(2)}) collective-permute-start(bf16[128,1024]{1,0:T(8,128)(2,1)} %get-tuple-element.15.refs_11_.refs_19_), channel_id=1, source_target_pairs={{0,1},{1,0},{2,3},{3,2},{4,5},{5,4},{6,7},{7,6},{8,9},{9,8},{10,11... | collective-permute-start | bytes 786440 | tf_op jit(solution)/shard_map/ppermute | solution.py:216
  3.4 1.3 %collective-permute-start.9 = (bf16[128,1024]{1,0:T(8,128)(2,1)}, bf16[128,1024]{1,0:T(8,128)(2,1)S(1)}, u32[]{:S(2)}, u32[]{:S(2)}) collective-permute-start(bf16[128,1024]{1,0:T(8,128)(2,1)} %get-tuple-element.20.refs_14_.refs_22_), channel_id=1, source_target_pairs={{0,2},{1,3},{2,4},{3,5},{4,6},{5,7},{8,10},{9,11},{10,12},{11,13},... | collective-permute-start | bytes 786440 | tf_op jit(solution)/shard_map/ppermute | solution.py:220
  4.7 0.8 slice_bitcast_fusion.1
  5.7 1.0 %select_reduce_fusion = bf16[4,8,2048]{2,1,0:T(8,128)(2,1)S(1)} fusion(pred[4,4]{1,0:T(4,128)(4,1)S(1)} %get-tuple-element.28, bf16[4,8,2048]{2,1,0:T(8,128)(2,1)} %param.9), kind=kLoop, calls=%fused_computation.2 | loop fusion | flops 458752 | bytes 262160 | tf_op jit(solution)/shard_map/reduce_sum | solution.py:249
  6.7 0.7 convert_convert_fusion
  7.5 0.6 collective-permute-start.1
  8.1 1.4 %collective-permute-start.2 = (bf16[8,2176]{1,0:T(8,128)(2,1)S(1)}, bf16[8,2176]{1,0:T(8,128)(2,1)S(1)}, u32[]{:S(2)}, u32[]{:S(2)}) collective-permute-start(bf16[8,2176]{1,0:T(8,128)(2,1)S(1)} %get-tuple-element.29), channel_id=1, source_target_pairs={{0,24},{8,0},{16,8},{24,16},{1,25},{9,1},{17,9},{25,17},{2,26},{10... | collective-permute-start | bytes 104456 | tf_op jit(solution)/shard_map/ppermute | solution.py:224
  9.5 1.4 %collective-permute-done = bf16[8,2176]{1,0:T(8,128)(2,1)S(1)} collective-permute-done((bf16[8,2176]{1,0:T(8,128)(2,1)S(1)}, bf16[8,2176]{1,0:T(8,128)(2,1)S(1)}, u32[]{:S(2)}, u32[]{:S(2)}) %collective-permute-start) | collective-permute-done | bytes 34848 | tf_op jit(solution)/shard_map/ppermute | solution.py:224
  10.9 0.7 collective-permute-done.1
  11.6 0.6 collective-permute-start.3
  12.2 1.3 %collective-permute-start.5 = (bf16[128,1024]{1,0:T(8,128)(2,1)S(1)}, bf16[128,1024]{1,0:T(8,128)(2,1)S(1)}, u32[]{:S(2)}, u32[]{:S(2)}) collective-permute-start(bf16[128,1024]{1,0:T(8,128)(2,1)S(1)} %collective-permute-done.4.refs_15_.refs_23_), channel_id=1, source_target_pairs={{0,2},{1,3},{2,4},{3,5},{4,6},{5,7},{8,10},{9,11},{10,12},{11,13},... | collective-permute-start | bytes 786440 | tf_op jit(solution)/shard_map/ppermute | solution.py:220
  13.6 10.2 %collective-permute-done.5.refs_17_.refs_25_ = bf16[128,1024]{1,0:T(8,128)(2,1)S(1)} collective-permute-done((bf16[128,1024]{1,0:T(8,128)(2,1)S(1)}, bf16[128,1024]{1,0:T(8,128)(2,1)S(1)}, u32[]{:S(2)}, u32[]{:S(2)}) %collective-permute-start.5) | collective-permute-done | bytes 262176 | tf_op jit(solution)/shard_map/ppermute | solution.py:220
  23.8 3.4 %collective-permute-start.13 = (bf16[256,1024]{1,0:T(8,128)(2,1)S(1)}, bf16[256,1024]{1,0:T(8,128)(2,1)S(1)}, u32[]{:S(2)}, u32[]{:S(2)}) collective-permute-start(bf16[256,1024]{1,0:T(8,128)(2,1)S(1)} %pad_maximum_fusion), channel_id=1, source_target_pairs={{2,3},{3,2},{4,5},{5,4},{6,7},{7,6},{10,11},{11,10},{12,13},{13,12... | collective-permute-start | bytes 1572872 | tf_op jit(solution)/shard_map/ppermute | solution.py:216
  27.3 2.4 %collective-permute-start.14 = (bf16[128,1024]{1,0:T(8,128)(2,1)S(1)}, bf16[128,1024]{1,0:T(8,128)(2,1)S(1)}, u32[]{:S(2)}, u32[]{:S(2)}) collective-permute-start(bf16[128,1024]{1,0:T(8,128)(2,1)S(1)} %copy-done.12), channel_id=1, source_target_pairs={{0,1},{2,3},{4,5},{6,7},{8,9},{10,11},{12,13},{14,15},{16,17},{18,... | collective-permute-start | bytes 786440 | tf_op jit(solution)/shard_map/ppermute | solution.py:232
  29.7 1.3 %collective-permute-start.10 = (bf16[128,1024]{1,0:T(8,128)(2,1)S(1)}, bf16[128,1024]{1,0:T(8,128)(2,1)S(1)}, u32[]{:S(2)}, u32[]{:S(2)}) collective-permute-start(bf16[128,1024]{1,0:T(8,128)(2,1)S(1)} %collective-permute-done.9.refs_16_.refs_24_), channel_id=1, source_target_pairs={{2,4},{3,5},{4,6},{5,7},{10,12},{11,13},{12,14},{13,15},{18,20},{1... | collective-permute-start | bytes 786440 | tf_op jit(solution)/shard_map/ppermute | solution.py:220
  31.0 1.3 %collective-permute-start.7 = (bf16[128,1024]{1,0:T(8,128)(2,1)S(1)}, bf16[128,1024]{1,0:T(8,128)(2,1)S(1)}, u32[]{:S(2)}, u32[]{:S(2)}) collective-permute-start(bf16[128,1024]{1,0:T(8,128)(2,1)S(1)} %collective-permute-done.5.refs_17_.refs_25_), channel_id=1, source_target_pairs={{2,4},{3,5},{4,6},{5,7},{10,12},{11,13},{12,14},{13,15},{18,20},{1... | collective-permute-start | bytes 786440 | tf_op jit(solution)/shard_map/ppermute | solution.py:220
  32.4 8.4 %collective-permute-done.10.refs_18_.refs_26_ = bf16[128,1024]{1,0:T(8,128)(2,1)S(1)} collective-permute-done((bf16[128,1024]{1,0:T(8,128)(2,1)S(1)}, bf16[128,1024]{1,0:T(8,128)(2,1)S(1)}, u32[]{:S(2)}, u32[]{:S(2)}) %collective-permute-start.10) | collective-permute-done | bytes 262176 | tf_op jit(solution)/shard_map/ppermute | solution.py:220
  40.8 1.3 %collective-permute-start.11 = (bf16[128,1024]{1,0:T(8,128)(2,1)S(1)}, bf16[128,1024]{1,0:T(8,128)(2,1)}, u32[]{:S(2)}, u32[]{:S(2)}) collective-permute-start(bf16[128,1024]{1,0:T(8,128)(2,1)S(1)} %collective-permute-done.10.refs_18_.refs_26_), channel_id=1, source_target_pairs={{4,6},{5,7},{12,14},{13,15},{20,22},{21,23},{28,30},{29,31}} | collective-permute-start | bytes 786440 | tf_op jit(solution)/shard_map/ppermute | solution.py:220
  42.1 4.3 %collective-permute-done.7.refs_19_.refs_27_ = bf16[128,1024]{1,0:T(8,128)(2,1)S(1)} collective-permute-done((bf16[128,1024]{1,0:T(8,128)(2,1)S(1)}, bf16[128,1024]{1,0:T(8,128)(2,1)S(1)}, u32[]{:S(2)}, u32[]{:S(2)}) %collective-permute-start.7) | collective-permute-done | bytes 262176 | tf_op jit(solution)/shard_map/ppermute | solution.py:220
  46.5 0.9 pad_maximum_fusion.1
  47.4 1.9 %collective-permute-start.16 = (bf16[256,1024]{1,0:T(8,128)(2,1)}, bf16[256,1024]{1,0:T(8,128)(2,1)S(1)}, u32[]{:S(2)}, u32[]{:S(2)}) collective-permute-start(bf16[256,1024]{1,0:T(8,128)(2,1)} %pad_maximum_fusion.1), channel_id=1, source_target_pairs={{4,5},{5,4},{6,7},{7,6},{12,13},{13,12},{14,15},{15,14},{20,21},{2... | collective-permute-start | bytes 1572872 | tf_op jit(solution)/shard_map/ppermute | solution.py:216
  49.3 1.3 %collective-permute-start.15 = (bf16[128,1024]{1,0:T(8,128)(2,1)S(1)}, bf16[128,1024]{1,0:T(8,128)(2,1)}, u32[]{:S(2)}, u32[]{:S(2)}) collective-permute-start(bf16[128,1024]{1,0:T(8,128)(2,1)S(1)} %collective-permute-done.7.refs_19_.refs_27_), channel_id=1, source_target_pairs={{4,6},{5,7},{12,14},{13,15},{20,22},{21,23},{28,30},{29,31}} | collective-permute-start | bytes 786440 | tf_op jit(solution)/shard_map/ppermute | solution.py:220
  50.6 7.5 %collective-permute-done.11.refs_20_.refs_28_ = bf16[128,1024]{1,0:T(8,128)(2,1)} collective-permute-done((bf16[128,1024]{1,0:T(8,128)(2,1)S(1)}, bf16[128,1024]{1,0:T(8,128)(2,1)}, u32[]{:S(2)}, u32[]{:S(2)}) %collective-permute-start.11) | collective-permute-done | bytes 262176 | tf_op jit(solution)/shard_map/ppermute | solution.py:220
  58.2 1.9 %collective-permute-start.18 = (bf16[128,1024]{1,0:T(8,128)(2,1)}, bf16[128,1024]{1,0:T(8,128)(2,1)}, u32[]{:S(2)}, u32[]{:S(2)}) collective-permute-start(bf16[128,1024]{1,0:T(8,128)(2,1)} %collective-permute-done.11.refs_20_.refs_28_), channel_id=1, source_target_pairs={{6,7},{7,6},{14,15},{15,14},{22,23},{23,22},{30,31},{31,30}} | collective-permute-start | bytes 786440 | tf_op jit(solution)/shard_map/ppermute | solution.py:216
  60.1 9.3 %collective-permute-done.15.refs_21_.refs_29_ = bf16[128,1024]{1,0:T(8,128)(2,1)} collective-permute-done((bf16[128,1024]{1,0:T(8,128)(2,1)S(1)}, bf16[128,1024]{1,0:T(8,128)(2,1)}, u32[]{:S(2)}, u32[]{:S(2)}) %collective-permute-start.15) | collective-permute-done | bytes 262176 | tf_op jit(solution)/shard_map/ppermute | solution.py:220
  69.4 1.9 %collective-permute-start.17 = (bf16[128,1024]{1,0:T(8,128)(2,1)}, bf16[128,1024]{1,0:T(8,128)(2,1)}, u32[]{:S(2)}, u32[]{:S(2)}) collective-permute-start(bf16[128,1024]{1,0:T(8,128)(2,1)} %collective-permute-done.15.refs_21_.refs_29_), channel_id=1, source_target_pairs={{6,7},{7,6},{14,15},{15,14},{22,23},{23,22},{30,31},{31,30}} | collective-permute-start | bytes 786440 | tf_op jit(solution)/shard_map/ppermute | solution.py:216
  72.2 4.9 %collective-permute-done.8.refs_3_.refs_8_.refs_12_.refs_5_.refs_9_ = bf16[64,2176]{1,0:T(8,128)(2,1)S(1)} collective-permute-done((bf16[64,2176]{1,0:T(8,128)(2,1)S(1)}, bf16[64,2176]{1,0:T(8,128)(2,1)S(1)}, u32[]{:S(2)}, u32[]{:S(2)}) %collective-permute-start.8) | collective-permute-done | bytes 278560 | tf_op jit(solution)/shard_map/ppermute | solution.py:224
  77.1 0.7 copy-done.6
  77.8 9.9 %shard_map.65 = (bf16[128,8192]{1,0:T(8,128)(2,1)}, f32[128,1280]{1,0:T(8,128)S(1)}, s32[1]{0:T(128)}) custom-call(s32[3]{0:T(128)S(1)} %add_add_fusion.1.meta_ref, s32[1,128]{1,0:T(1,128)S(1)} %copy-done, bf16[64,2176]{1,0:T(8,128)(2,1)} %copy-done.3, bf16[64,2176]{1,0:T(8,128)(2,1)} %copy-done.4, bf16[64,2176]{1,0:T(8,128)(2,1)} %copy-done.6, ...), custom_call_target="tpu_custom_call" | custom-call | tf_op jit(solution)/shard_map/pallas_call | solution.py:187
  87.8 0.8 copy-done.2
  88.6 10.5 %shard_map.66 = bf16[128,8192]{1,0:T(8,128)(2,1)} custom-call(s32[3]{0:T(128)S(1)} %add_add_fusion.meta_ref, f32[128,1280]{1,0:T(8,128)S(1)} %get-tuple-element.22.refs_0_, s32[1]{0:T(128)} %get-tuple-element.23.refs_1_, bf16[128,8192]{1,0:T(8,128)(2,1)} %bitcast.23, bf16[64,2176]{1,0:T(8,128)(2,1)} %copy-done.3, ...), custom_call_target="tpu_custom_call", output_to_operand_aliasing={{}: (28, {})} | custom-call | tf_op jit(solution)/shard_map/pallas_call | solution.py:187
  (54 shorter events, 0.7 us)
Async XLA Ops:
  0.0 77.8 %copy-start = (s32[1,128]{1,0:T(1,128)S(1)}, s32[1,128]{1,0:T(1,128)}, u32[]{:S(2)}) copy-start(s32[1,128]{1,0:T(1,128)} %refs_0_.1) | copy-start | bytes 1540
  1.9 25.4 %copy-start.12 = (bf16[128,1024]{1,0:T(8,128)(2,1)S(1)}, bf16[128,1024]{1,0:T(8,128)(2,1)}, u32[]{:S(2)}) copy-start(bf16[128,1024]{1,0:T(8,128)(2,1)} %get-tuple-element.20.refs_14_.refs_22_) | copy-start | bytes 786436
  1.9 10.3 %collective-permute-start.4 = (bf16[128,1024]{1,0:T(8,128)(2,1)}, bf16[128,1024]{1,0:T(8,128)(2,1)S(1)}, u32[]{:S(2)}, u32[]{:S(2)}) collective-permute-start(bf16[128,1024]{1,0:T(8,128)(2,1)} %get-tuple-element.15.refs_11_.refs_19_), channel_id=1, source_target_pairs={{0,1},{1,0},{2,3},{3,2},{4,5},{5,4},{6,7},{7,6},{8,9},{9,8},{10,11... | collective-permute-start | bytes 786440 | tf_op jit(solution)/shard_map/ppermute | solution.py:216
  3.4 10.1 %collective-permute-start.9 = (bf16[128,1024]{1,0:T(8,128)(2,1)}, bf16[128,1024]{1,0:T(8,128)(2,1)S(1)}, u32[]{:S(2)}, u32[]{:S(2)}) collective-permute-start(bf16[128,1024]{1,0:T(8,128)(2,1)} %get-tuple-element.20.refs_14_.refs_22_), channel_id=1, source_target_pairs={{0,2},{1,3},{2,4},{3,5},{4,6},{5,7},{8,10},{9,11},{10,12},{11,13},... | collective-permute-start | bytes 786440 | tf_op jit(solution)/shard_map/ppermute | solution.py:220
  7.5 3.4 %collective-permute-start = (bf16[8,2176]{1,0:T(8,128)(2,1)S(1)}, bf16[8,2176]{1,0:T(8,128)(2,1)S(1)}, u32[]{:S(2)}, u32[]{:S(2)}) collective-permute-start(bf16[8,2176]{1,0:T(8,128)(2,1)S(1)} %get-tuple-element.30), channel_id=1, source_target_pairs={{0,8},{8,16},{16,24},{24,0},{1,9},{9,17},{17,25},{25,1},{2,10},{10... | collective-permute-start | bytes 104456 | tf_op jit(solution)/shard_map/ppermute | solution.py:224
  7.5 4.1 %collective-permute-start.1 = (bf16[8,2176]{1,0:T(8,128)(2,1)S(1)}, bf16[8,2176]{1,0:T(8,128)(2,1)S(1)}, u32[]{:S(2)}, u32[]{:S(2)}) collective-permute-start(bf16[8,2176]{1,0:T(8,128)(2,1)S(1)} %get-tuple-element.31), channel_id=1, source_target_pairs={{0,16},{8,24},{16,0},{24,8},{1,17},{9,25},{17,1},{25,9},{2,18},{10... | collective-permute-start | bytes 104456 | tf_op jit(solution)/shard_map/ppermute | solution.py:224
  8.1 3.5 %collective-permute-start.2 = (bf16[8,2176]{1,0:T(8,128)(2,1)S(1)}, bf16[8,2176]{1,0:T(8,128)(2,1)S(1)}, u32[]{:S(2)}, u32[]{:S(2)}) collective-permute-start(bf16[8,2176]{1,0:T(8,128)(2,1)S(1)} %get-tuple-element.29), channel_id=1, source_target_pairs={{0,24},{8,0},{16,8},{24,16},{1,25},{9,1},{17,9},{25,17},{2,26},{10... | collective-permute-start | bytes 104456 | tf_op jit(solution)/shard_map/ppermute | solution.py:224
  11.6 20.7 %collective-permute-start.3 = (bf16[32,2176]{1,0:T(8,128)(2,1)S(1)}, bf16[32,2176]{1,0:T(8,128)(2,1)S(1)}, u32[]{:S(2)}, u32[]{:S(2)}) collective-permute-start(bf16[32,2176]{1,0:T(8,128)(2,1)S(1)} %pad_maximum_fusion.2), channel_id=1, source_target_pairs={{0,1},{1,0},{2,3},{3,2},{4,5},{5,4},{6,7},{7,6},{8,9},{9,8},{10,11... | collective-permute-start | bytes 417800 | tf_op jit(solution)/shard_map/ppermute | solution.py:216
  12.2 38.4 %copy-start.13 = (bf16[128,1024]{1,0:T(8,128)(2,1)}, bf16[128,1024]{1,0:T(8,128)(2,1)S(1)}, u32[]{:S(2)}) copy-start(bf16[128,1024]{1,0:T(8,128)(2,1)S(1)} %collective-permute-done.4.refs_15_.refs_23_) | copy-start | bytes 786436
  12.2 11.6 %collective-permute-start.5 = (bf16[128,1024]{1,0:T(8,128)(2,1)S(1)}, bf16[128,1024]{1,0:T(8,128)(2,1)S(1)}, u32[]{:S(2)}, u32[]{:S(2)}) collective-permute-start(bf16[128,1024]{1,0:T(8,128)(2,1)S(1)} %collective-permute-done.4.refs_15_.refs_23_), channel_id=1, source_target_pairs={{0,2},{1,3},{2,4},{3,5},{4,6},{5,7},{8,10},{9,11},{10,12},{11,13},... | collective-permute-start | bytes 786440 | tf_op jit(solution)/shard_map/ppermute | solution.py:220
  13.6 63.5 %copy-start.7 = (bf16[128,1024]{1,0:T(8,128)(2,1)}, bf16[128,1024]{1,0:T(8,128)(2,1)S(1)}, u32[]{:S(2)}) copy-start(bf16[128,1024]{1,0:T(8,128)(2,1)S(1)} %collective-permute-done.9.refs_16_.refs_24_) | copy-start | bytes 786436
  23.8 53.3 %copy-start.8 = (bf16[128,1024]{1,0:T(8,128)(2,1)}, bf16[128,1024]{1,0:T(8,128)(2,1)S(1)}, u32[]{:S(2)}) copy-start(bf16[128,1024]{1,0:T(8,128)(2,1)S(1)} %collective-permute-done.5.refs_17_.refs_25_) | copy-start | bytes 786436
  23.8 25.5 %collective-permute-start.13 = (bf16[256,1024]{1,0:T(8,128)(2,1)S(1)}, bf16[256,1024]{1,0:T(8,128)(2,1)S(1)}, u32[]{:S(2)}, u32[]{:S(2)}) collective-permute-start(bf16[256,1024]{1,0:T(8,128)(2,1)S(1)} %pad_maximum_fusion), channel_id=1, source_target_pairs={{2,3},{3,2},{4,5},{5,4},{6,7},{7,6},{10,11},{11,10},{12,13},{13,12... | collective-permute-start | bytes 1572872 | tf_op jit(solution)/shard_map/ppermute | solution.py:216
  27.3 22.0 %collective-permute-start.14 = (bf16[128,1024]{1,0:T(8,128)(2,1)S(1)}, bf16[128,1024]{1,0:T(8,128)(2,1)S(1)}, u32[]{:S(2)}, u32[]{:S(2)}) collective-permute-start(bf16[128,1024]{1,0:T(8,128)(2,1)S(1)} %copy-done.12), channel_id=1, source_target_pairs={{0,1},{2,3},{4,5},{6,7},{8,9},{10,11},{12,13},{14,15},{16,17},{18,... | collective-permute-start | bytes 786440 | tf_op jit(solution)/shard_map/ppermute | solution.py:232
  29.7 11.1 %collective-permute-start.10 = (bf16[128,1024]{1,0:T(8,128)(2,1)S(1)}, bf16[128,1024]{1,0:T(8,128)(2,1)S(1)}, u32[]{:S(2)}, u32[]{:S(2)}) collective-permute-start(bf16[128,1024]{1,0:T(8,128)(2,1)S(1)} %collective-permute-done.9.refs_16_.refs_24_), channel_id=1, source_target_pairs={{2,4},{3,5},{4,6},{5,7},{10,12},{11,13},{12,14},{13,15},{18,20},{1... | collective-permute-start | bytes 786440 | tf_op jit(solution)/shard_map/ppermute | solution.py:220
  31.0 15.4 %collective-permute-start.7 = (bf16[128,1024]{1,0:T(8,128)(2,1)S(1)}, bf16[128,1024]{1,0:T(8,128)(2,1)S(1)}, u32[]{:S(2)}, u32[]{:S(2)}) collective-permute-start(bf16[128,1024]{1,0:T(8,128)(2,1)S(1)} %collective-permute-done.5.refs_17_.refs_25_), channel_id=1, source_target_pairs={{2,4},{3,5},{4,6},{5,7},{10,12},{11,13},{12,14},{13,15},{18,20},{1... | collective-permute-start | bytes 786440 | tf_op jit(solution)/shard_map/ppermute | solution.py:220
  32.4 44.7 %copy-start.3 = (bf16[64,2176]{1,0:T(8,128)(2,1)}, bf16[64,2176]{1,0:T(8,128)(2,1)S(1)}, u32[]{:S(2)}) copy-start(bf16[64,2176]{1,0:T(8,128)(2,1)S(1)} %constant_dynamic-update-slice_fusion.refs_1_.refs_6_.refs_10_.refs_3_.refs_7_) | copy-start | bytes 835588
  32.4 25.8 %collective-permute-start.6 = (bf16[64,2176]{1,0:T(8,128)(2,1)S(1)}, bf16[64,2176]{1,0:T(8,128)(2,1)S(1)}, u32[]{:S(2)}, u32[]{:S(2)}) collective-permute-start(bf16[64,2176]{1,0:T(8,128)(2,1)S(1)} %constant_dynamic-update-slice_fusion.refs_1_.refs_6_.refs_10_.refs_3_.refs_7_), channel_id=1, source_target_pairs={{0,2},{1,3},{2,4},{3,5},{4,6},{5,7},{6,0},{7,1},{8,10},{9,11},{10,... | collective-permute-start | bytes 835592 | tf_op jit(solution)/shard_map/ppermute | solution.py:224
  40.8 36.3 %copy-start.9 = (bf16[128,1024]{1,0:T(8,128)(2,1)}, bf16[128,1024]{1,0:T(8,128)(2,1)S(1)}, u32[]{:S(2)}) copy-start(bf16[128,1024]{1,0:T(8,128)(2,1)S(1)} %collective-permute-done.10.refs_18_.refs_26_) | copy-start | bytes 786436
  40.8 17.3 %collective-permute-start.11 = (bf16[128,1024]{1,0:T(8,128)(2,1)S(1)}, bf16[128,1024]{1,0:T(8,128)(2,1)}, u32[]{:S(2)}, u32[]{:S(2)}) collective-permute-start(bf16[128,1024]{1,0:T(8,128)(2,1)S(1)} %collective-permute-done.10.refs_18_.refs_26_), channel_id=1, source_target_pairs={{4,6},{5,7},{12,14},{13,15},{20,22},{21,23},{28,30},{29,31}} | collective-permute-start | bytes 786440 | tf_op jit(solution)/shard_map/ppermute | solution.py:220
  46.5 30.7 %copy-start.10 = (bf16[128,1024]{1,0:T(8,128)(2,1)}, bf16[128,1024]{1,0:T(8,128)(2,1)S(1)}, u32[]{:S(2)}) copy-start(bf16[128,1024]{1,0:T(8,128)(2,1)S(1)} %collective-permute-done.7.refs_19_.refs_27_) | copy-start | bytes 786436
  47.4 40.4 %collective-permute-start.16 = (bf16[256,1024]{1,0:T(8,128)(2,1)}, bf16[256,1024]{1,0:T(8,128)(2,1)S(1)}, u32[]{:S(2)}, u32[]{:S(2)}) collective-permute-start(bf16[256,1024]{1,0:T(8,128)(2,1)} %pad_maximum_fusion.1), channel_id=1, source_target_pairs={{4,5},{5,4},{6,7},{7,6},{12,13},{13,12},{14,15},{15,14},{20,21},{2... | collective-permute-start | bytes 1572872 | tf_op jit(solution)/shard_map/ppermute | solution.py:216
  49.3 38.5 %copy-start.11 = (bf16[128,1024]{1,0:T(8,128)(2,1)}, bf16[128,1024]{1,0:T(8,128)(2,1)S(1)}, u32[]{:S(2)}) copy-start(bf16[128,1024]{1,0:T(8,128)(2,1)S(1)} %collective-permute-done.14.refs_12_.refs_20_) | copy-start | bytes 786436
  49.3 38.5 %copy-start.1 = (bf16[256,1024]{1,0:T(8,128)(2,1)}, bf16[256,1024]{1,0:T(8,128)(2,1)S(1)}, u32[]{:S(2)}) copy-start(bf16[256,1024]{1,0:T(8,128)(2,1)S(1)} %collective-permute-done.13.refs_13_.refs_14_.refs_21_.refs_22_) | copy-start | bytes 1572868
  49.3 20.1 %collective-permute-start.15 = (bf16[128,1024]{1,0:T(8,128)(2,1)S(1)}, bf16[128,1024]{1,0:T(8,128)(2,1)}, u32[]{:S(2)}, u32[]{:S(2)}) collective-permute-start(bf16[128,1024]{1,0:T(8,128)(2,1)S(1)} %collective-permute-done.7.refs_19_.refs_27_), channel_id=1, source_target_pairs={{4,6},{5,7},{12,14},{13,15},{20,22},{21,23},{28,30},{29,31}} | collective-permute-start | bytes 786440 | tf_op jit(solution)/shard_map/ppermute | solution.py:220
  58.2 14.0 %collective-permute-start.12 = (bf16[64,2176]{1,0:T(8,128)(2,1)S(1)}, bf16[64,2176]{1,0:T(8,128)(2,1)S(1)}, u32[]{:S(2)}, u32[]{:S(2)}) collective-permute-start(bf16[64,2176]{1,0:T(8,128)(2,1)S(1)} %constant_dynamic-update-slice_fusion.refs_1_.refs_6_.refs_10_.refs_3_.refs_7_), channel_id=1, source_target_pairs={{0,6},{1,7},{2,0},{3,1},{4,2},{5,3},{6,4},{7,5},{8,14},{9,15},{10,... | collective-permute-start | bytes 835592 | tf_op jit(solution)/shard_map/ppermute | solution.py:224
  58.2 18.9 %collective-permute-start.8 = (bf16[64,2176]{1,0:T(8,128)(2,1)S(1)}, bf16[64,2176]{1,0:T(8,128)(2,1)S(1)}, u32[]{:S(2)}, u32[]{:S(2)}) collective-permute-start(bf16[64,2176]{1,0:T(8,128)(2,1)S(1)} %constant_dynamic-update-slice_fusion.refs_1_.refs_6_.refs_10_.refs_3_.refs_7_), channel_id=1, source_target_pairs={{0,4},{1,5},{2,6},{3,7},{4,0},{5,1},{6,2},{7,3},{8,12},{9,13},{10,... | collective-permute-start | bytes 835592 | tf_op jit(solution)/shard_map/ppermute | solution.py:224
  58.2 19.0 %copy-start.4 = (bf16[64,2176]{1,0:T(8,128)(2,1)}, bf16[64,2176]{1,0:T(8,128)(2,1)S(1)}, u32[]{:S(2)}) copy-start(bf16[64,2176]{1,0:T(8,128)(2,1)S(1)} %collective-permute-done.6.refs_2_.refs_7_.refs_11_.refs_4_.refs_8_) | copy-start | bytes 835588
  58.2 29.6 %collective-permute-start.18 = (bf16[128,1024]{1,0:T(8,128)(2,1)}, bf16[128,1024]{1,0:T(8,128)(2,1)}, u32[]{:S(2)}, u32[]{:S(2)}) collective-permute-start(bf16[128,1024]{1,0:T(8,128)(2,1)} %collective-permute-done.11.refs_20_.refs_28_), channel_id=1, source_target_pairs={{6,7},{7,6},{14,15},{15,14},{22,23},{23,22},{30,31},{31,30}} | collective-permute-start | bytes 786440 | tf_op jit(solution)/shard_map/ppermute | solution.py:216
  69.4 18.4 %collective-permute-start.17 = (bf16[128,1024]{1,0:T(8,128)(2,1)}, bf16[128,1024]{1,0:T(8,128)(2,1)}, u32[]{:S(2)}, u32[]{:S(2)}) collective-permute-start(bf16[128,1024]{1,0:T(8,128)(2,1)} %collective-permute-done.15.refs_21_.refs_29_), channel_id=1, source_target_pairs={{6,7},{7,6},{14,15},{15,14},{22,23},{23,22},{30,31},{31,30}} | collective-permute-start | bytes 786440 | tf_op jit(solution)/shard_map/ppermute | solution.py:216
  72.2 5.0 %copy-start.5 = (bf16[64,2176]{1,0:T(8,128)(2,1)}, bf16[64,2176]{1,0:T(8,128)(2,1)S(1)}, u32[]{:S(2)}) copy-start(bf16[64,2176]{1,0:T(8,128)(2,1)S(1)} %collective-permute-done.12.refs_4_.refs_9_.refs_13_.refs_6_.refs_10_) | copy-start | bytes 835588
  87.8 0.8 copy-start.2
  (1 other events, 0.7 us)

commit v12 on v11

--- a/solution.py
+++ b/solution.py
@@ -234,14 +234,10 @@
     for step in range(1, steps + 1):
         one, two = straight[-2:]
         if step > 2:
-            two = after(two, crossed[2][0], upper)
+            one, two = after(one, crossed[-3]), after(two, crossed[-4], upper)
         one, two = climb(one, step), climb(two, step)
         straight += [one, two]
-        if step < steps:
-            both = swap(jnp.concatenate([two, one]), step)
-            crossed += [(both, 0), (both, 1)]
-        else:
-            crossed += [swap(two, step), swap(one, step)]
+        crossed += [swap(two, step), swap(one, step)]
 
     owners = (group + jnp.arange(groups, dtype=jnp.int32)) % groups
     pick = tile_plan[None, :, 0] == owners[:, None]
@@ -256,8 +252,9 @@
     came = [own_tiles[0]] + [shift(own_tiles[by], "prompt", by) for by in range(1, groups)]
     came = jnp.concatenate(came)
     prefix = [jnp.concatenate([came, swap(came, 0)])]
+    behind = [(), (crossed[5], straight[5]), (straight[6],)]
     for by in range(1, count // 2):
-        source = after(prefix[0], straight[min(2 * by + 1, len(straight) - 2)])
+        source = after(prefix[0], *behind[min(by, len(behind)) - 1])
         prefix.append(shift(source, "resp", 2 * by))
 
     def meta(first):

time: 99 us -> 87 us (0.88)
  the two profiles are of different devices: /device:TPU:26 before, /device:TPU:27 now
where the time goes in v12:
time: 87 us; the launch traced here: 86.5 us
  starting transfers between devices  38.1 us (44%)
  Pallas kernels  22.4 us (26%)
  waiting for transfers between devices  21.1 us (24%)
  other arithmetic  2.14 us (2%)
  local copies, waits for them, and re-layouts  1.61 us (2%)
  between operations  1.2 us (1%)
    ppermute x8, starting transfers between devices, swap(): lax.ppermute(value, 'resp', [(r, r ^ 1) for r in range(2 * first, count)])  22.8 us
    pallas_call x2, Pallas kernels, attend(): pl.pallas_call(functools.partial(attend_kernel, pairs, parts, tile, tiles...  20.5 us
    ppermute x6, waiting for transfers between devices, climb(): return lax.ppermute(value, 'resp', pairs)  11 us
    ppermute x6, waiting for transfers between devices, shift(): lax.ppermute(value, axis, [(r, (r + by) % size) for r in range(size)])  9.14 us
    ppermute x6, starting transfers between devices, climb(): return lax.ppermute(value, 'resp', pairs)  7.71 us
    ppermute x6, starting transfers between devices, shift(): lax.ppermute(value, axis, [(r, (r + by) % size) for r in range(size)])  5.42 us
    ppermute x1, starting transfers between devices, on_device(): upper = lax.ppermute(after(mine, partner), 'resp', upper)  2.15 us
    pallas_call x1, Pallas kernels, halves(): pl.pallas_call(halves_kernel, grid_spec=pltpu.PrefetchScalarGridSpec(num_...  1.85 us
  transfers between devices with their start and end apart: 21, of which 9 were waited for; matrix products, arithmetic and copies ran while one was open for 3% of the time, Pallas kernels for 11%

profile of v12, /device:TPU:27, one launch (start us, length us, event | category | flops | bytes accessed | tf_op | source)
XLA Modules:
  0.0 86.5 jit_solution(1304108397668606319)
XLA Ops:
  0.0 1.9 %shard_map.64 = (bf16[128,1024]{1,0:T(8,128)(2,1)}, bf16[128,1024]{1,0:T(8,128)(2,1)}) custom-call(s32[1]{0:T(128)} %bitcast.10.meta_ref, bf16[128,2048]{1,0:T(8,128)(2,1)} %bitcast.24, bf16[128,2048]{1,0:T(8,128)(2,1)} %bitcast.25), custom_call_target="tpu_custom_call" | custom-call | tf_op jit(solution)/shard_map/pallas_call | solution.py:29
  1.9 1.2 %collective-permute-start.8 = (bf16[128,1024]{1,0:T(8,128)(2,1)}, bf16[128,1024]{1,0:T(8,128)(2,1)S(1)}, u32[]{:S(2)}, u32[]{:S(2)}) collective-permute-start(bf16[128,1024]{1,0:T(8,128)(2,1)} %get-tuple-element.16.refs_11_.refs_19_), channel_id=1, source_target_pairs={{0,1},{1,0},{2,3},{3,2},{4,5},{5,4},{6,7},{7,6},{8,9},{9,8},{10,11... | collective-permute-start | bytes 786440 | tf_op jit(solution)/shard_map/ppermute | solution.py:216
  3.1 1.3 %collective-permute-start.5 = (bf16[128,1024]{1,0:T(8,128)(2,1)}, bf16[128,1024]{1,0:T(8,128)(2,1)S(1)}, u32[]{:S(2)}, u32[]{:S(2)}) collective-permute-start(bf16[128,1024]{1,0:T(8,128)(2,1)} %get-tuple-element.20.refs_14_.refs_22_), channel_id=1, source_target_pairs={{0,2},{1,3},{2,4},{3,5},{4,6},{5,7},{8,10},{9,11},{10,12},{11,13},... | collective-permute-start | bytes 786440 | tf_op jit(solution)/shard_map/ppermute | solution.py:220
  4.4 0.8 slice_bitcast_fusion.1
  5.4 1.0 %select_reduce_fusion = bf16[4,8,2048]{2,1,0:T(8,128)(2,1)S(1)} fusion(pred[4,4]{1,0:T(4,128)(4,1)S(1)} %get-tuple-element.28, bf16[4,8,2048]{2,1,0:T(8,128)(2,1)} %param.9), kind=kLoop, calls=%fused_computation | loop fusion | flops 458752 | bytes 262160 | tf_op jit(solution)/shard_map/reduce_sum | solution.py:245
  6.4 0.7 convert_convert_fusion
  7.1 1.1 %collective-permute-start = (bf16[8,2176]{1,0:T(8,128)(2,1)S(1)}, bf16[8,2176]{1,0:T(8,128)(2,1)S(1)}, u32[]{:S(2)}, u32[]{:S(2)}) collective-permute-start(bf16[8,2176]{1,0:T(8,128)(2,1)S(1)} %get-tuple-element.30), channel_id=1, source_target_pairs={{0,8},{8,16},{16,24},{24,0},{1,9},{9,17},{17,25},{25,1},{2,10},{10... | collective-permute-start | bytes 104456 | tf_op jit(solution)/shard_map/ppermute | solution.py:224
  8.3 1.2 %collective-permute-start.1 = (bf16[8,2176]{1,0:T(8,128)(2,1)S(1)}, bf16[8,2176]{1,0:T(8,128)(2,1)S(1)}, u32[]{:S(2)}, u32[]{:S(2)}) collective-permute-start(bf16[8,2176]{1,0:T(8,128)(2,1)S(1)} %get-tuple-element.31), channel_id=1, source_target_pairs={{0,16},{8,24},{16,0},{24,8},{1,17},{9,25},{17,1},{25,9},{2,18},{10... | collective-permute-start | bytes 104456 | tf_op jit(solution)/shard_map/ppermute | solution.py:224
  9.5 2.1 %collective-permute-done.1 = bf16[8,2176]{1,0:T(8,128)(2,1)S(1)} collective-permute-done((bf16[8,2176]{1,0:T(8,128)(2,1)S(1)}, bf16[8,2176]{1,0:T(8,128)(2,1)S(1)}, u32[]{:S(2)}, u32[]{:S(2)}) %collective-permute-start.1) | collective-permute-done | bytes 34848 | tf_op jit(solution)/shard_map/ppermute | solution.py:224
  11.6 1.5 %collective-permute-done.2 = bf16[8,2176]{1,0:T(8,128)(2,1)S(1)} collective-permute-done((bf16[8,2176]{1,0:T(8,128)(2,1)S(1)}, bf16[8,2176]{1,0:T(8,128)(2,1)S(1)}, u32[]{:S(2)}, u32[]{:S(2)}) %collective-permute-start.2) | collective-permute-done | bytes 34848 | tf_op jit(solution)/shard_map/ppermute | solution.py:224
  13.2 0.3 collective-permute-start.3
  13.5 1.3 %collective-permute-start.6 = (bf16[128,1024]{1,0:T(8,128)(2,1)S(1)}, bf16[128,1024]{1,0:T(8,128)(2,1)S(1)}, u32[]{:S(2)}, u32[]{:S(2)}) collective-permute-start(bf16[128,1024]{1,0:T(8,128)(2,1)S(1)} %collective-permute-done.5.refs_16_.refs_24_), channel_id=1, source_target_pairs={{2,4},{3,5},{4,6},{5,7},{10,12},{11,13},{12,14},{13,15},{18,20},{1... | collective-permute-start | bytes 786440 | tf_op jit(solution)/shard_map/ppermute | solution.py:220
  14.8 3.1 %collective-permute-start.12 = (bf16[128,1024]{1,0:T(8,128)(2,1)S(1)}, bf16[128,1024]{1,0:T(8,128)(2,1)S(1)}, u32[]{:S(2)}, u32[]{:S(2)}) collective-permute-start(bf16[128,1024]{1,0:T(8,128)(2,1)S(1)} %collective-permute-done.5.refs_16_.refs_24_), channel_id=1, source_target_pairs={{2,3},{3,2},{4,5},{5,4},{6,7},{7,6},{10,11},{11,10},{12,13},{13,12... | collective-permute-start | bytes 786440 | tf_op jit(solution)/shard_map/ppermute | solution.py:216
  18.0 1.3 %collective-permute-start.9 = (bf16[128,1024]{1,0:T(8,128)(2,1)S(1)}, bf16[128,1024]{1,0:T(8,128)(2,1)S(1)}, u32[]{:S(2)}, u32[]{:S(2)}) collective-permute-start(bf16[128,1024]{1,0:T(8,128)(2,1)S(1)} %collective-permute-done.8.refs_15_.refs_23_), channel_id=1, source_target_pairs={{0,2},{1,3},{2,4},{3,5},{4,6},{5,7},{8,10},{9,11},{10,12},{11,13},... | collective-permute-start | bytes 786440 | tf_op jit(solution)/shard_map/ppermute | solution.py:220
  19.3 2.1 %collective-permute-start.16 = (bf16[128,1024]{1,0:T(8,128)(2,1)}, bf16[128,1024]{1,0:T(8,128)(2,1)S(1)}, u32[]{:S(2)}, u32[]{:S(2)}) collective-permute-start(bf16[128,1024]{1,0:T(8,128)(2,1)} %get-tuple-element.20.refs_14_.refs_22_), channel_id=1, source_target_pairs={{0,1},{2,3},{4,5},{6,7},{8,9},{10,11},{12,13},{14,15},{16,17},{18,... | collective-permute-start | bytes 786440 | tf_op jit(solution)/shard_map/ppermute | solution.py:232
  21.4 2.6 %collective-permute-done.6.refs_18_.refs_26_ = bf16[128,1024]{1,0:T(8,128)(2,1)S(1)} collective-permute-done((bf16[128,1024]{1,0:T(8,128)(2,1)S(1)}, bf16[128,1024]{1,0:T(8,128)(2,1)S(1)}, u32[]{:S(2)}, u32[]{:S(2)}) %collective-permute-start.6) | collective-permute-done | bytes 262176 | tf_op jit(solution)/shard_map/ppermute | solution.py:220
  24.2 1.3 %collective-permute-start.13 = (bf16[128,1024]{1,0:T(8,128)(2,1)S(1)}, bf16[128,1024]{1,0:T(8,128)(2,1)S(1)}, u32[]{:S(2)}, u32[]{:S(2)}) collective-permute-start(bf16[128,1024]{1,0:T(8,128)(2,1)S(1)} %collective-permute-done.6.refs_18_.refs_26_), channel_id=1, source_target_pairs={{4,6},{5,7},{12,14},{13,15},{20,22},{21,23},{28,30},{29,31}} | collective-permute-start | bytes 786440 | tf_op jit(solution)/shard_map/ppermute | solution.py:220
  25.5 4.0 %collective-permute-start.7 = (bf16[128,1024]{1,0:T(8,128)(2,1)S(1)}, bf16[128,1024]{1,0:T(8,128)(2,1)S(1)}, u32[]{:S(2)}, u32[]{:S(2)}) collective-permute-start(bf16[128,1024]{1,0:T(8,128)(2,1)S(1)} %collective-permute-done.6.refs_18_.refs_26_), channel_id=1, source_target_pairs={{4,5},{5,4},{6,7},{7,6},{12,13},{13,12},{14,15},{15,14},{20,21},{2... | collective-permute-start | bytes 786440 | tf_op jit(solution)/shard_map/ppermute | solution.py:216
  29.7 1.3 %collective-permute-start.10 = (bf16[128,1024]{1,0:T(8,128)(2,1)S(1)}, bf16[128,1024]{1,0:T(8,128)(2,1)}, u32[]{:S(2)}, u32[]{:S(2)}) collective-permute-start(bf16[128,1024]{1,0:T(8,128)(2,1)S(1)} %collective-permute-done.9.refs_17_.refs_25_), channel_id=1, source_target_pairs={{2,4},{3,5},{4,6},{5,7},{10,12},{11,13},{12,14},{13,15},{18,20},{1... | collective-permute-start | bytes 786440 | tf_op jit(solution)/shard_map/ppermute | solution.py:220
  31.0 3.3 %collective-permute-start.15 = (bf16[128,1024]{1,0:T(8,128)(2,1)S(1)}, bf16[128,1024]{1,0:T(8,128)(2,1)S(1)}, u32[]{:S(2)}, u32[]{:S(2)}) collective-permute-start(bf16[128,1024]{1,0:T(8,128)(2,1)S(1)} %collective-permute-done.9.refs_17_.refs_25_), channel_id=1, source_target_pairs={{2,3},{3,2},{4,5},{5,4},{6,7},{7,6},{10,11},{11,10},{12,13},{13,12... | collective-permute-start | bytes 786440 | tf_op jit(solution)/shard_map/ppermute | solution.py:216
  34.4 6.1 %collective-permute-done.10.refs_19_.refs_27_ = bf16[128,1024]{1,0:T(8,128)(2,1)} collective-permute-done((bf16[128,1024]{1,0:T(8,128)(2,1)S(1)}, bf16[128,1024]{1,0:T(8,128)(2,1)}, u32[]{:S(2)}, u32[]{:S(2)}) %collective-permute-start.10) | collective-permute-done | bytes 262176 | tf_op jit(solution)/shard_map/ppermute | solution.py:220
  40.5 0.9 %collective-permute-done.15.refs_13_.refs_21_ = bf16[128,1024]{1,0:T(8,128)(2,1)S(1)} collective-permute-done((bf16[128,1024]{1,0:T(8,128)(2,1)S(1)}, bf16[128,1024]{1,0:T(8,128)(2,1)S(1)}, u32[]{:S(2)}, u32[]{:S(2)}) %collective-permute-start.15) | collective-permute-done | bytes 262176 | tf_op jit(solution)/shard_map/ppermute | solution.py:216
  41.4 1.3 %collective-permute-start.17 = (bf16[128,1024]{1,0:T(8,128)(2,1)}, bf16[128,1024]{1,0:T(8,128)(2,1)}, u32[]{:S(2)}, u32[]{:S(2)}) collective-permute-start(bf16[128,1024]{1,0:T(8,128)(2,1)} %collective-permute-done.10.refs_19_.refs_27_), channel_id=1, source_target_pairs={{4,6},{5,7},{12,14},{13,15},{20,22},{21,23},{28,30},{29,31}} | collective-permute-start | bytes 786440 | tf_op jit(solution)/shard_map/ppermute | solution.py:220
  42.7 3.0 %collective-permute-start.11 = (bf16[64,2176]{1,0:T(8,128)(2,1)S(1)}, bf16[64,2176]{1,0:T(8,128)(2,1)S(1)}, u32[]{:S(2)}, u32[]{:S(2)}) collective-permute-start(bf16[64,2176]{1,0:T(8,128)(2,1)S(1)} %constant_dynamic-update-slice_fusion.refs_1_.refs_6_.refs_10_.refs_3_.refs_7_), channel_id=1, source_target_pairs={{0,4},{1,5},{2,6},{3,7},{4,0},{5,1},{6,2},{7,3},{8,12},{9,13},{10,... | collective-permute-start | bytes 835592 | tf_op jit(solution)/shard_map/ppermute | solution.py:224
  45.7 3.4 %collective-permute-start.20 = (bf16[128,1024]{1,0:T(8,128)(2,1)S(1)}, bf16[128,1024]{1,0:T(8,128)(2,1)}, u32[]{:S(2)}, u32[]{:S(2)}) collective-permute-start(bf16[128,1024]{1,0:T(8,128)(2,1)S(1)} %collective-permute-done.13.refs_20_.refs_28_), channel_id=1, source_target_pairs={{6,7},{7,6},{14,15},{15,14},{22,23},{23,22},{30,31},{31,30}} | collective-permute-start | bytes 786440 | tf_op jit(solution)/shard_map/ppermute | solution.py:216
  49.1 1.9 %collective-permute-start.18 = (bf16[128,1024]{1,0:T(8,128)(2,1)}, bf16[128,1024]{1,0:T(8,128)(2,1)}, u32[]{:S(2)}, u32[]{:S(2)}) collective-permute-start(bf16[128,1024]{1,0:T(8,128)(2,1)} %collective-permute-done.10.refs_19_.refs_27_), channel_id=1, source_target_pairs={{4,5},{5,4},{6,7},{7,6},{12,13},{13,12},{14,15},{15,14},{20,21},{2... | collective-permute-start | bytes 786440 | tf_op jit(solution)/shard_map/ppermute | solution.py:216
  51.0 2.0 %collective-permute-done.17.refs_21_.refs_29_ = bf16[128,1024]{1,0:T(8,128)(2,1)} collective-permute-done((bf16[128,1024]{1,0:T(8,128)(2,1)}, bf16[128,1024]{1,0:T(8,128)(2,1)}, u32[]{:S(2)}, u32[]{:S(2)}) %collective-permute-start.17) | collective-permute-done | bytes 262176 | tf_op jit(solution)/shard_map/ppermute | solution.py:220
  53.0 5.6 %collective-permute-start.19 = (bf16[128,1024]{1,0:T(8,128)(2,1)}, bf16[128,1024]{1,0:T(8,128)(2,1)}, u32[]{:S(2)}, u32[]{:S(2)}) collective-permute-start(bf16[128,1024]{1,0:T(8,128)(2,1)} %collective-permute-done.17.refs_21_.refs_29_), channel_id=1, source_target_pairs={{6,7},{7,6},{14,15},{15,14},{22,23},{23,22},{30,31},{31,30}} | collective-permute-start | bytes 786440 | tf_op jit(solution)/shard_map/ppermute | solution.py:216
  59.4 5.5 %collective-permute-done.11.refs_3_.refs_8_.refs_12_.refs_5_.refs_9_ = bf16[64,2176]{1,0:T(8,128)(2,1)S(1)} collective-permute-done((bf16[64,2176]{1,0:T(8,128)(2,1)S(1)}, bf16[64,2176]{1,0:T(8,128)(2,1)S(1)}, u32[]{:S(2)}, u32[]{:S(2)}) %collective-permute-start.11) | collective-permute-done | bytes 278560 | tf_op jit(solution)/shard_map/ppermute | solution.py:224
  65.0 0.6 copy-done.3
  65.7 9.9 %shard_map.65 = (bf16[128,8192]{1,0:T(8,128)(2,1)}, f32[128,1280]{1,0:T(8,128)S(1)}, s32[1]{0:T(128)}) custom-call(s32[3]{0:T(128)S(1)} %add_add_fusion.1.meta_ref, s32[1,128]{1,0:T(1,128)S(1)} %copy-done, bf16[64,2176]{1,0:T(8,128)(2,1)} %copy-done.1, bf16[64,2176]{1,0:T(8,128)(2,1)} %copy-done.2, bf16[64,2176]{1,0:T(8,128)(2,1)} %copy-done.3, ...), custom_call_target="tpu_custom_call" | custom-call | tf_op jit(solution)/shard_map/pallas_call | solution.py:187
  75.8 10.6 %shard_map.66 = bf16[128,8192]{1,0:T(8,128)(2,1)} custom-call(s32[3]{0:T(128)S(1)} %add_add_fusion.meta_ref, f32[128,1280]{1,0:T(8,128)S(1)} %get-tuple-element.22.refs_0_, s32[1]{0:T(128)} %get-tuple-element.23.refs_1_, bf16[128,8192]{1,0:T(8,128)(2,1)} %bitcast.23, bf16[64,2176]{1,0:T(8,128)(2,1)} %copy-done.1, ...), custom_call_target="tpu_custom_call", output_to_operand_aliasing={{}: (28, {})} | custom-call | tf_op jit(solution)/shard_map/pallas_call | solution.py:187
  (56 shorter events, 1.0 us)
Async XLA Ops:
  0.0 65.7 %copy-start = (s32[1,128]{1,0:T(1,128)S(1)}, s32[1,128]{1,0:T(1,128)}, u32[]{:S(2)}) copy-start(s32[1,128]{1,0:T(1,128)} %refs_0_.1) | copy-start | bytes 1540
  1.9 16.1 %collective-permute-start.8 = (bf16[128,1024]{1,0:T(8,128)(2,1)}, bf16[128,1024]{1,0:T(8,128)(2,1)S(1)}, u32[]{:S(2)}, u32[]{:S(2)}) collective-permute-start(bf16[128,1024]{1,0:T(8,128)(2,1)} %get-tuple-element.16.refs_11_.refs_19_), channel_id=1, source_target_pairs={{0,1},{1,0},{2,3},{3,2},{4,5},{5,4},{6,7},{7,6},{8,9},{9,8},{10,11... | collective-permute-start | bytes 786440 | tf_op jit(solution)/shard_map/ppermute | solution.py:216
  3.1 10.4 %collective-permute-start.5 = (bf16[128,1024]{1,0:T(8,128)(2,1)}, bf16[128,1024]{1,0:T(8,128)(2,1)S(1)}, u32[]{:S(2)}, u32[]{:S(2)}) collective-permute-start(bf16[128,1024]{1,0:T(8,128)(2,1)} %get-tuple-element.20.refs_14_.refs_22_), channel_id=1, source_target_pairs={{0,2},{1,3},{2,4},{3,5},{4,6},{5,7},{8,10},{9,11},{10,12},{11,13},... | collective-permute-start | bytes 786440 | tf_op jit(solution)/shard_map/ppermute | solution.py:220
  7.1 2.4 %collective-permute-start = (bf16[8,2176]{1,0:T(8,128)(2,1)S(1)}, bf16[8,2176]{1,0:T(8,128)(2,1)S(1)}, u32[]{:S(2)}, u32[]{:S(2)}) collective-permute-start(bf16[8,2176]{1,0:T(8,128)(2,1)S(1)} %get-tuple-element.30), channel_id=1, source_target_pairs={{0,8},{8,16},{16,24},{24,0},{1,9},{9,17},{17,25},{25,1},{2,10},{10... | collective-permute-start | bytes 104456 | tf_op jit(solution)/shard_map/ppermute | solution.py:224
  8.3 3.3 %collective-permute-start.1 = (bf16[8,2176]{1,0:T(8,128)(2,1)S(1)}, bf16[8,2176]{1,0:T(8,128)(2,1)S(1)}, u32[]{:S(2)}, u32[]{:S(2)}) collective-permute-start(bf16[8,2176]{1,0:T(8,128)(2,1)S(1)} %get-tuple-element.31), channel_id=1, source_target_pairs={{0,16},{8,24},{16,0},{24,8},{1,17},{9,25},{17,1},{25,9},{2,18},{10... | collective-permute-start | bytes 104456 | tf_op jit(solution)/shard_map/ppermute | solution.py:224
  9.5 3.7 %collective-permute-start.2 = (bf16[8,2176]{1,0:T(8,128)(2,1)S(1)}, bf16[8,2176]{1,0:T(8,128)(2,1)S(1)}, u32[]{:S(2)}, u32[]{:S(2)}) collective-permute-start(bf16[8,2176]{1,0:T(8,128)(2,1)S(1)} %get-tuple-element.29), channel_id=1, source_target_pairs={{0,24},{8,0},{16,8},{24,16},{1,25},{9,1},{17,9},{25,17},{2,26},{10... | collective-permute-start | bytes 104456 | tf_op jit(solution)/shard_map/ppermute | solution.py:224
  13.2 17.8 %collective-permute-start.3 = (bf16[32,2176]{1,0:T(8,128)(2,1)S(1)}, bf16[32,2176]{1,0:T(8,128)(2,1)S(1)}, u32[]{:S(2)}, u32[]{:S(2)}) collective-permute-start(bf16[32,2176]{1,0:T(8,128)(2,1)S(1)} %pad_maximum_fusion), channel_id=1, source_target_pairs={{0,1},{1,0},{2,3},{3,2},{4,5},{5,4},{6,7},{7,6},{8,9},{9,8},{10,11... | collective-permute-start | bytes 417800 | tf_op jit(solution)/shard_map/ppermute | solution.py:216
  13.5 51.4 %copy-start.6 = (bf16[128,1024]{1,0:T(8,128)(2,1)}, bf16[128,1024]{1,0:T(8,128)(2,1)S(1)}, u32[]{:S(2)}) copy-start(bf16[128,1024]{1,0:T(8,128)(2,1)S(1)} %collective-permute-done.5.refs_16_.refs_24_) | copy-start | bytes 786436
  13.5 10.6 %collective-permute-start.6 = (bf16[128,1024]{1,0:T(8,128)(2,1)S(1)}, bf16[128,1024]{1,0:T(8,128)(2,1)S(1)}, u32[]{:S(2)}, u32[]{:S(2)}) collective-permute-start(bf16[128,1024]{1,0:T(8,128)(2,1)S(1)} %collective-permute-done.5.refs_16_.refs_24_), channel_id=1, source_target_pairs={{2,4},{3,5},{4,6},{5,7},{10,12},{11,13},{12,14},{13,15},{18,20},{1... | collective-permute-start | bytes 786440 | tf_op jit(solution)/shard_map/ppermute | solution.py:220
  14.8 9.4 %collective-permute-start.12 = (bf16[128,1024]{1,0:T(8,128)(2,1)S(1)}, bf16[128,1024]{1,0:T(8,128)(2,1)S(1)}, u32[]{:S(2)}, u32[]{:S(2)}) collective-permute-start(bf16[128,1024]{1,0:T(8,128)(2,1)S(1)} %collective-permute-done.5.refs_16_.refs_24_), channel_id=1, source_target_pairs={{2,3},{3,2},{4,5},{5,4},{6,7},{7,6},{10,11},{11,10},{12,13},{13,12... | collective-permute-start | bytes 786440 | tf_op jit(solution)/shard_map/ppermute | solution.py:216
  18.0 47.0 %copy-start.5 = (bf16[128,1024]{1,0:T(8,128)(2,1)}, bf16[128,1024]{1,0:T(8,128)(2,1)S(1)}, u32[]{:S(2)}) copy-start(bf16[128,1024]{1,0:T(8,128)(2,1)S(1)} %collective-permute-done.8.refs_15_.refs_23_) | copy-start | bytes 786436
  18.0 11.7 %collective-permute-start.9 = (bf16[128,1024]{1,0:T(8,128)(2,1)S(1)}, bf16[128,1024]{1,0:T(8,128)(2,1)S(1)}, u32[]{:S(2)}, u32[]{:S(2)}) collective-permute-start(bf16[128,1024]{1,0:T(8,128)(2,1)S(1)} %collective-permute-done.8.refs_15_.refs_23_), channel_id=1, source_target_pairs={{0,2},{1,3},{2,4},{3,5},{4,6},{5,7},{8,10},{9,11},{10,12},{11,13},... | collective-permute-start | bytes 786440 | tf_op jit(solution)/shard_map/ppermute | solution.py:220
  19.3 15.0 %collective-permute-start.16 = (bf16[128,1024]{1,0:T(8,128)(2,1)}, bf16[128,1024]{1,0:T(8,128)(2,1)S(1)}, u32[]{:S(2)}, u32[]{:S(2)}) collective-permute-start(bf16[128,1024]{1,0:T(8,128)(2,1)} %get-tuple-element.20.refs_14_.refs_22_), channel_id=1, source_target_pairs={{0,1},{2,3},{4,5},{6,7},{8,9},{10,11},{12,13},{14,15},{16,17},{18,... | collective-permute-start | bytes 786440 | tf_op jit(solution)/shard_map/ppermute | solution.py:232
  24.1 40.9 %copy-start.9 = (bf16[128,1024]{1,0:T(8,128)(2,1)}, bf16[128,1024]{1,0:T(8,128)(2,1)S(1)}, u32[]{:S(2)}) copy-start(bf16[128,1024]{1,0:T(8,128)(2,1)S(1)} %collective-permute-done.6.refs_18_.refs_26_) | copy-start | bytes 786436
  24.2 51.5 %copy-start.7 = (bf16[128,1024]{1,0:T(8,128)(2,1)}, bf16[128,1024]{1,0:T(8,128)(2,1)S(1)}, u32[]{:S(2)}) copy-start(bf16[128,1024]{1,0:T(8,128)(2,1)S(1)} %collective-permute-done.12.refs_14_.refs_22_) | copy-start | bytes 786436
  24.2 21.5 %collective-permute-start.13 = (bf16[128,1024]{1,0:T(8,128)(2,1)S(1)}, bf16[128,1024]{1,0:T(8,128)(2,1)S(1)}, u32[]{:S(2)}, u32[]{:S(2)}) collective-permute-start(bf16[128,1024]{1,0:T(8,128)(2,1)S(1)} %collective-permute-done.6.refs_18_.refs_26_), channel_id=1, source_target_pairs={{4,6},{5,7},{12,14},{13,15},{20,22},{21,23},{28,30},{29,31}} | collective-permute-start | bytes 786440 | tf_op jit(solution)/shard_map/ppermute | solution.py:220
  25.5 17.2 %collective-permute-start.7 = (bf16[128,1024]{1,0:T(8,128)(2,1)S(1)}, bf16[128,1024]{1,0:T(8,128)(2,1)S(1)}, u32[]{:S(2)}, u32[]{:S(2)}) collective-permute-start(bf16[128,1024]{1,0:T(8,128)(2,1)S(1)} %collective-permute-done.6.refs_18_.refs_26_), channel_id=1, source_target_pairs={{4,5},{5,4},{6,7},{7,6},{12,13},{13,12},{14,15},{15,14},{20,21},{2... | collective-permute-start | bytes 786440 | tf_op jit(solution)/shard_map/ppermute | solution.py:216
  29.7 35.2 %copy-start.10 = (bf16[128,1024]{1,0:T(8,128)(2,1)}, bf16[128,1024]{1,0:T(8,128)(2,1)S(1)}, u32[]{:S(2)}) copy-start(bf16[128,1024]{1,0:T(8,128)(2,1)S(1)} %collective-permute-done.9.refs_17_.refs_25_) | copy-start | bytes 786436
  29.7 10.8 %collective-permute-start.10 = (bf16[128,1024]{1,0:T(8,128)(2,1)S(1)}, bf16[128,1024]{1,0:T(8,128)(2,1)}, u32[]{:S(2)}, u32[]{:S(2)}) collective-permute-start(bf16[128,1024]{1,0:T(8,128)(2,1)S(1)} %collective-permute-done.9.refs_17_.refs_25_), channel_id=1, source_target_pairs={{2,4},{3,5},{4,6},{5,7},{10,12},{11,13},{12,14},{13,15},{18,20},{1... | collective-permute-start | bytes 786440 | tf_op jit(solution)/shard_map/ppermute | solution.py:220
  31.0 10.4 %collective-permute-start.15 = (bf16[128,1024]{1,0:T(8,128)(2,1)S(1)}, bf16[128,1024]{1,0:T(8,128)(2,1)S(1)}, u32[]{:S(2)}, u32[]{:S(2)}) collective-permute-start(bf16[128,1024]{1,0:T(8,128)(2,1)S(1)} %collective-permute-done.9.refs_17_.refs_25_), channel_id=1, source_target_pairs={{2,3},{3,2},{4,5},{5,4},{6,7},{7,6},{10,11},{11,10},{12,13},{13,12... | collective-permute-start | bytes 786440 | tf_op jit(solution)/shard_map/ppermute | solution.py:216
  34.3 30.7 %copy-start.1 = (bf16[64,2176]{1,0:T(8,128)(2,1)}, bf16[64,2176]{1,0:T(8,128)(2,1)S(1)}, u32[]{:S(2)}) copy-start(bf16[64,2176]{1,0:T(8,128)(2,1)S(1)} %constant_dynamic-update-slice_fusion.refs_1_.refs_6_.refs_10_.refs_3_.refs_7_) | copy-start | bytes 835588
  34.3 41.4 %copy-start.8 = (bf16[128,1024]{1,0:T(8,128)(2,1)}, bf16[128,1024]{1,0:T(8,128)(2,1)S(1)}, u32[]{:S(2)}) copy-start(bf16[128,1024]{1,0:T(8,128)(2,1)S(1)} %collective-permute-done.16.refs_12_.refs_20_) | copy-start | bytes 786436
  34.3 14.8 %collective-permute-start.4 = (bf16[64,2176]{1,0:T(8,128)(2,1)S(1)}, bf16[64,2176]{1,0:T(8,128)(2,1)S(1)}, u32[]{:S(2)}, u32[]{:S(2)}) collective-permute-start(bf16[64,2176]{1,0:T(8,128)(2,1)S(1)} %constant_dynamic-update-slice_fusion.refs_1_.refs_6_.refs_10_.refs_3_.refs_7_), channel_id=1, source_target_pairs={{0,2},{1,3},{2,4},{3,5},{4,6},{5,7},{6,0},{7,1},{8,10},{9,11},{10,... | collective-permute-start | bytes 835592 | tf_op jit(solution)/shard_map/ppermute | solution.py:224
  41.4 34.3 %copy-start.13 = (bf16[128,1024]{1,0:T(8,128)(2,1)}, bf16[128,1024]{1,0:T(8,128)(2,1)S(1)}, u32[]{:S(2)}) copy-start(bf16[128,1024]{1,0:T(8,128)(2,1)S(1)} %collective-permute-done.15.refs_13_.refs_21_) | copy-start | bytes 786436
  41.4 11.6 %collective-permute-start.17 = (bf16[128,1024]{1,0:T(8,128)(2,1)}, bf16[128,1024]{1,0:T(8,128)(2,1)}, u32[]{:S(2)}, u32[]{:S(2)}) collective-permute-start(bf16[128,1024]{1,0:T(8,128)(2,1)} %collective-permute-done.10.refs_19_.refs_27_), channel_id=1, source_target_pairs={{4,6},{5,7},{12,14},{13,15},{20,22},{21,23},{28,30},{29,31}} | collective-permute-start | bytes 786440 | tf_op jit(solution)/shard_map/ppermute | solution.py:220
  42.7 33.1 %copy-start.11 = (bf16[128,1024]{1,0:T(8,128)(2,1)}, bf16[128,1024]{1,0:T(8,128)(2,1)S(1)}, u32[]{:S(2)}) copy-start(bf16[128,1024]{1,0:T(8,128)(2,1)S(1)} %collective-permute-done.7.refs_16_.refs_24_) | copy-start | bytes 786436
  42.7 22.2 %collective-permute-start.11 = (bf16[64,2176]{1,0:T(8,128)(2,1)S(1)}, bf16[64,2176]{1,0:T(8,128)(2,1)S(1)}, u32[]{:S(2)}, u32[]{:S(2)}) collective-permute-start(bf16[64,2176]{1,0:T(8,128)(2,1)S(1)} %constant_dynamic-update-slice_fusion.refs_1_.refs_6_.refs_10_.refs_3_.refs_7_), channel_id=1, source_target_pairs={{0,4},{1,5},{2,6},{3,7},{4,0},{5,1},{6,2},{7,3},{8,12},{9,13},{10,... | collective-permute-start | bytes 835592 | tf_op jit(solution)/shard_map/ppermute | solution.py:224
  45.7 19.3 %copy-start.12 = (bf16[128,1024]{1,0:T(8,128)(2,1)}, bf16[128,1024]{1,0:T(8,128)(2,1)S(1)}, u32[]{:S(2)}) copy-start(bf16[128,1024]{1,0:T(8,128)(2,1)S(1)} %collective-permute-done.13.refs_20_.refs_28_) | copy-start | bytes 786436
  45.7 19.2 %collective-permute-start.14 = (bf16[64,2176]{1,0:T(8,128)(2,1)S(1)}, bf16[64,2176]{1,0:T(8,128)(2,1)S(1)}, u32[]{:S(2)}, u32[]{:S(2)}) collective-permute-start(bf16[64,2176]{1,0:T(8,128)(2,1)S(1)} %constant_dynamic-update-slice_fusion.refs_1_.refs_6_.refs_10_.refs_3_.refs_7_), channel_id=1, source_target_pairs={{0,6},{1,7},{2,0},{3,1},{4,2},{5,3},{6,4},{7,5},{8,14},{9,15},{10,... | collective-permute-start | bytes 835592 | tf_op jit(solution)/shard_map/ppermute | solution.py:224
  45.7 30.0 %collective-permute-start.20 = (bf16[128,1024]{1,0:T(8,128)(2,1)S(1)}, bf16[128,1024]{1,0:T(8,128)(2,1)}, u32[]{:S(2)}, u32[]{:S(2)}) collective-permute-start(bf16[128,1024]{1,0:T(8,128)(2,1)S(1)} %collective-permute-done.13.refs_20_.refs_28_), channel_id=1, source_target_pairs={{6,7},{7,6},{14,15},{15,14},{22,23},{23,22},{30,31},{31,30}} | collective-permute-start | bytes 786440 | tf_op jit(solution)/shard_map/ppermute | solution.py:216
  49.1 26.6 %collective-permute-start.18 = (bf16[128,1024]{1,0:T(8,128)(2,1)}, bf16[128,1024]{1,0:T(8,128)(2,1)}, u32[]{:S(2)}, u32[]{:S(2)}) collective-permute-start(bf16[128,1024]{1,0:T(8,128)(2,1)} %collective-permute-done.10.refs_19_.refs_27_), channel_id=1, source_target_pairs={{4,5},{5,4},{6,7},{7,6},{12,13},{13,12},{14,15},{15,14},{20,21},{2... | collective-permute-start | bytes 786440 | tf_op jit(solution)/shard_map/ppermute | solution.py:216
  53.0 22.7 %collective-permute-start.19 = (bf16[128,1024]{1,0:T(8,128)(2,1)}, bf16[128,1024]{1,0:T(8,128)(2,1)}, u32[]{:S(2)}, u32[]{:S(2)}) collective-permute-start(bf16[128,1024]{1,0:T(8,128)(2,1)} %collective-permute-done.17.refs_21_.refs_29_), channel_id=1, source_target_pairs={{6,7},{7,6},{14,15},{15,14},{22,23},{23,22},{30,31},{31,30}} | collective-permute-start | bytes 786440 | tf_op jit(solution)/shard_map/ppermute | solution.py:216
  (3 other events, 17.4 us)

commit v13 on v12

--- a/solution.py
+++ b/solution.py
@@ -41,23 +41,19 @@
     )(side.reshape(1), kv, kv)
 
 
-def attend_kernel(pairs, parts, tile, tiles, fresh, meta_ref, *refs):
-    s_ref, top_ref = refs[-2:]
-    inputs = 2 * parts + 4 * pairs
-    if fresh:
-        seg_ref, *ints_refs = refs[: 1 + parts]
-        q_ref, *inputs = refs[1 + parts : 2 + parts + inputs]
-        o_ref, bias_ref, reach_ref = refs[-5:-2]
-    else:
-        bias_ref, reach_ref, q_ref, *inputs = refs[: 3 + inputs]
-        o_ref = refs[-3]
-    pk_refs, pv_refs = inputs[:parts], inputs[parts : 2 * parts]
-    k_refs, v_refs = inputs[2 * parts :][: 2 * pairs], inputs[2 * parts + 2 * pairs :]
+def attend_kernel(pairs, parts, tile, tiles, meta_ref, seg_ref, *refs):
+    o_ref, bias_ref, reach_ref, s_ref, top_ref = refs[-5:]
+    ints_refs, (q_ref, *refs) = refs[:parts], refs[parts:-5]
+    pk_refs, pv_refs, refs = refs[:parts], refs[parts : 2 * parts], refs[2 * parts :]
+    halves_refs = [
+        (refs[at : at + 2 * pairs], refs[at + 2 * pairs : at + 4 * pairs])
+        for at in (0, 4 * pairs)
+    ]
     rows = q_ref.shape[0]
     step = 2 * rows
     span = pk_refs[0].shape[0]
     prefix_keys = parts * span
-    block, limit = meta_ref[0], meta_ref[2]
+    block, limit = meta_ref[0], meta_ref[3]
     scale = math.log2(math.e) / math.sqrt(HD)
     nt = (((1,), (1,)), ((), ()))
 
@@ -84,10 +80,9 @@
                 at = prefix_keys + (2 * k + j) * rows
                 bias_ref[:, at : at + rows] = jnp.where(seen, 0.0, FILL)
 
-    if fresh:
-        pl.when(pl.program_id(0) == 0)(masks)
-
-    def body(near):
+    pl.when(pl.program_id(0) == 0)(masks)
+
+    def body(near, k_refs, v_refs):
         each = step // span
         steps = prefix_keys // step + near + 1
 
@@ -136,70 +131,71 @@
                 score(slab + 1)
             weigh(slab)
 
-    for near in range(pairs):
-        pl.when(reach_ref[0] == near)(functools.partial(body, near))
-
-
-def attend(meta, queries, pieces, prefix, tile, tiles, segments=None, before=None):
+    second = pl.program_id(0) >= pl.num_programs(0) // 2
+    for half, refs_of_half in enumerate(halves_refs):
+        for near in range(pairs):
+            due = (reach_ref[0] == near) & (second == bool(half))
+            pl.when(due)(functools.partial(body, near, *refs_of_half))
+
+
+def attend(meta, segments, queries, straight, crossed, prefix, tile, tiles):
     rows = queries.shape[0]
     span = prefix[0].shape[0]
-    pairs, parts = len(pieces) // 2, len(prefix)
-    pieces, places = zip(*[piece if isinstance(piece, tuple) else (piece, 0) for piece in pieces])
-    heads = pieces[0].shape[1] // (2 * HD)
-    blocks = heads // BOTH
-    keys = rows * len(pieces) + span * parts
-    whole = pl.BlockSpec((rows, keys), lambda i, m: (0, 0))
-    scalar = pl.BlockSpec(memory_space=pltpu.SMEM)
-    wide = pl.BlockSpec((rows, BOTH * GQ * HD), lambda i, m: (0, m[1] + i))
-    fresh = before is None
+    pairs, parts = len(straight) // 2, len(prefix)
+    blocks = straight[0].shape[1] // (2 * HD) // BOTH
+    keys = rows * len(straight) + span * parts
+
+    def head(i, m):
+        return jnp.where(i < blocks, m[1] + i, m[2] + i - blocks)
+
+    def own(i):
+        return jnp.minimum(i, blocks - 1)
+
+    def other(i):
+        return jnp.maximum(i - blocks, 0)
+
+    wide = pl.BlockSpec((rows, BOTH * GQ * HD), lambda i, m: (0, head(i, m)))
+    shape = (rows, BOTH * HD)
     queries, *arrays = [
         pltpu.with_memory_space_constraint(array, pltpu.HBM)
-        for array in (queries, *prefix, *pieces)
+        for array in (queries, *prefix, *straight, *crossed)
     ]
-    prefix, pieces = arrays[:parts], arrays[parts:]
-    args = [meta, *([segments, *prefix] if fresh else before[1:])]
-    args += [queries, *prefix, *prefix, *pieces, *pieces]
-    if fresh:
-        ints = pl.BlockSpec((span, rows), lambda i, m: (0, 2 * KVH))
-        in_specs = [pl.BlockSpec((1, rows), lambda i, m: (0, 0)), *[ints] * parts]
-    else:
-        in_specs = [whole, scalar]
-    in_specs += [
+    prefix, straight, crossed = (
+        arrays[:parts],
+        arrays[parts : parts + 2 * pairs],
+        arrays[parts + 2 * pairs :],
+    )
+    values_at = KVH // BOTH
+    in_specs = [
+        pl.BlockSpec((1, rows), lambda i, m: (0, 0)),
+        *[pl.BlockSpec((span, rows), lambda i, m: (0, 2 * KVH))] * parts,
         wide,
-        *[pl.BlockSpec((span, BOTH * HD), lambda i, m: (0, m[1] + i))] * parts,
-        *[pl.BlockSpec((span, BOTH * HD), lambda i, m: (0, KVH // BOTH + m[1] + i))] * parts,
-        *[pl.BlockSpec((rows, BOTH * HD), lambda i, m, at=at: (at, i)) for at in places],
-        *[pl.BlockSpec((rows, BOTH * HD), lambda i, m, at=at: (at, blocks + i)) for at in places],
+        *[pl.BlockSpec((span, BOTH * HD), lambda i, m: (0, head(i, m)))] * parts,
+        *[pl.BlockSpec((span, BOTH * HD), lambda i, m: (0, values_at + head(i, m)))] * parts,
+        *[pl.BlockSpec(shape, lambda i, m: (0, own(i)))] * (2 * pairs),
+        *[pl.BlockSpec(shape, lambda i, m: (0, blocks + own(i)))] * (2 * pairs),
+        *[pl.BlockSpec(shape, lambda i, m: (0, other(i)))] * (2 * pairs),
+        *[pl.BlockSpec(shape, lambda i, m: (0, blocks + other(i)))] * (2 * pairs),
     ]
-    out_specs = [wide]
-    out_shape = [jax.ShapeDtypeStruct(queries.shape, queries.dtype)]
-    aliases = {}
-    if fresh:
-        out_specs += [whole, scalar]
-        out_shape += [
-            jax.ShapeDtypeStruct((rows, keys), jnp.float32),
-            jax.ShapeDtypeStruct((1,), jnp.int32),
-        ]
-    else:
-        args.append(before[0])
-        in_specs.append(pl.BlockSpec(memory_space=pl.ANY))
-        aliases = {len(args) - 1: 0}
+    args = [segments, *prefix, queries, *prefix, *prefix]
+    args += [*straight, *straight, *crossed, *crossed]
     return pl.pallas_call(
-        functools.partial(attend_kernel, pairs, parts, tile, tiles, fresh),
+        functools.partial(attend_kernel, pairs, parts, tile, tiles),
         grid_spec=pltpu.PrefetchScalarGridSpec(
             num_scalar_prefetch=1,
-            grid=(blocks,),
+            grid=(2 * blocks,),
             in_specs=in_specs,
-            out_specs=out_specs,
+            out_specs=wide,
             scratch_shapes=[
+                pltpu.VMEM((rows, keys), jnp.float32),
+                pltpu.SMEM((1,), jnp.int32),
                 pltpu.VMEM((2, SLAB * rows, keys), jnp.float32),
                 pltpu.VMEM((2, SLAB * rows, HD), jnp.float32),
             ],
         ),
-        out_shape=out_shape,
-        input_output_aliases=aliases,
-        compiler_params=pltpu.CompilerParams(vmem_limit_bytes=24 * 1024 * 1024),
-    )(*args)
+        out_shape=jax.ShapeDtypeStruct(queries.shape, queries.dtype),
+        compiler_params=pltpu.CompilerParams(vmem_limit_bytes=32 * 1024 * 1024),
+    )(meta, *args)
 
 
 def on_device(queries, resp_kv, resp_segments, prefix_kv, tile_plan, prompt_lengths):
@@ -257,14 +253,12 @@
         source = after(prefix[0], *behind[min(by, len(behind)) - 1])
         prefix.append(shift(source, "resp", 2 * by))
 
-    def meta(first):
-        return jnp.stack([block, first * (KVH // 2 // BOTH), prompt_lengths[0]])
-
-    done = attend(
-        meta(side), queries[0], straight, prefix, tile, tiles, segments=resp_segments
-    )
-    done = attend(meta(1 - side), queries[0], crossed, prefix, tile, tiles, before=done)
-    return done[0][None]
+    first = KVH // 2 // BOTH
+    meta = jnp.stack([block, side * first, (1 - side) * first, prompt_lengths[0]])
+    out = attend(
+        meta, resp_segments, queries[0], straight, crossed, prefix, tile, tiles
+    )
+    return out[None]
 
 
 def solution(mesh):

time: 87 us -> 92.4 us (1.062)
  the two profiles are of different devices: /device:TPU:27 before, /device:TPU:26 now
where the time goes in v13:
time: 92.4 us; the launch traced here: 92.6 us
  starting transfers between devices  41 us (44%)
  waiting for transfers between devices  28.1 us (30%)
  Pallas kernels  19.4 us (21%)
  other arithmetic  2.07 us (2%)
  between operations  1.2 us (1%)
    ppermute x8, starting transfers between devices, swap(): lax.ppermute(value, 'resp', [(r, r ^ 1) for r in range(2 * first, count)])  24.8 us
    ppermute x6, waiting for transfers between devices, climb(): return lax.ppermute(value, 'resp', pairs)  19.8 us
    pallas_call x1, Pallas kernels, attend(): pl.pallas_call(functools.partial(attend_kernel, pairs, parts, tile, tiles...  17.6 us
    ppermute x8, waiting for transfers between devices, swap(): lax.ppermute(value, 'resp', [(r, r ^ 1) for r in range(2 * first, count)])  7.86 us
    ppermute x6, starting transfers between devices, climb(): return lax.ppermute(value, 'resp', pairs)  7.72 us
    ppermute x6, starting transfers between devices, shift(): lax.ppermute(value, axis, [(r, (r + by) % size) for r in range(size)])  5.04 us
    ppermute x1, starting transfers between devices, on_device(): upper = lax.ppermute(after(mine, partner), 'resp', upper)  3.44 us
  transfers between devices with their start and end apart: 21, of which 8 were waited for; matrix products, arithmetic and copies ran while one was open for 0% of the time, Pallas kernels for 2%

profile of v13, /device:TPU:26, one launch (start us, length us, event | category | flops | bytes accessed | tf_op | source)
XLA Modules:
  0.0 92.6 jit_solution(2102215450630397431)
XLA Ops:
  0.0 0.8 slice_bitcast_fusion.1
  0.8 0.2 select_reduce_fusion.1
  1.0 1.0 %select_reduce_fusion = bf16[4,8,2048]{2,1,0:T(8,128)(2,1)S(1)} fusion(pred[4,4]{1,0:T(4,128)(4,1)S(1)} %get-tuple-element.22, bf16[4,8,2048]{2,1,0:T(8,128)(2,1)} %param.9), kind=kLoop, calls=%fused_computation | loop fusion | flops 458752 | bytes 262160 | tf_op jit(solution)/shard_map/reduce_sum | solution.py:241
  2.0 0.7 convert_convert_fusion
  2.8 0.5 collective-permute-start
  3.3 1.0 %collective-permute-start.1 = (bf16[8,2176]{1,0:T(8,128)(2,1)S(1)}, bf16[8,2176]{1,0:T(8,128)(2,1)S(1)}, u32[]{:S(2)}, u32[]{:S(2)}) collective-permute-start(bf16[8,2176]{1,0:T(8,128)(2,1)S(1)} %get-tuple-element.25), channel_id=1, source_target_pairs={{0,16},{8,24},{16,0},{24,8},{1,17},{9,25},{17,1},{25,9},{2,18},{10... | collective-permute-start | bytes 104456 | tf_op jit(solution)/shard_map/ppermute | solution.py:220
  4.3 1.8 %shard_map.64 = (bf16[128,1024]{1,0:T(8,128)(2,1)}, bf16[128,1024]{1,0:T(8,128)(2,1)}) custom-call(s32[1]{0:T(128)} %bitcast.10.meta_ref, bf16[128,2048]{1,0:T(8,128)(2,1)} %bitcast.23, bf16[128,2048]{1,0:T(8,128)(2,1)} %bitcast.24), custom_call_target="tpu_custom_call" | custom-call | tf_op jit(solution)/shard_map/pallas_call | solution.py:29
  6.2 1.5 %collective-permute-start.8 = (bf16[128,1024]{1,0:T(8,128)(2,1)}, bf16[128,1024]{1,0:T(8,128)(2,1)S(1)}, u32[]{:S(2)}, u32[]{:S(2)}) collective-permute-start(bf16[128,1024]{1,0:T(8,128)(2,1)} %get-tuple-element.13.refs_29_.refs_37_), channel_id=1, source_target_pairs={{0,1},{1,0},{2,3},{3,2},{4,5},{5,4},{6,7},{7,6},{8,9},{9,8},{10,11... | collective-permute-start | bytes 786440 | tf_op jit(solution)/shard_map/ppermute | solution.py:212
  7.7 1.3 %collective-permute-start.5 = (bf16[128,1024]{1,0:T(8,128)(2,1)}, bf16[128,1024]{1,0:T(8,128)(2,1)S(1)}, u32[]{:S(2)}, u32[]{:S(2)}) collective-permute-start(bf16[128,1024]{1,0:T(8,128)(2,1)} %get-tuple-element.17.refs_13_.refs_21_), channel_id=1, source_target_pairs={{0,2},{1,3},{2,4},{3,5},{4,6},{5,7},{8,10},{9,11},{10,12},{11,13},... | collective-permute-start | bytes 786440 | tf_op jit(solution)/shard_map/ppermute | solution.py:216
  9.0 0.6 collective-permute-start.3
  9.6 8.5 %collective-permute-done.5.refs_15_.refs_23_ = bf16[128,1024]{1,0:T(8,128)(2,1)S(1)} collective-permute-done((bf16[128,1024]{1,0:T(8,128)(2,1)}, bf16[128,1024]{1,0:T(8,128)(2,1)S(1)}, u32[]{:S(2)}, u32[]{:S(2)}) %collective-permute-start.5) | collective-permute-done | bytes 262176 | tf_op jit(solution)/shard_map/ppermute | solution.py:216
  18.1 2.4 %collective-permute-start.12 = (bf16[128,1024]{1,0:T(8,128)(2,1)S(1)}, bf16[128,1024]{1,0:T(8,128)(2,1)S(1)}, u32[]{:S(2)}, u32[]{:S(2)}) collective-permute-start(bf16[128,1024]{1,0:T(8,128)(2,1)S(1)} %collective-permute-done.5.refs_15_.refs_23_), channel_id=1, source_target_pairs={{2,3},{3,2},{4,5},{5,4},{6,7},{7,6},{10,11},{11,10},{12,13},{13,12... | collective-permute-start | bytes 786440 | tf_op jit(solution)/shard_map/ppermute | solution.py:212
  20.6 1.3 %collective-permute-start.6 = (bf16[128,1024]{1,0:T(8,128)(2,1)S(1)}, bf16[128,1024]{1,0:T(8,128)(2,1)S(1)}, u32[]{:S(2)}, u32[]{:S(2)}) collective-permute-start(bf16[128,1024]{1,0:T(8,128)(2,1)S(1)} %collective-permute-done.5.refs_15_.refs_23_), channel_id=1, source_target_pairs={{2,4},{3,5},{4,6},{5,7},{10,12},{11,13},{12,14},{13,15},{18,20},{1... | collective-permute-start | bytes 786440 | tf_op jit(solution)/shard_map/ppermute | solution.py:216
  21.9 1.3 %collective-permute-start.9 = (bf16[128,1024]{1,0:T(8,128)(2,1)S(1)}, bf16[128,1024]{1,0:T(8,128)(2,1)S(1)}, u32[]{:S(2)}, u32[]{:S(2)}) collective-permute-start(bf16[128,1024]{1,0:T(8,128)(2,1)S(1)} %collective-permute-done.8.refs_14_.refs_22_), channel_id=1, source_target_pairs={{0,2},{1,3},{2,4},{3,5},{4,6},{5,7},{8,10},{9,11},{10,12},{11,13},... | collective-permute-start | bytes 786440 | tf_op jit(solution)/shard_map/ppermute | solution.py:216
  23.2 3.4 %collective-permute-start.16 = (bf16[128,1024]{1,0:T(8,128)(2,1)}, bf16[128,1024]{1,0:T(8,128)(2,1)S(1)}, u32[]{:S(2)}, u32[]{:S(2)}) collective-permute-start(bf16[128,1024]{1,0:T(8,128)(2,1)} %get-tuple-element.17.refs_13_.refs_21_), channel_id=1, source_target_pairs={{0,1},{2,3},{4,5},{6,7},{8,9},{10,11},{12,13},{14,15},{16,17},{18,... | collective-permute-start | bytes 786440 | tf_op jit(solution)/shard_map/ppermute | solution.py:228
  26.6 0.9 %collective-permute-done.12.refs_32_.refs_40_ = bf16[128,1024]{1,0:T(8,128)(2,1)S(1)} collective-permute-done((bf16[128,1024]{1,0:T(8,128)(2,1)S(1)}, bf16[128,1024]{1,0:T(8,128)(2,1)S(1)}, u32[]{:S(2)}, u32[]{:S(2)}) %collective-permute-start.12) | collective-permute-done | bytes 262176 | tf_op jit(solution)/shard_map/ppermute | solution.py:212
  27.6 4.1 %collective-permute-done.6.refs_17_.refs_25_ = bf16[128,1024]{1,0:T(8,128)(2,1)S(1)} collective-permute-done((bf16[128,1024]{1,0:T(8,128)(2,1)S(1)}, bf16[128,1024]{1,0:T(8,128)(2,1)S(1)}, u32[]{:S(2)}, u32[]{:S(2)}) %collective-permute-start.6) | collective-permute-done | bytes 262176 | tf_op jit(solution)/shard_map/ppermute | solution.py:216
  31.7 1.3 %collective-permute-start.13 = (bf16[128,1024]{1,0:T(8,128)(2,1)S(1)}, bf16[128,1024]{1,0:T(8,128)(2,1)S(1)}, u32[]{:S(2)}, u32[]{:S(2)}) collective-permute-start(bf16[128,1024]{1,0:T(8,128)(2,1)S(1)} %collective-permute-done.6.refs_17_.refs_25_), channel_id=1, source_target_pairs={{4,6},{5,7},{12,14},{13,15},{20,22},{21,23},{28,30},{29,31}} | collective-permute-start | bytes 786440 | tf_op jit(solution)/shard_map/ppermute | solution.py:216
  33.0 4.3 %collective-permute-done.9.refs_16_.refs_24_ = bf16[128,1024]{1,0:T(8,128)(2,1)S(1)} collective-permute-done((bf16[128,1024]{1,0:T(8,128)(2,1)S(1)}, bf16[128,1024]{1,0:T(8,128)(2,1)S(1)}, u32[]{:S(2)}, u32[]{:S(2)}) %collective-permute-start.9) | collective-permute-done | bytes 262176 | tf_op jit(solution)/shard_map/ppermute | solution.py:216
  37.3 3.4 %collective-permute-start.15 = (bf16[128,1024]{1,0:T(8,128)(2,1)S(1)}, bf16[128,1024]{1,0:T(8,128)(2,1)S(1)}, u32[]{:S(2)}, u32[]{:S(2)}) collective-permute-start(bf16[128,1024]{1,0:T(8,128)(2,1)S(1)} %collective-permute-done.9.refs_16_.refs_24_), channel_id=1, source_target_pairs={{2,3},{3,2},{4,5},{5,4},{6,7},{7,6},{10,11},{11,10},{12,13},{13,12... | collective-permute-start | bytes 786440 | tf_op jit(solution)/shard_map/ppermute | solution.py:212
  40.7 1.3 %collective-permute-start.10 = (bf16[128,1024]{1,0:T(8,128)(2,1)S(1)}, bf16[128,1024]{1,0:T(8,128)(2,1)S(1)}, u32[]{:S(2)}, u32[]{:S(2)}) collective-permute-start(bf16[128,1024]{1,0:T(8,128)(2,1)S(1)} %collective-permute-done.9.refs_16_.refs_24_), channel_id=1, source_target_pairs={{2,4},{3,5},{4,6},{5,7},{10,12},{11,13},{12,14},{13,15},{18,20},{1... | collective-permute-start | bytes 786440 | tf_op jit(solution)/shard_map/ppermute | solution.py:216
  42.1 2.4 %collective-permute-start.7 = (bf16[128,1024]{1,0:T(8,128)(2,1)S(1)}, bf16[128,1024]{1,0:T(8,128)(2,1)}, u32[]{:S(2)}, u32[]{:S(2)}) collective-permute-start(bf16[128,1024]{1,0:T(8,128)(2,1)S(1)} %collective-permute-done.6.refs_17_.refs_25_), channel_id=1, source_target_pairs={{4,5},{5,4},{6,7},{7,6},{12,13},{13,12},{14,15},{15,14},{20,21},{2... | collective-permute-start | bytes 786440 | tf_op jit(solution)/shard_map/ppermute | solution.py:212
  44.6 3.4 %collective-permute-done.15.refs_31_.refs_39_ = bf16[128,1024]{1,0:T(8,128)(2,1)S(1)} collective-permute-done((bf16[128,1024]{1,0:T(8,128)(2,1)S(1)}, bf16[128,1024]{1,0:T(8,128)(2,1)S(1)}, u32[]{:S(2)}, u32[]{:S(2)}) %collective-permute-start.15) | collective-permute-done | bytes 262176 | tf_op jit(solution)/shard_map/ppermute | solution.py:212
  48.0 2.8 %collective-permute-done.10.refs_18_.refs_26_ = bf16[128,1024]{1,0:T(8,128)(2,1)S(1)} collective-permute-done((bf16[128,1024]{1,0:T(8,128)(2,1)S(1)}, bf16[128,1024]{1,0:T(8,128)(2,1)S(1)}, u32[]{:S(2)}, u32[]{:S(2)}) %collective-permute-start.10) | collective-permute-done | bytes 262176 | tf_op jit(solution)/shard_map/ppermute | solution.py:216
  50.8 1.3 %collective-permute-start.17 = (bf16[128,1024]{1,0:T(8,128)(2,1)S(1)}, bf16[128,1024]{1,0:T(8,128)(2,1)}, u32[]{:S(2)}, u32[]{:S(2)}) collective-permute-start(bf16[128,1024]{1,0:T(8,128)(2,1)S(1)} %collective-permute-done.10.refs_18_.refs_26_), channel_id=1, source_target_pairs={{4,6},{5,7},{12,14},{13,15},{20,22},{21,23},{28,30},{29,31}} | collective-permute-start | bytes 786440 | tf_op jit(solution)/shard_map/ppermute | solution.py:216
  52.2 3.4 %collective-permute-start.14 = (bf16[64,2176]{1,0:T(8,128)(2,1)S(1)}, bf16[64,2176]{1,0:T(8,128)(2,1)S(1)}, u32[]{:S(2)}, u32[]{:S(2)}) collective-permute-start(bf16[64,2176]{1,0:T(8,128)(2,1)S(1)} %constant_dynamic-update-slice_fusion.refs_0_.refs_5_.refs_9_), channel_id=1, source_target_pairs={{0,6},{1,7},{2,0},{3,1},{4,2},{5,3},{6,4},{7,5},{8,14},{9,15},{10,... | collective-permute-start | bytes 835592 | tf_op jit(solution)/shard_map/ppermute | solution.py:220
  55.6 4.1 %collective-permute-start.18 = (bf16[128,1024]{1,0:T(8,128)(2,1)S(1)}, bf16[128,1024]{1,0:T(8,128)(2,1)}, u32[]{:S(2)}, u32[]{:S(2)}) collective-permute-start(bf16[128,1024]{1,0:T(8,128)(2,1)S(1)} %collective-permute-done.10.refs_18_.refs_26_), channel_id=1, source_target_pairs={{4,5},{5,4},{6,7},{7,6},{12,13},{13,12},{14,15},{15,14},{20,21},{2... | collective-permute-start | bytes 786440 | tf_op jit(solution)/shard_map/ppermute | solution.py:212
  59.7 4.3 %collective-permute-start.20 = (bf16[128,1024]{1,0:T(8,128)(2,1)S(1)}, bf16[128,1024]{1,0:T(8,128)(2,1)}, u32[]{:S(2)}, u32[]{:S(2)}) collective-permute-start(bf16[128,1024]{1,0:T(8,128)(2,1)S(1)} %collective-permute-done.13.refs_19_.refs_27_), channel_id=1, source_target_pairs={{6,7},{7,6},{14,15},{15,14},{22,23},{23,22},{30,31},{31,30}} | collective-permute-start | bytes 786440 | tf_op jit(solution)/shard_map/ppermute | solution.py:212
  64.1 6.0 %collective-permute-start.19 = (bf16[128,1024]{1,0:T(8,128)(2,1)}, bf16[128,1024]{1,0:T(8,128)(2,1)}, u32[]{:S(2)}, u32[]{:S(2)}) collective-permute-start(bf16[128,1024]{1,0:T(8,128)(2,1)} %collective-permute-done.17.refs_20_.refs_28_), channel_id=1, source_target_pairs={{6,7},{7,6},{14,15},{15,14},{22,23},{23,22},{30,31},{31,30}} | collective-permute-start | bytes 786440 | tf_op jit(solution)/shard_map/ppermute | solution.py:212
  70.8 0.4 collective-permute-done.11.refs_2_.refs_7_.refs_11_
  71.3 3.5 %collective-permute-done.19.refs_35_.refs_43_ = bf16[128,1024]{1,0:T(8,128)(2,1)} collective-permute-done((bf16[128,1024]{1,0:T(8,128)(2,1)}, bf16[128,1024]{1,0:T(8,128)(2,1)}, u32[]{:S(2)}, u32[]{:S(2)}) %collective-permute-start.19) | collective-permute-done | bytes 262176 | tf_op jit(solution)/shard_map/ppermute | solution.py:212
  74.9 17.6 %shard_map.65 = bf16[128,8192]{1,0:T(8,128)(2,1)} custom-call(s32[4]{0:T(128)S(1)} %pad_add_fusion.meta_ref, s32[1,128]{1,0:T(1,128)S(1)} %copy-done, bf16[64,2176]{1,0:T(8,128)(2,1)} %copy-done.1, bf16[64,2176]{1,0:T(8,128)(2,1)} %copy-done.2, bf16[64,2176]{1,0:T(8,128)(2,1)} %copy-done.3, bf16[64,2176]{1,0:T(8,128)(2,1)} %copy-done.4, ...), custom_call_target="tpu_custom_call" | custom-call | tf_op jit(solution)/shard_map/pallas_call | solution.py:182
  (54 shorter events, 0.5 us)
Async XLA Ops:
  0.0 74.9 %copy-start = (s32[1,128]{1,0:T(1,128)S(1)}, s32[1,128]{1,0:T(1,128)}, u32[]{:S(2)}) copy-start(s32[1,128]{1,0:T(1,128)} %seg_ref.1) | copy-start | bytes 1540
  2.8 6.2 %collective-permute-start.2 = (bf16[8,2176]{1,0:T(8,128)(2,1)S(1)}, bf16[8,2176]{1,0:T(8,128)(2,1)S(1)}, u32[]{:S(2)}, u32[]{:S(2)}) collective-permute-start(bf16[8,2176]{1,0:T(8,128)(2,1)S(1)} %get-tuple-element.23), channel_id=1, source_target_pairs={{0,24},{8,0},{16,8},{24,16},{1,25},{9,1},{17,9},{25,17},{2,26},{10... | collective-permute-start | bytes 104456 | tf_op jit(solution)/shard_map/ppermute | solution.py:220
  2.8 6.2 %collective-permute-start = (bf16[8,2176]{1,0:T(8,128)(2,1)S(1)}, bf16[8,2176]{1,0:T(8,128)(2,1)S(1)}, u32[]{:S(2)}, u32[]{:S(2)}) collective-permute-start(bf16[8,2176]{1,0:T(8,128)(2,1)S(1)} %get-tuple-element.24), channel_id=1, source_target_pairs={{0,8},{8,16},{16,24},{24,0},{1,9},{9,17},{17,25},{25,1},{2,10},{10... | collective-permute-start | bytes 104456 | tf_op jit(solution)/shard_map/ppermute | solution.py:220
  3.3 5.7 %collective-permute-start.1 = (bf16[8,2176]{1,0:T(8,128)(2,1)S(1)}, bf16[8,2176]{1,0:T(8,128)(2,1)S(1)}, u32[]{:S(2)}, u32[]{:S(2)}) collective-permute-start(bf16[8,2176]{1,0:T(8,128)(2,1)S(1)} %get-tuple-element.25), channel_id=1, source_target_pairs={{0,16},{8,24},{16,0},{24,8},{1,17},{9,25},{17,1},{25,9},{2,18},{10... | collective-permute-start | bytes 104456 | tf_op jit(solution)/shard_map/ppermute | solution.py:220
  6.2 15.7 %collective-permute-start.8 = (bf16[128,1024]{1,0:T(8,128)(2,1)}, bf16[128,1024]{1,0:T(8,128)(2,1)S(1)}, u32[]{:S(2)}, u32[]{:S(2)}) collective-permute-start(bf16[128,1024]{1,0:T(8,128)(2,1)} %get-tuple-element.13.refs_29_.refs_37_), channel_id=1, source_target_pairs={{0,1},{1,0},{2,3},{3,2},{4,5},{5,4},{6,7},{7,6},{8,9},{9,8},{10,11... | collective-permute-start | bytes 786440 | tf_op jit(solution)/shard_map/ppermute | solution.py:212
  7.7 10.5 %collective-permute-start.5 = (bf16[128,1024]{1,0:T(8,128)(2,1)}, bf16[128,1024]{1,0:T(8,128)(2,1)S(1)}, u32[]{:S(2)}, u32[]{:S(2)}) collective-permute-start(bf16[128,1024]{1,0:T(8,128)(2,1)} %get-tuple-element.17.refs_13_.refs_21_), channel_id=1, source_target_pairs={{0,2},{1,3},{2,4},{3,5},{4,6},{5,7},{8,10},{9,11},{10,12},{11,13},... | collective-permute-start | bytes 786440 | tf_op jit(solution)/shard_map/ppermute | solution.py:216
  9.0 33.0 %collective-permute-start.3 = (bf16[32,2176]{1,0:T(8,128)(2,1)S(1)}, bf16[32,2176]{1,0:T(8,128)(2,1)S(1)}, u32[]{:S(2)}, u32[]{:S(2)}) collective-permute-start(bf16[32,2176]{1,0:T(8,128)(2,1)S(1)} %pad_maximum_fusion), channel_id=1, source_target_pairs={{0,1},{1,0},{2,3},{3,2},{4,5},{5,4},{6,7},{7,6},{8,9},{9,8},{10,11... | collective-permute-start | bytes 417800 | tf_op jit(solution)/shard_map/ppermute | solution.py:212
  18.1 56.6 %copy-start.6 = (bf16[128,1024]{1,0:T(8,128)(2,1)}, bf16[128,1024]{1,0:T(8,128)(2,1)S(1)}, u32[]{:S(2)}) copy-start(bf16[128,1024]{1,0:T(8,128)(2,1)S(1)} %collective-permute-done.5.refs_15_.refs_23_) | copy-start | bytes 786436
  18.1 9.4 %collective-permute-start.12 = (bf16[128,1024]{1,0:T(8,128)(2,1)S(1)}, bf16[128,1024]{1,0:T(8,128)(2,1)S(1)}, u32[]{:S(2)}, u32[]{:S(2)}) collective-permute-start(bf16[128,1024]{1,0:T(8,128)(2,1)S(1)} %collective-permute-done.5.refs_15_.refs_23_), channel_id=1, source_target_pairs={{2,3},{3,2},{4,5},{5,4},{6,7},{7,6},{10,11},{11,10},{12,13},{13,12... | collective-permute-start | bytes 786440 | tf_op jit(solution)/shard_map/ppermute | solution.py:212
  20.6 11.2 %collective-permute-start.6 = (bf16[128,1024]{1,0:T(8,128)(2,1)S(1)}, bf16[128,1024]{1,0:T(8,128)(2,1)S(1)}, u32[]{:S(2)}, u32[]{:S(2)}) collective-permute-start(bf16[128,1024]{1,0:T(8,128)(2,1)S(1)} %collective-permute-done.5.refs_15_.refs_23_), channel_id=1, source_target_pairs={{2,4},{3,5},{4,6},{5,7},{10,12},{11,13},{12,14},{13,15},{18,20},{1... | collective-permute-start | bytes 786440 | tf_op jit(solution)/shard_map/ppermute | solution.py:216
  21.9 52.9 %copy-start.5 = (bf16[128,1024]{1,0:T(8,128)(2,1)}, bf16[128,1024]{1,0:T(8,128)(2,1)S(1)}, u32[]{:S(2)}) copy-start(bf16[128,1024]{1,0:T(8,128)(2,1)S(1)} %collective-permute-done.8.refs_14_.refs_22_) | copy-start | bytes 786436
  21.9 15.4 %collective-permute-start.9 = (bf16[128,1024]{1,0:T(8,128)(2,1)S(1)}, bf16[128,1024]{1,0:T(8,128)(2,1)S(1)}, u32[]{:S(2)}, u32[]{:S(2)}) collective-permute-start(bf16[128,1024]{1,0:T(8,128)(2,1)S(1)} %collective-permute-done.8.refs_14_.refs_22_), channel_id=1, source_target_pairs={{0,2},{1,3},{2,4},{3,5},{4,6},{5,7},{8,10},{9,11},{10,12},{11,13},... | collective-permute-start | bytes 786440 | tf_op jit(solution)/shard_map/ppermute | solution.py:216
  23.2 21.3 %collective-permute-start.16 = (bf16[128,1024]{1,0:T(8,128)(2,1)}, bf16[128,1024]{1,0:T(8,128)(2,1)S(1)}, u32[]{:S(2)}, u32[]{:S(2)}) collective-permute-start(bf16[128,1024]{1,0:T(8,128)(2,1)} %get-tuple-element.17.refs_13_.refs_21_), channel_id=1, source_target_pairs={{0,1},{2,3},{4,5},{6,7},{8,9},{10,11},{12,13},{14,15},{16,17},{18,... | collective-permute-start | bytes 786440 | tf_op jit(solution)/shard_map/ppermute | solution.py:228
  27.6 47.2 %copy-start.7 = (bf16[128,1024]{1,0:T(8,128)(2,1)}, bf16[128,1024]{1,0:T(8,128)(2,1)S(1)}, u32[]{:S(2)}) copy-start(bf16[128,1024]{1,0:T(8,128)(2,1)S(1)} %collective-permute-done.12.refs_32_.refs_40_) | copy-start | bytes 786436
  31.7 43.1 %copy-start.8 = (bf16[128,1024]{1,0:T(8,128)(2,1)}, bf16[128,1024]{1,0:T(8,128)(2,1)S(1)}, u32[]{:S(2)}) copy-start(bf16[128,1024]{1,0:T(8,128)(2,1)S(1)} %collective-permute-done.6.refs_17_.refs_25_) | copy-start | bytes 786436
  31.7 20.4 %collective-permute-start.13 = (bf16[128,1024]{1,0:T(8,128)(2,1)S(1)}, bf16[128,1024]{1,0:T(8,128)(2,1)S(1)}, u32[]{:S(2)}, u32[]{:S(2)}) collective-permute-start(bf16[128,1024]{1,0:T(8,128)(2,1)S(1)} %collective-permute-done.6.refs_17_.refs_25_), channel_id=1, source_target_pairs={{4,6},{5,7},{12,14},{13,15},{20,22},{21,23},{28,30},{29,31}} | collective-permute-start | bytes 786440 | tf_op jit(solution)/shard_map/ppermute | solution.py:216
  37.3 37.5 %copy-start.9 = (bf16[128,1024]{1,0:T(8,128)(2,1)}, bf16[128,1024]{1,0:T(8,128)(2,1)S(1)}, u32[]{:S(2)}) copy-start(bf16[128,1024]{1,0:T(8,128)(2,1)S(1)} %collective-permute-done.9.refs_16_.refs_24_) | copy-start | bytes 786436
  37.3 10.7 %collective-permute-start.15 = (bf16[128,1024]{1,0:T(8,128)(2,1)S(1)}, bf16[128,1024]{1,0:T(8,128)(2,1)S(1)}, u32[]{:S(2)}, u32[]{:S(2)}) collective-permute-start(bf16[128,1024]{1,0:T(8,128)(2,1)S(1)} %collective-permute-done.9.refs_16_.refs_24_), channel_id=1, source_target_pairs={{2,3},{3,2},{4,5},{5,4},{6,7},{7,6},{10,11},{11,10},{12,13},{13,12... | collective-permute-start | bytes 786440 | tf_op jit(solution)/shard_map/ppermute | solution.py:212
  40.7 10.1 %collective-permute-start.10 = (bf16[128,1024]{1,0:T(8,128)(2,1)S(1)}, bf16[128,1024]{1,0:T(8,128)(2,1)S(1)}, u32[]{:S(2)}, u32[]{:S(2)}) collective-permute-start(bf16[128,1024]{1,0:T(8,128)(2,1)S(1)} %collective-permute-done.9.refs_16_.refs_24_), channel_id=1, source_target_pairs={{2,4},{3,5},{4,6},{5,7},{10,12},{11,13},{12,14},{13,15},{18,20},{1... | collective-permute-start | bytes 786440 | tf_op jit(solution)/shard_map/ppermute | solution.py:216
  42.1 32.7 %copy-start.1 = (bf16[64,2176]{1,0:T(8,128)(2,1)}, bf16[64,2176]{1,0:T(8,128)(2,1)S(1)}, u32[]{:S(2)}) copy-start(bf16[64,2176]{1,0:T(8,128)(2,1)S(1)} %constant_dynamic-update-slice_fusion.refs_0_.refs_5_.refs_9_) | copy-start | bytes 835588
  42.1 10.0 %collective-permute-start.7 = (bf16[128,1024]{1,0:T(8,128)(2,1)S(1)}, bf16[128,1024]{1,0:T(8,128)(2,1)}, u32[]{:S(2)}, u32[]{:S(2)}) collective-permute-start(bf16[128,1024]{1,0:T(8,128)(2,1)S(1)} %collective-permute-done.6.refs_17_.refs_25_), channel_id=1, source_target_pairs={{4,5},{5,4},{6,7},{7,6},{12,13},{13,12},{14,15},{15,14},{20,21},{2... | collective-permute-start | bytes 786440 | tf_op jit(solution)/shard_map/ppermute | solution.py:212
  44.5 30.3 %copy-start.10 = (bf16[128,1024]{1,0:T(8,128)(2,1)}, bf16[128,1024]{1,0:T(8,128)(2,1)S(1)}, u32[]{:S(2)}) copy-start(bf16[128,1024]{1,0:T(8,128)(2,1)S(1)} %collective-permute-done.16.refs_30_.refs_38_) | copy-start | bytes 786436
  44.5 15.2 %collective-permute-start.4 = (bf16[64,2176]{1,0:T(8,128)(2,1)S(1)}, bf16[64,2176]{1,0:T(8,128)(2,1)S(1)}, u32[]{:S(2)}, u32[]{:S(2)}) collective-permute-start(bf16[64,2176]{1,0:T(8,128)(2,1)S(1)} %constant_dynamic-update-slice_fusion.refs_0_.refs_5_.refs_9_), channel_id=1, source_target_pairs={{0,2},{1,3},{2,4},{3,5},{4,6},{5,7},{6,0},{7,1},{8,10},{9,11},{10,... | collective-permute-start | bytes 835592 | tf_op jit(solution)/shard_map/ppermute | solution.py:220
  48.0 26.8 %copy-start.12 = (bf16[128,1024]{1,0:T(8,128)(2,1)}, bf16[128,1024]{1,0:T(8,128)(2,1)S(1)}, u32[]{:S(2)}) copy-start(bf16[128,1024]{1,0:T(8,128)(2,1)S(1)} %collective-permute-done.15.refs_31_.refs_39_) | copy-start | bytes 786436
  50.8 24.0 %copy-start.13 = (bf16[128,1024]{1,0:T(8,128)(2,1)}, bf16[128,1024]{1,0:T(8,128)(2,1)S(1)}, u32[]{:S(2)}) copy-start(bf16[128,1024]{1,0:T(8,128)(2,1)S(1)} %collective-permute-done.10.refs_18_.refs_26_) | copy-start | bytes 786436
  50.8 13.2 %collective-permute-start.17 = (bf16[128,1024]{1,0:T(8,128)(2,1)S(1)}, bf16[128,1024]{1,0:T(8,128)(2,1)}, u32[]{:S(2)}, u32[]{:S(2)}) collective-permute-start(bf16[128,1024]{1,0:T(8,128)(2,1)S(1)} %collective-permute-done.10.refs_18_.refs_26_), channel_id=1, source_target_pairs={{4,6},{5,7},{12,14},{13,15},{20,22},{21,23},{28,30},{29,31}} | collective-permute-start | bytes 786440 | tf_op jit(solution)/shard_map/ppermute | solution.py:216
  52.1 22.7 %copy-start.11 = (bf16[128,1024]{1,0:T(8,128)(2,1)}, bf16[128,1024]{1,0:T(8,128)(2,1)S(1)}, u32[]{:S(2)}) copy-start(bf16[128,1024]{1,0:T(8,128)(2,1)S(1)} %collective-permute-done.13.refs_19_.refs_27_) | copy-start | bytes 786436
  52.1 19.1 %collective-permute-start.11 = (bf16[64,2176]{1,0:T(8,128)(2,1)S(1)}, bf16[64,2176]{1,0:T(8,128)(2,1)S(1)}, u32[]{:S(2)}, u32[]{:S(2)}) collective-permute-start(bf16[64,2176]{1,0:T(8,128)(2,1)S(1)} %constant_dynamic-update-slice_fusion.refs_0_.refs_5_.refs_9_), channel_id=1, source_target_pairs={{0,4},{1,5},{2,6},{3,7},{4,0},{5,1},{6,2},{7,3},{8,12},{9,13},{10,... | collective-permute-start | bytes 835592 | tf_op jit(solution)/shard_map/ppermute | solution.py:220
  52.2 19.1 %collective-permute-start.14 = (bf16[64,2176]{1,0:T(8,128)(2,1)S(1)}, bf16[64,2176]{1,0:T(8,128)(2,1)S(1)}, u32[]{:S(2)}, u32[]{:S(2)}) collective-permute-start(bf16[64,2176]{1,0:T(8,128)(2,1)S(1)} %constant_dynamic-update-slice_fusion.refs_0_.refs_5_.refs_9_), channel_id=1, source_target_pairs={{0,6},{1,7},{2,0},{3,1},{4,2},{5,3},{6,4},{7,5},{8,14},{9,15},{10,... | collective-permute-start | bytes 835592 | tf_op jit(solution)/shard_map/ppermute | solution.py:220
  55.6 15.3 %collective-permute-start.18 = (bf16[128,1024]{1,0:T(8,128)(2,1)S(1)}, bf16[128,1024]{1,0:T(8,128)(2,1)}, u32[]{:S(2)}, u32[]{:S(2)}) collective-permute-start(bf16[128,1024]{1,0:T(8,128)(2,1)S(1)} %collective-permute-done.10.refs_18_.refs_26_), channel_id=1, source_target_pairs={{4,5},{5,4},{6,7},{7,6},{12,13},{13,12},{14,15},{15,14},{20,21},{2... | collective-permute-start | bytes 786440 | tf_op jit(solution)/shard_map/ppermute | solution.py:212
  59.7 11.1 %collective-permute-start.20 = (bf16[128,1024]{1,0:T(8,128)(2,1)S(1)}, bf16[128,1024]{1,0:T(8,128)(2,1)}, u32[]{:S(2)}, u32[]{:S(2)}) collective-permute-start(bf16[128,1024]{1,0:T(8,128)(2,1)S(1)} %collective-permute-done.13.refs_19_.refs_27_), channel_id=1, source_target_pairs={{6,7},{7,6},{14,15},{15,14},{22,23},{23,22},{30,31},{31,30}} | collective-permute-start | bytes 786440 | tf_op jit(solution)/shard_map/ppermute | solution.py:212
  64.1 10.7 %collective-permute-start.19 = (bf16[128,1024]{1,0:T(8,128)(2,1)}, bf16[128,1024]{1,0:T(8,128)(2,1)}, u32[]{:S(2)}, u32[]{:S(2)}) collective-permute-start(bf16[128,1024]{1,0:T(8,128)(2,1)} %collective-permute-done.17.refs_20_.refs_28_), channel_id=1, source_target_pairs={{6,7},{7,6},{14,15},{15,14},{22,23},{23,22},{30,31},{31,30}} | collective-permute-start | bytes 786440 | tf_op jit(solution)/shard_map/ppermute | solution.py:212
  (3 other events, 22.3 us)

commit v14 on v12

--- a/solution.py
+++ b/solution.py
@@ -13,7 +13,7 @@
 HD = 128
 GQ = H // KVH
 REACH = 7
-SLAB = 2
+SLAB = 4
 BOTH = 2
 FILL = -1e30
 
@@ -198,7 +198,7 @@
         ),
         out_shape=out_shape,
         input_output_aliases=aliases,
-        compiler_params=pltpu.CompilerParams(vmem_limit_bytes=24 * 1024 * 1024),
+        compiler_params=pltpu.CompilerParams(vmem_limit_bytes=32 * 1024 * 1024),
     )(*args)
 
 

time: 87 us -> 87.2 us (level)
  the two profiles are of different devices: /device:TPU:27 before, /device:TPU:26 now
where the time goes in v14:
time: 87.2 us; the launch traced here: 86.7 us
  starting transfers between devices  39.7 us (46%)
  Pallas kernels  21.9 us (25%)
  waiting for transfers between devices  20.2 us (23%)
  other arithmetic  2.14 us (2%)
  local copies, waits for them, and re-layouts  1.61 us (2%)
  between operations  1.2 us (1%)
    ppermute x8, starting transfers between devices, swap(): lax.ppermute(value, 'resp', [(r, r ^ 1) for r in range(2 * first, count)])  22.1 us
    pallas_call x2, Pallas kernels, attend(): pl.pallas_call(functools.partial(attend_kernel, pairs, parts, tile, tiles...  20 us
    ppermute x6, waiting for transfers between devices, climb(): return lax.ppermute(value, 'resp', pairs)  12.7 us
    ppermute x6, starting transfers between devices, climb(): return lax.ppermute(value, 'resp', pairs)  7.7 us
    ppermute x6, waiting for transfers between devices, shift(): lax.ppermute(value, axis, [(r, (r + by) % size) for r in range(size)])  7.01 us
    ppermute x6, starting transfers between devices, shift(): lax.ppermute(value, axis, [(r, (r + by) % size) for r in range(size)])  6.45 us
    ppermute x1, starting transfers between devices, on_device(): upper = lax.ppermute(after(mine, partner), 'resp', upper)  3.44 us
    pallas_call x1, Pallas kernels, halves(): pl.pallas_call(halves_kernel, grid_spec=pltpu.PrefetchScalarGridSpec(num_...  1.85 us
  transfers between devices with their start and end apart: 21, of which 9 were waited for; matrix products, arithmetic and copies ran while one was open for 3% of the time, Pallas kernels for 11%

profile of v14, /device:TPU:26, one launch (start us, length us, event | category | flops | bytes accessed | tf_op | source)
XLA Modules:
  0.0 86.7 jit_solution(9031987551266035746)
XLA Ops:
  0.0 1.9 %shard_map.64 = (bf16[128,1024]{1,0:T(8,128)(2,1)}, bf16[128,1024]{1,0:T(8,128)(2,1)}) custom-call(s32[1]{0:T(128)} %bitcast.10.meta_ref, bf16[128,2048]{1,0:T(8,128)(2,1)} %bitcast.24, bf16[128,2048]{1,0:T(8,128)(2,1)} %bitcast.25), custom_call_target="tpu_custom_call" | custom-call | tf_op jit(solution)/shard_map/pallas_call | solution.py:29
  1.9 1.5 %collective-permute-start.8 = (bf16[128,1024]{1,0:T(8,128)(2,1)}, bf16[128,1024]{1,0:T(8,128)(2,1)S(1)}, u32[]{:S(2)}, u32[]{:S(2)}) collective-permute-start(bf16[128,1024]{1,0:T(8,128)(2,1)} %get-tuple-element.16.refs_11_.refs_19_), channel_id=1, source_target_pairs={{0,1},{1,0},{2,3},{3,2},{4,5},{5,4},{6,7},{7,6},{8,9},{9,8},{10,11... | collective-permute-start | bytes 786440 | tf_op jit(solution)/shard_map/ppermute | solution.py:216
  3.4 1.3 %collective-permute-start.5 = (bf16[128,1024]{1,0:T(8,128)(2,1)}, bf16[128,1024]{1,0:T(8,128)(2,1)S(1)}, u32[]{:S(2)}, u32[]{:S(2)}) collective-permute-start(bf16[128,1024]{1,0:T(8,128)(2,1)} %get-tuple-element.20.refs_14_.refs_22_), channel_id=1, source_target_pairs={{0,2},{1,3},{2,4},{3,5},{4,6},{5,7},{8,10},{9,11},{10,12},{11,13},... | collective-permute-start | bytes 786440 | tf_op jit(solution)/shard_map/ppermute | solution.py:220
  4.7 0.8 slice_bitcast_fusion.1
  5.6 1.0 %select_reduce_fusion = bf16[4,8,2048]{2,1,0:T(8,128)(2,1)S(1)} fusion(pred[4,4]{1,0:T(4,128)(4,1)S(1)} %get-tuple-element.28, bf16[4,8,2048]{2,1,0:T(8,128)(2,1)} %param.9), kind=kLoop, calls=%fused_computation | loop fusion | flops 458752 | bytes 262160 | tf_op jit(solution)/shard_map/reduce_sum | solution.py:245
  6.7 0.7 convert_convert_fusion
  7.5 0.6 collective-permute-start.1
  8.1 1.4 %collective-permute-start.2 = (bf16[8,2176]{1,0:T(8,128)(2,1)S(1)}, bf16[8,2176]{1,0:T(8,128)(2,1)S(1)}, u32[]{:S(2)}, u32[]{:S(2)}) collective-permute-start(bf16[8,2176]{1,0:T(8,128)(2,1)S(1)} %get-tuple-element.29), channel_id=1, source_target_pairs={{0,24},{8,0},{16,8},{24,16},{1,25},{9,1},{17,9},{25,17},{2,26},{10... | collective-permute-start | bytes 104456 | tf_op jit(solution)/shard_map/ppermute | solution.py:224
  9.5 1.4 %collective-permute-done = bf16[8,2176]{1,0:T(8,128)(2,1)S(1)} collective-permute-done((bf16[8,2176]{1,0:T(8,128)(2,1)S(1)}, bf16[8,2176]{1,0:T(8,128)(2,1)S(1)}, u32[]{:S(2)}, u32[]{:S(2)}) %collective-permute-start) | collective-permute-done | bytes 34848 | tf_op jit(solution)/shard_map/ppermute | solution.py:224
  10.8 0.7 collective-permute-done.1
  12.2 1.0 %collective-permute-done.5.refs_16_.refs_24_ = bf16[128,1024]{1,0:T(8,128)(2,1)S(1)} collective-permute-done((bf16[128,1024]{1,0:T(8,128)(2,1)}, bf16[128,1024]{1,0:T(8,128)(2,1)S(1)}, u32[]{:S(2)}, u32[]{:S(2)}) %collective-permute-start.5) | collective-permute-done | bytes 262176 | tf_op jit(solution)/shard_map/ppermute | solution.py:220
  13.2 1.3 %collective-permute-start.6 = (bf16[128,1024]{1,0:T(8,128)(2,1)S(1)}, bf16[128,1024]{1,0:T(8,128)(2,1)S(1)}, u32[]{:S(2)}, u32[]{:S(2)}) collective-permute-start(bf16[128,1024]{1,0:T(8,128)(2,1)S(1)} %collective-permute-done.5.refs_16_.refs_24_), channel_id=1, source_target_pairs={{2,4},{3,5},{4,6},{5,7},{10,12},{11,13},{12,14},{13,15},{18,20},{1... | collective-permute-start | bytes 786440 | tf_op jit(solution)/shard_map/ppermute | solution.py:220
  14.5 2.4 %collective-permute-start.12 = (bf16[128,1024]{1,0:T(8,128)(2,1)S(1)}, bf16[128,1024]{1,0:T(8,128)(2,1)S(1)}, u32[]{:S(2)}, u32[]{:S(2)}) collective-permute-start(bf16[128,1024]{1,0:T(8,128)(2,1)S(1)} %collective-permute-done.5.refs_16_.refs_24_), channel_id=1, source_target_pairs={{2,3},{3,2},{4,5},{5,4},{6,7},{7,6},{10,11},{11,10},{12,13},{13,12... | collective-permute-start | bytes 786440 | tf_op jit(solution)/shard_map/ppermute | solution.py:216
  17.0 1.3 %collective-permute-start.9 = (bf16[128,1024]{1,0:T(8,128)(2,1)S(1)}, bf16[128,1024]{1,0:T(8,128)(2,1)S(1)}, u32[]{:S(2)}, u32[]{:S(2)}) collective-permute-start(bf16[128,1024]{1,0:T(8,128)(2,1)S(1)} %collective-permute-done.8.refs_15_.refs_23_), channel_id=1, source_target_pairs={{0,2},{1,3},{2,4},{3,5},{4,6},{5,7},{8,10},{9,11},{10,12},{11,13},... | collective-permute-start | bytes 786440 | tf_op jit(solution)/shard_map/ppermute | solution.py:220
  18.3 3.4 %collective-permute-start.16 = (bf16[128,1024]{1,0:T(8,128)(2,1)}, bf16[128,1024]{1,0:T(8,128)(2,1)S(1)}, u32[]{:S(2)}, u32[]{:S(2)}) collective-permute-start(bf16[128,1024]{1,0:T(8,128)(2,1)} %get-tuple-element.20.refs_14_.refs_22_), channel_id=1, source_target_pairs={{0,1},{2,3},{4,5},{6,7},{8,9},{10,11},{12,13},{14,15},{16,17},{18,... | collective-permute-start | bytes 786440 | tf_op jit(solution)/shard_map/ppermute | solution.py:232
  21.7 2.6 %collective-permute-done.6.refs_18_.refs_26_ = bf16[128,1024]{1,0:T(8,128)(2,1)S(1)} collective-permute-done((bf16[128,1024]{1,0:T(8,128)(2,1)S(1)}, bf16[128,1024]{1,0:T(8,128)(2,1)S(1)}, u32[]{:S(2)}, u32[]{:S(2)}) %collective-permute-start.6) | collective-permute-done | bytes 262176 | tf_op jit(solution)/shard_map/ppermute | solution.py:220
  24.7 1.3 %collective-permute-start.13 = (bf16[128,1024]{1,0:T(8,128)(2,1)S(1)}, bf16[128,1024]{1,0:T(8,128)(2,1)S(1)}, u32[]{:S(2)}, u32[]{:S(2)}) collective-permute-start(bf16[128,1024]{1,0:T(8,128)(2,1)S(1)} %collective-permute-done.6.refs_18_.refs_26_), channel_id=1, source_target_pairs={{4,6},{5,7},{12,14},{13,15},{20,22},{21,23},{28,30},{29,31}} | collective-permute-start | bytes 786440 | tf_op jit(solution)/shard_map/ppermute | solution.py:220
  26.0 3.1 %collective-permute-start.7 = (bf16[128,1024]{1,0:T(8,128)(2,1)S(1)}, bf16[128,1024]{1,0:T(8,128)(2,1)S(1)}, u32[]{:S(2)}, u32[]{:S(2)}) collective-permute-start(bf16[128,1024]{1,0:T(8,128)(2,1)S(1)} %collective-permute-done.6.refs_18_.refs_26_), channel_id=1, source_target_pairs={{4,5},{5,4},{6,7},{7,6},{12,13},{13,12},{14,15},{15,14},{20,21},{2... | collective-permute-start | bytes 786440 | tf_op jit(solution)/shard_map/ppermute | solution.py:216
  29.2 0.6 collective-permute-done.9.refs_17_.refs_25_
  29.8 1.3 %collective-permute-start.10 = (bf16[128,1024]{1,0:T(8,128)(2,1)S(1)}, bf16[128,1024]{1,0:T(8,128)(2,1)}, u32[]{:S(2)}, u32[]{:S(2)}) collective-permute-start(bf16[128,1024]{1,0:T(8,128)(2,1)S(1)} %collective-permute-done.9.refs_17_.refs_25_), channel_id=1, source_target_pairs={{2,4},{3,5},{4,6},{5,7},{10,12},{11,13},{12,14},{13,15},{18,20},{1... | collective-permute-start | bytes 786440 | tf_op jit(solution)/shard_map/ppermute | solution.py:220
  31.1 3.0 %collective-permute-start.15 = (bf16[128,1024]{1,0:T(8,128)(2,1)S(1)}, bf16[128,1024]{1,0:T(8,128)(2,1)S(1)}, u32[]{:S(2)}, u32[]{:S(2)}) collective-permute-start(bf16[128,1024]{1,0:T(8,128)(2,1)S(1)} %collective-permute-done.9.refs_17_.refs_25_), channel_id=1, source_target_pairs={{2,3},{3,2},{4,5},{5,4},{6,7},{7,6},{10,11},{11,10},{12,13},{13,12... | collective-permute-start | bytes 786440 | tf_op jit(solution)/shard_map/ppermute | solution.py:216
  34.2 7.6 %collective-permute-done.10.refs_19_.refs_27_ = bf16[128,1024]{1,0:T(8,128)(2,1)} collective-permute-done((bf16[128,1024]{1,0:T(8,128)(2,1)S(1)}, bf16[128,1024]{1,0:T(8,128)(2,1)}, u32[]{:S(2)}, u32[]{:S(2)}) %collective-permute-start.10) | collective-permute-done | bytes 262176 | tf_op jit(solution)/shard_map/ppermute | solution.py:220
  41.8 1.3 %collective-permute-start.17 = (bf16[128,1024]{1,0:T(8,128)(2,1)}, bf16[128,1024]{1,0:T(8,128)(2,1)}, u32[]{:S(2)}, u32[]{:S(2)}) collective-permute-start(bf16[128,1024]{1,0:T(8,128)(2,1)} %collective-permute-done.10.refs_19_.refs_27_), channel_id=1, source_target_pairs={{4,6},{5,7},{12,14},{13,15},{20,22},{21,23},{28,30},{29,31}} | collective-permute-start | bytes 786440 | tf_op jit(solution)/shard_map/ppermute | solution.py:220
  43.1 4.3 %collective-permute-start.11 = (bf16[64,2176]{1,0:T(8,128)(2,1)S(1)}, bf16[64,2176]{1,0:T(8,128)(2,1)S(1)}, u32[]{:S(2)}, u32[]{:S(2)}) collective-permute-start(bf16[64,2176]{1,0:T(8,128)(2,1)S(1)} %constant_dynamic-update-slice_fusion.refs_1_.refs_6_.refs_10_.refs_3_.refs_7_), channel_id=1, source_target_pairs={{0,4},{1,5},{2,6},{3,7},{4,0},{5,1},{6,2},{7,3},{8,12},{9,13},{10,... | collective-permute-start | bytes 835592 | tf_op jit(solution)/shard_map/ppermute | solution.py:224
  47.5 2.7 %collective-permute-start.20 = (bf16[128,1024]{1,0:T(8,128)(2,1)S(1)}, bf16[128,1024]{1,0:T(8,128)(2,1)}, u32[]{:S(2)}, u32[]{:S(2)}) collective-permute-start(bf16[128,1024]{1,0:T(8,128)(2,1)S(1)} %collective-permute-done.13.refs_20_.refs_28_), channel_id=1, source_target_pairs={{6,7},{7,6},{14,15},{15,14},{22,23},{23,22},{30,31},{31,30}} | collective-permute-start | bytes 786440 | tf_op jit(solution)/shard_map/ppermute | solution.py:216
  50.2 3.1 %collective-permute-start.18 = (bf16[128,1024]{1,0:T(8,128)(2,1)}, bf16[128,1024]{1,0:T(8,128)(2,1)}, u32[]{:S(2)}, u32[]{:S(2)}) collective-permute-start(bf16[128,1024]{1,0:T(8,128)(2,1)} %collective-permute-done.10.refs_19_.refs_27_), channel_id=1, source_target_pairs={{4,5},{5,4},{6,7},{7,6},{12,13},{13,12},{14,15},{15,14},{20,21},{2... | collective-permute-start | bytes 786440 | tf_op jit(solution)/shard_map/ppermute | solution.py:216
  53.3 0.9 %collective-permute-done.17.refs_21_.refs_29_ = bf16[128,1024]{1,0:T(8,128)(2,1)} collective-permute-done((bf16[128,1024]{1,0:T(8,128)(2,1)}, bf16[128,1024]{1,0:T(8,128)(2,1)}, u32[]{:S(2)}, u32[]{:S(2)}) %collective-permute-start.17) | collective-permute-done | bytes 262176 | tf_op jit(solution)/shard_map/ppermute | solution.py:220
  54.3 5.6 %collective-permute-start.19 = (bf16[128,1024]{1,0:T(8,128)(2,1)}, bf16[128,1024]{1,0:T(8,128)(2,1)}, u32[]{:S(2)}, u32[]{:S(2)}) collective-permute-start(bf16[128,1024]{1,0:T(8,128)(2,1)} %collective-permute-done.17.refs_21_.refs_29_), channel_id=1, source_target_pairs={{6,7},{7,6},{14,15},{15,14},{22,23},{23,22},{30,31},{31,30}} | collective-permute-start | bytes 786440 | tf_op jit(solution)/shard_map/ppermute | solution.py:216
  60.7 4.9 %collective-permute-done.11.refs_3_.refs_8_.refs_12_.refs_5_.refs_9_ = bf16[64,2176]{1,0:T(8,128)(2,1)S(1)} collective-permute-done((bf16[64,2176]{1,0:T(8,128)(2,1)S(1)}, bf16[64,2176]{1,0:T(8,128)(2,1)S(1)}, u32[]{:S(2)}, u32[]{:S(2)}) %collective-permute-start.11) | collective-permute-done | bytes 278560 | tf_op jit(solution)/shard_map/ppermute | solution.py:224
  65.7 0.6 copy-done.3
  66.4 9.7 %shard_map.65 = (bf16[128,8192]{1,0:T(8,128)(2,1)}, f32[128,1280]{1,0:T(8,128)S(1)}, s32[1]{0:T(128)}) custom-call(s32[3]{0:T(128)S(1)} %add_add_fusion.1.meta_ref, s32[1,128]{1,0:T(1,128)S(1)} %copy-done, bf16[64,2176]{1,0:T(8,128)(2,1)} %copy-done.1, bf16[64,2176]{1,0:T(8,128)(2,1)} %copy-done.2, bf16[64,2176]{1,0:T(8,128)(2,1)} %copy-done.3, ...), custom_call_target="tpu_custom_call" | custom-call | tf_op jit(solution)/shard_map/pallas_call | solution.py:187
  76.2 10.3 %shard_map.66 = bf16[128,8192]{1,0:T(8,128)(2,1)} custom-call(s32[3]{0:T(128)S(1)} %add_add_fusion.meta_ref, f32[128,1280]{1,0:T(8,128)S(1)} %get-tuple-element.22.refs_0_, s32[1]{0:T(128)} %get-tuple-element.23.refs_1_, bf16[128,8192]{1,0:T(8,128)(2,1)} %bitcast.23, bf16[64,2176]{1,0:T(8,128)(2,1)} %copy-done.1, ...), custom_call_target="tpu_custom_call", output_to_operand_aliasing={{}: (28, {})} | custom-call | tf_op jit(solution)/shard_map/pallas_call | solution.py:187
  (56 shorter events, 1.8 us)
Async XLA Ops:
  0.0 66.4 %copy-start = (s32[1,128]{1,0:T(1,128)S(1)}, s32[1,128]{1,0:T(1,128)}, u32[]{:S(2)}) copy-start(s32[1,128]{1,0:T(1,128)} %refs_0_.1) | copy-start | bytes 1540
  1.9 15.1 %collective-permute-start.8 = (bf16[128,1024]{1,0:T(8,128)(2,1)}, bf16[128,1024]{1,0:T(8,128)(2,1)S(1)}, u32[]{:S(2)}, u32[]{:S(2)}) collective-permute-start(bf16[128,1024]{1,0:T(8,128)(2,1)} %get-tuple-element.16.refs_11_.refs_19_), channel_id=1, source_target_pairs={{0,1},{1,0},{2,3},{3,2},{4,5},{5,4},{6,7},{7,6},{8,9},{9,8},{10,11... | collective-permute-start | bytes 786440 | tf_op jit(solution)/shard_map/ppermute | solution.py:216
  3.4 9.9 %collective-permute-start.5 = (bf16[128,1024]{1,0:T(8,128)(2,1)}, bf16[128,1024]{1,0:T(8,128)(2,1)S(1)}, u32[]{:S(2)}, u32[]{:S(2)}) collective-permute-start(bf16[128,1024]{1,0:T(8,128)(2,1)} %get-tuple-element.20.refs_14_.refs_22_), channel_id=1, source_target_pairs={{0,2},{1,3},{2,4},{3,5},{4,6},{5,7},{8,10},{9,11},{10,12},{11,13},... | collective-permute-start | bytes 786440 | tf_op jit(solution)/shard_map/ppermute | solution.py:220
  7.4 3.4 %collective-permute-start = (bf16[8,2176]{1,0:T(8,128)(2,1)S(1)}, bf16[8,2176]{1,0:T(8,128)(2,1)S(1)}, u32[]{:S(2)}, u32[]{:S(2)}) collective-permute-start(bf16[8,2176]{1,0:T(8,128)(2,1)S(1)} %get-tuple-element.30), channel_id=1, source_target_pairs={{0,8},{8,16},{16,24},{24,0},{1,9},{9,17},{17,25},{25,1},{2,10},{10... | collective-permute-start | bytes 104456 | tf_op jit(solution)/shard_map/ppermute | solution.py:224
  7.5 4.1 %collective-permute-start.1 = (bf16[8,2176]{1,0:T(8,128)(2,1)S(1)}, bf16[8,2176]{1,0:T(8,128)(2,1)S(1)}, u32[]{:S(2)}, u32[]{:S(2)}) collective-permute-start(bf16[8,2176]{1,0:T(8,128)(2,1)S(1)} %get-tuple-element.31), channel_id=1, source_target_pairs={{0,16},{8,24},{16,0},{24,8},{1,17},{9,25},{17,1},{25,9},{2,18},{10... | collective-permute-start | bytes 104456 | tf_op jit(solution)/shard_map/ppermute | solution.py:224
  8.1 3.5 %collective-permute-start.2 = (bf16[8,2176]{1,0:T(8,128)(2,1)S(1)}, bf16[8,2176]{1,0:T(8,128)(2,1)S(1)}, u32[]{:S(2)}, u32[]{:S(2)}) collective-permute-start(bf16[8,2176]{1,0:T(8,128)(2,1)S(1)} %get-tuple-element.29), channel_id=1, source_target_pairs={{0,24},{8,0},{16,8},{24,16},{1,25},{9,1},{17,9},{25,17},{2,26},{10... | collective-permute-start | bytes 104456 | tf_op jit(solution)/shard_map/ppermute | solution.py:224
  11.6 19.5 %collective-permute-start.3 = (bf16[32,2176]{1,0:T(8,128)(2,1)S(1)}, bf16[32,2176]{1,0:T(8,128)(2,1)S(1)}, u32[]{:S(2)}, u32[]{:S(2)}) collective-permute-start(bf16[32,2176]{1,0:T(8,128)(2,1)S(1)} %pad_maximum_fusion), channel_id=1, source_target_pairs={{0,1},{1,0},{2,3},{3,2},{4,5},{5,4},{6,7},{7,6},{8,9},{9,8},{10,11... | collective-permute-start | bytes 417800 | tf_op jit(solution)/shard_map/ppermute | solution.py:216
  13.2 52.4 %copy-start.6 = (bf16[128,1024]{1,0:T(8,128)(2,1)}, bf16[128,1024]{1,0:T(8,128)(2,1)S(1)}, u32[]{:S(2)}) copy-start(bf16[128,1024]{1,0:T(8,128)(2,1)S(1)} %collective-permute-done.5.refs_16_.refs_24_) | copy-start | bytes 786436
  13.2 11.1 %collective-permute-start.6 = (bf16[128,1024]{1,0:T(8,128)(2,1)S(1)}, bf16[128,1024]{1,0:T(8,128)(2,1)S(1)}, u32[]{:S(2)}, u32[]{:S(2)}) collective-permute-start(bf16[128,1024]{1,0:T(8,128)(2,1)S(1)} %collective-permute-done.5.refs_16_.refs_24_), channel_id=1, source_target_pairs={{2,4},{3,5},{4,6},{5,7},{10,12},{11,13},{12,14},{13,15},{18,20},{1... | collective-permute-start | bytes 786440 | tf_op jit(solution)/shard_map/ppermute | solution.py:220
  14.5 10.2 %collective-permute-start.12 = (bf16[128,1024]{1,0:T(8,128)(2,1)S(1)}, bf16[128,1024]{1,0:T(8,128)(2,1)S(1)}, u32[]{:S(2)}, u32[]{:S(2)}) collective-permute-start(bf16[128,1024]{1,0:T(8,128)(2,1)S(1)} %collective-permute-done.5.refs_16_.refs_24_), channel_id=1, source_target_pairs={{2,3},{3,2},{4,5},{5,4},{6,7},{7,6},{10,11},{11,10},{12,13},{13,12... | collective-permute-start | bytes 786440 | tf_op jit(solution)/shard_map/ppermute | solution.py:216
  17.0 48.6 %copy-start.5 = (bf16[128,1024]{1,0:T(8,128)(2,1)}, bf16[128,1024]{1,0:T(8,128)(2,1)S(1)}, u32[]{:S(2)}) copy-start(bf16[128,1024]{1,0:T(8,128)(2,1)S(1)} %collective-permute-done.8.refs_15_.refs_23_) | copy-start | bytes 786436
  17.0 12.8 %collective-permute-start.9 = (bf16[128,1024]{1,0:T(8,128)(2,1)S(1)}, bf16[128,1024]{1,0:T(8,128)(2,1)S(1)}, u32[]{:S(2)}, u32[]{:S(2)}) collective-permute-start(bf16[128,1024]{1,0:T(8,128)(2,1)S(1)} %collective-permute-done.8.refs_15_.refs_23_), channel_id=1, source_target_pairs={{0,2},{1,3},{2,4},{3,5},{4,6},{5,7},{8,10},{9,11},{10,12},{11,13},... | collective-permute-start | bytes 786440 | tf_op jit(solution)/shard_map/ppermute | solution.py:220
  18.3 15.9 %collective-permute-start.16 = (bf16[128,1024]{1,0:T(8,128)(2,1)}, bf16[128,1024]{1,0:T(8,128)(2,1)S(1)}, u32[]{:S(2)}, u32[]{:S(2)}) collective-permute-start(bf16[128,1024]{1,0:T(8,128)(2,1)} %get-tuple-element.20.refs_14_.refs_22_), channel_id=1, source_target_pairs={{0,1},{2,3},{4,5},{6,7},{8,9},{10,11},{12,13},{14,15},{16,17},{18,... | collective-permute-start | bytes 786440 | tf_op jit(solution)/shard_map/ppermute | solution.py:232
  24.3 41.3 %copy-start.9 = (bf16[128,1024]{1,0:T(8,128)(2,1)}, bf16[128,1024]{1,0:T(8,128)(2,1)S(1)}, u32[]{:S(2)}) copy-start(bf16[128,1024]{1,0:T(8,128)(2,1)S(1)} %collective-permute-done.6.refs_18_.refs_26_) | copy-start | bytes 786436
  24.7 51.4 %copy-start.7 = (bf16[128,1024]{1,0:T(8,128)(2,1)}, bf16[128,1024]{1,0:T(8,128)(2,1)S(1)}, u32[]{:S(2)}) copy-start(bf16[128,1024]{1,0:T(8,128)(2,1)S(1)} %collective-permute-done.12.refs_14_.refs_22_) | copy-start | bytes 786436
  24.7 22.7 %collective-permute-start.13 = (bf16[128,1024]{1,0:T(8,128)(2,1)S(1)}, bf16[128,1024]{1,0:T(8,128)(2,1)S(1)}, u32[]{:S(2)}, u32[]{:S(2)}) collective-permute-start(bf16[128,1024]{1,0:T(8,128)(2,1)S(1)} %collective-permute-done.6.refs_18_.refs_26_), channel_id=1, source_target_pairs={{4,6},{5,7},{12,14},{13,15},{20,22},{21,23},{28,30},{29,31}} | collective-permute-start | bytes 786440 | tf_op jit(solution)/shard_map/ppermute | solution.py:220
  26.0 17.1 %collective-permute-start.7 = (bf16[128,1024]{1,0:T(8,128)(2,1)S(1)}, bf16[128,1024]{1,0:T(8,128)(2,1)S(1)}, u32[]{:S(2)}, u32[]{:S(2)}) collective-permute-start(bf16[128,1024]{1,0:T(8,128)(2,1)S(1)} %collective-permute-done.6.refs_18_.refs_26_), channel_id=1, source_target_pairs={{4,5},{5,4},{6,7},{7,6},{12,13},{13,12},{14,15},{15,14},{20,21},{2... | collective-permute-start | bytes 786440 | tf_op jit(solution)/shard_map/ppermute | solution.py:216
  29.8 35.8 %copy-start.10 = (bf16[128,1024]{1,0:T(8,128)(2,1)}, bf16[128,1024]{1,0:T(8,128)(2,1)S(1)}, u32[]{:S(2)}) copy-start(bf16[128,1024]{1,0:T(8,128)(2,1)S(1)} %collective-permute-done.9.refs_17_.refs_25_) | copy-start | bytes 786436
  29.8 12.0 %collective-permute-start.10 = (bf16[128,1024]{1,0:T(8,128)(2,1)S(1)}, bf16[128,1024]{1,0:T(8,128)(2,1)}, u32[]{:S(2)}, u32[]{:S(2)}) collective-permute-start(bf16[128,1024]{1,0:T(8,128)(2,1)S(1)} %collective-permute-done.9.refs_17_.refs_25_), channel_id=1, source_target_pairs={{2,4},{3,5},{4,6},{5,7},{10,12},{11,13},{12,14},{13,15},{18,20},{1... | collective-permute-start | bytes 786440 | tf_op jit(solution)/shard_map/ppermute | solution.py:220
  31.1 10.7 %collective-permute-start.15 = (bf16[128,1024]{1,0:T(8,128)(2,1)S(1)}, bf16[128,1024]{1,0:T(8,128)(2,1)S(1)}, u32[]{:S(2)}, u32[]{:S(2)}) collective-permute-start(bf16[128,1024]{1,0:T(8,128)(2,1)S(1)} %collective-permute-done.9.refs_17_.refs_25_), channel_id=1, source_target_pairs={{2,3},{3,2},{4,5},{5,4},{6,7},{7,6},{10,11},{11,10},{12,13},{13,12... | collective-permute-start | bytes 786440 | tf_op jit(solution)/shard_map/ppermute | solution.py:216
  34.1 31.5 %copy-start.1 = (bf16[64,2176]{1,0:T(8,128)(2,1)}, bf16[64,2176]{1,0:T(8,128)(2,1)S(1)}, u32[]{:S(2)}) copy-start(bf16[64,2176]{1,0:T(8,128)(2,1)S(1)} %constant_dynamic-update-slice_fusion.refs_1_.refs_6_.refs_10_.refs_3_.refs_7_) | copy-start | bytes 835588
  34.2 42.0 %copy-start.8 = (bf16[128,1024]{1,0:T(8,128)(2,1)}, bf16[128,1024]{1,0:T(8,128)(2,1)S(1)}, u32[]{:S(2)}) copy-start(bf16[128,1024]{1,0:T(8,128)(2,1)S(1)} %collective-permute-done.16.refs_12_.refs_20_) | copy-start | bytes 786436
  34.2 16.0 %collective-permute-start.4 = (bf16[64,2176]{1,0:T(8,128)(2,1)S(1)}, bf16[64,2176]{1,0:T(8,128)(2,1)S(1)}, u32[]{:S(2)}, u32[]{:S(2)}) collective-permute-start(bf16[64,2176]{1,0:T(8,128)(2,1)S(1)} %constant_dynamic-update-slice_fusion.refs_1_.refs_6_.refs_10_.refs_3_.refs_7_), channel_id=1, source_target_pairs={{0,2},{1,3},{2,4},{3,5},{4,6},{5,7},{6,0},{7,1},{8,10},{9,11},{10,... | collective-permute-start | bytes 835592 | tf_op jit(solution)/shard_map/ppermute | solution.py:224
  41.8 34.3 %copy-start.13 = (bf16[128,1024]{1,0:T(8,128)(2,1)}, bf16[128,1024]{1,0:T(8,128)(2,1)S(1)}, u32[]{:S(2)}) copy-start(bf16[128,1024]{1,0:T(8,128)(2,1)S(1)} %collective-permute-done.15.refs_13_.refs_21_) | copy-start | bytes 786436
  41.8 12.5 %collective-permute-start.17 = (bf16[128,1024]{1,0:T(8,128)(2,1)}, bf16[128,1024]{1,0:T(8,128)(2,1)}, u32[]{:S(2)}, u32[]{:S(2)}) collective-permute-start(bf16[128,1024]{1,0:T(8,128)(2,1)} %collective-permute-done.10.refs_19_.refs_27_), channel_id=1, source_target_pairs={{4,6},{5,7},{12,14},{13,15},{20,22},{21,23},{28,30},{29,31}} | collective-permute-start | bytes 786440 | tf_op jit(solution)/shard_map/ppermute | solution.py:220
  43.1 33.1 %copy-start.11 = (bf16[128,1024]{1,0:T(8,128)(2,1)}, bf16[128,1024]{1,0:T(8,128)(2,1)S(1)}, u32[]{:S(2)}) copy-start(bf16[128,1024]{1,0:T(8,128)(2,1)S(1)} %collective-permute-done.7.refs_16_.refs_24_) | copy-start | bytes 786436
  43.1 22.5 %collective-permute-start.11 = (bf16[64,2176]{1,0:T(8,128)(2,1)S(1)}, bf16[64,2176]{1,0:T(8,128)(2,1)S(1)}, u32[]{:S(2)}, u32[]{:S(2)}) collective-permute-start(bf16[64,2176]{1,0:T(8,128)(2,1)S(1)} %constant_dynamic-update-slice_fusion.refs_1_.refs_6_.refs_10_.refs_3_.refs_7_), channel_id=1, source_target_pairs={{0,4},{1,5},{2,6},{3,7},{4,0},{5,1},{6,2},{7,3},{8,12},{9,13},{10,... | collective-permute-start | bytes 835592 | tf_op jit(solution)/shard_map/ppermute | solution.py:224
  47.5 18.2 %copy-start.12 = (bf16[128,1024]{1,0:T(8,128)(2,1)}, bf16[128,1024]{1,0:T(8,128)(2,1)S(1)}, u32[]{:S(2)}) copy-start(bf16[128,1024]{1,0:T(8,128)(2,1)S(1)} %collective-permute-done.13.refs_20_.refs_28_) | copy-start | bytes 786436
  47.5 18.1 %collective-permute-start.14 = (bf16[64,2176]{1,0:T(8,128)(2,1)S(1)}, bf16[64,2176]{1,0:T(8,128)(2,1)S(1)}, u32[]{:S(2)}, u32[]{:S(2)}) collective-permute-start(bf16[64,2176]{1,0:T(8,128)(2,1)S(1)} %constant_dynamic-update-slice_fusion.refs_1_.refs_6_.refs_10_.refs_3_.refs_7_), channel_id=1, source_target_pairs={{0,6},{1,7},{2,0},{3,1},{4,2},{5,3},{6,4},{7,5},{8,14},{9,15},{10,... | collective-permute-start | bytes 835592 | tf_op jit(solution)/shard_map/ppermute | solution.py:224
  47.5 28.6 %collective-permute-start.20 = (bf16[128,1024]{1,0:T(8,128)(2,1)S(1)}, bf16[128,1024]{1,0:T(8,128)(2,1)}, u32[]{:S(2)}, u32[]{:S(2)}) collective-permute-start(bf16[128,1024]{1,0:T(8,128)(2,1)S(1)} %collective-permute-done.13.refs_20_.refs_28_), channel_id=1, source_target_pairs={{6,7},{7,6},{14,15},{15,14},{22,23},{23,22},{30,31},{31,30}} | collective-permute-start | bytes 786440 | tf_op jit(solution)/shard_map/ppermute | solution.py:216
  50.2 25.9 %collective-permute-start.18 = (bf16[128,1024]{1,0:T(8,128)(2,1)}, bf16[128,1024]{1,0:T(8,128)(2,1)}, u32[]{:S(2)}, u32[]{:S(2)}) collective-permute-start(bf16[128,1024]{1,0:T(8,128)(2,1)} %collective-permute-done.10.refs_19_.refs_27_), channel_id=1, source_target_pairs={{4,5},{5,4},{6,7},{7,6},{12,13},{13,12},{14,15},{15,14},{20,21},{2... | collective-permute-start | bytes 786440 | tf_op jit(solution)/shard_map/ppermute | solution.py:216
  54.3 21.8 %collective-permute-start.19 = (bf16[128,1024]{1,0:T(8,128)(2,1)}, bf16[128,1024]{1,0:T(8,128)(2,1)}, u32[]{:S(2)}, u32[]{:S(2)}) collective-permute-start(bf16[128,1024]{1,0:T(8,128)(2,1)} %collective-permute-done.17.refs_21_.refs_29_), channel_id=1, source_target_pairs={{6,7},{7,6},{14,15},{15,14},{22,23},{23,22},{30,31},{31,30}} | collective-permute-start | bytes 786440 | tf_op jit(solution)/shard_map/ppermute | solution.py:216
  (3 other events, 17.0 us)

commit v15 on v14

--- a/solution.py
+++ b/solution.py
@@ -18,9 +18,10 @@
 FILL = -1e30
 
 
-def halves_kernel(meta_ref, a_ref, b_ref, mine_ref, theirs_ref):
-    mine_ref[...] = a_ref[...]
-    theirs_ref[...] = b_ref[...]
+def halves_kernel(meta_ref, *refs):
+    half = refs[0].shape[1]
+    for i, ref in enumerate(refs[:4]):
+        refs[4 + i // 2][:, i % 2 * half : (i % 2 + 1) * half] = ref[...]
 
 
 def halves(kv, side):
@@ -30,15 +31,17 @@
         halves_kernel,
         grid_spec=pltpu.PrefetchScalarGridSpec(
             num_scalar_prefetch=1,
-            grid=(2,),
+            grid=(1,),
             in_specs=[
-                pl.BlockSpec(shape, lambda i, m: (0, 2 * i + m[0])),
-                pl.BlockSpec(shape, lambda i, m: (0, 2 * i + 1 - m[0])),
+                pl.BlockSpec(shape, lambda i, m: (0, m[0])),
+                pl.BlockSpec(shape, lambda i, m: (0, 2 + m[0])),
+                pl.BlockSpec(shape, lambda i, m: (0, 1 - m[0])),
+                pl.BlockSpec(shape, lambda i, m: (0, 3 - m[0])),
             ],
-            out_specs=[pl.BlockSpec(shape, lambda i, m: (0, i))] * 2,
+            out_specs=[pl.BlockSpec((rows, 2 * half), lambda i, m: (0, 0))] * 2,
         ),
         out_shape=[jax.ShapeDtypeStruct((rows, 2 * half), kv.dtype)] * 2,
-    )(side.reshape(1), kv, kv)
+    )(side.reshape(1), kv, kv, kv, kv)
 
 
 def attend_kernel(pairs, parts, tile, tiles, fresh, meta_ref, *refs):
@@ -152,11 +155,9 @@
     scalar = pl.BlockSpec(memory_space=pltpu.SMEM)
     wide = pl.BlockSpec((rows, BOTH * GQ * HD), lambda i, m: (0, m[1] + i))
     fresh = before is None
-    queries, *arrays = [
-        pltpu.with_memory_space_constraint(array, pltpu.HBM)
-        for array in (queries, *prefix, *pieces)
+    queries, *pieces = [
+        pltpu.with_memory_space_constraint(array, pltpu.HBM) for array in (queries, *pieces)
     ]
-    prefix, pieces = arrays[:parts], arrays[parts:]
     args = [meta, *([segments, *prefix] if fresh else before[1:])]
     args += [queries, *prefix, *prefix, *pieces, *pieces]
     if fresh:

time: 87.2 us -> 86.6 us (level)
  the two profiles are of different devices: /device:TPU:26 before, /device:TPU:24 now
where the time goes in v15:
time: 86.6 us; the launch traced here: 87.3 us
  starting transfers between devices  43.3 us (50%)
  Pallas kernels  21.9 us (25%)
  waiting for transfers between devices  20.2 us (23%)
  between operations  1.19 us (1%)
    ppermute x8, starting transfers between devices, swap(): lax.ppermute(value, 'resp', [(r, r ^ 1) for r in range(2 * first, count)])  25.8 us
    pallas_call x2, Pallas kernels, attend(): pl.pallas_call(functools.partial(attend_kernel, pairs, parts, tile, tiles...  19.9 us
    ppermute x6, waiting for transfers between devices, climb(): return lax.ppermute(value, 'resp', pairs)  16.7 us
    ppermute x6, starting transfers between devices, climb(): return lax.ppermute(value, 'resp', pairs)  7.7 us
    ppermute x6, starting transfers between devices, shift(): lax.ppermute(value, axis, [(r, (r + by) % size) for r in range(size)])  6.45 us
    ppermute x1, starting transfers between devices, on_device(): upper = lax.ppermute(after(mine, partner), 'resp', upper)  3.44 us
    ppermute x6, waiting for transfers between devices, shift(): lax.ppermute(value, axis, [(r, (r + by) % size) for r in range(size)])  2.76 us
    pallas_call x1, Pallas kernels, halves(): pl.pallas_call(halves_kernel, grid_spec=pltpu.PrefetchScalarGridSpec(num_...  1.95 us
  transfers between devices with their start and end apart: 21, of which 10 were waited for; matrix products, arithmetic and copies ran while one was open for 1% of the time, Pallas kernels for 11%

profile of v15, /device:TPU:24, one launch (start us, length us, event | category | flops | bytes accessed | tf_op | source)
XLA Modules:
  0.0 87.3 jit_solution(12748997386827533184)
XLA Ops:
  0.0 1.9 %shard_map.64 = (bf16[128,1024]{1,0:T(8,128)(2,1)}, bf16[128,1024]{1,0:T(8,128)(2,1)}) custom-call(s32[1]{0:T(128)} %bitcast.10.meta_ref, bf16[128,2048]{1,0:T(8,128)(2,1)} %bitcast.22, bf16[128,2048]{1,0:T(8,128)(2,1)} %bitcast.23, bf16[128,2048]{1,0:T(8,128)(2,1)} %bitcast.24, bf16[128,2048]{1,0:T(8,128)(2,1)} %bitcast.25), custom_call_target="tpu_custom_call" | custom-call | tf_op jit(solution)/shard_map/pallas_call | solution.py:30
  2.0 1.5 %collective-permute-start.8 = (bf16[128,1024]{1,0:T(8,128)(2,1)}, bf16[128,1024]{1,0:T(8,128)(2,1)S(1)}, u32[]{:S(2)}, u32[]{:S(2)}) collective-permute-start(bf16[128,1024]{1,0:T(8,128)(2,1)} %get-tuple-element.16.refs_11_.refs_19_), channel_id=1, source_target_pairs={{0,1},{1,0},{2,3},{3,2},{4,5},{5,4},{6,7},{7,6},{8,9},{9,8},{10,11... | collective-permute-start | bytes 786440 | tf_op jit(solution)/shard_map/ppermute | solution.py:217
  3.5 1.3 %collective-permute-start.5 = (bf16[128,1024]{1,0:T(8,128)(2,1)}, bf16[128,1024]{1,0:T(8,128)(2,1)S(1)}, u32[]{:S(2)}, u32[]{:S(2)}) collective-permute-start(bf16[128,1024]{1,0:T(8,128)(2,1)} %get-tuple-element.20.refs_14_.refs_22_), channel_id=1, source_target_pairs={{0,2},{1,3},{2,4},{3,5},{4,6},{5,7},{8,10},{9,11},{10,12},{11,13},... | collective-permute-start | bytes 786440 | tf_op jit(solution)/shard_map/ppermute | solution.py:221
  5.3 1.6 %collective-permute-start.1 = (bf16[8,2176]{1,0:T(8,128)(2,1)S(1)}, bf16[8,2176]{1,0:T(8,128)(2,1)S(1)}, u32[]{:S(2)}, u32[]{:S(2)}) collective-permute-start(bf16[8,2176]{1,0:T(8,128)(2,1)S(1)} %get-tuple-element.31), channel_id=1, source_target_pairs={{0,16},{8,24},{16,0},{24,8},{1,17},{9,25},{17,1},{25,9},{2,18},{10... | collective-permute-start | bytes 104456 | tf_op jit(solution)/shard_map/ppermute | solution.py:225
  6.9 1.4 %collective-permute-start.2 = (bf16[8,2176]{1,0:T(8,128)(2,1)S(1)}, bf16[8,2176]{1,0:T(8,128)(2,1)S(1)}, u32[]{:S(2)}, u32[]{:S(2)}) collective-permute-start(bf16[8,2176]{1,0:T(8,128)(2,1)S(1)} %get-tuple-element.29), channel_id=1, source_target_pairs={{0,24},{8,0},{16,8},{24,16},{1,25},{9,1},{17,9},{25,17},{2,26},{10... | collective-permute-start | bytes 104456 | tf_op jit(solution)/shard_map/ppermute | solution.py:225
  8.3 0.4 collective-permute-done
  8.7 0.7 collective-permute-done.1
  9.3 0.6 collective-permute-done.2
  9.9 0.6 collective-permute-start.3
  10.5 2.9 %collective-permute-done.5.refs_16_.refs_24_ = bf16[128,1024]{1,0:T(8,128)(2,1)S(1)} collective-permute-done((bf16[128,1024]{1,0:T(8,128)(2,1)}, bf16[128,1024]{1,0:T(8,128)(2,1)S(1)}, u32[]{:S(2)}, u32[]{:S(2)}) %collective-permute-start.5) | collective-permute-done | bytes 262176 | tf_op jit(solution)/shard_map/ppermute | solution.py:221
  13.3 1.3 %collective-permute-start.6 = (bf16[128,1024]{1,0:T(8,128)(2,1)S(1)}, bf16[128,1024]{1,0:T(8,128)(2,1)S(1)}, u32[]{:S(2)}, u32[]{:S(2)}) collective-permute-start(bf16[128,1024]{1,0:T(8,128)(2,1)S(1)} %collective-permute-done.5.refs_16_.refs_24_), channel_id=1, source_target_pairs={{2,4},{3,5},{4,6},{5,7},{10,12},{11,13},{12,14},{13,15},{18,20},{1... | collective-permute-start | bytes 786440 | tf_op jit(solution)/shard_map/ppermute | solution.py:221
  14.6 2.4 %collective-permute-start.12 = (bf16[128,1024]{1,0:T(8,128)(2,1)S(1)}, bf16[128,1024]{1,0:T(8,128)(2,1)S(1)}, u32[]{:S(2)}, u32[]{:S(2)}) collective-permute-start(bf16[128,1024]{1,0:T(8,128)(2,1)S(1)} %collective-permute-done.5.refs_16_.refs_24_), channel_id=1, source_target_pairs={{2,3},{3,2},{4,5},{5,4},{6,7},{7,6},{10,11},{11,10},{12,13},{13,12... | collective-permute-start | bytes 786440 | tf_op jit(solution)/shard_map/ppermute | solution.py:217
  17.1 1.3 %collective-permute-start.9 = (bf16[128,1024]{1,0:T(8,128)(2,1)S(1)}, bf16[128,1024]{1,0:T(8,128)(2,1)S(1)}, u32[]{:S(2)}, u32[]{:S(2)}) collective-permute-start(bf16[128,1024]{1,0:T(8,128)(2,1)S(1)} %collective-permute-done.8.refs_15_.refs_23_), channel_id=1, source_target_pairs={{0,2},{1,3},{2,4},{3,5},{4,6},{5,7},{8,10},{9,11},{10,12},{11,13},... | collective-permute-start | bytes 786440 | tf_op jit(solution)/shard_map/ppermute | solution.py:221
  18.4 3.4 %collective-permute-start.16 = (bf16[128,1024]{1,0:T(8,128)(2,1)}, bf16[128,1024]{1,0:T(8,128)(2,1)S(1)}, u32[]{:S(2)}, u32[]{:S(2)}) collective-permute-start(bf16[128,1024]{1,0:T(8,128)(2,1)} %get-tuple-element.20.refs_14_.refs_22_), channel_id=1, source_target_pairs={{0,1},{2,3},{4,5},{6,7},{8,9},{10,11},{12,13},{14,15},{16,17},{18,... | collective-permute-start | bytes 786440 | tf_op jit(solution)/shard_map/ppermute | solution.py:233
  21.8 0.8 collective-permute-done.6.refs_18_.refs_26_
  22.6 0.8 collective-permute-done.12.refs_14_.refs_22_
  23.4 1.3 %collective-permute-start.13 = (bf16[128,1024]{1,0:T(8,128)(2,1)S(1)}, bf16[128,1024]{1,0:T(8,128)(2,1)S(1)}, u32[]{:S(2)}, u32[]{:S(2)}) collective-permute-start(bf16[128,1024]{1,0:T(8,128)(2,1)S(1)} %collective-permute-done.6.refs_18_.refs_26_), channel_id=1, source_target_pairs={{4,6},{5,7},{12,14},{13,15},{20,22},{21,23},{28,30},{29,31}} | collective-permute-start | bytes 786440 | tf_op jit(solution)/shard_map/ppermute | solution.py:221
  24.7 3.6 %collective-permute-start.7 = (bf16[128,1024]{1,0:T(8,128)(2,1)S(1)}, bf16[128,1024]{1,0:T(8,128)(2,1)S(1)}, u32[]{:S(2)}, u32[]{:S(2)}) collective-permute-start(bf16[128,1024]{1,0:T(8,128)(2,1)S(1)} %collective-permute-done.6.refs_18_.refs_26_), channel_id=1, source_target_pairs={{4,5},{5,4},{6,7},{7,6},{12,13},{13,12},{14,15},{15,14},{20,21},{2... | collective-permute-start | bytes 786440 | tf_op jit(solution)/shard_map/ppermute | solution.py:217
  28.3 0.5 collective-permute-done.9.refs_17_.refs_25_
  28.8 1.3 %collective-permute-start.10 = (bf16[128,1024]{1,0:T(8,128)(2,1)S(1)}, bf16[128,1024]{1,0:T(8,128)(2,1)}, u32[]{:S(2)}, u32[]{:S(2)}) collective-permute-start(bf16[128,1024]{1,0:T(8,128)(2,1)S(1)} %collective-permute-done.9.refs_17_.refs_25_), channel_id=1, source_target_pairs={{2,4},{3,5},{4,6},{5,7},{10,12},{11,13},{12,14},{13,15},{18,20},{1... | collective-permute-start | bytes 786440 | tf_op jit(solution)/shard_map/ppermute | solution.py:221
  30.1 3.6 %collective-permute-start.15 = (bf16[128,1024]{1,0:T(8,128)(2,1)S(1)}, bf16[128,1024]{1,0:T(8,128)(2,1)S(1)}, u32[]{:S(2)}, u32[]{:S(2)}) collective-permute-start(bf16[128,1024]{1,0:T(8,128)(2,1)S(1)} %collective-permute-done.9.refs_17_.refs_25_), channel_id=1, source_target_pairs={{2,3},{3,2},{4,5},{5,4},{6,7},{7,6},{10,11},{11,10},{12,13},{13,12... | collective-permute-start | bytes 786440 | tf_op jit(solution)/shard_map/ppermute | solution.py:217
  33.9 7.2 %collective-permute-done.10.refs_19_.refs_27_ = bf16[128,1024]{1,0:T(8,128)(2,1)} collective-permute-done((bf16[128,1024]{1,0:T(8,128)(2,1)S(1)}, bf16[128,1024]{1,0:T(8,128)(2,1)}, u32[]{:S(2)}, u32[]{:S(2)}) %collective-permute-start.10) | collective-permute-done | bytes 262176 | tf_op jit(solution)/shard_map/ppermute | solution.py:221
  41.1 1.3 %collective-permute-start.17 = (bf16[128,1024]{1,0:T(8,128)(2,1)}, bf16[128,1024]{1,0:T(8,128)(2,1)}, u32[]{:S(2)}, u32[]{:S(2)}) collective-permute-start(bf16[128,1024]{1,0:T(8,128)(2,1)} %collective-permute-done.10.refs_19_.refs_27_), channel_id=1, source_target_pairs={{4,6},{5,7},{12,14},{13,15},{20,22},{21,23},{28,30},{29,31}} | collective-permute-start | bytes 786440 | tf_op jit(solution)/shard_map/ppermute | solution.py:221
  42.4 3.1 %collective-permute-start.11 = (bf16[64,2176]{1,0:T(8,128)(2,1)S(1)}, bf16[64,2176]{1,0:T(8,128)(2,1)S(1)}, u32[]{:S(2)}, u32[]{:S(2)}) collective-permute-start(bf16[64,2176]{1,0:T(8,128)(2,1)S(1)} %constant_dynamic-update-slice_fusion.refs_1_.refs_6_.refs_10_.refs_3_.refs_7_), channel_id=1, source_target_pairs={{0,4},{1,5},{2,6},{3,7},{4,0},{5,1},{6,2},{7,3},{8,12},{9,13},{10,... | collective-permute-start | bytes 835592 | tf_op jit(solution)/shard_map/ppermute | solution.py:225
  45.5 0.2 collective-permute-start.14
  45.8 3.6 %collective-permute-start.20 = (bf16[128,1024]{1,0:T(8,128)(2,1)S(1)}, bf16[128,1024]{1,0:T(8,128)(2,1)}, u32[]{:S(2)}, u32[]{:S(2)}) collective-permute-start(bf16[128,1024]{1,0:T(8,128)(2,1)S(1)} %collective-permute-done.13.refs_20_.refs_28_), channel_id=1, source_target_pairs={{6,7},{7,6},{14,15},{15,14},{22,23},{23,22},{30,31},{31,30}} | collective-permute-start | bytes 786440 | tf_op jit(solution)/shard_map/ppermute | solution.py:217
  49.4 1.1 %collective-permute-done.4.refs_2_.refs_7_.refs_11_.refs_4_.refs_8_ = bf16[64,2176]{1,0:T(8,128)(2,1)S(1)} collective-permute-done((bf16[64,2176]{1,0:T(8,128)(2,1)S(1)}, bf16[64,2176]{1,0:T(8,128)(2,1)S(1)}, u32[]{:S(2)}, u32[]{:S(2)}) %collective-permute-start.4) | collective-permute-done | bytes 278560 | tf_op jit(solution)/shard_map/ppermute | solution.py:225
  50.6 3.1 %collective-permute-start.18 = (bf16[128,1024]{1,0:T(8,128)(2,1)}, bf16[128,1024]{1,0:T(8,128)(2,1)}, u32[]{:S(2)}, u32[]{:S(2)}) collective-permute-start(bf16[128,1024]{1,0:T(8,128)(2,1)} %collective-permute-done.10.refs_19_.refs_27_), channel_id=1, source_target_pairs={{4,5},{5,4},{6,7},{7,6},{12,13},{13,12},{14,15},{15,14},{20,21},{2... | collective-permute-start | bytes 786440 | tf_op jit(solution)/shard_map/ppermute | solution.py:217
  53.6 5.3 %collective-permute-done.17.refs_21_.refs_29_ = bf16[128,1024]{1,0:T(8,128)(2,1)} collective-permute-done((bf16[128,1024]{1,0:T(8,128)(2,1)}, bf16[128,1024]{1,0:T(8,128)(2,1)}, u32[]{:S(2)}, u32[]{:S(2)}) %collective-permute-start.17) | collective-permute-done | bytes 262176 | tf_op jit(solution)/shard_map/ppermute | solution.py:221
  59.0 7.3 %collective-permute-start.19 = (bf16[128,1024]{1,0:T(8,128)(2,1)}, bf16[128,1024]{1,0:T(8,128)(2,1)}, u32[]{:S(2)}, u32[]{:S(2)}) collective-permute-start(bf16[128,1024]{1,0:T(8,128)(2,1)} %collective-permute-done.17.refs_21_.refs_29_), channel_id=1, source_target_pairs={{6,7},{7,6},{14,15},{15,14},{22,23},{23,22},{30,31},{31,30}} | collective-permute-start | bytes 786440 | tf_op jit(solution)/shard_map/ppermute | solution.py:217
  67.1 9.7 %shard_map.65 = (bf16[128,8192]{1,0:T(8,128)(2,1)}, f32[128,1280]{1,0:T(8,128)S(1)}, s32[1]{0:T(128)}) custom-call(s32[3]{0:T(128)S(1)} %add_add_fusion.1.meta_ref, s32[1,128]{1,0:T(1,128)S(1)} %copy-done, bf16[64,2176]{1,0:T(8,128)(2,1)S(1)} %constant_dynamic-update-slice_fusion.refs_1_.refs_6_.refs_10_.refs_3_.refs_7_, ...), custom_call_target="tpu_custom_call" | custom-call | tf_op jit(solution)/shard_map/pallas_call | solution.py:188
  76.9 10.3 %shard_map.66 = bf16[128,8192]{1,0:T(8,128)(2,1)} custom-call(s32[3]{0:T(128)S(1)} %add_add_fusion.meta_ref, f32[128,1280]{1,0:T(8,128)S(1)} %get-tuple-element.22.refs_0_, s32[1]{0:T(128)} %get-tuple-element.23.refs_1_, bf16[128,8192]{1,0:T(8,128)(2,1)} %bitcast.27, ...), custom_call_target="tpu_custom_call", output_to_operand_aliasing={{}: (28, {})} | custom-call | tf_op jit(solution)/shard_map/pallas_call | solution.py:188
  (52 shorter events, 0.8 us)
Async XLA Ops:
  0.0 5.0 %copy-start.10 = (bf16[4,8,2048]{2,1,0:T(8,128)(2,1)S(1)}, bf16[4,8,2048]{2,1,0:T(8,128)(2,1)}, u32[]{:S(2)}) copy-start(bf16[4,8,2048]{2,1,0:T(8,128)(2,1)} %param.9) | copy-start | bytes 393220
  0.0 5.1 %copy-start = (s32[1,128]{1,0:T(1,128)S(1)}, s32[1,128]{1,0:T(1,128)}, u32[]{:S(2)}) copy-start(s32[1,128]{1,0:T(1,128)} %refs_0_.1) | copy-start | bytes 1540
  2.0 15.1 %collective-permute-start.8 = (bf16[128,1024]{1,0:T(8,128)(2,1)}, bf16[128,1024]{1,0:T(8,128)(2,1)S(1)}, u32[]{:S(2)}, u32[]{:S(2)}) collective-permute-start(bf16[128,1024]{1,0:T(8,128)(2,1)} %get-tuple-element.16.refs_11_.refs_19_), channel_id=1, source_target_pairs={{0,1},{1,0},{2,3},{3,2},{4,5},{5,4},{6,7},{7,6},{8,9},{9,8},{10,11... | collective-permute-start | bytes 786440 | tf_op jit(solution)/shard_map/ppermute | solution.py:217
  3.5 9.9 %collective-permute-start.5 = (bf16[128,1024]{1,0:T(8,128)(2,1)}, bf16[128,1024]{1,0:T(8,128)(2,1)S(1)}, u32[]{:S(2)}, u32[]{:S(2)}) collective-permute-start(bf16[128,1024]{1,0:T(8,128)(2,1)} %get-tuple-element.20.refs_14_.refs_22_), channel_id=1, source_target_pairs={{0,2},{1,3},{2,4},{3,5},{4,6},{5,7},{8,10},{9,11},{10,12},{11,13},... | collective-permute-start | bytes 786440 | tf_op jit(solution)/shard_map/ppermute | solution.py:221
  5.2 3.4 %collective-permute-start = (bf16[8,2176]{1,0:T(8,128)(2,1)S(1)}, bf16[8,2176]{1,0:T(8,128)(2,1)S(1)}, u32[]{:S(2)}, u32[]{:S(2)}) collective-permute-start(bf16[8,2176]{1,0:T(8,128)(2,1)S(1)} %get-tuple-element.30), channel_id=1, source_target_pairs={{0,8},{8,16},{16,24},{24,0},{1,9},{9,17},{17,25},{25,1},{2,10},{10... | collective-permute-start | bytes 104456 | tf_op jit(solution)/shard_map/ppermute | solution.py:225
  5.3 4.0 %collective-permute-start.1 = (bf16[8,2176]{1,0:T(8,128)(2,1)S(1)}, bf16[8,2176]{1,0:T(8,128)(2,1)S(1)}, u32[]{:S(2)}, u32[]{:S(2)}) collective-permute-start(bf16[8,2176]{1,0:T(8,128)(2,1)S(1)} %get-tuple-element.31), channel_id=1, source_target_pairs={{0,16},{8,24},{16,0},{24,8},{1,17},{9,25},{17,1},{25,9},{2,18},{10... | collective-permute-start | bytes 104456 | tf_op jit(solution)/shard_map/ppermute | solution.py:225
  6.9 3.0 %collective-permute-start.2 = (bf16[8,2176]{1,0:T(8,128)(2,1)S(1)}, bf16[8,2176]{1,0:T(8,128)(2,1)S(1)}, u32[]{:S(2)}, u32[]{:S(2)}) collective-permute-start(bf16[8,2176]{1,0:T(8,128)(2,1)S(1)} %get-tuple-element.29), channel_id=1, source_target_pairs={{0,24},{8,0},{16,8},{24,16},{1,25},{9,1},{17,9},{25,17},{2,26},{10... | collective-permute-start | bytes 104456 | tf_op jit(solution)/shard_map/ppermute | solution.py:225
  9.9 20.2 %collective-permute-start.3 = (bf16[32,2176]{1,0:T(8,128)(2,1)S(1)}, bf16[32,2176]{1,0:T(8,128)(2,1)S(1)}, u32[]{:S(2)}, u32[]{:S(2)}) collective-permute-start(bf16[32,2176]{1,0:T(8,128)(2,1)S(1)} %pad_maximum_fusion), channel_id=1, source_target_pairs={{0,1},{1,0},{2,3},{3,2},{4,5},{5,4},{6,7},{7,6},{8,9},{9,8},{10,11... | collective-permute-start | bytes 417800 | tf_op jit(solution)/shard_map/ppermute | solution.py:217
  13.3 53.7 %copy-start.2 = (bf16[128,1024]{1,0:T(8,128)(2,1)}, bf16[128,1024]{1,0:T(8,128)(2,1)S(1)}, u32[]{:S(2)}) copy-start(bf16[128,1024]{1,0:T(8,128)(2,1)S(1)} %collective-permute-done.5.refs_16_.refs_24_) | copy-start | bytes 786436
  13.3 9.3 %collective-permute-start.6 = (bf16[128,1024]{1,0:T(8,128)(2,1)S(1)}, bf16[128,1024]{1,0:T(8,128)(2,1)S(1)}, u32[]{:S(2)}, u32[]{:S(2)}) collective-permute-start(bf16[128,1024]{1,0:T(8,128)(2,1)S(1)} %collective-permute-done.5.refs_16_.refs_24_), channel_id=1, source_target_pairs={{2,4},{3,5},{4,6},{5,7},{10,12},{11,13},{12,14},{13,15},{18,20},{1... | collective-permute-start | bytes 786440 | tf_op jit(solution)/shard_map/ppermute | solution.py:221
  14.6 8.8 %collective-permute-start.12 = (bf16[128,1024]{1,0:T(8,128)(2,1)S(1)}, bf16[128,1024]{1,0:T(8,128)(2,1)S(1)}, u32[]{:S(2)}, u32[]{:S(2)}) collective-permute-start(bf16[128,1024]{1,0:T(8,128)(2,1)S(1)} %collective-permute-done.5.refs_16_.refs_24_), channel_id=1, source_target_pairs={{2,3},{3,2},{4,5},{5,4},{6,7},{7,6},{10,11},{11,10},{12,13},{13,12... | collective-permute-start | bytes 786440 | tf_op jit(solution)/shard_map/ppermute | solution.py:217
  17.1 50.0 %copy-start.1 = (bf16[128,1024]{1,0:T(8,128)(2,1)}, bf16[128,1024]{1,0:T(8,128)(2,1)S(1)}, u32[]{:S(2)}) copy-start(bf16[128,1024]{1,0:T(8,128)(2,1)S(1)} %collective-permute-done.8.refs_15_.refs_23_) | copy-start | bytes 786436
  17.1 11.8 %collective-permute-start.9 = (bf16[128,1024]{1,0:T(8,128)(2,1)S(1)}, bf16[128,1024]{1,0:T(8,128)(2,1)S(1)}, u32[]{:S(2)}, u32[]{:S(2)}) collective-permute-start(bf16[128,1024]{1,0:T(8,128)(2,1)S(1)} %collective-permute-done.8.refs_15_.refs_23_), channel_id=1, source_target_pairs={{0,2},{1,3},{2,4},{3,5},{4,6},{5,7},{8,10},{9,11},{10,12},{11,13},... | collective-permute-start | bytes 786440 | tf_op jit(solution)/shard_map/ppermute | solution.py:221
  18.4 15.4 %collective-permute-start.16 = (bf16[128,1024]{1,0:T(8,128)(2,1)}, bf16[128,1024]{1,0:T(8,128)(2,1)S(1)}, u32[]{:S(2)}, u32[]{:S(2)}) collective-permute-start(bf16[128,1024]{1,0:T(8,128)(2,1)} %get-tuple-element.20.refs_14_.refs_22_), channel_id=1, source_target_pairs={{0,1},{2,3},{4,5},{6,7},{8,9},{10,11},{12,13},{14,15},{16,17},{18,... | collective-permute-start | bytes 786440 | tf_op jit(solution)/shard_map/ppermute | solution.py:233
  22.6 44.5 %copy-start.5 = (bf16[128,1024]{1,0:T(8,128)(2,1)}, bf16[128,1024]{1,0:T(8,128)(2,1)S(1)}, u32[]{:S(2)}) copy-start(bf16[128,1024]{1,0:T(8,128)(2,1)S(1)} %collective-permute-done.6.refs_18_.refs_26_) | copy-start | bytes 786436
  23.4 53.4 %copy-start.3 = (bf16[128,1024]{1,0:T(8,128)(2,1)}, bf16[128,1024]{1,0:T(8,128)(2,1)S(1)}, u32[]{:S(2)}) copy-start(bf16[128,1024]{1,0:T(8,128)(2,1)S(1)} %collective-permute-done.12.refs_14_.refs_22_) | copy-start | bytes 786436
  23.4 22.1 %collective-permute-start.13 = (bf16[128,1024]{1,0:T(8,128)(2,1)S(1)}, bf16[128,1024]{1,0:T(8,128)(2,1)S(1)}, u32[]{:S(2)}, u32[]{:S(2)}) collective-permute-start(bf16[128,1024]{1,0:T(8,128)(2,1)S(1)} %collective-permute-done.6.refs_18_.refs_26_), channel_id=1, source_target_pairs={{4,6},{5,7},{12,14},{13,15},{20,22},{21,23},{28,30},{29,31}} | collective-permute-start | bytes 786440 | tf_op jit(solution)/shard_map/ppermute | solution.py:221
  24.7 17.7 %collective-permute-start.7 = (bf16[128,1024]{1,0:T(8,128)(2,1)S(1)}, bf16[128,1024]{1,0:T(8,128)(2,1)S(1)}, u32[]{:S(2)}, u32[]{:S(2)}) collective-permute-start(bf16[128,1024]{1,0:T(8,128)(2,1)S(1)} %collective-permute-done.6.refs_18_.refs_26_), channel_id=1, source_target_pairs={{4,5},{5,4},{6,7},{7,6},{12,13},{13,12},{14,15},{15,14},{20,21},{2... | collective-permute-start | bytes 786440 | tf_op jit(solution)/shard_map/ppermute | solution.py:217
  28.8 38.3 %copy-start.6 = (bf16[128,1024]{1,0:T(8,128)(2,1)}, bf16[128,1024]{1,0:T(8,128)(2,1)S(1)}, u32[]{:S(2)}) copy-start(bf16[128,1024]{1,0:T(8,128)(2,1)S(1)} %collective-permute-done.9.refs_17_.refs_25_) | copy-start | bytes 786436
  28.8 12.2 %collective-permute-start.10 = (bf16[128,1024]{1,0:T(8,128)(2,1)S(1)}, bf16[128,1024]{1,0:T(8,128)(2,1)}, u32[]{:S(2)}, u32[]{:S(2)}) collective-permute-start(bf16[128,1024]{1,0:T(8,128)(2,1)S(1)} %collective-permute-done.9.refs_17_.refs_25_), channel_id=1, source_target_pairs={{2,4},{3,5},{4,6},{5,7},{10,12},{11,13},{12,14},{13,15},{18,20},{1... | collective-permute-start | bytes 786440 | tf_op jit(solution)/shard_map/ppermute | solution.py:221
  30.1 10.9 %collective-permute-start.15 = (bf16[128,1024]{1,0:T(8,128)(2,1)S(1)}, bf16[128,1024]{1,0:T(8,128)(2,1)S(1)}, u32[]{:S(2)}, u32[]{:S(2)}) collective-permute-start(bf16[128,1024]{1,0:T(8,128)(2,1)S(1)} %collective-permute-done.9.refs_17_.refs_25_), channel_id=1, source_target_pairs={{2,3},{3,2},{4,5},{5,4},{6,7},{7,6},{10,11},{11,10},{12,13},{13,12... | collective-permute-start | bytes 786440 | tf_op jit(solution)/shard_map/ppermute | solution.py:217
  33.8 43.0 %copy-start.4 = (bf16[128,1024]{1,0:T(8,128)(2,1)}, bf16[128,1024]{1,0:T(8,128)(2,1)S(1)}, u32[]{:S(2)}) copy-start(bf16[128,1024]{1,0:T(8,128)(2,1)S(1)} %collective-permute-done.16.refs_12_.refs_20_) | copy-start | bytes 786436
  33.8 16.7 %collective-permute-start.4 = (bf16[64,2176]{1,0:T(8,128)(2,1)S(1)}, bf16[64,2176]{1,0:T(8,128)(2,1)S(1)}, u32[]{:S(2)}, u32[]{:S(2)}) collective-permute-start(bf16[64,2176]{1,0:T(8,128)(2,1)S(1)} %constant_dynamic-update-slice_fusion.refs_1_.refs_6_.refs_10_.refs_3_.refs_7_), channel_id=1, source_target_pairs={{0,2},{1,3},{2,4},{3,5},{4,6},{5,7},{6,0},{7,1},{8,10},{9,11},{10,... | collective-permute-start | bytes 835592 | tf_op jit(solution)/shard_map/ppermute | solution.py:225
  41.1 35.8 %copy-start.9 = (bf16[128,1024]{1,0:T(8,128)(2,1)}, bf16[128,1024]{1,0:T(8,128)(2,1)S(1)}, u32[]{:S(2)}) copy-start(bf16[128,1024]{1,0:T(8,128)(2,1)S(1)} %collective-permute-done.15.refs_13_.refs_21_) | copy-start | bytes 786436
  41.1 17.9 %collective-permute-start.17 = (bf16[128,1024]{1,0:T(8,128)(2,1)}, bf16[128,1024]{1,0:T(8,128)(2,1)}, u32[]{:S(2)}, u32[]{:S(2)}) collective-permute-start(bf16[128,1024]{1,0:T(8,128)(2,1)} %collective-permute-done.10.refs_19_.refs_27_), channel_id=1, source_target_pairs={{4,6},{5,7},{12,14},{13,15},{20,22},{21,23},{28,30},{29,31}} | collective-permute-start | bytes 786440 | tf_op jit(solution)/shard_map/ppermute | solution.py:221
  42.4 34.5 %copy-start.7 = (bf16[128,1024]{1,0:T(8,128)(2,1)}, bf16[128,1024]{1,0:T(8,128)(2,1)S(1)}, u32[]{:S(2)}) copy-start(bf16[128,1024]{1,0:T(8,128)(2,1)S(1)} %collective-permute-done.7.refs_16_.refs_24_) | copy-start | bytes 786436
  42.4 24.7 %collective-permute-start.11 = (bf16[64,2176]{1,0:T(8,128)(2,1)S(1)}, bf16[64,2176]{1,0:T(8,128)(2,1)S(1)}, u32[]{:S(2)}, u32[]{:S(2)}) collective-permute-start(bf16[64,2176]{1,0:T(8,128)(2,1)S(1)} %constant_dynamic-update-slice_fusion.refs_1_.refs_6_.refs_10_.refs_3_.refs_7_), channel_id=1, source_target_pairs={{0,4},{1,5},{2,6},{3,7},{4,0},{5,1},{6,2},{7,3},{8,12},{9,13},{10,... | collective-permute-start | bytes 835592 | tf_op jit(solution)/shard_map/ppermute | solution.py:225
  45.5 21.6 %copy-start.8 = (bf16[128,1024]{1,0:T(8,128)(2,1)}, bf16[128,1024]{1,0:T(8,128)(2,1)S(1)}, u32[]{:S(2)}) copy-start(bf16[128,1024]{1,0:T(8,128)(2,1)S(1)} %collective-permute-done.13.refs_20_.refs_28_) | copy-start | bytes 786436
  45.5 21.6 %collective-permute-start.14 = (bf16[64,2176]{1,0:T(8,128)(2,1)S(1)}, bf16[64,2176]{1,0:T(8,128)(2,1)S(1)}, u32[]{:S(2)}, u32[]{:S(2)}) collective-permute-start(bf16[64,2176]{1,0:T(8,128)(2,1)S(1)} %constant_dynamic-update-slice_fusion.refs_1_.refs_6_.refs_10_.refs_3_.refs_7_), channel_id=1, source_target_pairs={{0,6},{1,7},{2,0},{3,1},{4,2},{5,3},{6,4},{7,5},{8,14},{9,15},{10,... | collective-permute-start | bytes 835592 | tf_op jit(solution)/shard_map/ppermute | solution.py:225
  45.8 31.1 %collective-permute-start.20 = (bf16[128,1024]{1,0:T(8,128)(2,1)S(1)}, bf16[128,1024]{1,0:T(8,128)(2,1)}, u32[]{:S(2)}, u32[]{:S(2)}) collective-permute-start(bf16[128,1024]{1,0:T(8,128)(2,1)S(1)} %collective-permute-done.13.refs_20_.refs_28_), channel_id=1, source_target_pairs={{6,7},{7,6},{14,15},{15,14},{22,23},{23,22},{30,31},{31,30}} | collective-permute-start | bytes 786440 | tf_op jit(solution)/shard_map/ppermute | solution.py:217
  50.6 26.3 %collective-permute-start.18 = (bf16[128,1024]{1,0:T(8,128)(2,1)}, bf16[128,1024]{1,0:T(8,128)(2,1)}, u32[]{:S(2)}, u32[]{:S(2)}) collective-permute-start(bf16[128,1024]{1,0:T(8,128)(2,1)} %collective-permute-done.10.refs_19_.refs_27_), channel_id=1, source_target_pairs={{4,5},{5,4},{6,7},{7,6},{12,13},{13,12},{14,15},{15,14},{20,21},{2... | collective-permute-start | bytes 786440 | tf_op jit(solution)/shard_map/ppermute | solution.py:217
  59.0 17.9 %collective-permute-start.19 = (bf16[128,1024]{1,0:T(8,128)(2,1)}, bf16[128,1024]{1,0:T(8,128)(2,1)}, u32[]{:S(2)}, u32[]{:S(2)}) collective-permute-start(bf16[128,1024]{1,0:T(8,128)(2,1)} %collective-permute-done.17.refs_21_.refs_29_), channel_id=1, source_target_pairs={{6,7},{7,6},{14,15},{15,14},{22,23},{23,22},{30,31},{31,30}} | collective-permute-start | bytes 786440 | tf_op jit(solution)/shard_map/ppermute | solution.py:217
  (1 other events, 4.8 us)
